TPU v7x, 32 devices: a whole 2x2x4 slice. The times are simulated.
32 devices in a mesh: fsdp: 4 (over z), context: 4 (over x, core), tensor: 2 (over y).
Axes of the slice: x: 2, y: 2, z: 4, core: 2. Of those that a mesh axis runs over, the one named last changes fastest.
Arguments:
- tokens: bfloat16 [2, 4, 2048, 1024], P(None, 'fsdp', 'context'), may hold values from -6 to 6
- cotangent: bfloat16 [2, 4, 2048, 1024], P(None, 'fsdp', 'context'), may hold values from -6 to 6
- doc_lengths: int32 [2, 4, 4], P(None, 'fsdp'), may hold values from 1 to 2045, as said below
- mixer_gain: bfloat16 [1024], P('fsdp'), may hold values from 0.5 to 1.5
- w_query: bfloat16 [1024, 512], P('fsdp', 'tensor'), may hold values from -0.1875 to 0.1875
- key_matrix: bfloat16 [1024, 128], P('fsdp', 'tensor'), may hold values from -0.1875 to 0.1875
- value_matrix: bfloat16 [1024, 128], P('fsdp', 'tensor'), may hold values from -0.1875 to 0.1875
- mamba_gate_weight: bfloat16 [1024, 1536], P('fsdp', 'tensor'), may hold values from -0.1875 to 0.1875
- mamba_input_weight: bfloat16 [1024, 1536], P('fsdp', 'tensor'), may hold values from -0.1875 to 0.1875
- w_bproj: bfloat16 [1024, 128], P('fsdp'), may hold values from -0.09375 to 0.09375
- w_cproj: bfloat16 [1024, 128], P('fsdp'), may hold values from -0.09375 to 0.09375
- w_dt: bfloat16 [1024, 24], P('fsdp', 'tensor'), may hold values from -0.1875 to 0.1875
- a_log: float32 [24], P('tensor'), may hold values from -6 to 0
- dt_bias: float32 [24], P('tensor'), may hold values from -5 to -1
- d_skip: float32 [24], P('tensor'), may hold values from 0.5 to 1.5
- w_attn_out: bfloat16 [512, 1024], P('tensor', 'fsdp'), may hold values from -0.25 to 0.25
- w_mixer_out: bfloat16 [1536, 1024], P('tensor', 'fsdp'), may hold values from -0.15625 to 0.15625
- ffn_gain: bfloat16 [1024], P('fsdp'), may hold values from 0.5 to 1.5
- w_gate: bfloat16 [1024, 2048], P('fsdp', 'tensor'), may hold values from -0.1875 to 0.1875
- w_up: bfloat16 [1024, 2048], P('fsdp', 'tensor'), may hold values from -0.1875 to 0.1875
- w_down: bfloat16 [2048, 1024], P('tensor', 'fsdp'), may hold values from -0.25 to 0.25
Outputs:
- layer_out: bfloat16 [2, 4, 2048, 1024], P(None, 'fsdp', 'context')
- grad_tokens: float32 [2, 4, 2048, 1024], P(None, 'fsdp', 'context')
- grad_mixer_gain: float32 [1024], P('fsdp')
- grad_query: float32 [1024, 512], P('fsdp', 'tensor')
- grad_key: float32 [1024, 128], P('fsdp', 'tensor')
- grad_value: float32 [1024, 128], P('fsdp', 'tensor')
- grad_z: float32 [1024, 1536], P('fsdp', 'tensor')
- grad_xin: float32 [1024, 1536], P('fsdp', 'tensor')
- grad_bproj: float32 [1024, 128], P('fsdp')
- grad_cproj: float32 [1024, 128], P('fsdp')
- grad_dt: float32 [1024, 24], P('fsdp', 'tensor')
- grad_a_log: float32 [24], P('tensor')
- grad_dt_bias: float32 [24], P('tensor')
- grad_d_skip: float32 [24], P('tensor')
- grad_attn_out: float32 [512, 1024], P('tensor', 'fsdp')
- grad_mixer_out: float32 [1536, 1024], P('tensor', 'fsdp')
- grad_ffn_gain: float32 [1024], P('fsdp')
- grad_gate: float32 [1024, 2048], P('fsdp', 'tensor')
- grad_up: float32 [1024, 2048], P('fsdp', 'tensor')
- grad_down: float32 [2048, 1024], P('tensor', 'fsdp')
Inputs may be any that keep to these rules, and one draw needn't show every extreme that they name: `doc_lengths`: the 4 lengths of a sequence sum to 2048.
All inputs are finite; a program needn't handle non-finite values.
Results may differ from a plain program's by a relative error of at most 0.019.
Values may be sent and summed in bfloat16 or wider, within the bound.
No kernel may reach another device: no remote copies, remote signals or barrier semaphores. Data moves between devices by JAX's collectives and lax.ppermute only.
A program may use at most 160 MiB of HBM per device.

v0:
```python
import jax
import jax.numpy as jnp
from jax import lax
from jax.sharding import PartitionSpec as P

HEAD_WIDTH = 64


EPSILON = 1e-06
PRECISE = lax.Precision.HIGHEST


def carried_in(x, axis, combine, identity):
    length, index = (lax.axis_size(axis), lax.axis_index(axis))
    everything = jax.tree.map(lambda part: lax.all_gather(part, axis), x)
    start = jax.tree.map(
        lambda part, zero: jnp.broadcast_to(jnp.asarray(zero, part.dtype), part.shape), x, identity
    )

    def step(k, before):
        reached = k < index
        new = combine(before, jax.tree.map(lambda part: part[k], everything))
        return jax.tree.map(lambda a, b: jnp.where(reached, a, b), new, before)

    return lax.fori_loop(0, length, step, start)


def carried_in_2(x, axis, combine, identity):
    length, index = (lax.axis_size(axis), lax.axis_index(axis))
    everything = jax.tree.map(
        lambda part, kind: lax.all_gather(part.astype(kind), axis),
        x,
        jax.tree.map(lambda a: jnp.bfloat16 if a.dtype == jnp.float32 else a.dtype, x),
    )
    start = jax.tree.map(
        lambda part, zero: jnp.broadcast_to(jnp.asarray(zero, part.dtype), part.shape), x, identity
    )

    def step(k, before):
        at = length - 1 - k
        reached = at > index
        new = combine(
            before, jax.tree.map(lambda part, own: part[at].astype(own.dtype), everything, x)
        )
        return jax.tree.map(lambda a, b: jnp.where(reached, a, b), new, before)

    return lax.fori_loop(0, length, step, start)


def segment_ids(doc_lens, positions):
    doc_ends = jnp.cumsum(doc_lens, axis=-1)
    return jnp.sum((doc_ends[:, None, :] <= positions[None, :, None]).astype(jnp.int32), axis=2)


def state_chain(earlier, later_part):
    return (
        earlier[0] * later_part[0],
        later_part[0][:, :, None, None] * earlier[1] + later_part[1],
    )


def decay_terms(raw_step, a_log, dt_bias):
    step_size = jax.nn.softplus(raw_step + dt_bias)
    log_rate = -jnp.exp(a_log) * step_size
    block_len = raw_step.shape[1]
    tri_lower = (jnp.arange(block_len)[:, None] >= jnp.arange(block_len)[None, :]).astype(
        jnp.float32
    )
    log_decay = jnp.einsum("tu,suh->sht", tri_lower, log_rate, precision=PRECISE)
    return (jnp.swapaxes(step_size, 1, 2), log_decay)


def mixer_values(
    x_in, b_in, c_in, step_in, z_in, log_a, bias_in, skip_in, state_in, inside, carried
):
    step_size, log_decay = decay_terms(step_in, log_a, bias_in)
    log_gap = jnp.where(
        inside[:, None], log_decay[:, :, :, None] - log_decay[:, :, None, :], -10000.0
    )
    inner_prod = jnp.einsum("stn,sun->stu", c_in, b_in, precision=PRECISE)
    kernel = jnp.exp(log_gap) * inner_prod[:, None] * step_size[:, :, None, :]
    result = jnp.einsum("shtu,suhp->sthp", kernel, x_in, precision=PRECISE)
    entering = jnp.where(carried[:, None, :], jnp.exp(log_decay), 0.0)
    state_read = jnp.einsum("stn,shpn->sthp", c_in, state_in, precision=PRECISE)
    result = result + state_read * jnp.swapaxes(entering, 1, 2)[..., None] + skip_in[:, None] * x_in
    return result * jax.nn.silu(z_in)


def mixer_state(x_in, b_in, step_in, log_a, bias_in, closing, carried_last):
    step_size, log_decay = decay_terms(step_in, log_a, bias_in)
    final_log = log_decay[:, :, -1:]
    weights = jnp.where(closing[:, None, :], jnp.exp(final_log - log_decay), 0.0) * step_size
    span_state = jnp.einsum("sht,sthp,stn->shpn", weights, x_in, b_in, precision=PRECISE)
    passing = jnp.where(carried_last[:, None], jnp.exp(final_log[:, :, 0]), 0.0)
    return (passing, span_state)


def norm_forward(hidden, gain_vec):
    inv_scale = lax.rsqrt(jnp.mean(hidden * hidden, axis=-1, keepdims=True) + EPSILON)
    return (inv_scale, (hidden * inv_scale * gain_vec).astype(jnp.bfloat16))


def norm_backward(hidden, inv_scale, gain_vec, d_normed):
    weighted = gain_vec * d_normed
    d_hidden = inv_scale * weighted - hidden * inv_scale**3 * jnp.mean(
        weighted * hidden, axis=-1, keepdims=True
    )
    return (d_hidden, jnp.sum(d_normed * hidden * inv_scale, axis=0))


def mat_mul(left, right):
    return jnp.dot(left, right, preferred_element_type=jnp.float32)


def mat_mul_t(left, right):
    return lax.dot_general(
        left, right, (((1,), (1,)), ((), ())), preferred_element_type=jnp.float32
    )


def outer_sum(left, right):
    return lax.dot_general(
        left, right, (((0,), (0,)), ((), ())), preferred_element_type=jnp.float32
    )


def masked_scores(queries, projected_keys, allowed):
    scores = (
        jnp.einsum("stgqd,sjgd->sgqtj", queries, projected_keys, preferred_element_type=jnp.float32)
        * 0.125
    )
    return jnp.where(allowed[:, None, None], scores, -1e30)


def per_device(
    tokens,
    cotangent,
    doc_lengths,
    mixer_gain,
    w_query,
    key_matrix,
    value_matrix,
    mamba_gate_weight,
    mamba_input_weight,
    w_bproj,
    w_cproj,
    w_dt,
    a_log,
    dt_bias,
    d_skip,
    w_attn_out,
    w_mixer_out,
    ffn_gain,
    w_gate,
    w_up,
    w_down,
):
    micro_count, seq_count, block_len, model_dim = tokens.shape
    row_count = seq_count * block_len
    ssm_heads = w_dt.shape[1]
    ssm_dim = mamba_gate_weight.shape[1] // ssm_heads
    kv_heads = key_matrix.shape[1] // HEAD_WIDTH
    q_group = w_query.shape[1] // (HEAD_WIDTH * kv_heads)
    kv_width = kv_heads * HEAD_WIDTH
    state_dim = w_bproj.shape[1]
    ctx_index = lax.axis_index("context")
    full_len = lax.axis_size("context") * block_len

    def fetch_weights():
        return (
            lax.all_gather(mixer_gain, "fsdp", axis=0, tiled=True),
            lax.all_gather(w_query, "fsdp", axis=0, tiled=True),
            lax.all_gather(key_matrix, "fsdp", axis=0, tiled=True),
            lax.all_gather(value_matrix, "fsdp", axis=0, tiled=True),
            lax.all_gather(mamba_gate_weight, "fsdp", axis=0, tiled=True),
            lax.all_gather(mamba_input_weight, "fsdp", axis=0, tiled=True),
            lax.all_gather(w_bproj, "fsdp", axis=0, tiled=True),
            lax.all_gather(w_cproj, "fsdp", axis=0, tiled=True),
            lax.all_gather(w_dt, "fsdp", axis=0, tiled=True),
            lax.all_gather(ffn_gain, "fsdp", axis=0, tiled=True),
            lax.all_gather(w_gate, "fsdp", axis=0, tiled=True),
            lax.all_gather(w_up, "fsdp", axis=0, tiled=True),
            lax.all_gather(w_attn_out, "fsdp", axis=1, tiled=True),
            lax.all_gather(w_mixer_out, "fsdp", axis=1, tiled=True),
            lax.all_gather(w_down, "fsdp", axis=1, tiled=True),
        )

    layer_outs = []
    input_grads = []
    totals = None
    for micro_step in range(micro_count):
        gathered = fetch_weights()
        (
            gain_one,
            q_weight,
            k_weight,
            v_weight,
            z_weight,
            x_weight,
            b_weight,
            c_weight,
            dt_weight,
            gain_two,
            gate_weight,
            up_weight,
            attn_weight,
            mixer_weight,
            down_weight,
        ) = gathered
        kv_weight = jnp.concatenate([k_weight, v_weight], axis=1)
        inputs = tokens[micro_step].reshape(row_count, model_dim).astype(jnp.float32)
        doc_lens = doc_lengths[micro_step]
        gain_f1 = gain_one.astype(jnp.float32)
        scale_one, first_normed_input = norm_forward(inputs, gain_f1)
        queries = mat_mul(first_normed_input, q_weight).astype(jnp.bfloat16)
        kv_here = (
            mat_mul(first_normed_input, kv_weight)
            .astype(jnp.bfloat16)
            .reshape(seq_count, block_len, 2 * kv_width)
        )
        z_raw = mat_mul(first_normed_input, z_weight)
        x_raw = mat_mul(first_normed_input, x_weight)
        b_raw = mat_mul(first_normed_input, b_weight)
        c_raw = mat_mul(first_normed_input, c_weight)
        step_raw = mat_mul(first_normed_input, dt_weight)
        kv_all = lax.all_gather(kv_here, "context", axis=1, tiled=True)
        keys_all = kv_all[:, :, :kv_width].reshape(seq_count, full_len, kv_heads, HEAD_WIDTH)
        values_all = kv_all[:, :, kv_width:].reshape(seq_count, full_len, kv_heads, HEAD_WIDTH)
        q_heads = queries.reshape(seq_count, block_len, kv_heads, q_group, HEAD_WIDTH)
        positions = jnp.arange(full_len)
        seg_all = segment_ids(doc_lens, positions)
        seg_here = lax.dynamic_slice_in_dim(seg_all, ctx_index * block_len, block_len, 1)
        seg_prev = segment_ids(doc_lens, jnp.reshape(ctx_index * block_len - 1, (1,)))
        q_pos = ctx_index * block_len + jnp.arange(block_len)
        allowed = (positions[None, None, :] <= q_pos[None, :, None]) & (
            seg_all[:, None, :] == seg_here[:, :, None]
        )
        scores = masked_scores(q_heads, keys_all, allowed)
        row_max = jnp.max(scores, axis=-1, keepdims=True)
        log_total = row_max + jnp.log(jnp.sum(jnp.exp(scores - row_max), axis=-1, keepdims=True))
        attn_prob = jnp.exp(scores - log_total).astype(jnp.bfloat16)
        attended = jnp.einsum(
            "sgqtj,sjgd->stgqd", attn_prob, values_all, preferred_element_type=jnp.float32
        )
        attended = attended.astype(jnp.bfloat16).reshape(row_count, -1)
        x_ssm = x_raw.reshape(seq_count, block_len, ssm_heads, ssm_dim)
        z_ssm = z_raw.reshape(seq_count, block_len, ssm_heads, ssm_dim)
        b_ssm = b_raw.reshape(seq_count, block_len, state_dim)
        c_ssm = c_raw.reshape(seq_count, block_len, state_dim)
        step_ssm = step_raw.reshape(seq_count, block_len, ssm_heads)
        tri_mask = jnp.arange(block_len)[:, None] >= jnp.arange(block_len)[None, :]
        inside = tri_mask[None] & (seg_here[:, :, None] == seg_here[:, None, :])
        carried = seg_here == seg_prev
        closing = seg_here == seg_here[:, -1:]
        passing, span_state = mixer_state(
            x_ssm, b_ssm, step_ssm, a_log, dt_bias, closing, carried[:, -1]
        )
        unit_part = (jnp.ones_like(passing), jnp.zeros_like(span_state))
        prior_part = carried_in((passing, span_state), "context", state_chain, unit_part)
        entering_state = prior_part[1]
        gated = mixer_values(
            x_ssm,
            b_ssm,
            c_ssm,
            step_ssm,
            z_ssm,
            a_log,
            dt_bias,
            d_skip,
            entering_state,
            inside,
            carried,
        )
        gated_low = gated.reshape(row_count, -1).astype(jnp.bfloat16)
        mixed = lax.psum(
            mat_mul(attended, attn_weight) + mat_mul(gated_low, mixer_weight), "tensor"
        )
        hidden_one = inputs + mixed
        gain_f2 = gain_two.astype(jnp.float32)
        scale_two, normed_two = norm_forward(hidden_one, gain_f2)
        gate_pre = mat_mul(normed_two, gate_weight)
        up_pre = mat_mul(normed_two, up_weight)
        activated = (jax.nn.silu(gate_pre) * up_pre).astype(jnp.bfloat16)
        ffn_out = lax.psum(mat_mul(activated, down_weight).astype(jnp.bfloat16), "tensor").astype(
            jnp.float32
        )
        layer_outs.append(
            (hidden_one + ffn_out).astype(jnp.bfloat16).reshape(seq_count, block_len, model_dim)
        )
        gathered = fetch_weights()
        (
            gain_one,
            q_weight,
            k_weight,
            v_weight,
            z_weight,
            x_weight,
            b_weight,
            c_weight,
            dt_weight,
            gain_two,
            gate_weight,
            up_weight,
            attn_weight,
            mixer_weight,
            down_weight,
        ) = gathered
        kv_weight = jnp.concatenate([k_weight, v_weight], axis=1)
        d_out = cotangent[micro_step].reshape(row_count, model_dim)
        d_act = mat_mul_t(d_out, down_weight)
        sig_gate = jax.nn.sigmoid(gate_pre)
        d_gate = (d_act * up_pre * sig_gate * (1.0 + gate_pre * (1.0 - sig_gate))).astype(
            jnp.bfloat16
        )
        d_up = (d_act * gate_pre * sig_gate).astype(jnp.bfloat16)
        grad_down = outer_sum(activated, d_out)
        grad_gate = outer_sum(normed_two, d_gate)
        grad_up = outer_sum(normed_two, d_up)
        d_normed_two = lax.psum(
            mat_mul_t(d_gate, gate_weight) + mat_mul_t(d_up, up_weight), "tensor"
        )
        d_hidden, grad_gain_two = norm_backward(hidden_one, scale_two, gain_f2, d_normed_two)
        d_hidden = d_hidden + d_out.astype(jnp.float32)
        d_mixed = d_hidden.astype(jnp.bfloat16)
        grad_attn_out = outer_sum(attended, d_mixed)
        grad_mixer_out = outer_sum(gated_low, d_mixed)
        d_attended = mat_mul_t(d_mixed, attn_weight).astype(jnp.bfloat16)
        d_attended = d_attended.reshape(seq_count, block_len, kv_heads, q_group, HEAD_WIDTH)
        d_gated = mat_mul_t(d_mixed, mixer_weight).reshape(seq_count, block_len, ssm_heads, ssm_dim)
        scores = masked_scores(q_heads, keys_all, allowed)
        prob_full = jnp.exp(scores - log_total)
        d_prob = jnp.einsum(
            "stgqd,sjgd->sgqtj", d_attended, values_all, preferred_element_type=jnp.float32
        )
        d_values = jnp.einsum(
            "sgqtj,stgqd->sjgd",
            prob_full.astype(jnp.bfloat16),
            d_attended,
            preferred_element_type=jnp.float32,
        )
        d_scores = prob_full * (d_prob - jnp.sum(prob_full * d_prob, axis=-1, keepdims=True))
        d_scores = d_scores.astype(jnp.bfloat16)
        d_queries = (
            jnp.einsum("sgqtj,sjgd->stgqd", d_scores, keys_all, preferred_element_type=jnp.float32)
            * 0.125
        )
        d_queries = d_queries.astype(jnp.bfloat16).reshape(row_count, -1)
        d_keys = (
            jnp.einsum("sgqtj,stgqd->sjgd", d_scores, q_heads, preferred_element_type=jnp.float32)
            * 0.125
        )
        d_kv_all = jnp.concatenate(
            [
                d_keys.reshape(seq_count, full_len, kv_width),
                d_values.reshape(seq_count, full_len, kv_width),
            ],
            axis=2,
        )
        d_kv = lax.psum_scatter(
            d_kv_all.astype(jnp.bfloat16), "context", scatter_dimension=1, tiled=True
        ).astype(jnp.float32)
        d_kv = d_kv.astype(jnp.bfloat16).reshape(row_count, 2 * kv_width)

        def values_of(x_in, b_in, c_in, step_in, z_in, log_a, bias_in, skip_in, state_in):
            return mixer_values(
                x_in, b_in, c_in, step_in, z_in, log_a, bias_in, skip_in, state_in, inside, carried
            )

        pull_values = jax.vjp(
            values_of, x_ssm, b_ssm, c_ssm, step_ssm, z_ssm, a_log, dt_bias, d_skip, entering_state
        )[1]
        gx_one, gb_one, gc_one, gstep_one, gz_one, ga_one, gbias_one, gskip, local_g = pull_values(
            d_gated
        )
        later_g = carried_in_2((passing, local_g), "context", state_chain, unit_part)[1]
        d_passing = jnp.sum(later_g * entering_state, axis=(2, 3))

        def state_of(x_in, b_in, step_in, log_a, bias_in):
            return mixer_state(x_in, b_in, step_in, log_a, bias_in, closing, carried[:, -1])

        pull_state = jax.vjp(state_of, x_ssm, b_ssm, step_ssm, a_log, dt_bias)[1]
        gx_two, gb_two, gstep_two, ga_two, gbias_two = pull_state((d_passing, later_g))
        d_x = (gx_one + gx_two).reshape(row_count, -1).astype(jnp.bfloat16)
        d_z = gz_one.reshape(row_count, -1).astype(jnp.bfloat16)
        d_step = (gstep_one + gstep_two).reshape(row_count, -1).astype(jnp.bfloat16)
        d_b_part = (gb_one + gb_two).reshape(row_count, state_dim)
        d_c_part = gc_one.reshape(row_count, state_dim)
        d_normed_part = (
            mat_mul_t(d_queries, q_weight)
            + mat_mul_t(d_kv, kv_weight)
            + mat_mul_t(d_z, z_weight)
            + mat_mul_t(d_x, x_weight)
            + mat_mul_t(d_step, dt_weight)
        )
        summed = (
            lax.psum(d_normed_part.astype(jnp.bfloat16), "tensor").astype(jnp.float32),
            lax.psum(d_b_part.astype(jnp.bfloat16), "tensor").astype(jnp.float32),
            lax.psum(d_c_part.astype(jnp.bfloat16), "tensor").astype(jnp.float32),
        )
        d_b = summed[1].astype(jnp.bfloat16)
        d_c = summed[2].astype(jnp.bfloat16)
        d_normed_one = summed[0] + mat_mul_t(d_b, b_weight) + mat_mul_t(d_c, c_weight)
        d_inputs, grad_gain_one = norm_backward(inputs, scale_one, gain_f1, d_normed_one)
        input_grads.append((d_inputs + d_hidden).reshape(seq_count, block_len, model_dim))
        grad_kv = outer_sum(first_normed_input, d_kv)
        g_two = outer_sum(first_normed_input, d_queries)
        g_three = grad_kv[:, :kv_width]
        g_four = grad_kv[:, kv_width:]
        g_five = outer_sum(first_normed_input, d_z)
        g_six = outer_sum(first_normed_input, d_x)
        g_seven = outer_sum(first_normed_input, d_b)
        g_eight = outer_sum(first_normed_input, d_c)
        g_nine = outer_sum(first_normed_input, d_step)
        s_one = lax.psum_scatter(
            grad_gain_one.astype(jnp.bfloat16), "fsdp", scatter_dimension=0, tiled=True
        )
        s_two = lax.psum_scatter(
            g_two.astype(jnp.bfloat16), "fsdp", scatter_dimension=0, tiled=True
        )
        s_three = lax.psum_scatter(
            g_three.astype(jnp.bfloat16), "fsdp", scatter_dimension=0, tiled=True
        )
        s_four = lax.psum_scatter(
            g_four.astype(jnp.bfloat16), "fsdp", scatter_dimension=0, tiled=True
        )
        s_five = lax.psum_scatter(
            g_five.astype(jnp.bfloat16), "fsdp", scatter_dimension=0, tiled=True
        )
        s_six = lax.psum_scatter(
            g_six.astype(jnp.bfloat16), "fsdp", scatter_dimension=0, tiled=True
        )
        s_seven = lax.psum_scatter(
            g_seven.astype(jnp.bfloat16), "fsdp", scatter_dimension=0, tiled=True
        )
        s_eight = lax.psum_scatter(
            g_eight.astype(jnp.bfloat16), "fsdp", scatter_dimension=0, tiled=True
        )
        s_nine = lax.psum_scatter(
            g_nine.astype(jnp.bfloat16), "fsdp", scatter_dimension=0, tiled=True
        )
        s_ten = lax.psum_scatter(
            grad_gain_two.astype(jnp.bfloat16), "fsdp", scatter_dimension=0, tiled=True
        )
        s_eleven = lax.psum_scatter(
            grad_gate.astype(jnp.bfloat16), "fsdp", scatter_dimension=0, tiled=True
        )
        s_twelve = lax.psum_scatter(
            grad_up.astype(jnp.bfloat16), "fsdp", scatter_dimension=0, tiled=True
        )
        s_thirteen = lax.psum_scatter(
            grad_attn_out.astype(jnp.bfloat16), "fsdp", scatter_dimension=1, tiled=True
        )
        s_fourteen = lax.psum_scatter(
            grad_mixer_out.astype(jnp.bfloat16), "fsdp", scatter_dimension=1, tiled=True
        )
        s_fifteen = lax.psum_scatter(
            grad_down.astype(jnp.bfloat16), "fsdp", scatter_dimension=1, tiled=True
        )
        reduce_shard_sums = (
            lax.psum(s_one, "context").astype(jnp.float32),
            lax.psum(s_two, "context").astype(jnp.float32),
            lax.psum(s_three, "context").astype(jnp.float32),
            lax.psum(s_four, "context").astype(jnp.float32),
            lax.psum(s_five, "context").astype(jnp.float32),
            lax.psum(s_six, "context").astype(jnp.float32),
            lax.psum(s_seven, "context").astype(jnp.float32),
            lax.psum(s_eight, "context").astype(jnp.float32),
            lax.psum(s_nine, "context").astype(jnp.float32),
            lax.psum(s_ten, "context").astype(jnp.float32),
            lax.psum(s_eleven, "context").astype(jnp.float32),
            lax.psum(s_twelve, "context").astype(jnp.float32),
            lax.psum(s_thirteen, "context").astype(jnp.float32),
            lax.psum(s_fourteen, "context").astype(jnp.float32),
            lax.psum(s_fifteen, "context").astype(jnp.float32),
        )
        h_one = ga_one + ga_two
        h_two = gbias_one + gbias_two
        reduce_head_sums = lax.psum((h_one, h_two, gskip), ("fsdp", "context"))
        reduced = (tuple(reduce_shard_sums), tuple(reduce_head_sums))
        totals = reduced if totals is None else jax.tree.map(jnp.add, totals, reduced)
    shard_sums, head_sums = totals
    return (
        jnp.stack(layer_outs),
        jnp.stack(input_grads),
        shard_sums[0],
        shard_sums[1],
        shard_sums[2],
        shard_sums[3],
        shard_sums[4],
        shard_sums[5],
        shard_sums[6],
        shard_sums[7],
        shard_sums[8],
        head_sums[0],
        head_sums[1],
        head_sums[2],
        shard_sums[12],
        shard_sums[13],
        shard_sums[9],
        shard_sums[10],
        shard_sums[11],
        shard_sums[14],
    )


def solution(mesh):
    return jax.shard_map(
        per_device,
        mesh=mesh,
        in_specs=(
            P(None, "fsdp", "context", None),
            P(None, "fsdp", "context", None),
            P(None, "fsdp", None),
            P("fsdp"),
            P("fsdp", "tensor"),
            P("fsdp", "tensor"),
            P("fsdp", "tensor"),
            P("fsdp", "tensor"),
            P("fsdp", "tensor"),
            P("fsdp", None),
            P("fsdp", None),
            P("fsdp", "tensor"),
            P("tensor"),
            P("tensor"),
            P("tensor"),
            P("tensor", "fsdp"),
            P("tensor", "fsdp"),
            P("fsdp"),
            P("fsdp", "tensor"),
            P("fsdp", "tensor"),
            P("tensor", "fsdp"),
        ),
        out_specs=(
            P(None, "fsdp", "context", None),
            P(None, "fsdp", "context", None),
            P("fsdp"),
            P("fsdp", "tensor"),
            P("fsdp", "tensor"),
            P("fsdp", "tensor"),
            P("fsdp", "tensor"),
            P("fsdp", "tensor"),
            P("fsdp", None),
            P("fsdp", None),
            P("fsdp", "tensor"),
            P("tensor"),
            P("tensor"),
            P("tensor"),
            P("tensor", "fsdp"),
            P("tensor", "fsdp"),
            P("fsdp"),
            P("fsdp", "tensor"),
            P("fsdp", "tensor"),
            P("tensor", "fsdp"),
        ),
        check_vma=False,
    )
```

profile of v0, /device:TPU:0, one launch (start us, length us, event | category | flops | bytes accessed | tf_op | source)
XLA Modules:
  0.0 2124.7 jit_solution(2862652399918839865)
XLA Ops:
  10.4 12.6 all-gather.10
  27.7 13.4 all_gather.65
  47.3 14.1 all_gather.67
  91.5 13.4 all_gather.59
  104.8 14.1 all_gather.60
  123.7 14.5 all_gather.66
  142.2 21.8 %all_gather.62 = bf16[1024,256]{1,0:T(8,128)(2,1)S(1)} all-gather(bf16[256,256]{1,0:T(8,128)(2,1)S(1)} %copy-done.166), channel_id=1, replica_groups=mesh['fsdp'=4,'context'=4,'tensor'=2] {'fsdp'}, dimensions={0}, use_global_device_ids=true | all-gather | bytes 655360 | tf_op jit(solution)/shard_map/all_gather | solution.py:172
  166.4 18.1 all_gather.63
  211.7 7.6 all-gather.3
  219.3 7.5 all-gather
  287.4 16.6 fusion.149
  309.9 14.4 fusion.146
  329.4 10.5 all-gather.11
  339.9 96.0 %all-reduce.21.cloned.1.call-done = (f32[512,1024]{1,0:T(8,128)}, f32[512,1024]{1,0:T(8,128)}) async-done(((f32[512,1024]{1,0:T(8,128)}, f32[512,1024]{1,0:T(8,128)}), (f32[512,1024]{1,0:T(8,128)}, f32[512,1024]{1,0:T(8,128)})) %all-reduce.21.cloned.1.call-update) | async-done | bytes 4194320 | tf_op jit(solution)/shard_map/psum | solution.py:275
  442.9 40.7 %all-gather.29.cloned.1.call-done = bf16[1024,1024]{1,0:T(8,128)(2,1)} async-done(((bf16[256,1024]{1,0:T(8,128)(2,1)}), bf16[1024,1024]{1,0:T(8,128)(2,1)}) %all-gather.29.cloned.1.call-update) | async-done | bytes 2097168 | tf_op jit(solution)/shard_map/all_gather | solution.py:182
  488.1 41.8 %all-gather.27.cloned.1.call-done = bf16[1024,1024]{1,0:T(8,128)(2,1)} async-done(((bf16[256,1024]{1,0:T(8,128)(2,1)}), bf16[1024,1024]{1,0:T(8,128)(2,1)}) %all-gather.27.cloned.1.call-update) | async-done | bytes 2097168 | tf_op jit(solution)/shard_map/all_gather | solution.py:181
  539.7 36.8 %all-gather.31.cloned.1.call-done = bf16[1024,1024]{1,0:T(8,128)(2,1)} async-done(((bf16[1024,256]{1,0:T(8,128)(2,1)}), bf16[1024,1024]{1,0:T(8,128)(2,1)}) %all-gather.31.cloned.1.call-update) | async-done | bytes 2097168 | tf_op jit(solution)/shard_map/all_gather | solution.py:185
  576.5 6.3 multiply_convert_fusion.2
  634.9 69.8 %all-reduce.19.cloned.1.call-done = (f32[512,1024]{1,0:T(8,128)}, f32[512,1024]{1,0:T(8,128)}) async-done(((f32[512,1024]{1,0:T(8,128)}, f32[512,1024]{1,0:T(8,128)}), (f32[512,1024]{1,0:T(8,128)}, f32[512,1024]{1,0:T(8,128)})) %all-reduce.19.cloned.1.call-update) | async-done | bytes 4194320 | tf_op jit(solution)/shard_map/psum | solution.py:319
  722.2 17.2 fusion.135
  739.5 20.1 fusion.45
  768.9 9.0 all-gather.7
  777.9 7.0 while.63
  801.3 8.8 all-gather.6
  818.2 8.9 fusion.104
  827.1 13.0 fusion.4
  840.2 8.5 fusion.41
  854.4 8.9 fusion.105
  863.3 12.9 fusion.7
  876.3 8.5 fusion.40
  905.8 20.6 fusion.43
  939.3 14.9 fusion.137
  960.6 14.9 fusion.141
  990.1 16.5 fusion.132
  1098.3 56.9 %all-reduce.27.cloned.1.call-done = (bf16[512,1024]{1,0:T(8,128)(2,1)}, bf16[512,1024]{1,0:T(8,128)(2,1)}, bf16[512,128]{1,0:T(8,128)(2,1)}, bf16[512,1024]{1,0:...) async-done(((bf16[512,1024]{1,0:T(8,128)(2,1)}, bf16[512,1024]{1,0:T(8,128)(2,1)}, ...) | async-done | bytes 4718608 | tf_op jit(solution)/shard_map/psum | solution.py:284
  1170.6 11.8 all-reduce.11
  1184.8 12.0 reduce-scatter.61.cloned.1.call-done
  1196.7 20.1 reduce-scatter.43.cloned.1.call-done
  1216.9 19.4 reduce-scatter.39.cloned.1.call-done
  1236.3 19.5 reduce-scatter.41.cloned.1.call-done
  1255.9 19.6 reduce-scatter.37.cloned.1.call-done
  1275.9 31.1 %all-reduce.6 = (f32[12]{0:T(128)}, f32[12]{0:T(128)}, f32[12]{0:T(128)}) all-reduce(f32[12]{0:T(128)S(1)} %add_multiply_fusion, f32[12]{0:T(128)S(1)} %add_add_fusion.2, f32[12]{0:T(128)S(1)} %add.793), channel_id=1, replica_groups=mesh['fsdp'=4,'context'=4,'tensor'=2] {'fsdp','context'}, use_global_device_ids=true, to_apply=%region_96.98 | all-reduce | flops 36 | bytes 288 | tf_op jit(solution)/shard_map/psum | solution.py:478
  1307.1 12.8 reduce-scatter.81.cloned.1.call-done
  1319.9 45.7 %reduce-scatter.77.cloned.1.call-done = bf16[256,1024]{1,0:T(8,128)(2,1)} async-done(((bf16[1024,1024]{1,0:T(8,128)(2,1)}), bf16[256,1024]{1,0:T(8,128)(2,1)}) %reduce-scatter.77.cloned.1.call-update) | async-done | bytes 524304 | tf_op jit(solution)/shard_map/reduce_scatter | solution.py:447
  1365.5 45.6 %reduce-scatter.73.cloned.1.call-done = bf16[256,1024]{1,0:T(8,128)(2,1)} async-done(((bf16[1024,1024]{1,0:T(8,128)(2,1)}), bf16[256,1024]{1,0:T(8,128)(2,1)}) %reduce-scatter.73.cloned.1.call-update) | async-done | bytes 524304 | tf_op jit(solution)/shard_map/reduce_scatter | solution.py:444
  1411.1 45.5 %reduce-scatter.75.cloned.1.call-done = bf16[256,1024]{1,0:T(8,128)(2,1)} async-done(((bf16[1024,1024]{1,0:T(8,128)(2,1)}), bf16[256,1024]{1,0:T(8,128)(2,1)}) %reduce-scatter.75.cloned.1.call-update) | async-done | bytes 524304 | tf_op jit(solution)/shard_map/reduce_scatter | solution.py:444
  1456.6 45.5 %reduce-scatter.79.cloned.1.call-done = bf16[256,1024]{1,0:T(8,128)(2,1)} async-done(((bf16[1024,1024]{1,0:T(8,128)(2,1)}), bf16[256,1024]{1,0:T(8,128)(2,1)}) %reduce-scatter.79.cloned.1.call-update) | async-done | bytes 524304 | tf_op jit(solution)/shard_map/reduce_scatter | solution.py:447
  1502.1 45.5 %reduce-scatter.83.cloned.1.call-done = bf16[1024,256]{1,0:T(8,128)(2,1)} async-done(((bf16[1024,1024]{1,0:T(8,128)(2,1)}), bf16[1024,256]{1,0:T(8,128)(2,1)}) %reduce-scatter.83.cloned.1.call-update) | async-done | bytes 524304 | tf_op jit(solution)/shard_map/reduce_scatter | solution.py:456
  1547.6 23.2 %reduce-scatter.65.cloned.1.call-done = bf16[256,256]{1,0:T(8,128)(2,1)} async-done(((bf16[256,1024]{1,0:T(8,128)(2,1)}), bf16[256,256]{1,0:T(8,128)(2,1)}) %reduce-scatter.65.cloned.1.call-update) | async-done | bytes 131088 | tf_op jit(solution)/shard_map/reduce_scatter | solution.py:450
  1570.9 22.2 %reduce-scatter.67.cloned.1.call-done = bf16[256,256]{1,0:T(8,128)(2,1)} async-done(((bf16[256,1024]{1,0:T(8,128)(2,1)}), bf16[256,256]{1,0:T(8,128)(2,1)}) %reduce-scatter.67.cloned.1.call-update) | async-done | bytes 131088 | tf_op jit(solution)/shard_map/reduce_scatter | solution.py:450
  1593.0 22.4 %reduce-scatter.35.cloned.1.call-done = bf16[256,256]{1,0:T(8,128)(2,1)} async-done(((bf16[1024,256]{1,0:T(8,128)(2,1)}), bf16[256,256]{1,0:T(8,128)(2,1)}) %reduce-scatter.35.cloned.1.call-update) | async-done | bytes 131088 | tf_op jit(solution)/shard_map/reduce_scatter | solution.py:417
  1615.4 22.4 %reduce-scatter.33.cloned.1.call-done = bf16[256,256]{1,0:T(8,128)(2,1)} async-done(((bf16[1024,256]{1,0:T(8,128)(2,1)}), bf16[256,256]{1,0:T(8,128)(2,1)}) %reduce-scatter.33.cloned.1.call-update) | async-done | bytes 131088 | tf_op jit(solution)/shard_map/reduce_scatter | solution.py:417
  1637.8 35.8 %reduce-scatter.69.cloned.1.call-done = bf16[768,256]{1,0:T(8,128)(2,1)} async-done(((bf16[768,1024]{1,0:T(8,128)(2,1)}), bf16[768,256]{1,0:T(8,128)(2,1)}) %reduce-scatter.69.cloned.1.call-update) | async-done | bytes 393232 | tf_op jit(solution)/shard_map/reduce_scatter | solution.py:453
  1673.6 36.7 %reduce-scatter.71.cloned.1.call-done = bf16[768,256]{1,0:T(8,128)(2,1)} async-done(((bf16[768,1024]{1,0:T(8,128)(2,1)}), bf16[768,256]{1,0:T(8,128)(2,1)}) %reduce-scatter.71.cloned.1.call-update) | async-done | bytes 393232 | tf_op jit(solution)/shard_map/reduce_scatter | solution.py:453
  1710.3 36.7 %reduce-scatter.45.cloned.1.call-done = bf16[256,768]{1,0:T(8,128)(2,1)} async-done(((bf16[1024,768]{1,0:T(8,128)(2,1)}), bf16[256,768]{1,0:T(8,128)(2,1)}) %reduce-scatter.45.cloned.1.call-update) | async-done | bytes 393232 | tf_op jit(solution)/shard_map/reduce_scatter | solution.py:426
  1747.0 36.6 %reduce-scatter.47.cloned.1.call-done = bf16[256,768]{1,0:T(8,128)(2,1)} async-done(((bf16[1024,768]{1,0:T(8,128)(2,1)}), bf16[256,768]{1,0:T(8,128)(2,1)}) %reduce-scatter.47.cloned.1.call-update) | async-done | bytes 393232 | tf_op jit(solution)/shard_map/reduce_scatter | solution.py:426
  1783.6 36.7 %reduce-scatter.51.cloned.1.call-done = bf16[256,768]{1,0:T(8,128)(2,1)} async-done(((bf16[1024,768]{1,0:T(8,128)(2,1)}), bf16[256,768]{1,0:T(8,128)(2,1)}) %reduce-scatter.51.cloned.1.call-update) | async-done | bytes 393232 | tf_op jit(solution)/shard_map/reduce_scatter | solution.py:429
  1820.3 36.7 %reduce-scatter.49.cloned.1.call-done = bf16[256,768]{1,0:T(8,128)(2,1)} async-done(((bf16[1024,768]{1,0:T(8,128)(2,1)}), bf16[256,768]{1,0:T(8,128)(2,1)}) %reduce-scatter.49.cloned.1.call-update) | async-done | bytes 393232 | tf_op jit(solution)/shard_map/reduce_scatter | solution.py:429
  1857.0 21.4 %reduce-scatter.59.cloned.1.call-done = bf16[256,128]{1,0:T(8,128)(2,1)} async-done(((bf16[1024,128]{1,0:T(8,128)(2,1)}), bf16[256,128]{1,0:T(8,128)(2,1)}) %reduce-scatter.59.cloned.1.call-update) | async-done | bytes 65552 | tf_op jit(solution)/shard_map/reduce_scatter | solution.py:435
  1878.5 20.6 reduce-scatter.55.cloned.1.call-done
  1899.1 20.9 reduce-scatter.57.cloned.1.call-done
  1919.9 20.6 reduce-scatter.53.cloned.1.call-done
  1952.2 23.4 %all-reduce.23.cloned.1.call-done = (bf16[256]{0:T(256)(128)(2,1)}, bf16[256]{0:T(256)(128)(2,1)}, bf16[256,64]{0,1:T(8,128)(2,1)}, bf16[256,64]{0,1:T(8,128)(2,...) async-done(((bf16[256]{0:T(256)(128)(2,1)}, ...) | async-done | bytes 145424 | tf_op jit(solution)/shard_map/psum | solution.py:460
  1982.2 121.3 %all-reduce.25.cloned.1.call-done = (bf16[256,256]{1,0:T(8,128)(2,1)}, bf16[256,256]{1,0:T(8,128)(2,1)}, bf16[256,768]{1,0:T(8,128)(2,1)}, bf16[256,768]{1,0:T(8...) async-done(((bf16[256,256]{1,0:T(8,128)(2,1)}, ...) | async-done | bytes 6291472 | tf_op jit(solution)/shard_map/psum | solution.py:461
  (931 shorter events, 497.4 us)
Async XLA Ops:
  7.2 54.7 %all-gather.21.cloned.1.call-start = ((), (), s32[]{:S(2)}) async-start(), calls=%async_computation.28 | async-start | bytes 1966080 | tf_op jit(solution)/shard_map/all_gather | solution.py:176
  7.9 251.4 %all-gather.23.cloned.1.call-start = ((), (), s32[]{:S(2)}) async-start(), calls=%async_computation.29 | async-start | bytes 1966080 | tf_op jit(solution)/shard_map/all_gather | solution.py:175
  8.7 264.0 %all-gather.33.cloned.1.call-start = ((), (), s32[]{:S(2)}) async-start(), calls=%async_computation.62 | async-start | bytes 1966080 | tf_op jit(solution)/shard_map/all_gather | solution.py:15
  41.1 33.1 %copy-start.125 = (bf16[1024,12]{0,1:T(8,128)(2,1)}, bf16[1024,12]{0,1:T(8,128)(2,1)S(1)}, u32[]{:S(2)}) copy-start(bf16[1024,12]{0,1:T(8,128)(2,1)S(1)} %all_gather.65) | copy-start | bytes 73732
  43.9 215.5 %copy-start.2 = (bf16[512,1024]{1,0:T(8,128)(2,1)}, bf16[512,1024]{1,0:T(8,128)(2,1)S(1)}, u32[]{:S(2)}) copy-start(bf16[512,1024]{1,0:T(8,128)(2,1)S(1)} %get-tuple-element.831) | copy-start | bytes 3145732
  43.9 222.1 %copy-start.4 = (bf16[512,1024]{1,0:T(8,128)(2,1)}, bf16[512,1024]{1,0:T(8,128)(2,1)S(1)}, u32[]{:S(2)}) copy-start(bf16[512,1024]{1,0:T(8,128)(2,1)S(1)} %get-tuple-element.832) | copy-start | bytes 3145732
  44.0 30.7 %copy-start.255 = (f32[12]{0:T(128)}, f32[12]{0:T(128)S(1)}, u32[]{:S(2)}) copy-start(f32[12]{0:T(128)S(1)} %exponential_negate_fusion) | copy-start | bytes 148
  44.4 96.9 %copy-start.44 = (f32[512,12]{1,0:T(8,128)}, f32[512,12]{1,0:T(8,128)S(1)}, u32[]{:S(2)}) copy-start(f32[512,12]{1,0:T(8,128)S(1)} %convolution_add_fusion.7) | copy-start | bytes 73732
  72.2 207.7 %all-gather.35.cloned.1.call-start = ((), (), s32[]{:S(2)}) async-start(), calls=%async_computation.63 | async-start | bytes 1966080 | tf_op jit(solution)/shard_map/all_gather | solution.py:15
  74.6 65.8 %copy-start.47 = (f32[512,12]{1,0:T(8,128)}, f32[512,12]{1,0:T(8,128)S(1)}, u32[]{:S(2)}) copy-start(f32[512,12]{1,0:T(8,128)S(1)} %convolution_add_fusion.6) | copy-start | bytes 73732
  88.4 215.5 %all-gather.25.cloned.1.call-start = ((), (), s32[]{:S(2)}) async-start(), calls=%async_computation.30 | async-start | bytes 1966080 | tf_op jit(solution)/shard_map/all_gather | solution.py:184
  89.0 347.0 %all-reduce.21.cloned.1.call-start = ((), (), s32[]{:S(2)}) async-start(), calls=%async_computation.65 | async-start | bytes 8388608 | tf_op jit(solution)/shard_map/psum | solution.py:275
  89.6 31.6 %copy-start.256 = (f32[12]{0:T(128)S(1)}, f32[12]{0:T(128)}, u32[]{:S(2)}) copy-start(f32[12]{0:T(128)} %copy-done.255) | copy-start | bytes 148
  142.2 24.2 %copy-start.167 = (bf16[256,256]{1,0:T(8,128)(2,1)S(1)}, bf16[256,256]{1,0:T(8,128)(2,1)}, u32[]{:S(2)}) copy-start(bf16[256,256]{1,0:T(8,128)(2,1)} %param.45) | copy-start | bytes 393220
  187.5 51.1 %copy-start.14 = (pred[512,2048]{0,1:T(8,128)(4,1)}, pred[512,2048]{0,1:T(8,128)(4,1)S(1)}, u32[]{:S(2)}) copy-start(pred[512,2048]{0,1:T(8,128)(4,1)S(1)} %get-tuple-element.863) | copy-start | bytes 3145732
  219.3 33.7 %copy-start.75 = (bf16[2048,128]{1,0:T(8,128)(2,1)}, bf16[2048,128]{1,0:T(8,128)(2,1)S(1)}, u32[]{:S(2)}) copy-start(bf16[2048,128]{1,0:T(8,128)(2,1)S(1)} %all-gather.3) | copy-start | bytes 1572868
  259.3 66.0 %copy-start.103 = (bf16[64,4,512]{2,0,1:T(8,128)(2,1)}, bf16[64,4,512]{2,0,1:T(8,128)(2,1)S(1)}, u32[]{:S(2)}) copy-start(bf16[64,4,512]{2,0,1:T(8,128)(2,1)S(1)} %convolution_convert_fusion.26) | copy-start | bytes 786436
  277.3 520.6 %copy-start.29 = (f32[1,12,64,128]{3,2,1,0:T(8,128)}, f32[1,12,64,128]{3,2,1,0:T(8,128)S(1)}, u32[]{:S(2)}) copy-start(f32[1,12,64,128]{3,2,1,0:T(8,128)S(1)} %get-tuple-element.476) | copy-start | bytes 1179652
  327.1 156.4 %all-gather.29.cloned.1.call-start = ((), (), s32[]{:S(2)}) async-start(), calls=%async_computation.32 | async-start | bytes 2621440 | tf_op jit(solution)/shard_map/all_gather | solution.py:182
  327.9 202.0 %all-gather.27.cloned.1.call-start = ((), (), s32[]{:S(2)}) async-start(), calls=%async_computation.31 | async-start | bytes 2621440 | tf_op jit(solution)/shard_map/all_gather | solution.py:181
  328.6 247.9 %all-gather.31.cloned.1.call-start = ((), (), s32[]{:S(2)}) async-start(), calls=%async_computation.33 | async-start | bytes 2621440 | tf_op jit(solution)/shard_map/all_gather | solution.py:185
  329.4 375.3 %all-reduce.19.cloned.1.call-start = ((), (), s32[]{:S(2)}) async-start(), calls=%async_computation.64 | async-start | bytes 8388608 | tf_op jit(solution)/shard_map/psum | solution.py:319
  439.4 269.9 %copy-start.6 = (f32[512,1024]{1,0:T(8,128)}, f32[512,1024]{1,0:T(8,128)S(1)}, u32[]{:S(2)}) copy-start(f32[512,1024]{1,0:T(8,128)S(1)} %get-tuple-element.834) | copy-start | bytes 6291460
  598.1 422.1 %reduce-scatter.31.cloned.1.call-start = ((), (), s32[]{:S(2)}) async-start(), calls=%async_computation.35 | async-start | bytes 655360 | tf_op jit(solution)/shard_map/reduce_scatter | solution.py:359
  632.6 72.1 %copy-start.198 = (f32[512]{0:T(512)S(1)}, f32[512]{0:T(512)}, u32[]{:S(2)}) copy-start(f32[512]{0:T(512)} %copy-done.197) | copy-start | bytes 6148
  905.8 25.5 %copy-start.52 = (f32[512,128]{1,0:T(8,128)S(1)}, f32[512,128]{1,0:T(8,128)}, u32[]{:S(2)}) copy-start(f32[512,128]{1,0:T(8,128)} %fusion.393) | copy-start | bytes 786436
  979.7 48.4 %reduce-scatter.29.cloned.1.call-start = ((), (), s32[]{:S(2)}) async-start(), calls=%async_computation.34 | async-start | bytes 655360 | tf_op jit(solution)/shard_map/reduce_scatter | solution.py:359
  1006.6 148.5 %all-reduce.27.cloned.1.call-start = ((), (), s32[]{:S(2)}) async-start(), calls=%async_computation.68 | async-start | bytes 9437184 | tf_op jit(solution)/shard_map/psum | solution.py:284
  1033.4 151.4 %reduce-scatter.63.cloned.1.call-start = ((), (), s32[]{:S(2)}) async-start(), calls=%async_computation.51 | async-start | bytes 40960 | tf_op jit(solution)/shard_map/reduce_scatter | solution.py:438
  1036.0 160.8 %reduce-scatter.61.cloned.1.call-start = ((), (), s32[]{:S(2)}) async-start(), calls=%async_computation.50 | async-start | bytes 40960 | tf_op jit(solution)/shard_map/reduce_scatter | solution.py:438
  1037.1 179.7 %reduce-scatter.43.cloned.1.call-start = ((), (), s32[]{:S(2)}) async-start(), calls=%async_computation.41 | async-start | bytes 163840 | tf_op jit(solution)/shard_map/reduce_scatter | solution.py:423
  1038.4 197.9 %reduce-scatter.39.cloned.1.call-start = ((), (), s32[]{:S(2)}) async-start(), calls=%async_computation.39 | async-start | bytes 163840 | tf_op jit(solution)/shard_map/reduce_scatter | solution.py:420
  1039.0 216.8 %reduce-scatter.41.cloned.1.call-start = ((), (), s32[]{:S(2)}) async-start(), calls=%async_computation.40 | async-start | bytes 163840 | tf_op jit(solution)/shard_map/reduce_scatter | solution.py:423
  1040.3 235.1 %reduce-scatter.37.cloned.1.call-start = ((), (), s32[]{:S(2)}) async-start(), calls=%async_computation.38 | async-start | bytes 163840 | tf_op jit(solution)/shard_map/reduce_scatter | solution.py:420
  1041.1 278.8 %reduce-scatter.81.cloned.1.call-start = ((), (), s32[]{:S(2)}) async-start(), calls=%async_computation.60 | async-start | bytes 2621440 | tf_op jit(solution)/shard_map/reduce_scatter | solution.py:456
  1045.0 320.5 %reduce-scatter.77.cloned.1.call-start = ((), (), s32[]{:S(2)}) async-start(), calls=%async_computation.58 | async-start | bytes 2621440 | tf_op jit(solution)/shard_map/reduce_scatter | solution.py:447
  1050.1 361.0 %reduce-scatter.73.cloned.1.call-start = ((), (), s32[]{:S(2)}) async-start(), calls=%async_computation.56 | async-start | bytes 2621440 | tf_op jit(solution)/shard_map/reduce_scatter | solution.py:444
  1054.1 402.5 %reduce-scatter.75.cloned.1.call-start = ((), (), s32[]{:S(2)}) async-start(), calls=%async_computation.57 | async-start | bytes 2621440 | tf_op jit(solution)/shard_map/reduce_scatter | solution.py:444
  1059.2 442.9 %reduce-scatter.79.cloned.1.call-start = ((), (), s32[]{:S(2)}) async-start(), calls=%async_computation.59 | async-start | bytes 2621440 | tf_op jit(solution)/shard_map/reduce_scatter | solution.py:447
  1063.2 484.4 %reduce-scatter.83.cloned.1.call-start = ((), (), s32[]{:S(2)}) async-start(), calls=%async_computation.61 | async-start | bytes 2621440 | tf_op jit(solution)/shard_map/reduce_scatter | solution.py:456
  1068.3 502.6 %reduce-scatter.65.cloned.1.call-start = ((), (), s32[]{:S(2)}) async-start(), calls=%async_computation.52 | async-start | bytes 655360 | tf_op jit(solution)/shard_map/reduce_scatter | solution.py:450
  1071.1 522.0 %reduce-scatter.67.cloned.1.call-start = ((), (), s32[]{:S(2)}) async-start(), calls=%async_computation.53 | async-start | bytes 655360 | tf_op jit(solution)/shard_map/reduce_scatter | solution.py:450
  1073.3 542.1 %reduce-scatter.35.cloned.1.call-start = ((), (), s32[]{:S(2)}) async-start(), calls=%async_computation.37 | async-start | bytes 655360 | tf_op jit(solution)/shard_map/reduce_scatter | solution.py:417
  1074.9 562.9 %reduce-scatter.33.cloned.1.call-start = ((), (), s32[]{:S(2)}) async-start(), calls=%async_computation.36 | async-start | bytes 655360 | tf_op jit(solution)/shard_map/reduce_scatter | solution.py:417
  1077.4 596.2 %reduce-scatter.69.cloned.1.call-start = ((), (), s32[]{:S(2)}) async-start(), calls=%async_computation.54 | async-start | bytes 1966080 | tf_op jit(solution)/shard_map/reduce_scatter | solution.py:453
  1081.1 629.3 %reduce-scatter.71.cloned.1.call-start = ((), (), s32[]{:S(2)}) async-start(), calls=%async_computation.55 | async-start | bytes 1966080 | tf_op jit(solution)/shard_map/reduce_scatter | solution.py:453
  1084.4 662.6 %reduce-scatter.45.cloned.1.call-start = ((), (), s32[]{:S(2)}) async-start(), calls=%async_computation.42 | async-start | bytes 1966080 | tf_op jit(solution)/shard_map/reduce_scatter | solution.py:426
  1088.1 695.5 %reduce-scatter.47.cloned.1.call-start = ((), (), s32[]{:S(2)}) async-start(), calls=%async_computation.43 | async-start | bytes 1966080 | tf_op jit(solution)/shard_map/reduce_scatter | solution.py:426
  1090.6 729.7 %reduce-scatter.51.cloned.1.call-start = ((), (), s32[]{:S(2)}) async-start(), calls=%async_computation.45 | async-start | bytes 1966080 | tf_op jit(solution)/shard_map/reduce_scatter | solution.py:429
  1094.2 61.0 %copy-start.5 = (bf16[512,1024]{1,0:T(8,128)(2,1)S(1)}, bf16[512,1024]{1,0:T(8,128)(2,1)}, u32[]{:S(2)}) copy-start(bf16[512,1024]{1,0:T(8,128)(2,1)} %copy-done.4) | copy-start | bytes 3145732
  1094.2 762.8 %reduce-scatter.49.cloned.1.call-start = ((), (), s32[]{:S(2)}) async-start(), calls=%async_computation.44 | async-start | bytes 1966080 | tf_op jit(solution)/shard_map/reduce_scatter | solution.py:429
  1098.2 61.4 %copy-start.254 = (u32[32]{0:T(128)S(1)}, u32[32]{0:T(128)}, u32[]{:S(2)}) copy-start(u32[32]{0:T(128)} %constant.216) | copy-start | bytes 388
  1098.2 62.7 %copy-start.228 = (f32[12]{0:T(128)S(1)}, f32[12]{0:T(128)}, u32[]{:S(2)}) copy-start(f32[12]{0:T(128)} %param.42) | copy-start | bytes 148
  1098.2 62.7 %copy-start.229 = (f32[12]{0:T(128)S(1)}, f32[12]{0:T(128)}, u32[]{:S(2)}) copy-start(f32[12]{0:T(128)} %get-tuple-element.699) | copy-start | bytes 148
  1098.2 62.7 %copy-start.230 = (f32[12]{0:T(128)S(1)}, f32[12]{0:T(128)}, u32[]{:S(2)}) copy-start(f32[12]{0:T(128)} %get-tuple-element.697) | copy-start | bytes 148
  1098.2 62.7 %copy-start.3 = (bf16[512,1024]{1,0:T(8,128)(2,1)S(1)}, bf16[512,1024]{1,0:T(8,128)(2,1)}, u32[]{:S(2)}) copy-start(bf16[512,1024]{1,0:T(8,128)(2,1)} %copy-done.2) | copy-start | bytes 3145732
  1098.2 780.2 %reduce-scatter.59.cloned.1.call-start = ((), (), s32[]{:S(2)}) async-start(), calls=%async_computation.49 | async-start | bytes 327680 | tf_op jit(solution)/shard_map/reduce_scatter | solution.py:435
  1157.3 741.7 %reduce-scatter.55.cloned.1.call-start = ((), (), s32[]{:S(2)}) async-start(), calls=%async_computation.47 | async-start | bytes 327680 | tf_op jit(solution)/shard_map/reduce_scatter | solution.py:432
  1159.6 760.4 %reduce-scatter.57.cloned.1.call-start = ((), (), s32[]{:S(2)}) async-start(), calls=%async_computation.48 | async-start | bytes 327680 | tf_op jit(solution)/shard_map/reduce_scatter | solution.py:435
  1162.2 778.4 %reduce-scatter.53.cloned.1.call-start = ((), (), s32[]{:S(2)}) async-start(), calls=%async_computation.46 | async-start | bytes 327680 | tf_op jit(solution)/shard_map/reduce_scatter | solution.py:432
  1163.9 811.7 %all-reduce.23.cloned.1.call-start = ((), (), s32[]{:S(2)}) async-start(), calls=%async_computation.66 | async-start | bytes 299008 | tf_op jit(solution)/shard_map/psum | solution.py:460
  1168.1 107.4 %copy-start.220 = (f32[768]{0:T(1024)S(1)}, f32[768]{0:T(1024)}, u32[]{:S(2)}) copy-start(f32[768]{0:T(1024)} %get-tuple-element.823) | copy-start | bytes 9220
  1168.1 107.5 %copy-start.221 = (f32[768]{0:T(1024)S(1)}, f32[768]{0:T(1024)}, u32[]{:S(2)}) copy-start(f32[768]{0:T(1024)} %get-tuple-element.825) | copy-start | bytes 9220
  1275.5 828.0 %all-reduce.25.cloned.1.call-start = ((), (), s32[]{:S(2)}) async-start(), calls=%async_computation.67 | async-start | bytes 12582912 | tf_op jit(solution)/shard_map/psum | solution.py:461
  (253 other events, 1429.5 us)
Sparse Core Ops, SparseCore 0:
  9.6 41.9 all-gather.20
  53.1 35.9 all-gather.22
  91.2 18.3 all-gather.32
  111.6 19.6 all-gather.34
  132.7 50.8 all-gather.24
  327.3 108.6 all-reduce.20
  437.6 45.9 all-gather.28
  485.2 44.6 all-gather.26
  531.5 44.9 all-gather.30
  598.2 106.4 all-reduce.18
  979.8 21.3 reduce-scatter.30
  1006.8 21.3 reduce-scatter.28
  1033.5 121.6 all-reduce.26
  1157.9 18.9 reduce-scatter.62
  1179.6 17.1 reduce-scatter.60
  1199.5 17.3 reduce-scatter.42
  1219.0 17.3 reduce-scatter.38
  1238.5 17.3 reduce-scatter.40
  1258.1 17.3 reduce-scatter.36
  1277.7 42.1 reduce-scatter.80
  1322.2 43.3 reduce-scatter.76
  1367.9 43.1 reduce-scatter.72
  1413.4 43.1 reduce-scatter.74
  1458.9 43.1 reduce-scatter.78
  1504.4 43.1 reduce-scatter.82
  1549.9 20.9 reduce-scatter.64
  1573.1 19.9 reduce-scatter.66
  1595.4 19.9 reduce-scatter.34
  1617.8 19.9 reduce-scatter.32
  1640.0 33.5 reduce-scatter.68
  1676.0 34.2 reduce-scatter.70
  1712.7 34.2 reduce-scatter.44
  1749.3 34.2 reduce-scatter.46
  1786.0 34.2 reduce-scatter.50
  1822.7 34.2 reduce-scatter.48
  1859.8 18.6 reduce-scatter.58
  1881.1 17.8 reduce-scatter.54
  1902.0 17.8 reduce-scatter.56
  1922.6 17.8 reduce-scatter.52
  1945.6 29.9 all-reduce.22
  1979.5 123.9 all-reduce.24
where the time goes:
time: 2140 us; the launch traced here: 2120 us
  waiting for transfers between devices  1220 us (57%)
  matrix products  440 us (21%)
  blocking collectives  229 us (11%)
  other arithmetic  122 us (6%)
  local copies, waits for them, and re-layouts  92.4 us (4%)
    dot_general x8, matrix products, mixer_values(): result = jnp.einsum('shtu,suhp->sthp', kernel, x_in, precision=PRECISE)  135 us
    psum x1, waiting for transfers between devices, per_device(): lax.psum(s_two, 'context').astype(jnp.float32)  121 us
    psum x1, waiting for transfers between devices, per_device(): lax.psum(mat_mul(attended, attn_weight) + mat_mul(gated_low, mixer_weight...  96 us
    reduce_scatter x2, waiting for transfers between devices, per_device(): lax.psum_scatter(grad_gate.astype(jnp.bfloat16), 'fsdp', scatter_dimensio...  91.1 us
    reduce_scatter x2, waiting for transfers between devices, per_device(): lax.psum_scatter(grad_up.astype(jnp.bfloat16), 'fsdp', scatter_dimension=...  91.1 us
    reduce_scatter x2, waiting for transfers between devices, per_device(): lax.psum_scatter(g_six.astype(jnp.bfloat16), 'fsdp', scatter_dimension=0,...  73.4 us
    reduce_scatter x2, waiting for transfers between devices, per_device(): lax.psum_scatter(g_five.astype(jnp.bfloat16), 'fsdp', scatter_dimension=0...  73.3 us
    reduce_scatter x2, waiting for transfers between devices, per_device(): lax.psum_scatter(grad_mixer_out.astype(jnp.bfloat16), 'fsdp', scatter_dim...  72.5 us
  transfers between devices with their start and end apart: 41, of which 34 were waited for; matrix products, arithmetic and copies ran while one was open for 15% of the time, Pallas kernels for 0%

commit v1 on v0

v1 whole, which is shorter than its diff:
```python
import jax
import jax.numpy as jnp
from jax import lax
from jax.sharding import PartitionSpec as P

HEAD_WIDTH = 64
EPSILON = 1e-06
LOW = jnp.bfloat16
F32 = jnp.float32


def swap_context(x, bit):
    size = lax.axis_size("context")
    return lax.ppermute(x, "context", [(i, i ^ bit) for i in range(size)])


def from_next(x, axis, step=1):
    size = lax.axis_size(axis)
    return lax.ppermute(x, axis, [((i + step) % size, i) for i in range(size)])


def context_bits():
    size = lax.axis_size("context")
    return [1 << k for k in range(size.bit_length() - 1)]


def spread_context(x):
    held = [(0, x)]
    for bit in reversed(context_bits()):
        held = held + [(off ^ bit, swap_context(part, bit)) for off, part in held]
    return held


def gather_context(x):
    size, index = lax.axis_size("context"), lax.axis_index("context")
    out = jnp.zeros((size,) + x.shape, x.dtype)
    for off, part in spread_context(x):
        out = lax.dynamic_update_index_in_dim(out, part, index ^ off, 0)
    return out


def gather_rows(shard, stacked):
    nf, nc = lax.axis_size("fsdp"), lax.axis_size("context")
    fi, ci = lax.axis_index("fsdp"), lax.axis_index("context")
    rows, cols = shard.shape
    part = rows // nc
    full = jnp.zeros((nf, nc, part, cols), shard.dtype)
    full = lax.dynamic_update_slice(full, shard.reshape(1, nc, part, cols), (fi, 0, 0, 0))
    cur = lax.dynamic_slice(shard, (ci * part, 0), (part, cols))
    steps = []
    for k in range(1, nf):
        cur = from_next(cur, "fsdp")
        steps.append((k, cur))
    if stacked:
        pieces = spread_context(jnp.stack([cur for _, cur in steps]))
        pieces = [(k, off, arr[k - 1]) for off, arr in pieces for k, _ in steps]
    else:
        pieces = [(k, off, arr) for k, cur in steps for off, arr in spread_context(cur)]
    for k, off, arr in pieces:
        full = lax.dynamic_update_slice(full, arr[None, None], ((fi + k) % nf, ci ^ off, 0, 0))
    return full.reshape(nf * rows, cols)


def scatter_rows(grad):
    nf, nc = lax.axis_size("fsdp"), lax.axis_size("context")
    fi, ci = lax.axis_index("fsdp"), lax.axis_index("context")
    rows, cols = grad.shape
    part = rows // (nf * nc)
    acc = grad
    left = nc
    for bit in context_bits():
        left //= 2
        view = acc.reshape(nf, left, 2, part, cols)
        mine = (ci & bit) // bit
        away = lax.dynamic_index_in_dim(view, 1 - mine, 2, keepdims=False)
        keep = lax.dynamic_index_in_dim(view, mine, 2, keepdims=False)
        acc = (keep.astype(F32) + swap_context(away, bit).astype(F32)).astype(LOW)
    acc = acc.reshape(nf, part, cols)
    total = lax.dynamic_index_in_dim(acc, fi, 0, keepdims=False).astype(F32)
    for k in range(1, nf):
        away = lax.dynamic_index_in_dim(acc, (fi - k) % nf, 0, keepdims=False)
        total = total + from_next(away, "fsdp", k).astype(F32)
    done = gather_context(total.astype(LOW))
    return done.reshape(rows // nf, cols).astype(F32)


def all_sum(x):
    for bit in context_bits():
        x = x + swap_context(x, bit)
    size, bit = lax.axis_size("fsdp"), 1
    while bit < size:
        x = x + lax.ppermute(x, "fsdp", [(i, i ^ bit) for i in range(size)])
        bit *= 2
    return x


def tensor_sum(x):
    low = x.astype(LOW)
    size = lax.axis_size("tensor")
    other = lax.ppermute(low, "tensor", [(i, (i + 1) % size) for i in range(size)])
    return low.astype(F32) + other.astype(F32)


def mat_mul(left, right):
    return jnp.dot(left, right, preferred_element_type=F32)


def mat_mul_t(left, right):
    return lax.dot_general(left, right, (((1,), (1,)), ((), ())), preferred_element_type=F32)


def outer_sum(left, right):
    return lax.dot_general(left, right, (((0,), (0,)), ((), ())), preferred_element_type=F32)


def norm_forward(hidden, gain_vec):
    inv_scale = lax.rsqrt(jnp.mean(hidden * hidden, axis=-1, keepdims=True) + EPSILON)
    return inv_scale, (hidden * inv_scale * gain_vec).astype(LOW)


def norm_backward(hidden, inv_scale, gain_vec, d_normed):
    weighted = gain_vec * d_normed
    return inv_scale * weighted - hidden * inv_scale**3 * jnp.mean(
        weighted * hidden, axis=-1, keepdims=True
    )


def segment_ids(doc_lens, positions):
    count = doc_lens.shape[-1]
    upto = jnp.arange(count)[:, None] >= jnp.arange(count)[None, :]
    ends = jnp.sum(jnp.where(upto, doc_lens[:, None, :], 0), axis=-1)
    return jnp.sum((ends[:, None, :] <= positions[None, :, None]).astype(jnp.int32), axis=2)


def decay_terms(raw_step, a_log, dt_bias):
    step_size = jax.nn.softplus(raw_step + dt_bias)
    log_rate = -jnp.exp(a_log) * step_size
    block_len = raw_step.shape[0]
    lower = (jnp.arange(block_len)[:, None] >= jnp.arange(block_len)[None, :]).astype(F32)
    log_decay = jnp.einsum("tu,uh->ht", lower, log_rate, precision=lax.Precision.HIGHEST)
    return step_size.T, log_decay


def mixer_values(x_in, b_in, c_in, step_in, z_in, log_a, bias_in, skip_in, state_in, inside, carried):
    step_size, log_decay = decay_terms(step_in, log_a, bias_in)
    log_gap = jnp.where(inside[None], log_decay[:, :, None] - log_decay[:, None, :], -10000.0)
    inner = jnp.einsum("tn,un->tu", c_in, b_in)
    kernel = jnp.exp(log_gap) * inner[None] * step_size[:, None, :]
    result = jnp.einsum("htu,uhp->thp", kernel, x_in)
    entering = jnp.where(carried[None, :], jnp.exp(log_decay), 0.0)
    state_read = jnp.einsum("tn,hpn->thp", c_in, state_in)
    result = result + state_read * entering.T[..., None] + skip_in[:, None] * x_in
    return result * jax.nn.silu(z_in)


def mixer_state(x_in, b_in, step_in, log_a, bias_in, closing, carried_last):
    step_size, log_decay = decay_terms(step_in, log_a, bias_in)
    final_log = log_decay[:, -1:]
    weights = jnp.where(closing[None, :], jnp.exp(final_log - log_decay), 0.0) * step_size
    span_state = jnp.einsum("ht,thp,tn->hpn", weights, x_in, b_in)
    passing = jnp.where(carried_last, jnp.exp(final_log[:, 0]), 0.0)
    return passing, span_state


def masked_scores(queries, keys, allowed):
    scores = jnp.einsum("tgqd,jgd->gqtj", queries, keys, preferred_element_type=F32) * 0.125
    return jnp.where(allowed[None, None], scores, -1e30)


def per_device(
    tokens, cotangent, doc_lengths, mixer_gain, w_query, key_matrix, value_matrix, mamba_gate_weight,
    mamba_input_weight, w_bproj, w_cproj, w_dt, a_log, dt_bias, d_skip, w_attn_out, w_mixer_out,
    ffn_gain, w_gate, w_up, w_down,
):
    micro_count, seq_count, block_len, model_dim = tokens.shape
    rows_here = mixer_gain.shape[0]
    heads = w_dt.shape[1]
    ssm_dim = mamba_gate_weight.shape[1]
    head_dim = ssm_dim // heads
    q_dim = w_query.shape[1]
    kv_dim = key_matrix.shape[1]
    kv_heads = kv_dim // HEAD_WIDTH
    q_group = q_dim // kv_dim
    state_dim = w_bproj.shape[1]
    ff_dim = w_gate.shape[1]
    ci = lax.axis_index("context")
    nc = lax.axis_size("context")
    full_len = nc * block_len
    units = [(m, s) for m in range(micro_count) for s in range(seq_count)]

    pad = -(heads + 2) % 128
    first = jnp.concatenate(
        [w_query, key_matrix, value_matrix, w_bproj, w_cproj, w_dt, mixer_gain[:, None], ffn_gain[:, None],
         jnp.zeros((rows_here, pad), LOW)], axis=1)
    second = jnp.concatenate([mamba_gate_weight, mamba_input_weight], axis=1)
    third = jnp.concatenate([w_attn_out.T, w_mixer_out.T], axis=1)
    fourth = jnp.concatenate([w_gate, w_up, w_down.T], axis=1)
    first = gather_rows(first, False)
    second = gather_rows(second, False)
    third = gather_rows(third, True)
    fourth = gather_rows(fourth, True)
    at_b = q_dim + 2 * kv_dim
    at_dt = at_b + 2 * state_dim
    gain_one = first[:, at_dt + heads].astype(F32)
    gain_two = first[:, at_dt + heads + 1].astype(F32)
    gate_up = fourth[:, : 2 * ff_dim]
    down_t = fourth[:, 2 * ff_dim :]

    saved = {}
    positions = jnp.arange(full_len)
    q_pos = ci * block_len + jnp.arange(block_len)
    tri = jnp.arange(block_len)[:, None] >= jnp.arange(block_len)[None, :]
    nothing = (jnp.ones((heads,), F32), jnp.zeros((heads, head_dim, state_dim), F32))

    for u in units:
        v = saved[u] = {}
        v["x"] = tokens[u].astype(F32)
        v["r1"], v["n1"] = norm_forward(v["x"], gain_one)
        p_one = mat_mul(v["n1"], first)
        v["q"] = p_one[:, :q_dim].astype(LOW)
        kv = p_one[:, q_dim:at_b].astype(LOW)
        v["b"] = p_one[:, at_b : at_b + state_dim]
        v["c"] = p_one[:, at_b + state_dim : at_dt]
        v["dr"] = p_one[:, at_dt : at_dt + heads]
        p_two = mat_mul(v["n1"], second)
        v["z"] = p_two[:, :ssm_dim].reshape(block_len, heads, head_dim)
        v["xs"] = p_two[:, ssm_dim:].reshape(block_len, heads, head_dim)
        kv_all = gather_context(kv).reshape(full_len, 2 * kv_dim)
        v["k_all"] = kv_all[:, :kv_dim].reshape(full_len, kv_heads, HEAD_WIDTH)
        v["v_all"] = kv_all[:, kv_dim:].reshape(full_len, kv_heads, HEAD_WIDTH)
        doc_lens = doc_lengths[u][None]
        seg_all = segment_ids(doc_lens, positions)[0]
        seg_here = lax.dynamic_slice_in_dim(seg_all, ci * block_len, block_len, 0)
        seg_prev = segment_ids(doc_lens, jnp.reshape(ci * block_len - 1, (1,)))[0]
        v["allowed"] = (positions[None, :] <= q_pos[:, None]) & (seg_all[None, :] == seg_here[:, None])
        v["inside"] = tri & (seg_here[:, None] == seg_here[None, :])
        v["carried"] = seg_here == seg_prev
        v["closing"] = seg_here == seg_here[-1:]
        v["passing"], v["span"] = mixer_state(
            v["xs"], v["b"], v["dr"], a_log, dt_bias, v["closing"], v["carried"][-1])
        passes = gather_context(v["passing"])
        spans = gather_context(v["span"].astype(LOW))
        v["passes"] = passes
        state = nothing[1]
        for k in range(nc - 1):
            new = passes[k][:, None, None] * state + spans[k].astype(F32)
            state = jnp.where(k < ci, new, state)
        v["state"] = state
    for u in units:
        v = saved[u]
        scores = masked_scores(v["q"].reshape(block_len, kv_heads, q_group, HEAD_WIDTH), v["k_all"], v["allowed"])
        row_max = jnp.max(scores, axis=-1, keepdims=True)
        v["lse"] = row_max + jnp.log(jnp.sum(jnp.exp(scores - row_max), axis=-1, keepdims=True))
        prob = jnp.exp(scores - v["lse"]).astype(LOW)
        v["o"] = jnp.einsum("gqtj,jgd->tgqd", prob, v["v_all"], preferred_element_type=F32).astype(LOW).reshape(block_len, q_dim)
        gated = mixer_values(v["xs"], v["b"], v["c"], v["dr"], v["z"], a_log, dt_bias, d_skip, v["state"], v["inside"], v["carried"])
        v["og"] = jnp.concatenate([v["o"], gated.reshape(block_len, ssm_dim).astype(LOW)], axis=1)
        v["m"] = tensor_sum(mat_mul_t(v["og"], third))

    layer_outs = []
    for u in units:
        v = saved[u]
        v["h1"] = v["x"] + v["m"]
        v["r2"], v["n2"] = norm_forward(v["h1"], gain_two)
        ab = mat_mul(v["n2"], gate_up)
        a, b = ab[:, :ff_dim], ab[:, ff_dim:]
        sig = jax.nn.sigmoid(a)
        v["f"] = (a * sig * b).astype(LOW)
        out = tensor_sum(mat_mul_t(v["f"], down_t))
        layer_outs.append((v["h1"] + out).astype(LOW))
        v["dy"] = cotangent[u]
        df = mat_mul(v["dy"], down_t)
        v["dab"] = jnp.concatenate(
            [(df * b * sig * (1.0 + a * (1.0 - sig))).astype(LOW), (df * a * sig).astype(LOW)], axis=1)
        v["dn2"] = tensor_sum(mat_mul_t(v["dab"], gate_up))
    g_gate_up = sum(outer_sum(saved[u]["n2"], saved[u]["dab"]) for u in units).astype(LOW)
    g_down = sum(outer_sum(saved[u]["dy"], saved[u]["f"]) for u in units).astype(LOW)
    g_fourth = scatter_rows(jnp.concatenate([g_gate_up, g_down], axis=1))

    g_gain_two = 0.0
    for u in units:
        v = saved[u]
        d_hidden = norm_backward(v["h1"], v["r2"], gain_two, v["dn2"]) + v["dy"].astype(F32)
        g_gain_two = g_gain_two + jnp.sum(v["dn2"] * v["h1"] * v["r2"], axis=0)
        v["dh"] = d_hidden
        v["dm"] = d_hidden.astype(LOW)
        v["dog"] = mat_mul(v["dm"], third)
    g_third = scatter_rows(sum(outer_sum(saved[u]["dm"], saved[u]["og"]) for u in units).astype(LOW))
    head_grads = 0.0
    for u in units:
        v = saved[u]
        d_att = v["dog"][:, :q_dim].astype(LOW).reshape(block_len, kv_heads, q_group, HEAD_WIDTH)
        d_gated = v["dog"][:, q_dim:].reshape(block_len, heads, head_dim)

        def values_of(x_in, b_in, c_in, step_in, z_in, log_a, bias_in, skip_in, state_in):
            return mixer_values(x_in, b_in, c_in, step_in, z_in, log_a, bias_in, skip_in, state_in, v["inside"], v["carried"])

        pull = jax.vjp(values_of, v["xs"], v["b"], v["c"], v["dr"], v["z"], a_log, dt_bias, d_skip, v["state"])[1]
        gx1, gb1, gc1, gdr1, gz, ga1, gbias1, gskip, local = pull(d_gated)
        locals_ = gather_context(local.astype(LOW))
        later = nothing[1]
        for k in range(nc - 1, 0, -1):
            new = v["passes"][k][:, None, None] * later + locals_[k].astype(F32)
            later = jnp.where(k > ci, new, later)
        d_pass = jnp.sum(later * v["state"], axis=(1, 2))

        def state_of(x_in, b_in, step_in, log_a, bias_in):
            return mixer_state(x_in, b_in, step_in, log_a, bias_in, v["closing"], v["carried"][-1])

        gx2, gb2, gdr2, ga2, gbias2 = jax.vjp(state_of, v["xs"], v["b"], v["dr"], a_log, dt_bias)[1]((d_pass, later))
        head_grads = head_grads + jnp.stack([ga1 + ga2, gbias1 + gbias2, gskip])
        v["dzx"] = jnp.concatenate([gz.reshape(block_len, ssm_dim), (gx1 + gx2).reshape(block_len, ssm_dim)], axis=1).astype(LOW)
        v["ddr"] = (gdr1 + gdr2).astype(LOW)
        v["dbc"] = tensor_sum(jnp.concatenate([gb1 + gb2, gc1], axis=1)).astype(LOW)
        v["dbc_part"] = jnp.concatenate([gb1 + gb2, gc1], axis=1).astype(LOW)

        q4 = v["q"].reshape(block_len, kv_heads, q_group, HEAD_WIDTH)
        prob = jnp.exp(masked_scores(q4, v["k_all"], v["allowed"]) - v["lse"])
        d_prob = jnp.einsum("tgqd,jgd->gqtj", d_att, v["v_all"], preferred_element_type=F32)
        d_values = jnp.einsum("gqtj,tgqd->jgd", prob.astype(LOW), d_att, preferred_element_type=F32)
        d_scores = (prob * (d_prob - jnp.sum(prob * d_prob, axis=-1, keepdims=True))).astype(LOW)
        dq = jnp.einsum("gqtj,jgd->tgqd", d_scores, v["k_all"], preferred_element_type=F32) * 0.125
        d_keys = jnp.einsum("gqtj,tgqd->jgd", d_scores, q4, preferred_element_type=F32) * 0.125
        v["dq"] = dq.astype(LOW).reshape(block_len, q_dim)
        part = jnp.concatenate([d_keys.reshape(full_len, kv_dim), d_values.reshape(full_len, kv_dim)], axis=1)
        part = part.astype(LOW).reshape(nc, block_len, 2 * kv_dim)
        left = nc
        for bit in context_bits():
            left //= 2
            view = part.reshape(left, 2, block_len, 2 * kv_dim)
            mine = (ci & bit) // bit
            away = lax.dynamic_index_in_dim(view, 1 - mine, 1, keepdims=False)
            keep = lax.dynamic_index_in_dim(view, mine, 1, keepdims=False)
            part = (keep.astype(F32) + swap_context(away, bit).astype(F32)).astype(LOW)
        v["dkv"] = part.reshape(block_len, 2 * kv_dim)
        zeros = jnp.zeros((block_len, pad + 2), LOW)
        v["d_first"] = jnp.concatenate([v["dq"], v["dkv"], v["dbc"], v["ddr"], zeros], axis=1)
        v["d_first_part"] = jnp.concatenate([v["dq"], v["dkv"], v["dbc_part"], v["ddr"], zeros], axis=1)
    g_second = scatter_rows(sum(outer_sum(saved[u]["n1"], saved[u]["dzx"]) for u in units).astype(LOW))
    input_grads = []
    g_gain_one = 0.0
    for u in units:
        v = saved[u]
        dn1 = tensor_sum(mat_mul_t(v["d_first_part"], first) + mat_mul_t(v["dzx"], second))
        g_gain_one = g_gain_one + jnp.sum(dn1 * v["x"] * v["r1"], axis=0)
        input_grads.append(v["dh"] + norm_backward(v["x"], v["r1"], gain_one, dn1))
    g_first = sum(outer_sum(saved[u]["n1"], saved[u]["d_first"]) for u in units)
    at_gain = at_dt + heads
    g_first = jnp.concatenate(
        [g_first[:, :at_gain], g_gain_one[:, None], g_gain_two[:, None], g_first[:, at_gain + 2 :]], axis=1)
    g_first = scatter_rows(g_first.astype(LOW))
    head_grads = all_sum(head_grads)

    shape = (micro_count, seq_count, block_len, model_dim)
    at_k, at_v = q_dim, q_dim + kv_dim
    return (
        jnp.stack(layer_outs).reshape(shape),
        jnp.stack(input_grads).reshape(shape),
        g_first[:, at_gain],
        g_first[:, :at_k],
        g_first[:, at_k:at_v],
        g_first[:, at_v:at_b],
        g_second[:, :ssm_dim],
        g_second[:, ssm_dim:],
        g_first[:, at_b : at_b + state_dim],
        g_first[:, at_b + state_dim : at_dt],
        g_first[:, at_dt:at_gain],
        head_grads[0],
        head_grads[1],
        head_grads[2],
        g_third[:, :q_dim].T,
        g_third[:, q_dim:].T,
        g_first[:, at_gain + 1],
        g_fourth[:, :ff_dim],
        g_fourth[:, ff_dim : 2 * ff_dim],
        g_fourth[:, 2 * ff_dim :].T,
    )


def solution(mesh):
    rows, cols = P("fsdp", "tensor"), P("tensor", "fsdp")
    acts = P(None, "fsdp", "context", None)
    return jax.shard_map(
        per_device,
        mesh=mesh,
        in_specs=(
            acts, acts, P(None, "fsdp", None), P("fsdp"), rows, rows, rows, rows, rows, P("fsdp", None),
            P("fsdp", None), rows, P("tensor"), P("tensor"), P("tensor"), cols, cols, P("fsdp"), rows, rows, cols,
        ),
        out_specs=(
            acts, acts, P("fsdp"), rows, rows, rows, rows, rows, P("fsdp", None), P("fsdp", None), rows,
            P("tensor"), P("tensor"), P("tensor"), cols, cols, P("fsdp"), rows, rows, cols,
        ),
        check_vma=False,
    )
```

time: 2140 us -> 992 us (0.46)
  waiting for transfers between devices: 1220 us -> 259 us
  blocking collectives: 229 us -> 0 us
  matrix products: 440 us -> 260 us
  local copies, waits for them, and re-layouts: 92.4 us -> 230 us
  starting transfers between devices: 2.68 us -> 84.9 us
    reduce_scatter x28 -> x0, waiting for transfers between devices: 727 us -> none  [the longest x2 91.1 us: per_device(): lax.psum_scatter(grad_gate.astype(jnp.bfloat16), 'fsdp', scatter_dimensio...]
    psum x5 -> x0, waiting for transfers between devices: 367 us -> none  [the longest x1 121 us: per_device(): lax.psum(s_two, 'context').astype(jnp.float32)]
    ppermute x0 -> x110, waiting for transfers between devices: none -> 259 us  [the longest x10 127 us: tensor_sum(): lax.ppermute(low, 'tensor', [(i, (i + 1) % size) for i in range(size)])]
    all_gather x17 -> x0, blocking collectives: 186 us -> none  [the longest x4 27.9 us: carried_in_2(): lax.all_gather(part.astype(kind), axis)]
    dot_general x70 -> x52, matrix products: 320 us -> 198 us  [the longest x6 42.2 us: mixer_values(): result = jnp.einsum('htu,uhp->thp', kernel, x_in)]
    all_gather x8 -> x0, waiting for transfers between devices: 119 us -> none  [the longest x1 41.8 us: fetch_weights(): lax.all_gather(w_gate, 'fsdp', axis=0, tiled=True)]
    ppermute x0 -> x110, starting transfers between devices: none -> 84.9 us  [the longest x74 37.9 us: swap_context(): return lax.ppermute(x, 'context', [(i, i ^ bit) for i in range(size)])]
    dynamic_update_slice x0 -> x93, local copies, waits for them, and re-layouts: none -> 74.4 us  [the longest x48 37.6 us: gather_rows(): lax.dynamic_update_slice(full, arr[None, None], ((fi + k) % nf, ci ^ off,...]
  transfers between devices with their start and end apart: 41 -> 110, of which waited for: 34 -> 38; matrix products, arithmetic and copies ran while one was open for 15% -> 60% of each run, Pallas kernels for 0% -> 0%
where the time goes in v1:
time: 992 us; the launch traced here: 981 us
  matrix products  260 us (26%)
  waiting for transfers between devices  259 us (26%)
  local copies, waits for them, and re-layouts  230 us (23%)
  other arithmetic  143 us (14%)
  starting transfers between devices  84.9 us (9%)
    ppermute x10, waiting for transfers between devices, tensor_sum(): lax.ppermute(low, 'tensor', [(i, (i + 1) % size) for i in range(size)])  127 us
    ppermute x74, waiting for transfers between devices, swap_context(): return lax.ppermute(x, 'context', [(i, i ^ bit) for i in range(size)])  76.8 us
    ppermute x24, waiting for transfers between devices, from_next(): return lax.ppermute(x, axis, [((i + step) % size, i) for i in range(size)])  53.4 us
    dot_general x6, matrix products, mixer_values(): result = jnp.einsum('htu,uhp->thp', kernel, x_in)  42.2 us
    ppermute x74, starting transfers between devices, swap_context(): return lax.ppermute(x, 'context', [(i, i ^ bit) for i in range(size)])  37.9 us
    dynamic_update_slice x48, local copies, waits for them, and re-layouts, gather_rows(): lax.dynamic_update_slice(full, arr[None, None], ((fi + k) % nf, ci ^ off,...  37.6 us
    dot_general x10, matrix products, mat_mul_t(): lax.dot_general(left, right, (((1,), (1,)), ((), ())), preferred_element_...  37.3 us
    ppermute x24, starting transfers between devices, from_next(): return lax.ppermute(x, axis, [((i + step) % size, i) for i in range(size)])  33.8 us
  transfers between devices with their start and end apart: 110, of which 38 were waited for; matrix products, arithmetic and copies ran while one was open for 60% of the time, Pallas kernels for 0%

profile of v1, /device:TPU:0, one launch (start us, length us, event | category | flops | bytes accessed | tf_op | source)
XLA Modules:
  0.0 980.7 jit_solution(14607618912492712028)
XLA Ops:
  5.3 5.0 collective-permute-start.40
  24.3 3.6 fusion.56
  51.5 3.7 collective-permute-start.4
  68.1 5.5 collective-permute-done.35
  165.9 5.7 dynamic_update_slice.322
  175.9 3.9 fusion.21
  179.9 3.7 exponential_reduce_fusion
  188.2 5.7 dynamic_update_slice.323
  195.1 8.7 fusion.20
  203.8 9.2 exponential_reduce_fusion.1
  213.1 9.2 convolution_convert_fusion.5
  222.4 6.5 convolution_convert_fusion.4
  249.8 3.8 fusion.362
  263.1 3.8 fusion.358
  299.2 5.6 multiply_convert_fusion.4
  312.4 5.5 multiply_convert_fusion.5
  321.9 12.3 %collective-permute-done.56 = bf16[512,1024]{1,0:T(8,128)(2,1)S(1)} collective-permute-done((bf16[512,1024]{1,0:T(8,128)(2,1)S(1)}, bf16[512,1024]{1,0:T(8,128)(2,1)S(1)}, u32[]{:S(2)}, u32[]{:S(2)}) %collective-permute-start.56) | collective-permute-done | bytes 1048608 | tf_op jit(solution)/shard_map/ppermute | solution.py:100
  334.2 21.9 %collective-permute-done.39 = bf16[512,1024]{1,0:T(8,128)(2,1)S(1)} collective-permute-done((bf16[512,1024]{1,0:T(8,128)(2,1)S(1)}, bf16[512,1024]{1,0:T(8,128)(2,1)S(1)}, u32[]{:S(2)}, u32[]{:S(2)}) %collective-permute-start.39) | collective-permute-done | bytes 1048608 | tf_op jit(solution)/shard_map/ppermute | solution.py:100
  375.0 3.5 fusion.115
  378.4 3.4 fusion.160
  386.5 3.9 fusion.127
  390.4 3.9 convolution_convert_fusion
  396.3 4.8 pad_maximum_fusion
  401.1 3.7 dynamic-slice_bitcast_fusion
  404.8 6.0 collective-permute-done.65
  410.9 22.5 %collective-permute-done.58 = bf16[512,1024]{1,0:T(8,128)(2,1)} collective-permute-done((bf16[512,1024]{1,0:T(8,128)(2,1)S(1)}, bf16[512,1024]{1,0:T(8,128)(2,1)}, u32[]{:S(2)}, u32[]{:S(2)}) %collective-permute-start.58) | collective-permute-done | bytes 1048608 | tf_op jit(solution)/shard_map/ppermute | solution.py:100
  433.3 4.0 multiply_reduce_fusion.5
  437.4 18.4 %collective-permute-done.46 = bf16[512,1024]{1,0:T(8,128)(2,1)} collective-permute-done((bf16[512,1024]{1,0:T(8,128)(2,1)}, bf16[512,1024]{1,0:T(8,128)(2,1)}, u32[]{:S(2)}, u32[]{:S(2)}) %collective-permute-start.46) | collective-permute-done | bytes 1048608 | tf_op jit(solution)/shard_map/ppermute | solution.py:100
  455.8 20.9 %collective-permute-done.57 = bf16[512,1024]{1,0:T(8,128)(2,1)} collective-permute-done((bf16[512,1024]{1,0:T(8,128)(2,1)}, bf16[512,1024]{1,0:T(8,128)(2,1)}, u32[]{:S(2)}, u32[]{:S(2)}) %collective-permute-start.57) | collective-permute-done | bytes 1048608 | tf_op jit(solution)/shard_map/ppermute | solution.py:100
  476.7 5.3 convert_add_fusion.7
  482.1 3.4 fusion.243
  493.4 5.6 multiply_reduce_fusion.15
  499.0 10.2 %fusion.27 = (f32[12,512]{1,0:T(8,128)}, f32[12,512]{1,0:T(8,128)}, f32[12,512]{1,0:T(8,128)}, bf16[512,512]{1,0:T(8,128)(2,1)}) fusion(f32[12,512]{1,0:T(8,128)S(1)} %copy-done.175, f32[512,512]{1,0:T(8,128)S(1)} %copy-done.90, f32[12,512]{1,0:T(8,128)S(1)} %copy-done.136, pred[512,512]{1,0:T(8,128)(4,1)S(1)} %copy-done.131, ...), kind=kOutput, calls=%fused_computation.42 | convolution fusion | flops 443267072 | bytes 5103616 | tf_op jit(solution)/shard_map/transpose(jvp(htu,uhp->thp))/dot_general | solution.py:149
  518.3 5.1 multiply_reduce_fusion.14
  523.4 10.6 %fusion.29 = (f32[12,512]{1,0:T(8,128)}, f32[12,512]{1,0:T(8,128)}, f32[12,512]{1,0:T(8,128)}, bf16[512,512]{1,0:T(8,128)(2,1)}) fusion(f32[12,512]{1,0:T(8,128)S(1)} %copy-done.173, f32[512,512]{1,0:T(8,128)S(1)} %copy-done.88, f32[12,512]{1,0:T(8,128)S(1)} %copy-done.140, pred[512,512]{1,0:T(8,128)(4,1)S(1)} %copy-done.129, ...), kind=kOutput, calls=%fused_computation.44 | convolution fusion | flops 443267072 | bytes 5103616 | tf_op jit(solution)/shard_map/transpose(jvp(htu,uhp->thp))/dot_general | solution.py:149
  540.0 8.9 fusion.87
  549.0 12.7 %fusion.3 = (f32[4,512]{1,0:T(4,128)S(1)}, f32[2048,512,4]{1,0,2:T(8,128)}) fusion(f32[2048,512,4]{1,0,2:T(8,128)} %get-tuple-element.329, f32[4,512]{1,0:T(4,128)S(1)} %copy-done.157, pred[512,2048]{0,1:T(8,128)(4,1)S(1)} %copy-done.17, bf16[512,4,64]{0,2,1:T(8,128)(2,1)S(1)} %bitcast.1161, bf16[2048,128]{0,1:T(8,128)(2,1)S(1)} %bitcast.1150), kind=kOutput, calls=%fused_computation.9 | convolution fusion | flops 557840384 | bytes 35143680 | tf_op jit(solution)/shard_map/tgqd,jgd->gqtj/dot_general | solution.py:319
  561.7 8.5 fusion.24
  577.1 8.9 fusion.86
  586.1 12.9 %fusion = (f32[4,512]{1,0:T(4,128)S(1)}, f32[2048,512,4]{1,0,2:T(8,128)}) fusion(f32[2048,512,4]{1,0,2:T(8,128)} %copy-done, f32[4,512]{1,0:T(4,128)S(1)} %copy-done.117, pred[512,2048]{0,1:T(8,128)(4,1)S(1)} %copy-done.4, bf16[512,4,64]{0,2,1:T(8,128)(2,1)S(1)} %bitcast.1156, bf16[2048,128]{1,0:T(8,128)(2,1)} %bitcast.122), kind=kOutput, calls=%fused_computation.4 | convolution fusion | flops 557840384 | bytes 35405824 | tf_op jit(solution)/shard_map/tgqd,jgd->gqtj/dot_general | solution.py:319
  599.1 8.7 fusion.25
  663.2 3.8 fusion.141
  667.0 4.7 fusion.228
  671.7 5.1 fusion.229
  677.6 3.4 multiply_reduce_fusion.10
  696.3 6.6 fusion.136
  703.0 5.1 fusion.227
  716.3 4.8 concatenate.130
  721.1 4.4 add_convert_fusion.6
  733.0 5.7 concatenate.124
  739.5 4.3 add_convert_fusion.7
  751.8 3.9 concatenate.133
  760.2 6.0 concatenate.135
  780.5 19.8 %collective-permute-done.64 = bf16[512,1024]{1,0:T(8,128)(2,1)} collective-permute-done((bf16[512,1024]{1,0:T(8,128)(2,1)}, bf16[512,1024]{1,0:T(8,128)(2,1)}, u32[]{:S(2)}, u32[]{:S(2)}) %collective-permute-start.64) | collective-permute-done | bytes 1048608 | tf_op jit(solution)/shard_map/ppermute | solution.py:100
  800.2 3.7 fusion.97
  807.3 4.1 fusion.92
  819.6 5.8 collective-permute-done.97
  845.4 21.5 %collective-permute-done.75 = bf16[4,1,64,768]{3,2,1,0:T(8,128)(2,1)S(1)} collective-permute-done((bf16[4,1,64,768]{3,2,1,0:T(8,128)(2,1)S(1)}, bf16[4,1,64,768]{3,2,1,0:T(8,128)(2,1)S(1)}, u32[]{:S(2)}, u32[]{:S(2)}) %collective-permute-start.75) | collective-permute-done | bytes 393248 | tf_op jit(solution)/shard_map/ppermute | solution.py:14
  873.3 4.3 collective-permute-done.77
  881.6 27.5 %collective-permute-done.79 = bf16[64,768]{1,0:T(8,128)(2,1)S(1)} collective-permute-done((bf16[64,768]{1,0:T(8,128)(2,1)S(1)}, bf16[64,768]{1,0:T(8,128)(2,1)S(1)}, u32[]{:S(2)}, u32[]{:S(2)}) %collective-permute-start.79) | collective-permute-done | bytes 98336 | tf_op jit(solution)/shard_map/ppermute | solution.py:14
  921.3 3.5 collective-permute-done.87
  930.9 8.6 collective-permute-done.104
  939.5 24.8 %collective-permute-done.105 = bf16[64,3072]{1,0:T(8,128)(2,1)S(1)} collective-permute-done((bf16[64,3072]{1,0:T(8,128)(2,1)S(1)}, bf16[64,3072]{1,0:T(8,128)(2,1)S(1)}, u32[]{:S(2)}, u32[]{:S(2)}) %collective-permute-start.105) | collective-permute-done | bytes 393248 | tf_op jit(solution)/shard_map/ppermute | solution.py:19
  967.4 8.0 collective-permute-done.107
  (1069 shorter events, 467.9 us)
Async XLA Ops:
  5.3 72.8 %collective-permute-start.40 = (bf16[64,3072]{1,0:T(8,128)(2,1)}, bf16[64,3072]{1,0:T(8,128)(2,1)S(1)}, u32[]{:S(2)}, u32[]{:S(2)}) collective-permute-start(bf16[64,3072]{1,0:T(8,128)(2,1)} %constant_dynamic-slice_fusion.6), channel_id=1, source_target_pairs={{8,0},{16,8},{24,16},{0,24},{9,1},{17,9},{25,17},{1,25},{10,2},{18... | collective-permute-start | bytes 1179656 | tf_op jit(solution)/shard_map/ppermute | solution.py:19
  12.0 36.6 %collective-permute-start = (bf16[64,768]{1,0:T(8,128)(2,1)}, bf16[64,768]{1,0:T(8,128)(2,1)}, u32[]{:S(2)}, u32[]{:S(2)}) collective-permute-start(bf16[64,768]{1,0:T(8,128)(2,1)} %constant_dynamic-slice_fusion.8), channel_id=1, source_target_pairs={{8,0},{16,8},{24,16},{0,24},{9,1},{17,9},{25,17},{1,25},{10,2},{18... | collective-permute-start | bytes 294920 | tf_op jit(solution)/shard_map/ppermute | solution.py:19
  13.5 45.2 %collective-permute-start.15 = (bf16[64,1536]{1,0:T(8,128)(2,1)}, bf16[64,1536]{1,0:T(8,128)(2,1)}, u32[]{:S(2)}, u32[]{:S(2)}) collective-permute-start(bf16[64,1536]{1,0:T(8,128)(2,1)} %constant_dynamic-slice_fusion.7), channel_id=1, source_target_pairs={{8,0},{16,8},{24,16},{0,24},{9,1},{17,9},{25,17},{1,25},{10,2},{18... | collective-permute-start | bytes 589832 | tf_op jit(solution)/shard_map/ppermute | solution.py:19
  15.8 35.7 %collective-permute-start.33 = (bf16[64,1024]{1,0:T(8,128)(2,1)}, bf16[64,1024]{1,0:T(8,128)(2,1)}, u32[]{:S(2)}, u32[]{:S(2)}) collective-permute-start(bf16[64,1024]{1,0:T(8,128)(2,1)} %fusion.379), channel_id=1, source_target_pairs={{8,0},{16,8},{24,16},{0,24},{9,1},{17,9},{25,17},{1,25},{10,2},{18... | collective-permute-start | bytes 393224 | tf_op jit(solution)/shard_map/ppermute | solution.py:19
  50.6 10.2 %collective-permute-start.2 = (bf16[64,768]{1,0:T(8,128)(2,1)}, bf16[64,768]{1,0:T(8,128)(2,1)S(1)}, u32[]{:S(2)}, u32[]{:S(2)}) collective-permute-start(bf16[64,768]{1,0:T(8,128)(2,1)} %collective-permute-done), channel_id=1, source_target_pairs={{0,2},{2,0},{4,6},{6,4},{1,3},{3,1},{5,7},{7,5},{8,10},{10,8},{12,... | collective-permute-start | bytes 294920 | tf_op jit(solution)/shard_map/ppermute | solution.py:14
  62.6 15.5 %collective-permute-start.8 = (bf16[64,768]{1,0:T(8,128)(2,1)S(1)}, bf16[64,768]{1,0:T(8,128)(2,1)S(1)}, u32[]{:S(2)}, u32[]{:S(2)}) collective-permute-start(bf16[64,768]{1,0:T(8,128)(2,1)S(1)} %collective-permute-done.4), channel_id=1, source_target_pairs={{8,0},{16,8},{24,16},{0,24},{9,1},{17,9},{25,17},{1,25},{10,2},{18... | collective-permute-start | bytes 294920 | tf_op jit(solution)/shard_map/ppermute | solution.py:19
  66.0 13.6 %collective-permute-start.16 = (bf16[64,1536]{1,0:T(8,128)(2,1)}, bf16[64,1536]{1,0:T(8,128)(2,1)S(1)}, u32[]{:S(2)}, u32[]{:S(2)}) collective-permute-start(bf16[64,1536]{1,0:T(8,128)(2,1)} %collective-permute-done.15), channel_id=1, source_target_pairs={{0,4},{2,6},{4,0},{6,2},{1,5},{3,7},{5,1},{7,3},{8,12},{10,14},{12... | collective-permute-start | bytes 589832 | tf_op jit(solution)/shard_map/ppermute | solution.py:14
  67.5 14.4 %collective-permute-start.17 = (bf16[64,1536]{1,0:T(8,128)(2,1)}, bf16[64,1536]{1,0:T(8,128)(2,1)S(1)}, u32[]{:S(2)}, u32[]{:S(2)}) collective-permute-start(bf16[64,1536]{1,0:T(8,128)(2,1)} %collective-permute-done.15), channel_id=1, source_target_pairs={{0,2},{2,0},{4,6},{6,4},{1,3},{3,1},{5,7},{7,5},{8,10},{10,8},{12,... | collective-permute-start | bytes 589832 | tf_op jit(solution)/shard_map/ppermute | solution.py:14
  73.6 72.1 %collective-permute-start.19 = (bf16[64,1536]{1,0:T(8,128)(2,1)}, bf16[64,1536]{1,0:T(8,128)(2,1)}, u32[]{:S(2)}, u32[]{:S(2)}) collective-permute-start(bf16[64,1536]{1,0:T(8,128)(2,1)} %collective-permute-done.15), channel_id=1, source_target_pairs={{8,0},{16,8},{24,16},{0,24},{9,1},{17,9},{25,17},{1,25},{10,2},{18... | collective-permute-start | bytes 589832 | tf_op jit(solution)/shard_map/ppermute | solution.py:19
  80.5 148.3 %collective-permute-start.36 = (bf16[3,64,1024]{2,1,0:T(8,128)(2,1)}, bf16[3,64,1024]{2,1,0:T(8,128)(2,1)}, u32[]{:S(2)}, u32[]{:S(2)}) collective-permute-start(bf16[3,64,1024]{2,1,0:T(8,128)(2,1)} %pad_maximum_fusion.23), channel_id=1, source_target_pairs={{0,4},{2,6},{4,0},{6,2},{1,5},{3,7},{5,1},{7,3},{8,12},{10,14},{12... | collective-permute-start | bytes 1179656 | tf_op jit(solution)/shard_map/ppermute | solution.py:14
  81.9 151.7 %collective-permute-start.37 = (bf16[3,64,1024]{2,1,0:T(8,128)(2,1)}, bf16[3,64,1024]{2,1,0:T(8,128)(2,1)}, u32[]{:S(2)}, u32[]{:S(2)}) collective-permute-start(bf16[3,64,1024]{2,1,0:T(8,128)(2,1)} %pad_maximum_fusion.23), channel_id=1, source_target_pairs={{0,2},{2,0},{4,6},{6,4},{1,3},{3,1},{5,7},{7,5},{8,10},{10,8},{12,... | collective-permute-start | bytes 1179656 | tf_op jit(solution)/shard_map/ppermute | solution.py:14
  83.4 155.4 %collective-permute-start.41 = (bf16[64,3072]{1,0:T(8,128)(2,1)S(1)}, bf16[64,3072]{1,0:T(8,128)(2,1)}, u32[]{:S(2)}, u32[]{:S(2)}) collective-permute-start(bf16[64,3072]{1,0:T(8,128)(2,1)S(1)} %collective-permute-done.40), channel_id=1, source_target_pairs={{8,0},{16,8},{24,16},{0,24},{9,1},{17,9},{25,17},{1,25},{10,2},{18... | collective-permute-start | bytes 1179656 | tf_op jit(solution)/shard_map/ppermute | solution.py:19
  115.2 20.5 %collective-permute-start.50 = (f32[12]{0:T(128)}, f32[12]{0:T(128)}, u32[]{:S(2)}, u32[]{:S(2)}) collective-permute-start(f32[12]{0:T(128)} %broadcast_select_fusion.1), channel_id=1, source_target_pairs={{0,4},{2,6},{4,0},{6,2},{1,5},{3,7},{5,1},{7,3},{8,12},{10,14},{12... | collective-permute-start | bytes 152 | tf_op jit(solution)/shard_map/ppermute | solution.py:14
  159.4 12.2 %collective-permute-start.47 = (bf16[512,128]{1,0:T(8,128)(2,1)}, bf16[512,128]{1,0:T(8,128)(2,1)}, u32[]{:S(2)}, u32[]{:S(2)}) collective-permute-start(bf16[512,128]{1,0:T(8,128)(2,1)} %slice.462), channel_id=1, source_target_pairs={{0,4},{2,6},{4,0},{6,2},{1,5},{3,7},{5,1},{7,3},{8,12},{10,14},{12... | collective-permute-start | bytes 393224 | tf_op jit(solution)/shard_map/ppermute | solution.py:14
  163.7 21.9 %collective-permute-start.23 = (bf16[64,1536]{1,0:T(8,128)(2,1)}, bf16[64,1536]{1,0:T(8,128)(2,1)}, u32[]{:S(2)}, u32[]{:S(2)}) collective-permute-start(bf16[64,1536]{1,0:T(8,128)(2,1)} %collective-permute-done.19), channel_id=1, source_target_pairs={{8,0},{16,8},{24,16},{0,24},{9,1},{17,9},{25,17},{1,25},{10,2},{18... | collective-permute-start | bytes 589832 | tf_op jit(solution)/shard_map/ppermute | solution.py:19
  174.9 10.9 %collective-permute-start.14 = (bf16[512,128]{1,0:T(8,128)(2,1)}, bf16[512,128]{1,0:T(8,128)(2,1)}, u32[]{:S(2)}, u32[]{:S(2)}) collective-permute-start(bf16[512,128]{1,0:T(8,128)(2,1)} %copy-done.151), channel_id=1, source_target_pairs={{0,2},{2,0},{4,6},{6,4},{1,3},{3,1},{5,7},{7,5},{8,10},{10,8},{12,... | collective-permute-start | bytes 393224 | tf_op jit(solution)/shard_map/ppermute | solution.py:14
  185.6 58.0 %collective-permute-start.22 = (bf16[64,1536]{1,0:T(8,128)(2,1)}, bf16[64,1536]{1,0:T(8,128)(2,1)}, u32[]{:S(2)}, u32[]{:S(2)}) collective-permute-start(bf16[64,1536]{1,0:T(8,128)(2,1)} %collective-permute-done.20), channel_id=1, source_target_pairs={{0,2},{2,0},{4,6},{6,4},{1,3},{3,1},{5,7},{7,5},{8,10},{10,8},{12,... | collective-permute-start | bytes 589832 | tf_op jit(solution)/shard_map/ppermute | solution.py:14
  185.8 61.0 %collective-permute-start.24 = (bf16[64,1536]{1,0:T(8,128)(2,1)}, bf16[64,1536]{1,0:T(8,128)(2,1)}, u32[]{:S(2)}, u32[]{:S(2)}) collective-permute-start(bf16[64,1536]{1,0:T(8,128)(2,1)} %collective-permute-done.23), channel_id=1, source_target_pairs={{0,4},{2,6},{4,0},{6,2},{1,5},{3,7},{5,1},{7,3},{8,12},{10,14},{12... | collective-permute-start | bytes 589832 | tf_op jit(solution)/shard_map/ppermute | solution.py:14
  228.8 19.6 %collective-permute-start.25 = (bf16[64,1536]{1,0:T(8,128)(2,1)}, bf16[64,1536]{1,0:T(8,128)(2,1)S(1)}, u32[]{:S(2)}, u32[]{:S(2)}) collective-permute-start(bf16[64,1536]{1,0:T(8,128)(2,1)} %collective-permute-done.23), channel_id=1, source_target_pairs={{0,2},{2,0},{4,6},{6,4},{1,3},{3,1},{5,7},{7,5},{8,10},{10,8},{12,... | collective-permute-start | bytes 589832 | tf_op jit(solution)/shard_map/ppermute | solution.py:14
  233.6 49.2 %collective-permute-start.38 = (bf16[3,64,1024]{2,1,0:T(8,128)(2,1)}, bf16[3,64,1024]{2,1,0:T(8,128)(2,1)}, u32[]{:S(2)}, u32[]{:S(2)}) collective-permute-start(bf16[3,64,1024]{2,1,0:T(8,128)(2,1)} %collective-permute-done.36), channel_id=1, source_target_pairs={{0,2},{2,0},{4,6},{6,4},{1,3},{3,1},{5,7},{7,5},{8,10},{10,8},{12,... | collective-permute-start | bytes 1179656 | tf_op jit(solution)/shard_map/ppermute | solution.py:14
  238.8 48.8 %collective-permute-start.42 = (bf16[64,3072]{1,0:T(8,128)(2,1)}, bf16[64,3072]{1,0:T(8,128)(2,1)}, u32[]{:S(2)}, u32[]{:S(2)}) collective-permute-start(bf16[64,3072]{1,0:T(8,128)(2,1)} %collective-permute-done.41), channel_id=1, source_target_pairs={{8,0},{16,8},{24,16},{0,24},{9,1},{17,9},{25,17},{1,25},{10,2},{18... | collective-permute-start | bytes 1179656 | tf_op jit(solution)/shard_map/ppermute | solution.py:19
  261.4 30.8 %collective-permute-start.53 = (bf16[12,64,128]{2,1,0:T(8,128)(2,1)S(1)}, bf16[12,64,128]{2,1,0:T(8,128)(2,1)}, u32[]{:S(2)}, u32[]{:S(2)}) collective-permute-start(bf16[12,64,128]{2,1,0:T(8,128)(2,1)S(1)} %get-tuple-element.331), channel_id=1, source_target_pairs={{0,4},{2,6},{4,0},{6,2},{1,5},{3,7},{5,1},{7,3},{8,12},{10,14},{12... | collective-permute-start | bytes 589832 | tf_op jit(solution)/shard_map/ppermute | solution.py:14
  262.9 32.7 %collective-permute-start.54 = (bf16[12,64,128]{2,1,0:T(8,128)(2,1)S(1)}, bf16[12,64,128]{2,1,0:T(8,128)(2,1)}, u32[]{:S(2)}, u32[]{:S(2)}) collective-permute-start(bf16[12,64,128]{2,1,0:T(8,128)(2,1)S(1)} %get-tuple-element.331), channel_id=1, source_target_pairs={{0,2},{2,0},{4,6},{6,4},{1,3},{3,1},{5,7},{7,5},{8,10},{10,8},{12,... | collective-permute-start | bytes 589832 | tf_op jit(solution)/shard_map/ppermute | solution.py:14
  279.2 14.4 %collective-permute-start.30 = (bf16[12,64,128]{2,1,0:T(8,128)(2,1)}, bf16[12,64,128]{2,1,0:T(8,128)(2,1)}, u32[]{:S(2)}, u32[]{:S(2)}) collective-permute-start(bf16[12,64,128]{2,1,0:T(8,128)(2,1)} %get-tuple-element.323), channel_id=1, source_target_pairs={{0,4},{2,6},{4,0},{6,2},{1,5},{3,7},{5,1},{7,3},{8,12},{10,14},{12... | collective-permute-start | bytes 589832 | tf_op jit(solution)/shard_map/ppermute | solution.py:14
  282.8 14.0 %collective-permute-start.31 = (bf16[12,64,128]{2,1,0:T(8,128)(2,1)}, bf16[12,64,128]{2,1,0:T(8,128)(2,1)S(1)}, u32[]{:S(2)}, u32[]{:S(2)}) collective-permute-start(bf16[12,64,128]{2,1,0:T(8,128)(2,1)} %get-tuple-element.323), channel_id=1, source_target_pairs={{0,2},{2,0},{4,6},{6,4},{1,3},{3,1},{5,7},{7,5},{8,10},{10,8},{12,... | collective-permute-start | bytes 589832 | tf_op jit(solution)/shard_map/ppermute | solution.py:14
  288.8 32.8 %collective-permute-start.43 = (bf16[3,64,3072]{2,1,0:T(8,128)(2,1)S(1)}, bf16[3,64,3072]{2,1,0:T(8,128)(2,1)S(1)}, u32[]{:S(2)}, u32[]{:S(2)}) collective-permute-start(bf16[3,64,3072]{2,1,0:T(8,128)(2,1)S(1)} %pad_maximum_fusion.11), channel_id=1, source_target_pairs={{0,4},{2,6},{4,0},{6,2},{1,5},{3,7},{5,1},{7,3},{8,12},{10,14},{12... | collective-permute-start | bytes 3538952 | tf_op jit(solution)/shard_map/ppermute | solution.py:14
  292.2 29.6 %collective-permute-start.44 = (bf16[3,64,3072]{2,1,0:T(8,128)(2,1)S(1)}, bf16[3,64,3072]{2,1,0:T(8,128)(2,1)S(1)}, u32[]{:S(2)}, u32[]{:S(2)}) collective-permute-start(bf16[3,64,3072]{2,1,0:T(8,128)(2,1)S(1)} %pad_maximum_fusion.11), channel_id=1, source_target_pairs={{0,2},{2,0},{4,6},{6,4},{1,3},{3,1},{5,7},{7,5},{8,10},{10,8},{12,... | collective-permute-start | bytes 3538952 | tf_op jit(solution)/shard_map/ppermute | solution.py:14
  295.6 14.2 %collective-permute-start.32 = (bf16[12,64,128]{2,1,0:T(8,128)(2,1)}, bf16[12,64,128]{2,1,0:T(8,128)(2,1)S(1)}, u32[]{:S(2)}, u32[]{:S(2)}) collective-permute-start(bf16[12,64,128]{2,1,0:T(8,128)(2,1)} %collective-permute-done.30), channel_id=1, source_target_pairs={{0,2},{2,0},{4,6},{6,4},{1,3},{3,1},{5,7},{7,5},{8,10},{10,8},{12,... | collective-permute-start | bytes 589832 | tf_op jit(solution)/shard_map/ppermute | solution.py:14
  308.2 26.0 %collective-permute-start.56 = (bf16[512,1024]{1,0:T(8,128)(2,1)S(1)}, bf16[512,1024]{1,0:T(8,128)(2,1)S(1)}, u32[]{:S(2)}, u32[]{:S(2)}) collective-permute-start(bf16[512,1024]{1,0:T(8,128)(2,1)S(1)} %convolution_convert_fusion.1), channel_id=1, source_target_pairs={{0,1},{1,0},{2,3},{3,2},{4,5},{5,4},{6,7},{7,6},{8,9},{9,8},{10,11... | collective-permute-start | bytes 3145736 | tf_op jit(solution)/shard_map/ppermute | solution.py:100
  321.1 35.0 %collective-permute-start.39 = (bf16[512,1024]{1,0:T(8,128)(2,1)S(1)}, bf16[512,1024]{1,0:T(8,128)(2,1)S(1)}, u32[]{:S(2)}, u32[]{:S(2)}) collective-permute-start(bf16[512,1024]{1,0:T(8,128)(2,1)S(1)} %convolution_convert_fusion.3), channel_id=1, source_target_pairs={{0,1},{1,0},{2,3},{3,2},{4,5},{5,4},{6,7},{7,6},{8,9},{9,8},{10,11... | collective-permute-start | bytes 3145736 | tf_op jit(solution)/shard_map/ppermute | solution.py:100
  321.6 36.7 %collective-permute-start.45 = (bf16[3,64,3072]{2,1,0:T(8,128)(2,1)S(1)}, bf16[3,64,3072]{2,1,0:T(8,128)(2,1)S(1)}, u32[]{:S(2)}, u32[]{:S(2)}) collective-permute-start(bf16[3,64,3072]{2,1,0:T(8,128)(2,1)S(1)} %collective-permute-done.43), channel_id=1, source_target_pairs={{0,2},{2,0},{4,6},{6,4},{1,3},{3,1},{5,7},{7,5},{8,10},{10,8},{12,... | collective-permute-start | bytes 3538952 | tf_op jit(solution)/shard_map/ppermute | solution.py:14
  384.4 26.5 %collective-permute-start.65 = (bf16[512,1024]{1,0:T(8,128)(2,1)}, bf16[512,1024]{1,0:T(8,128)(2,1)}, u32[]{:S(2)}, u32[]{:S(2)}) collective-permute-start(bf16[512,1024]{1,0:T(8,128)(2,1)} %fusion.160), channel_id=1, source_target_pairs={{0,1},{1,0},{2,3},{3,2},{4,5},{5,4},{6,7},{7,6},{8,9},{9,8},{10,11... | collective-permute-start | bytes 3145736 | tf_op jit(solution)/shard_map/ppermute | solution.py:100
  386.0 47.4 %collective-permute-start.58 = (bf16[512,1024]{1,0:T(8,128)(2,1)S(1)}, bf16[512,1024]{1,0:T(8,128)(2,1)}, u32[]{:S(2)}, u32[]{:S(2)}) collective-permute-start(bf16[512,1024]{1,0:T(8,128)(2,1)S(1)} %fusion.157), channel_id=1, source_target_pairs={{0,1},{1,0},{2,3},{3,2},{4,5},{5,4},{6,7},{7,6},{8,9},{9,8},{10,11... | collective-permute-start | bytes 3145736 | tf_op jit(solution)/shard_map/ppermute | solution.py:100
  394.3 61.5 %collective-permute-start.46 = (bf16[512,1024]{1,0:T(8,128)(2,1)}, bf16[512,1024]{1,0:T(8,128)(2,1)}, u32[]{:S(2)}, u32[]{:S(2)}) collective-permute-start(bf16[512,1024]{1,0:T(8,128)(2,1)} %convolution_convert_fusion.2), channel_id=1, source_target_pairs={{0,1},{1,0},{2,3},{3,2},{4,5},{5,4},{6,7},{7,6},{8,9},{9,8},{10,11... | collective-permute-start | bytes 3145736 | tf_op jit(solution)/shard_map/ppermute | solution.py:100
  395.8 80.9 %collective-permute-start.57 = (bf16[512,1024]{1,0:T(8,128)(2,1)}, bf16[512,1024]{1,0:T(8,128)(2,1)}, u32[]{:S(2)}, u32[]{:S(2)}) collective-permute-start(bf16[512,1024]{1,0:T(8,128)(2,1)} %convolution_convert_fusion), channel_id=1, source_target_pairs={{0,1},{1,0},{2,3},{3,2},{4,5},{5,4},{6,7},{7,6},{8,9},{9,8},{10,11... | collective-permute-start | bytes 3145736 | tf_op jit(solution)/shard_map/ppermute | solution.py:100
  404.8 437.5 %collective-permute-start.102 = (bf16[4,2,64,3072]{3,2,1,0:T(8,128)(2,1)}, bf16[4,2,64,3072]{3,2,1,0:T(8,128)(2,1)}, u32[]{:S(2)}, u32[]{:S(2)}) collective-permute-start(bf16[4,2,64,3072]{3,2,1,0:T(8,128)(2,1)} %dynamic-slice_bitcast_fusion), channel_id=1, source_target_pairs={{0,2},{2,0},{4,6},{6,4},{1,3},{3,1},{5,7},{7,5},{8,10},{10,8},{12,... | collective-permute-start | bytes 9437192 | tf_op jit(solution)/shard_map/ppermute | solution.py:14
  511.4 135.9 %collective-permute-start.61 = (bf16[12,64,128]{2,1,0:T(8,128)(2,1)}, bf16[12,64,128]{2,1,0:T(8,128)(2,1)}, u32[]{:S(2)}, u32[]{:S(2)}) collective-permute-start(bf16[12,64,128]{2,1,0:T(8,128)(2,1)} %get-tuple-element.339), channel_id=1, source_target_pairs={{0,4},{2,6},{4,0},{6,2},{1,5},{3,7},{5,1},{7,3},{8,12},{10,14},{12... | collective-permute-start | bytes 589832 | tf_op jit(solution)/shard_map/ppermute | solution.py:14
  512.1 136.8 %collective-permute-start.62 = (bf16[12,64,128]{2,1,0:T(8,128)(2,1)}, bf16[12,64,128]{2,1,0:T(8,128)(2,1)}, u32[]{:S(2)}, u32[]{:S(2)}) collective-permute-start(bf16[12,64,128]{2,1,0:T(8,128)(2,1)} %get-tuple-element.339), channel_id=1, source_target_pairs={{0,2},{2,0},{4,6},{6,4},{1,3},{3,1},{5,7},{7,5},{8,10},{10,8},{12,... | collective-permute-start | bytes 589832 | tf_op jit(solution)/shard_map/ppermute | solution.py:14
  537.4 112.8 %collective-permute-start.68 = (bf16[12,64,128]{2,1,0:T(8,128)(2,1)}, bf16[12,64,128]{2,1,0:T(8,128)(2,1)}, u32[]{:S(2)}, u32[]{:S(2)}) collective-permute-start(bf16[12,64,128]{2,1,0:T(8,128)(2,1)} %get-tuple-element.345), channel_id=1, source_target_pairs={{0,4},{2,6},{4,0},{6,2},{1,5},{3,7},{5,1},{7,3},{8,12},{10,14},{12... | collective-permute-start | bytes 589832 | tf_op jit(solution)/shard_map/ppermute | solution.py:14
  538.5 113.0 %collective-permute-start.69 = (bf16[12,64,128]{2,1,0:T(8,128)(2,1)}, bf16[12,64,128]{2,1,0:T(8,128)(2,1)}, u32[]{:S(2)}, u32[]{:S(2)}) collective-permute-start(bf16[12,64,128]{2,1,0:T(8,128)(2,1)} %get-tuple-element.345), channel_id=1, source_target_pairs={{0,2},{2,0},{4,6},{6,4},{1,3},{3,1},{5,7},{7,5},{8,10},{10,8},{12,... | collective-permute-start | bytes 589832 | tf_op jit(solution)/shard_map/ppermute | solution.py:14
  647.4 126.4 %collective-permute-start.94 = (bf16[4,2,64,1024]{3,2,1,0:T(8,128)(2,1)}, bf16[4,2,64,1024]{3,2,1,0:T(8,128)(2,1)}, u32[]{:S(2)}, u32[]{:S(2)}) collective-permute-start(bf16[4,2,64,1024]{3,2,1,0:T(8,128)(2,1)} %dynamic-slice_bitcast_fusion.2), channel_id=1, source_target_pairs={{0,2},{2,0},{4,6},{6,4},{1,3},{3,1},{5,7},{7,5},{8,10},{10,8},{12,... | collective-permute-start | bytes 3145736 | tf_op jit(solution)/shard_map/ppermute | solution.py:14
  653.9 74.4 %collective-permute-start.60 = (bf16[1,512,128]{1,2,0:T(8,128)(2,1)}, bf16[1,512,128]{1,2,0:T(8,128)(2,1)}, u32[]{:S(2)}, u32[]{:S(2)}) collective-permute-start(bf16[1,512,128]{1,2,0:T(8,128)(2,1)} %constant_dynamic-slice_fusion.5), channel_id=1, source_target_pairs={{0,4},{2,6},{4,0},{6,2},{1,5},{3,7},{5,1},{7,3},{8,12},{10,14},{12... | collective-permute-start | bytes 393224 | tf_op jit(solution)/shard_map/ppermute | solution.py:14
  655.4 59.7 %collective-permute-start.67 = (bf16[1,512,128]{1,2,0:T(8,128)(2,1)}, bf16[1,512,128]{1,2,0:T(8,128)(2,1)}, u32[]{:S(2)}, u32[]{:S(2)}) collective-permute-start(bf16[1,512,128]{1,2,0:T(8,128)(2,1)} %constant_dynamic-slice_fusion.4), channel_id=1, source_target_pairs={{0,4},{2,6},{4,0},{6,2},{1,5},{3,7},{5,1},{7,3},{8,12},{10,14},{12... | collective-permute-start | bytes 393224 | tf_op jit(solution)/shard_map/ppermute | solution.py:14
  696.0 34.8 %collective-permute-start.90 = (f32[3,12]{1,0:T(4,128)}, f32[3,12]{1,0:T(4,128)}, u32[]{:S(2)}, u32[]{:S(2)}) collective-permute-start(f32[3,12]{1,0:T(4,128)} %maximum_add_fusion), channel_id=1, source_target_pairs={{0,2},{2,0},{4,6},{6,4},{1,3},{3,1},{5,7},{7,5},{8,10},{10,8},{12,... | collective-permute-start | bytes 440 | tf_op jit(solution)/shard_map/ppermute | solution.py:14
  715.1 121.2 %collective-permute-start.82 = (bf16[4,2,64,1536]{3,2,1,0:T(8,128)(2,1)}, bf16[4,2,64,1536]{3,2,1,0:T(8,128)(2,1)}, u32[]{:S(2)}, u32[]{:S(2)}) collective-permute-start(bf16[4,2,64,1536]{3,2,1,0:T(8,128)(2,1)} %dynamic-slice_bitcast_fusion.1), channel_id=1, source_target_pairs={{0,2},{2,0},{4,6},{6,4},{1,3},{3,1},{5,7},{7,5},{8,10},{10,8},{12,... | collective-permute-start | bytes 4718600 | tf_op jit(solution)/shard_map/ppermute | solution.py:14
  728.3 21.1 %collective-permute-start.72 = (bf16[512,256]{0,1:T(8,128)(2,1)}, bf16[512,256]{0,1:T(8,128)(2,1)S(1)}, u32[]{:S(2)}, u32[]{:S(2)}) collective-permute-start(bf16[512,256]{0,1:T(8,128)(2,1)} %pad_maximum_fusion.24), channel_id=1, source_target_pairs={{0,1},{1,0},{2,3},{3,2},{4,5},{5,4},{6,7},{7,6},{8,9},{9,8},{10,11... | collective-permute-start | bytes 786440 | tf_op jit(solution)/shard_map/ppermute | solution.py:100
  748.4 9.6 collective-permute-start.73
  749.5 31.0 %collective-permute-start.71 = (bf16[512,1024]{1,0:T(8,128)(2,1)}, bf16[512,1024]{1,0:T(8,128)(2,1)}, u32[]{:S(2)}, u32[]{:S(2)}) collective-permute-start(bf16[512,1024]{1,0:T(8,128)(2,1)} %add_convert_fusion.6), channel_id=1, source_target_pairs={{0,1},{1,0},{2,3},{3,2},{4,5},{5,4},{6,7},{7,6},{8,9},{9,8},{10,11... | collective-permute-start | bytes 3145736 | tf_op jit(solution)/shard_map/ppermute | solution.py:100
  758.0 42.2 %collective-permute-start.64 = (bf16[512,1024]{1,0:T(8,128)(2,1)}, bf16[512,1024]{1,0:T(8,128)(2,1)}, u32[]{:S(2)}, u32[]{:S(2)}) collective-permute-start(bf16[512,1024]{1,0:T(8,128)(2,1)} %add_convert_fusion.7), channel_id=1, source_target_pairs={{0,1},{1,0},{2,3},{3,2},{4,5},{5,4},{6,7},{7,6},{8,9},{9,8},{10,11... | collective-permute-start | bytes 3145736 | tf_op jit(solution)/shard_map/ppermute | solution.py:100
  776.6 34.8 %collective-permute-start.95 = (bf16[4,1,64,1024]{3,2,1,0:T(8,128)(2,1)}, bf16[4,1,64,1024]{3,2,1,0:T(8,128)(2,1)}, u32[]{:S(2)}, u32[]{:S(2)}) collective-permute-start(bf16[4,1,64,1024]{3,2,1,0:T(8,128)(2,1)} %constant_dynamic-slice_fusion.1), channel_id=1, source_target_pairs={{0,4},{2,6},{4,0},{6,2},{1,5},{3,7},{5,1},{7,3},{8,12},{10,14},{12... | collective-permute-start | bytes 1572872 | tf_op jit(solution)/shard_map/ppermute | solution.py:14
  814.9 10.4 %collective-permute-start.97 = (bf16[64,1024]{1,0:T(8,128)(2,1)S(1)}, bf16[64,1024]{1,0:T(8,128)(2,1)S(1)}, u32[]{:S(2)}, u32[]{:S(2)}) collective-permute-start(bf16[64,1024]{1,0:T(8,128)(2,1)S(1)} %get-tuple-element.275), channel_id=1, source_target_pairs={{16,0},{24,8},{0,16},{8,24},{17,1},{25,9},{1,17},{9,25},{18,2},{26... | collective-permute-start | bytes 393224 | tf_op jit(solution)/shard_map/ppermute | solution.py:19
  819.6 20.5 %collective-permute-start.74 = (bf16[4,2,64,768]{3,2,1,0:T(8,128)(2,1)}, bf16[4,2,64,768]{3,2,1,0:T(8,128)(2,1)}, u32[]{:S(2)}, u32[]{:S(2)}) collective-permute-start(bf16[4,2,64,768]{3,2,1,0:T(8,128)(2,1)} %dynamic-slice_bitcast_fusion.3), channel_id=1, source_target_pairs={{0,2},{2,0},{4,6},{6,4},{1,3},{3,1},{5,7},{7,5},{8,10},{10,8},{12,... | collective-permute-start | bytes 2359304 | tf_op jit(solution)/shard_map/ppermute | solution.py:14
  838.8 40.3 %collective-permute-start.83 = (bf16[4,1,64,1536]{3,2,1,0:T(8,128)(2,1)S(1)}, bf16[4,1,64,1536]{3,2,1,0:T(8,128)(2,1)S(1)}, u32[]{:S(2)}, u32[]{:S(2)}) collective-permute-start(bf16[4,1,64,1536]{3,2,1,0:T(8,128)(2,1)S(1)} %constant_dynamic-slice_fusion.2), channel_id=1, source_target_pairs={{0,4},{2,6},{4,0},{6,2},{1,5},{3,7},{5,1},{7,3},{8,12},{10,14},{12... | collective-permute-start | bytes 2359304 | tf_op jit(solution)/shard_map/ppermute | solution.py:14
  841.5 25.4 %collective-permute-start.75 = (bf16[4,1,64,768]{3,2,1,0:T(8,128)(2,1)S(1)}, bf16[4,1,64,768]{3,2,1,0:T(8,128)(2,1)S(1)}, u32[]{:S(2)}, u32[]{:S(2)}) collective-permute-start(bf16[4,1,64,768]{3,2,1,0:T(8,128)(2,1)S(1)} %constant_dynamic-slice_fusion.3), channel_id=1, source_target_pairs={{0,4},{2,6},{4,0},{6,2},{1,5},{3,7},{5,1},{7,3},{8,12},{10,14},{12... | collective-permute-start | bytes 1179656 | tf_op jit(solution)/shard_map/ppermute | solution.py:14
  868.1 9.5 collective-permute-start.77
  872.0 52.9 %collective-permute-start.103 = (bf16[4,1,64,3072]{3,2,1,0:T(8,128)(2,1)}, bf16[4,1,64,3072]{3,2,1,0:T(8,128)(2,1)}, u32[]{:S(2)}, u32[]{:S(2)}) collective-permute-start(bf16[4,1,64,3072]{3,2,1,0:T(8,128)(2,1)} %constant_dynamic-slice_fusion), channel_id=1, source_target_pairs={{0,4},{2,6},{4,0},{6,2},{1,5},{3,7},{5,1},{7,3},{8,12},{10,14},{12... | collective-permute-start | bytes 4718600 | tf_op jit(solution)/shard_map/ppermute | solution.py:14
  877.7 31.4 %collective-permute-start.79 = (bf16[64,768]{1,0:T(8,128)(2,1)S(1)}, bf16[64,768]{1,0:T(8,128)(2,1)S(1)}, u32[]{:S(2)}, u32[]{:S(2)}) collective-permute-start(bf16[64,768]{1,0:T(8,128)(2,1)S(1)} %get-tuple-element.217), channel_id=1, source_target_pairs={{0,4},{2,6},{4,0},{6,2},{1,5},{3,7},{5,1},{7,3},{8,12},{10,14},{12... | collective-permute-start | bytes 294920 | tf_op jit(solution)/shard_map/ppermute | solution.py:14
  879.1 30.9 %collective-permute-start.80 = (bf16[64,768]{1,0:T(8,128)(2,1)S(1)}, bf16[64,768]{1,0:T(8,128)(2,1)S(1)}, u32[]{:S(2)}, u32[]{:S(2)}) collective-permute-start(bf16[64,768]{1,0:T(8,128)(2,1)S(1)} %get-tuple-element.217), channel_id=1, source_target_pairs={{0,2},{2,0},{4,6},{6,4},{1,3},{3,1},{5,7},{7,5},{8,10},{10,8},{12,... | collective-permute-start | bytes 294920 | tf_op jit(solution)/shard_map/ppermute | solution.py:14
  880.2 36.2 %collective-permute-start.84 = (bf16[64,1536]{1,0:T(8,128)(2,1)}, bf16[64,1536]{1,0:T(8,128)(2,1)}, u32[]{:S(2)}, u32[]{:S(2)}) collective-permute-start(bf16[64,1536]{1,0:T(8,128)(2,1)} %get-tuple-element.268), channel_id=1, source_target_pairs={{8,0},{16,8},{24,16},{0,24},{9,1},{17,9},{25,17},{1,25},{10,2},{18... | collective-permute-start | bytes 589832 | tf_op jit(solution)/shard_map/ppermute | solution.py:19
  880.7 35.7 %collective-permute-start.85 = (bf16[64,1536]{1,0:T(8,128)(2,1)}, bf16[64,1536]{1,0:T(8,128)(2,1)}, u32[]{:S(2)}, u32[]{:S(2)}) collective-permute-start(bf16[64,1536]{1,0:T(8,128)(2,1)} %get-tuple-element.270), channel_id=1, source_target_pairs={{16,0},{24,8},{0,16},{8,24},{17,1},{25,9},{1,17},{9,25},{18,2},{26... | collective-permute-start | bytes 589832 | tf_op jit(solution)/shard_map/ppermute | solution.py:19
  927.0 12.5 %collective-permute-start.104 = (bf16[64,3072]{1,0:T(8,128)(2,1)S(1)}, bf16[64,3072]{1,0:T(8,128)(2,1)S(1)}, u32[]{:S(2)}, u32[]{:S(2)}) collective-permute-start(bf16[64,3072]{1,0:T(8,128)(2,1)S(1)} %get-tuple-element.261), channel_id=1, source_target_pairs={{8,0},{16,8},{24,16},{0,24},{9,1},{17,9},{25,17},{1,25},{10,2},{18... | collective-permute-start | bytes 1179656 | tf_op jit(solution)/shard_map/ppermute | solution.py:19
  930.0 34.3 %collective-permute-start.105 = (bf16[64,3072]{1,0:T(8,128)(2,1)S(1)}, bf16[64,3072]{1,0:T(8,128)(2,1)S(1)}, u32[]{:S(2)}, u32[]{:S(2)}) collective-permute-start(bf16[64,3072]{1,0:T(8,128)(2,1)S(1)} %get-tuple-element.263), channel_id=1, source_target_pairs={{16,0},{24,8},{0,16},{8,24},{17,1},{25,9},{1,17},{9,25},{18,2},{26... | collective-permute-start | bytes 1179656 | tf_op jit(solution)/shard_map/ppermute | solution.py:19
  930.0 34.3 %collective-permute-start.106 = (bf16[64,3072]{1,0:T(8,128)(2,1)S(1)}, bf16[64,3072]{1,0:T(8,128)(2,1)S(1)}, u32[]{:S(2)}, u32[]{:S(2)}) collective-permute-start(bf16[64,3072]{1,0:T(8,128)(2,1)S(1)} %get-tuple-element.262), channel_id=1, source_target_pairs={{24,0},{0,8},{8,16},{16,24},{25,1},{1,9},{9,17},{17,25},{26,2},{2,... | collective-permute-start | bytes 1179656 | tf_op jit(solution)/shard_map/ppermute | solution.py:19
  964.7 10.8 %collective-permute-start.107 = (bf16[64,3072]{1,0:T(8,128)(2,1)S(1)}, bf16[64,3072]{1,0:T(8,128)(2,1)S(1)}, u32[]{:S(2)}, u32[]{:S(2)}) collective-permute-start(bf16[64,3072]{1,0:T(8,128)(2,1)S(1)} %get-tuple-element.203), channel_id=1, source_target_pairs={{0,4},{2,6},{4,0},{6,2},{1,5},{3,7},{5,1},{7,3},{8,12},{10,14},{12... | collective-permute-start | bytes 1179656 | tf_op jit(solution)/shard_map/ppermute | solution.py:14
  (302 other events, 2641.2 us)

commit v2 on v1

v2 whole, which is shorter than its diff:
```python
import jax
import jax.numpy as jnp
from jax import lax
from jax.experimental import pallas as pl
from jax.experimental.pallas import tpu as pltpu
from jax.sharding import PartitionSpec as P

HEAD_WIDTH = 64
EPSILON = 1e-06
LOW = jnp.bfloat16
F32 = jnp.float32
NEGATIVE = -1e30
PRECISE = lax.Precision.HIGHEST


def swap_context(x, bit):
    size = lax.axis_size("context")
    return lax.ppermute(x, "context", [(i, i ^ bit) for i in range(size)])


def from_next(x, axis, step=1):
    size = lax.axis_size(axis)
    return lax.ppermute(x, axis, [((i + step) % size, i) for i in range(size)])


def context_bits():
    size = lax.axis_size("context")
    return [1 << k for k in range(size.bit_length() - 1)]


def spread_context(x):
    held = [(0, x)]
    for bit in reversed(context_bits()):
        held = held + [(off ^ bit, swap_context(part, bit)) for off, part in held]
    return held


def gather_context(x):
    size, index = lax.axis_size("context"), lax.axis_index("context")
    out = jnp.zeros((size,) + x.shape, x.dtype)
    for off, part in spread_context(x):
        out = lax.dynamic_update_index_in_dim(out, part, index ^ off, 0)
    return out


def gather_rows(shard, stacked):
    nf, nc = lax.axis_size("fsdp"), lax.axis_size("context")
    fi, ci = lax.axis_index("fsdp"), lax.axis_index("context")
    rows, cols = shard.shape
    part = rows // nc
    full = jnp.zeros((nf, nc, part, cols), shard.dtype)
    full = lax.dynamic_update_slice(full, shard.reshape(1, nc, part, cols), (fi, 0, 0, 0))
    cur = lax.dynamic_slice(shard, (ci * part, 0), (part, cols))
    steps = []
    for k in range(1, nf):
        cur = from_next(cur, "fsdp")
        steps.append((k, cur))
    if stacked:
        pieces = spread_context(jnp.stack([cur for _, cur in steps]))
        pieces = [(k, off, arr[k - 1]) for off, arr in pieces for k, _ in steps]
    else:
        pieces = [(k, off, arr) for k, cur in steps for off, arr in spread_context(cur)]
    for k, off, arr in pieces:
        full = lax.dynamic_update_slice(full, arr[None, None], ((fi + k) % nf, ci ^ off, 0, 0))
    return full.reshape(nf * rows, cols)


def reduce_rows(grad):
    nf, nc = lax.axis_size("fsdp"), lax.axis_size("context")
    fi, ci = lax.axis_index("fsdp"), lax.axis_index("context")
    rows, cols = grad.shape
    part = rows // (nf * nc)
    acc = grad
    left = nc
    for bit in context_bits():
        left //= 2
        view = acc.reshape(nf, left, 2, part, cols)
        mine = (ci & bit) // bit
        away = lax.dynamic_index_in_dim(view, 1 - mine, 2, keepdims=False)
        keep = lax.dynamic_index_in_dim(view, mine, 2, keepdims=False)
        acc = (keep.astype(F32) + swap_context(away, bit).astype(F32)).astype(LOW)
    acc = acc.reshape(nf, part, cols)
    total = lax.dynamic_index_in_dim(acc, fi, 0, keepdims=False).astype(F32)
    for k in range(1, nf):
        away = lax.dynamic_index_in_dim(acc, (fi - k) % nf, 0, keepdims=False)
        total = total + from_next(away, "fsdp", k).astype(F32)
    return total


def share_rows(part):
    done = gather_context(part.astype(LOW))
    return done.reshape(-1, part.shape[1])


def scatter_rows(grad):
    return share_rows(reduce_rows(grad)).astype(F32)


def all_sum(x):
    for bit in context_bits():
        x = x + swap_context(x, bit)
    size, bit = lax.axis_size("fsdp"), 1
    while bit < size:
        x = x + lax.ppermute(x, "fsdp", [(i, i ^ bit) for i in range(size)])
        bit *= 2
    return x


def tensor_sum(x):
    low = x.astype(LOW)
    size = lax.axis_size("tensor")
    other = lax.ppermute(low, "tensor", [(i, (i + 1) % size) for i in range(size)])
    return low.astype(F32) + other.astype(F32)


def mat_mul(left, right):
    return jnp.dot(left, right, preferred_element_type=F32)


def mat_mul_t(left, right):
    return lax.dot_general(left, right, (((1,), (1,)), ((), ())), preferred_element_type=F32)


def outer_sum(left, right):
    return lax.dot_general(left, right, (((0,), (0,)), ((), ())), preferred_element_type=F32)


def norm_forward(hidden, gain_vec):
    inv_scale = lax.rsqrt(jnp.mean(hidden * hidden, axis=-1, keepdims=True) + EPSILON)
    return inv_scale, (hidden * inv_scale * gain_vec).astype(LOW)


def norm_backward(hidden, inv_scale, gain_vec, d_normed):
    weighted = gain_vec * d_normed
    return inv_scale * weighted - hidden * inv_scale**3 * jnp.mean(
        weighted * hidden, axis=-1, keepdims=True
    )


def segment_ids(doc_lens, positions):
    count = doc_lens.shape[-1]
    upto = jnp.arange(count)[:, None] >= jnp.arange(count)[None, :]
    ends = jnp.sum(jnp.where(upto, doc_lens[:, None, :], 0), axis=-1)
    return jnp.sum((ends[:, None, :] <= positions[None, :, None]).astype(jnp.int32), axis=2)


def kernel_params(limit=48):
    return pltpu.CompilerParams(vmem_limit_bytes=limit * 2**20)


def nt_dot(left, right):
    return lax.dot_general(left, right, (((1,), (1,)), ((), ())), preferred_element_type=F32)


def tn_dot(left, right):
    return lax.dot_general(left, right, (((0,), (0,)), ((), ())), preferred_element_type=F32)


def nn_dot(left, right):
    return jnp.dot(left, right, preferred_element_type=F32)


def attention_forward(q, kv_all, seg_here, seg_all, span):
    rows, q_dim = q.shape
    heads = q_dim // HEAD_WIDTH
    length = kv_all.shape[0]

    def body(span_ref, q_ref, kv_ref, seg_q_ref, seg_k_ref, o_ref, lse_ref, bias, top, low, acc):
        top[...] = jnp.full_like(top, NEGATIVE)
        low[...] = jnp.zeros_like(low)
        acc[...] = jnp.zeros_like(acc)
        own = span_ref[1]

        def step(i, carry):
            j = own - i
            at = pl.multiple_of(j * rows, rows)
            keys = kv_ref[pl.ds(at, rows), :HEAD_WIDTH]
            turned = kv_ref[pl.ds(at, rows), :].astype(F32).T[HEAD_WIDTH:].astype(LOW)
            u = lax.broadcasted_iota(jnp.int32, (rows, rows), 0)
            t = lax.broadcasted_iota(jnp.int32, (rows, rows), 1)
            seen = (seg_k_ref[pl.ds(at, rows), :] == seg_q_ref[...]) & ((u <= t) | (j < own))
            bias[...] = jnp.where(seen, 0.0, NEGATIVE)
            for h in range(heads):
                lanes = slice(h * HEAD_WIDTH, (h + 1) * HEAD_WIDTH)
                s = nt_dot(keys, q_ref[:, lanes]) + bias[...]
                before = top[h : h + 1, :]
                now = jnp.maximum(before, jnp.max(s, axis=0, keepdims=True))
                p = jnp.exp(s - now)
                scale = jnp.exp(before - now)
                top[h : h + 1, :] = now
                low[h : h + 1, :] = low[h : h + 1, :] * scale + jnp.sum(p, axis=0, keepdims=True)
                acc[lanes, :] = acc[lanes, :] * scale + nn_dot(turned, p.astype(LOW))
            return carry

        lax.fori_loop(0, own - span_ref[0] + 1, step, 0)
        for h in range(heads):
            lanes = slice(h * HEAD_WIDTH, (h + 1) * HEAD_WIDTH)
            acc[lanes, :] = acc[lanes, :] / low[h : h + 1, :]
        o_ref[...] = acc[...].T.astype(LOW)
        lse_ref[...] = top[...] + jnp.log(low[...])

    return pl.pallas_call(
        body,
        out_shape=(jax.ShapeDtypeStruct((rows, q_dim), LOW), jax.ShapeDtypeStruct((8, rows), F32)),
        in_specs=[pl.BlockSpec(memory_space=pltpu.SMEM)] + [pl.BlockSpec(memory_space=pltpu.VMEM)] * 4,
        out_specs=[pl.BlockSpec(memory_space=pltpu.VMEM)] * 2,
        scratch_shapes=[
            pltpu.VMEM((rows, rows), F32),
            pltpu.VMEM((8, rows), F32),
            pltpu.VMEM((8, rows), F32),
            pltpu.VMEM((q_dim, rows), F32),
        ],
        compiler_params=kernel_params(),
        cost_estimate=pl.CostEstimate(flops=16 * rows * length * q_dim, bytes_accessed=4 * rows * q_dim, transcendentals=heads * rows * length),
        name="attention_forward",
    )(span, q, kv_all, seg_here.reshape(1, rows), seg_all.reshape(length, 1))


def attention_backward(q, do, o, kv_all, lse, seg_here, seg_all, span):
    rows, q_dim = q.shape
    heads = q_dim // HEAD_WIDTH
    length = kv_all.shape[0]
    sub = min(256, rows)

    def body(span_ref, q_ref, do_ref, o_ref, kv_ref, lse_ref, seg_q_ref, seg_k_ref, dq_ref, dkv_ref, bias, dq_acc, dk_acc, dv_acc, delta):
        own = span_ref[1]
        dq_acc[...] = jnp.zeros_like(dq_acc)
        dkv_ref[...] = jnp.zeros_like(dkv_ref)
        both = do_ref[...].astype(F32) * o_ref[...].astype(F32)
        lane = lax.broadcasted_iota(jnp.int32, (rows, 128), 1)
        columns = jnp.zeros((rows, 128), F32)
        for h in range(heads):
            total = jnp.sum(both[:, h * HEAD_WIDTH : (h + 1) * HEAD_WIDTH], axis=1, keepdims=True)
            columns = jnp.where(lane == h, total, columns)
        delta[...] = columns.T[:8]

        def step(i, carry):
            j = own - i
            at = pl.multiple_of(j * rows, rows)
            same = seg_k_ref[pl.ds(at, rows), :] == seg_q_ref[...]
            u = lax.broadcasted_iota(jnp.int32, (rows, rows), 0)
            t = lax.broadcasted_iota(jnp.int32, (rows, rows), 1)
            seen = same & ((u <= t) | (j < own))
            bias[...] = jnp.where(seen, 0.0, NEGATIVE)
            for r in range(0, rows, sub):
                keys = kv_ref[pl.ds(pl.multiple_of(at + r, sub), sub), :HEAD_WIDTH]
                values = kv_ref[pl.ds(pl.multiple_of(at + r, sub), sub), HEAD_WIDTH:]
                dk = jnp.zeros((sub, HEAD_WIDTH), F32)
                dv = jnp.zeros((sub, HEAD_WIDTH), F32)
                for h in range(heads):
                    lanes = slice(h * HEAD_WIDTH, (h + 1) * HEAD_WIDTH)
                    q_h, do_h = q_ref[:, lanes], do_ref[:, lanes]
                    p = jnp.exp(nt_dot(keys, q_h) + (bias[r : r + sub, :] - lse_ref[h : h + 1, :]))
                    ds = (p * (nt_dot(values, do_h) - delta[h : h + 1, :])).astype(LOW)
                    dv = dv + nn_dot(p.astype(LOW), do_h)
                    dk = dk + nn_dot(ds, q_h)
                    dq_acc[:, lanes] = dq_acc[:, lanes] + tn_dot(ds, keys)
                dkv_ref[pl.ds(pl.multiple_of(at + r, sub), sub), :HEAD_WIDTH] = dk.astype(LOW)
                dkv_ref[pl.ds(pl.multiple_of(at + r, sub), sub), HEAD_WIDTH:] = dv.astype(LOW)
            return carry

        lax.fori_loop(0, own - span_ref[0] + 1, step, 0)
        dq_ref[...] = (dq_acc[...] * 0.125).astype(LOW)

    return pl.pallas_call(
        body,
        out_shape=(jax.ShapeDtypeStruct((rows, q_dim), LOW), jax.ShapeDtypeStruct((length, 2 * HEAD_WIDTH), LOW)),
        in_specs=[pl.BlockSpec(memory_space=pltpu.SMEM)] + [pl.BlockSpec(memory_space=pltpu.VMEM)] * 7,
        out_specs=[pl.BlockSpec(memory_space=pltpu.VMEM)] * 2,
        scratch_shapes=[
            pltpu.VMEM((rows, rows), F32),
            pltpu.VMEM((rows, q_dim), F32),
            pltpu.VMEM((rows, HEAD_WIDTH), F32),
            pltpu.VMEM((rows, HEAD_WIDTH), F32),
            pltpu.VMEM((8, rows), F32),
        ],
        compiler_params=kernel_params(),
        cost_estimate=pl.CostEstimate(flops=40 * rows * length * q_dim, bytes_accessed=4 * rows * q_dim, transcendentals=heads * rows * length),
        name="attention_backward",
    )(span, q, do, o, kv_all, lse, seg_here.reshape(1, rows), seg_all.reshape(length, 1))


def halves(columns, first, lane):
    return jnp.where(lane < 64, columns[:, first : first + 1], columns[:, first + 1 : first + 2])


def mamba_state(per_head, at, left, right, gate=None):
    rows, width = right.shape
    state = left.shape[1]
    pairs = width // 128
    gates = () if gate is None else (gate,)

    def body(head_ref, left_ref, right_ref, *rest):
        out_ref = rest[-1]
        lane = lax.broadcasted_iota(jnp.int32, (rows, 128), 1)
        turned = left_ref[...].astype(F32).T.astype(LOW)
        for i in range(pairs):
            lanes = slice(i * 128, (i + 1) * 128)
            value = right_ref[:, lanes].astype(F32)
            if gates:
                z = rest[0][:, lanes].astype(F32)
                value = value * z * jax.nn.sigmoid(z)
            weight = halves(head_ref[i].T, at, lane)
            out_ref[:, lanes] = nn_dot(turned, (value * weight).astype(LOW)).astype(LOW)

    return pl.pallas_call(
        body,
        out_shape=jax.ShapeDtypeStruct((state, width), LOW),
        in_specs=[pl.BlockSpec(memory_space=pltpu.VMEM)] * (3 + len(gates)),
        out_specs=pl.BlockSpec(memory_space=pltpu.VMEM),
        compiler_params=kernel_params(),
        cost_estimate=pl.CostEstimate(flops=2 * rows * width * state, bytes_accessed=4 * rows * width, transcendentals=0),
        name="mamba_state",
    )(per_head, left, right, *gates)


def pair_spec(rows):
    return pl.BlockSpec((rows, 128), lambda i: (0, i))


def whole_spec(shape):
    return pl.BlockSpec(shape, lambda i: (0,) * len(shape))


def mamba_forward(per_head, xs, z, b, c, state_in, skip, seg_col, seg_row):
    rows, width = xs.shape
    pairs = width // 128
    blk = min(256, rows)

    def body(head_ref, xs_ref, z_ref, b_ref, c_ref, state_ref, skip_ref, seg_col_ref, seg_row_ref, y_ref, g_ref, inner, x_dt):
        @pl.when(pl.program_id(0) == 0)
        def _():
            t = lax.broadcasted_iota(jnp.int32, (rows, rows), 0)
            u = lax.broadcasted_iota(jnp.int32, (rows, rows), 1)
            seen = (seg_col_ref[...] == seg_row_ref[...]) & (u <= t)
            inner[...] = jnp.where(seen, nt_dot(c_ref[...], b_ref[...]), 0.0)

        lane = lax.broadcasted_iota(jnp.int32, (rows, 128), 1)
        by_row = head_ref[0]
        by_col = by_row.T
        xs_f = xs_ref[...].astype(F32)
        x_dt[...] = (xs_f * halves(by_col, 2, lane)).astype(LOW)
        read = nn_dot(c_ref[...], state_ref[...]) * halves(by_col, 4, lane)
        for i in range(rows // blk):
            part = slice(i * blk, (i + 1) * blk)
            sums = []
            for h in range(2):
                total = None
                for j in range(i + 1):
                    other = slice(j * blk, (j + 1) * blk)
                    gap = by_col[part, h : h + 1] - by_row[h : h + 1, other]
                    kernel = jnp.exp(jnp.minimum(gap, 0.0)) * inner[part, other]
                    term = nn_dot(kernel.astype(LOW), x_dt[other, :])
                    total = term if total is None else total + term
                sums.append(total)
            y = jnp.where(lane[part] < 64, sums[0], sums[1]) + read[part]
            y_ref[part, :] = y
            z_f = z_ref[part, :].astype(F32)
            g_ref[part, :] = ((y + skip_ref[...] * xs_f[part]) * z_f * jax.nn.sigmoid(z_f)).astype(LOW)

    state = b.shape[1]
    return pl.pallas_call(
        body,
        grid=(pairs,),
        out_shape=(jax.ShapeDtypeStruct((rows, width), F32), jax.ShapeDtypeStruct((rows, width), LOW)),
        in_specs=[
            pl.BlockSpec((1, 8, rows), lambda i: (i, 0, 0)), pair_spec(rows), pair_spec(rows), whole_spec((rows, state)),
            whole_spec((rows, state)), pair_spec(state), pair_spec(1), whole_spec((rows, 1)), whole_spec((1, rows)),
        ],
        out_specs=[pair_spec(rows), pair_spec(rows)],
        scratch_shapes=[pltpu.VMEM((rows, rows), F32), pltpu.VMEM((rows, 128), LOW)],
        compiler_params=kernel_params(),
        cost_estimate=pl.CostEstimate(flops=8 * rows * rows * width, bytes_accessed=10 * rows * width, transcendentals=rows * rows * width // 64),
        name="mamba_forward",
    )(per_head, xs, z, b, c, state_in, skip, seg_col, seg_row)


def mamba_backward(per_head, xs, z, y, dg, b, c, state_in, later, skip, seg_col, seg_row):
    rows, width = xs.shape
    pairs = width // 128
    blk = min(256, rows)
    state = b.shape[1]

    def body(head_ref, xs_ref, z_ref, y_ref, dg_ref, b_ref, c_ref, state_ref, later_ref, skip_ref, seg_col_ref, seg_row_ref,
             dxs_ref, dz_ref, db_ref, dc_ref, stats_ref, inner, d_inner, dy_low, x_low):
        @pl.when(pl.program_id(0) == 0)
        def _():
            u = lax.broadcasted_iota(jnp.int32, (rows, rows), 0)
            t = lax.broadcasted_iota(jnp.int32, (rows, rows), 1)
            seen = (seg_col_ref[...] == seg_row_ref[...]) & (u <= t)
            inner[...] = jnp.where(seen, nt_dot(b_ref[...], c_ref[...]), 0.0)
            d_inner[...] = jnp.zeros_like(d_inner)
            db_ref[...] = jnp.zeros_like(db_ref)
            dc_ref[...] = jnp.zeros_like(dc_ref)

        lane = lax.broadcasted_iota(jnp.int32, (rows, 128), 1)
        by_row = head_ref[0]
        by_col = by_row.T
        xs_f = xs_ref[...].astype(F32)
        z_f = z_ref[...].astype(F32)
        sig = jax.nn.sigmoid(z_f)
        d_gate = dg_ref[...].astype(F32)
        d_y = d_gate * z_f * sig
        y_core = y_ref[...]
        dz_ref[...] = (d_gate * (y_core + skip_ref[...] * xs_f) * sig * (1.0 + z_f * (1.0 - sig))).astype(LOW)
        dy_low[...] = d_y.astype(LOW)
        dt = halves(by_col, 2, lane)
        x_dt = xs_f * dt
        x_low[...] = x_dt.astype(LOW)
        closing = halves(by_col, 6, lane)
        from_later = nn_dot(b_ref[...], later_ref[...]) * closing
        db_ref[...] += nt_dot((x_dt * closing).astype(LOW), later_ref[...])
        dc_ref[...] += nt_dot((d_y * halves(by_col, 4, lane)).astype(LOW), state_ref[...])
        count = rows // blk
        columns = jnp.zeros((rows, 128), F32)
        d_x_parts = []
        for j in range(count):
            part = slice(j * blk, (j + 1) * blk)
            sums = []
            for h in range(2):
                own = (lane[part] < 64) if h == 0 else (lane[part] >= 64)
                x_h = jnp.where(own, x_low[part, :].astype(F32), 0.0).astype(LOW)
                total = None
                for i in range(j, count):
                    other = slice(i * blk, (i + 1) * blk)
                    gap = by_row[h : h + 1, other] - by_col[part, h : h + 1]
                    decay = jnp.exp(jnp.minimum(gap, 0.0))
                    term = nn_dot((decay * inner[part, other]).astype(LOW), dy_low[other, :])
                    total = term if total is None else total + term
                    d_inner[part, other] += decay * nt_dot(x_h, dy_low[other, :])
                sums.append(total)
            d_x_parts.append(jnp.where(lane[part] < 64, sums[0], sums[1]))
        d_x = jnp.concatenate(d_x_parts, axis=0) if count > 1 else d_x_parts[0]
        d_x = d_x + from_later
        dxs_ref[...] = (d_x * dt + skip_ref[...] * d_y).astype(LOW)
        rounded_x = x_low[...].astype(F32)
        rounded_dy = dy_low[...].astype(F32)
        for at, value in enumerate((d_x * xs_f, rounded_dy * y_core - rounded_x * d_x, rounded_x * from_later, d_y * xs_f)):
            for h in range(2):
                own = (lane < 64) if h == 0 else (lane >= 64)
                total = jnp.sum(jnp.where(own, value, 0.0), axis=1, keepdims=True)
                columns = jnp.where(lane == 2 * at + h, total, columns)
        stats_ref[0] = columns.T[:8]

        @pl.when(pl.program_id(0) == pairs - 1)
        def _():
            u = lax.broadcasted_iota(jnp.int32, (rows, rows), 0)
            t = lax.broadcasted_iota(jnp.int32, (rows, rows), 1)
            seen = (seg_col_ref[...] == seg_row_ref[...]) & (u <= t)
            low = jnp.where(seen, d_inner[...], 0.0).astype(LOW)
            db_ref[...] += nn_dot(low, c_ref[...])
            dc_ref[...] += tn_dot(low, b_ref[...])

    return pl.pallas_call(
        body,
        grid=(pairs,),
        out_shape=(
            jax.ShapeDtypeStruct((rows, width), LOW), jax.ShapeDtypeStruct((rows, width), LOW),
            jax.ShapeDtypeStruct((rows, state), F32), jax.ShapeDtypeStruct((rows, state), F32),
            jax.ShapeDtypeStruct((pairs, 8, rows), F32),
        ),
        in_specs=[
            pl.BlockSpec((1, 8, rows), lambda i: (i, 0, 0)), pair_spec(rows), pair_spec(rows), pair_spec(rows), pair_spec(rows),
            whole_spec((rows, state)), whole_spec((rows, state)), pair_spec(state), pair_spec(state), pair_spec(1),
            whole_spec((rows, 1)), whole_spec((1, rows)),
        ],
        out_specs=[
            pair_spec(rows), pair_spec(rows), whole_spec((rows, state)), whole_spec((rows, state)),
            pl.BlockSpec((1, 8, rows), lambda i: (i, 0, 0)),
        ],
        scratch_shapes=[
            pltpu.VMEM((rows, rows), F32), pltpu.VMEM((rows, rows), F32), pltpu.VMEM((rows, 128), LOW), pltpu.VMEM((rows, 128), LOW),
        ],
        compiler_params=kernel_params(),
        cost_estimate=pl.CostEstimate(flops=24 * rows * rows * width, bytes_accessed=16 * rows * width, transcendentals=rows * rows * width // 64),
        name="mamba_backward",
    )(per_head, xs, z, y, dg, b, c, state_in, later, skip, seg_col, seg_row)

def per_device(
    tokens, cotangent, doc_lengths, mixer_gain, w_query, key_matrix, value_matrix, mamba_gate_weight,
    mamba_input_weight, w_bproj, w_cproj, w_dt, a_log, dt_bias, d_skip, w_attn_out, w_mixer_out,
    ffn_gain, w_gate, w_up, w_down,
):
    micro_count, seq_count, block_len, model_dim = tokens.shape
    rows_here = mixer_gain.shape[0]
    heads = w_dt.shape[1]
    ssm_dim = mamba_gate_weight.shape[1]
    head_dim = ssm_dim // heads
    q_dim = w_query.shape[1]
    kv_dim = key_matrix.shape[1]
    state_dim = w_bproj.shape[1]
    ff_dim = w_gate.shape[1]
    ci = lax.axis_index("context")
    nc = lax.axis_size("context")
    full_len = nc * block_len
    units = micro_count * seq_count
    pairs = heads // 2

    def fill(width):
        return jnp.zeros((rows_here, -width % 128), LOW)

    first = jnp.concatenate(
        [w_query, key_matrix, value_matrix, mixer_gain[:, None], ffn_gain[:, None], fill(q_dim + 2 * kv_dim + 2)], axis=1)
    second = jnp.concatenate([mamba_gate_weight, mamba_input_weight, w_bproj, w_cproj, w_dt, fill(heads)], axis=1)
    third = jnp.concatenate([w_attn_out.T, w_mixer_out.T], axis=1)
    fourth = jnp.concatenate([w_gate, w_up, w_down.T], axis=1)
    first = gather_rows(first, False)
    second = gather_rows(second, False)
    third = gather_rows(third, True)
    fourth = gather_rows(fourth, True)
    at_gain = q_dim + 2 * kv_dim
    at_b = 2 * ssm_dim
    at_dt = at_b + 2 * state_dim
    gain_one = first[:, at_gain].astype(F32)
    gain_two = first[:, at_gain + 1].astype(F32)
    gate_up = fourth[:, : 2 * ff_dim]
    down_t = fourth[:, 2 * ff_dim :]
    both = (units, block_len)

    positions = jnp.arange(full_len)
    doc_lens = doc_lengths.reshape(units, -1)
    seg_all = segment_ids(doc_lens, positions)
    seg_here = lax.dynamic_slice_in_dim(seg_all, ci * block_len, block_len, 1)
    seg_prev = segment_ids(doc_lens, jnp.reshape(ci * block_len - 1, (1,)))
    lowest = jnp.min(jnp.where(seg_all == seg_here[:, :1], positions, full_len), axis=1) // block_len
    spans = jnp.stack([lowest, jnp.broadcast_to(ci, lowest.shape)], axis=1).astype(jnp.int32)
    carried = (seg_here == seg_prev)[:, None, :]
    closing = (seg_here == seg_here[:, -1:])[:, None, :]
    tri = (jnp.arange(block_len)[:, None] <= jnp.arange(block_len)[None, :]).astype(F32)
    skip_row = jnp.repeat(d_skip, head_dim)[None]

    x = tokens.reshape(units * block_len, model_dim).astype(F32)
    r1, n1 = norm_forward(x, gain_one)
    p_one = mat_mul(n1, first)
    q = (p_one[:, :q_dim].astype(LOW) * jnp.asarray(0.125, LOW)).reshape(both + (q_dim,))
    kv = p_one[:, q_dim:at_gain].astype(LOW).reshape(both + (2 * kv_dim,))
    kv_all = jnp.swapaxes(gather_context(kv), 0, 1).reshape(units, full_len, 2 * kv_dim)
    p_two = mat_mul(n1, second)
    zx = p_two[:, :at_b].astype(LOW).reshape(both + (at_b,))
    bc = p_two[:, at_b:at_dt].astype(LOW).reshape(both + (2 * state_dim,))
    dr = jnp.swapaxes(p_two[:, at_dt : at_dt + heads].reshape(both + (heads,)), 1, 2) + dt_bias[:, None]
    dt = jax.nn.softplus(dr)
    rate = -jnp.exp(a_log)[:, None]
    decay = jnp.einsum("sht,tu->shu", rate * dt, tri, precision=PRECISE)
    last = decay[:, :, -1:]
    entering = jnp.where(carried, jnp.exp(decay), 0.0)
    leaving = jnp.where(closing, jnp.exp(last - decay), 0.0)
    passing = entering[:, :, -1]

    def packed(*parts):
        stacked = jnp.stack([part.reshape(units, pairs, 2, block_len) for part in parts], axis=2)
        return stacked.reshape(units, pairs, 8, block_len)

    per_head = packed(decay, dt, entering, leaving)
    per_head_two = packed(decay, dt, entering, leaving * dt)
    x_of = [zx[u, :, ssm_dim:] for u in range(units)]
    z_of = [zx[u, :, :ssm_dim] for u in range(units)]
    b_of = [bc[u, :, :state_dim] for u in range(units)]
    c_of = [bc[u, :, state_dim:] for u in range(units)]
    seg_col = [seg_here[u][:, None] for u in range(units)]
    seg_row = [seg_here[u][None] for u in range(units)]
    span = jnp.stack([mamba_state(per_head_two[u], 6, b_of[u], x_of[u]) for u in range(units)])
    pass_row = jnp.repeat(passing, head_dim, axis=1)[:, None, :]
    pass_high = pass_row.astype(LOW)
    pass_low = (pass_row - pass_high.astype(F32)).astype(LOW)
    sent = jnp.concatenate([span, pass_high, pass_low, jnp.zeros((units, 14, ssm_dim), LOW)], axis=1)
    spans_all = gather_context(sent).astype(F32)
    passes_all = spans_all[:, :, state_dim : state_dim + 1] + spans_all[:, :, state_dim + 1 : state_dim + 2]
    state = jnp.zeros((units, state_dim, ssm_dim), F32)
    for k in range(nc - 1):
        state = jnp.where(k < ci, passes_all[k] * state + spans_all[k, :, :state_dim], state)
    state_low = state.astype(LOW)

    o, lse, y, og, m = [], [], [], [], []
    for u in range(units):
        o_u, lse_u = attention_forward(q[u], kv_all[u], seg_here[u], seg_all[u], spans[u])
        y_u, g_u = mamba_forward(per_head[u], x_of[u], z_of[u], b_of[u], c_of[u], state_low[u], skip_row, seg_col[u], seg_row[u])
        o.append(o_u)
        lse.append(lse_u)
        y.append(y_u)
        og.append(jnp.concatenate([o_u, g_u], axis=1))
        m.append(tensor_sum(mat_mul_t(og[u], third)))

    layer_outs, h1, r2, n2, f, dab, dn2 = [], [], [], [], [], [], []
    dy = [cotangent.reshape(both + (model_dim,))[u] for u in range(units)]
    for u in range(units):
        h1.append(x[u * block_len : (u + 1) * block_len] + m[u])
        r2_u, n2_u = norm_forward(h1[u], gain_two)
        r2.append(r2_u)
        n2.append(n2_u)
        ab = mat_mul(n2[u], gate_up)
        a, b = ab[:, :ff_dim], ab[:, ff_dim:]
        sig = jax.nn.sigmoid(a)
        f.append((a * sig * b).astype(LOW))
        df = mat_mul(dy[u], down_t)
        dab.append(jnp.concatenate(
            [(df * b * sig * (1.0 + a * (1.0 - sig))).astype(LOW), (df * a * sig).astype(LOW)], axis=1))
        dn2.append(tensor_sum(mat_mul_t(dab[u], gate_up)))
    for u in range(units):
        layer_outs.append((h1[u] + tensor_sum(mat_mul_t(f[u], down_t))).astype(LOW))
    g_gate_up = sum(outer_sum(n2[u], dab[u]) for u in range(units)).astype(LOW)
    g_down = sum(outer_sum(dy[u], f[u]) for u in range(units)).astype(LOW)
    g_fourth = scatter_rows(jnp.concatenate([g_gate_up, g_down], axis=1))

    g_gain_two = 0.0
    dh, dm, dog, local = [], [], [], []
    for u in range(units):
        dh.append(norm_backward(h1[u], r2[u], gain_two, dn2[u]) + dy[u].astype(F32))
        g_gain_two = g_gain_two + jnp.sum(dn2[u] * h1[u] * r2[u], axis=0)
        dm.append(dh[u].astype(LOW))
        dog.append(mat_mul(dm[u], third).astype(LOW))
        local.append(mamba_state(per_head[u], 4, c_of[u], dog[u][:, q_dim:], z_of[u]))
    g_third = scatter_rows(sum(outer_sum(dm[u], og[u]) for u in range(units)).astype(LOW))
    locals_all = gather_context(jnp.stack(local)).astype(F32)
    later = jnp.zeros((units, state_dim, ssm_dim), F32)
    for k in range(nc - 1, 0, -1):
        later = jnp.where(k > ci, passes_all[k] * later + locals_all[k], later)
    later_low = later.astype(LOW)
    d_pass = jnp.sum((later * state).reshape(units, state_dim, heads, head_dim), axis=(1, 3))
    d_second, stats, dq, dkv = [], [], [], []
    for u in range(units):
        dxs, dz, db, dc, stat = mamba_backward(
            per_head[u], x_of[u], z_of[u], y[u], dog[u][:, q_dim:], b_of[u], c_of[u], state_low[u], later_low[u],
            skip_row, seg_col[u], seg_row[u])
        d_second.append((dz, dxs, db, dc))
        stats.append(stat)
    stats = jnp.stack(stats).reshape(units, pairs, 4, 2, block_len)
    stats = jnp.swapaxes(stats, 1, 2).reshape(units, 4, heads, block_len)
    d_end = jnp.sum(stats[:, 2], axis=2) + d_pass * passing
    d_decay = stats[:, 1] + jnp.where(jnp.arange(block_len) == block_len - 1, d_end[:, :, None], 0.0)
    d_rate = jnp.einsum("shu,tu->sht", d_decay, tri, precision=PRECISE)
    ddr = (stats[:, 0] + rate * d_rate) * jax.nn.sigmoid(dr)
    head_grads = all_sum(jnp.stack([
        jnp.sum(d_rate * rate * dt, axis=(0, 2)), jnp.sum(ddr, axis=(0, 2)), jnp.sum(stats[:, 3], axis=(0, 2))]))
    ddr = jnp.swapaxes(ddr, 1, 2).astype(LOW)
    d_second = [
        jnp.concatenate([dz, dxs, db.astype(LOW), dc.astype(LOW), ddr[u], jnp.zeros((block_len, -heads % 128), LOW)], axis=1)
        for u, (dz, dxs, db, dc) in enumerate(d_second)]
    g_second = reduce_rows(sum(outer_sum(n1[u * block_len : (u + 1) * block_len], d_second[u]) for u in range(units)).astype(LOW))
    g_second = jnp.concatenate(
        [g_second[:, :at_b], tensor_sum(g_second[:, at_b:at_dt]), g_second[:, at_dt:]], axis=1)
    g_second = share_rows(g_second).astype(F32)
    for u in range(units):
        dq_u, part = attention_backward(
            q[u], dog[u][:, :q_dim], o[u], kv_all[u], lse[u], seg_here[u], seg_all[u], spans[u])
        part = part.reshape(nc, block_len, 2 * kv_dim)
        left = nc
        for bit in context_bits():
            left //= 2
            view = part.reshape(left, 2, block_len, 2 * kv_dim)
            mine = (ci & bit) // bit
            away = lax.dynamic_index_in_dim(view, 1 - mine, 1, keepdims=False)
            keep = lax.dynamic_index_in_dim(view, mine, 1, keepdims=False)
            part = (keep.astype(F32) + swap_context(away, bit).astype(F32)).astype(LOW)
        dq.append(dq_u)
        dkv.append(part.reshape(block_len, 2 * kv_dim))
    input_grads = []
    g_gain_one = 0.0
    d_first = []
    for u in range(units):
        at = slice(u * block_len, (u + 1) * block_len)
        d_first.append(jnp.concatenate([dq[u], dkv[u], jnp.zeros((block_len, first.shape[1] - at_gain), LOW)], axis=1))
        part = mat_mul_t(d_first[u], first) + mat_mul_t(d_second[u], second)
        g_gain_one = g_gain_one + jnp.sum(part * x[at] * r1[at], axis=0)
        input_grads.append(dh[u] + norm_backward(x[at], r1[at], gain_one, tensor_sum(part)))
    g_first = sum(outer_sum(n1[u * block_len : (u + 1) * block_len], d_first[u][:, :at_gain]) for u in range(units))
    g_first = jnp.concatenate(
        [g_first, g_gain_one[:, None], g_gain_two[:, None], jnp.zeros((model_dim, first.shape[1] - at_gain - 2), F32)], axis=1)
    g_first = reduce_rows(g_first.astype(LOW))
    gains = g_first[:, at_gain:]
    lane = jnp.arange(gains.shape[1])[None]
    gains = jnp.where(lane == 0, tensor_sum(gains), gains)
    g_first = share_rows(jnp.concatenate([g_first[:, :at_gain], gains], axis=1)).astype(F32)

    shape = (micro_count, seq_count, block_len, model_dim)
    at_k, at_v = q_dim, q_dim + kv_dim
    return (
        jnp.stack(layer_outs).reshape(shape),
        jnp.stack(input_grads).reshape(shape),
        g_first[:, at_gain],
        g_first[:, :at_k],
        g_first[:, at_k:at_v],
        g_first[:, at_v:at_gain],
        g_second[:, :ssm_dim],
        g_second[:, ssm_dim:at_b],
        g_second[:, at_b : at_b + state_dim],
        g_second[:, at_b + state_dim : at_dt],
        g_second[:, at_dt : at_dt + heads],
        head_grads[0],
        head_grads[1],
        head_grads[2],
        g_third[:, :q_dim].T,
        g_third[:, q_dim:].T,
        g_first[:, at_gain + 1],
        g_fourth[:, :ff_dim],
        g_fourth[:, ff_dim : 2 * ff_dim],
        g_fourth[:, 2 * ff_dim :].T,
    )


def solution(mesh):
    rows, cols = P("fsdp", "tensor"), P("tensor", "fsdp")
    acts = P(None, "fsdp", "context", None)
    return jax.shard_map(
        per_device,
        mesh=mesh,
        in_specs=(
            acts, acts, P(None, "fsdp", None), P("fsdp"), rows, rows, rows, rows, rows, P("fsdp", None),
            P("fsdp", None), rows, P("tensor"), P("tensor"), P("tensor"), cols, cols, P("fsdp"), rows, rows, cols,
        ),
        out_specs=(
            acts, acts, P("fsdp"), rows, rows, rows, rows, rows, P("fsdp", None), P("fsdp", None), rows,
            P("tensor"), P("tensor"), P("tensor"), cols, cols, P("fsdp"), rows, rows, cols,
        ),
        check_vma=False,
    )
```

time: 992 us -> 743 us (0.75)
  the two profiles are of different devices: /device:TPU:0 before, /device:TPU:11 now
where the time goes in v2:
time: 743 us; the launch traced here: 732 us
  waiting for transfers between devices  206 us (28%)
  local copies, waits for them, and re-layouts  142 us (19%)
  starting transfers between devices  103 us (14%)
  Pallas kernels  102 us (14%)
  matrix products  99.2 us (13%)
  other arithmetic  75 us (10%)
    ppermute x10, waiting for transfers between devices, tensor_sum(): lax.ppermute(low, 'tensor', [(i, (i + 1) % size) for i in range(size)])  80.6 us
    ppermute x59, waiting for transfers between devices, swap_context(): return lax.ppermute(x, 'context', [(i, i ^ bit) for i in range(size)])  72.2 us
    ppermute x59, starting transfers between devices, swap_context(): return lax.ppermute(x, 'context', [(i, i ^ bit) for i in range(size)])  56.7 us
    ppermute x24, waiting for transfers between devices, from_next(): return lax.ppermute(x, axis, [((i + step) % size, i) for i in range(size)])  53.2 us
    dot_general x10, matrix products, mat_mul_t(): lax.dot_general(left, right, (((1,), (1,)), ((), ())), preferred_element_...  36.1 us
    ppermute x24, starting transfers between devices, from_next(): return lax.ppermute(x, axis, [((i + step) % size, i) for i in range(size)])  35.8 us
    unnamed x367, local copies, waits for them, and re-layouts  33.5 us
    dot_general x10, matrix products, outer_sum(): lax.dot_general(left, right, (((0,), (0,)), ((), ())), preferred_element_...  33.3 us
  transfers between devices with their start and end apart: 95, of which 32 were waited for; matrix products, arithmetic and copies ran while one was open for 35% of the time, Pallas kernels for 14%

profile of v2, /device:TPU:11, one launch (start us, length us, event | category | flops | bytes accessed | tf_op | source)
XLA Modules:
  0.0 732.3 jit_solution(9676179970453305383)
XLA Ops:
  9.0 3.3 collective-permute-start.15
  34.8 3.4 broadcast_in_dim.375
  43.3 2.9 collective-permute-start.2
  51.5 3.8 collective-permute-start.31
  64.3 4.0 collective-permute-start.32
  85.1 9.5 %collective-permute-done.20 = bf16[64,1920]{1,0:T(8,128)(2,1)S(1)} collective-permute-done((bf16[64,1920]{1,0:T(8,128)(2,1)S(1)}, bf16[64,1920]{1,0:T(8,128)(2,1)S(1)}, u32[]{:S(2)}, u32[]{:S(2)}) %collective-permute-start.20) | collective-permute-done | bytes 245792 | tf_op jit(solution)/shard_map/ppermute | solution.py:18
  97.8 3.4 collective-permute-done.23
  109.2 3.4 collective-permute-start.39
  112.8 10.3 %attention_forward.2 = (bf16[512,256]{1,0:T(8,128)(2,1)S(1)}, f32[8,512]{1,0:T(8,128)S(1)}) custom-call(s32[2]{0:T(128)S(1)} %get-tuple-element.160.span_ref, bf16[512,256]{1,0:T(8,128)(2,1)S(1)} %get-tuple-element.217.q_ref, bf16[2048,128]{1,0:T(8,128)(2,1)S(1)} %bitcast.637, s32[1,512]{1,0:T(1,128)S(1)} %get-tuple-element.243.seg_q_ref.seg_row_ref, ...), custom_call_target="tpu_custom_call" | custom-call | flops 4294967296 | bytes 524288 | tf_op jit(solution)/shard_map/attention_forward/pallas_call | solution.py:202
  123.1 10.1 %attention_forward.3 = (bf16[512,256]{1,0:T(8,128)(2,1)S(1)}, f32[8,512]{1,0:T(8,128)S(1)}) custom-call(s32[2]{0:T(128)S(1)} %get-tuple-element.161.span_ref, bf16[512,256]{1,0:T(8,128)(2,1)S(1)} %get-tuple-element.218.q_ref, bf16[2048,128]{1,0:T(8,128)(2,1)S(1)} %bitcast.635, s32[1,512]{1,0:T(1,128)S(1)} %get-tuple-element.244.seg_q_ref.seg_row_ref, ...), custom_call_target="tpu_custom_call" | custom-call | flops 4294967296 | bytes 524288 | tf_op jit(solution)/shard_map/attention_forward/pallas_call | solution.py:202
  140.0 6.5 fusion.168
  146.7 2.9 copy-done.146
  151.4 3.7 slice.533
  194.4 6.5 mamba_forward.2
  204.8 6.7 mamba_forward.3
  225.2 3.4 collective-permute-done.36
  228.6 22.4 %collective-permute-done.44 = bf16[512,1024]{1,0:T(8,128)(2,1)S(1)} collective-permute-done((bf16[512,1024]{1,0:T(8,128)(2,1)S(1)}, bf16[512,1024]{1,0:T(8,128)(2,1)S(1)}, u32[]{:S(2)}, u32[]{:S(2)}) %collective-permute-start.44) | collective-permute-done | bytes 1048608 | tf_op jit(solution)/shard_map/ppermute | solution.py:112
  256.6 4.7 fusion.10
  261.4 3.5 fusion.20
  264.9 3.9 convolution_convert_fusion.4
  270.1 4.6 fusion.26
  278.8 4.6 fusion.8
  283.4 3.5 fusion.15
  287.0 6.6 fusion.29
  293.8 3.8 convolution_convert_fusion.2
  299.2 4.0 add_convert_fusion
  303.2 3.8 fusion.25
  307.0 4.8 pad_maximum_fusion
  311.8 3.9 dynamic-slice_bitcast_fusion
  315.7 8.4 %collective-permute-done.49 = bf16[512,1024]{1,0:T(8,128)(2,1)} collective-permute-done((bf16[512,1024]{1,0:T(8,128)(2,1)}, bf16[512,1024]{1,0:T(8,128)(2,1)}, u32[]{:S(2)}, u32[]{:S(2)}) %collective-permute-start.49) | collective-permute-done | bytes 1048608 | tf_op jit(solution)/shard_map/ppermute | solution.py:112
  324.2 3.8 multiply_reduce_fusion.2
  328.0 18.6 %collective-permute-done.45 = bf16[512,1024]{1,0:T(8,128)(2,1)} collective-permute-done((bf16[512,1024]{1,0:T(8,128)(2,1)}, bf16[512,1024]{1,0:T(8,128)(2,1)}, u32[]{:S(2)}, u32[]{:S(2)}) %collective-permute-start.45) | collective-permute-done | bytes 1048608 | tf_op jit(solution)/shard_map/ppermute | solution.py:112
  346.6 22.5 %collective-permute-done.43 = bf16[512,1024]{1,0:T(8,128)(2,1)} collective-permute-done((bf16[512,1024]{1,0:T(8,128)(2,1)}, bf16[512,1024]{1,0:T(8,128)(2,1)}, u32[]{:S(2)}, u32[]{:S(2)}) %collective-permute-start.43) | collective-permute-done | bytes 1048608 | tf_op jit(solution)/shard_map/ppermute | solution.py:112
  369.1 5.2 convert_add_fusion.5
  384.7 3.3 fusion.93
  388.0 16.7 %attention_backward.2 = (bf16[512,256]{1,0:T(8,128)(2,1)S(1)}, bf16[2048,128]{1,0:T(8,128)(2,1)S(1)}) custom-call(s32[2]{0:T(128)S(1)} %copy-done.63, bf16[512,256]{1,0:T(8,128)(2,1)S(1)} %copy-done.56, bf16[512,256]{1,0:T(8,128)(2,1)S(1)} %slice.587.do_ref, bf16[512,256]{1,0:T(8,128)(2,1)S(1)} %copy-done.52, bf16[2048,128]{1,0:T(8,128)(2,1)S(1)} %bitcast.638, ...), custom_call_target="tpu_custom_call" | custom-call | flops 10737418240 | bytes 524288 | tf_op jit(solution)/shard_map/attention_backward/pallas_call | solution.py:265
  406.3 16.6 %attention_backward.3 = (bf16[512,256]{1,0:T(8,128)(2,1)S(1)}, bf16[2048,128]{1,0:T(8,128)(2,1)S(1)}) custom-call(s32[2]{0:T(128)S(1)} %get-tuple-element.161.span_ref, bf16[512,256]{1,0:T(8,128)(2,1)S(1)} %copy-done.54, bf16[512,256]{1,0:T(8,128)(2,1)S(1)} %slice.601.do_ref, bf16[512,256]{1,0:T(8,128)(2,1)S(1)} %copy-done.50, ...), custom_call_target="tpu_custom_call" | custom-call | flops 10737418240 | bytes 524288 | tf_op jit(solution)/shard_map/attention_backward/pallas_call | solution.py:265
  426.6 4.4 add_convert_fusion.3
  449.1 14.7 %mamba_backward.2 = (bf16[512,768]{1,0:T(8,128)(2,1)S(1)}, bf16[512,768]{1,0:T(8,128)(2,1)S(1)}, f32[512,128]{1,0:T(8,128)S(1)}, f32[512,128]{1,0:T(8,128)S(1)}, f32[6,8,512]{2,1,0:T(8,128)S(1)}) custom-call(f32[6,8,512]{2,1,0:T(8,128)S(1)} %copy-done.33, bf16[512,768]{1,0:T(8,128)(2,1)S(1)} %get-tuple-element.190.right_ref.xs_ref, ...), custom_call_target="tpu_custom_call" | custom-call | flops 4831838208 | bytes 6291456 | tf_op jit(solution)/shard_map/mamba_backward/pallas_call | solution.py:454
  465.3 14.3 %mamba_backward.3 = (bf16[512,768]{1,0:T(8,128)(2,1)S(1)}, bf16[512,768]{1,0:T(8,128)(2,1)S(1)}, f32[512,128]{1,0:T(8,128)S(1)}, f32[512,128]{1,0:T(8,128)S(1)}, f32[6,8,512]{2,1,0:T(8,128)S(1)}) custom-call(f32[6,8,512]{2,1,0:T(8,128)S(1)} %copy-done.31, bf16[512,768]{1,0:T(8,128)(2,1)S(1)} %get-tuple-element.189.right_ref.xs_ref, ...), custom_call_target="tpu_custom_call" | custom-call | flops 4831838208 | bytes 6291456 | tf_op jit(solution)/shard_map/mamba_backward/pallas_call | solution.py:454
  489.4 3.4 concatenate.123
  492.7 5.2 fusion.171
  498.0 5.6 fusion.53
  509.6 5.2 fusion.172
  520.3 4.1 collective-permute-start.77
  526.2 5.7 add_convert_fusion.1
  531.9 6.2 collective-permute-done.80
  542.6 7.6 %collective-permute-start.87 = (bf16[4,2,64,3072]{3,2,1,0:T(8,128)(2,1)}, bf16[4,2,64,3072]{3,2,1,0:T(8,128)(2,1)}, u32[]{:S(2)}, u32[]{:S(2)}) collective-permute-start(bf16[4,2,64,3072]{3,2,1,0:T(8,128)(2,1)} %dynamic-slice_bitcast_fusion), channel_id=1, source_target_pairs={{0,2},{2,0},{4,6},{6,4},{1,3},{3,1},{5,7},{7,5},{8,10},{10,8},{12,... | collective-permute-start | bytes 9437192 | tf_op jit(solution)/shard_map/ppermute | solution.py:18
  554.3 4.0 collective-permute-done.84
  561.0 4.1 multiply_reduce_fusion.6
  570.2 4.2 add_bitcast_fusion.1
  581.5 4.0 fusion
  585.6 3.4 collective-permute-done.58
  594.0 3.3 collective-permute-done.59
  597.6 2.7 collective-permute-done.62
  607.3 21.8 %collective-permute-done.63 = bf16[64,512]{1,0:T(8,128)(2,1)S(1)} collective-permute-done((bf16[64,512]{1,0:T(8,128)(2,1)S(1)}, bf16[64,512]{1,0:T(8,128)(2,1)S(1)}, u32[]{:S(2)}, u32[]{:S(2)}) %collective-permute-start.63) | collective-permute-done | bytes 65568 | tf_op jit(solution)/shard_map/ppermute | solution.py:18
  629.1 5.3 collective-permute-start.65
  642.3 7.9 %collective-permute-done.67 = bf16[4,1,64,1920]{3,2,1,0:T(8,128)(2,1)} collective-permute-done((bf16[4,1,64,1920]{3,2,1,0:T(8,128)(2,1)}, bf16[4,1,64,1920]{3,2,1,0:T(8,128)(2,1)}, u32[]{:S(2)}, u32[]{:S(2)}) %collective-permute-start.67) | collective-permute-done | bytes 983072 | tf_op jit(solution)/shard_map/ppermute | solution.py:18
  659.7 8.1 %collective-permute-done.69 = bf16[64,1920]{1,0:T(8,128)(2,1)S(1)} collective-permute-done((bf16[64,1920]{1,0:T(8,128)(2,1)S(1)}, bf16[64,1920]{1,0:T(8,128)(2,1)S(1)}, u32[]{:S(2)}, u32[]{:S(2)}) %collective-permute-start.69) | collective-permute-done | bytes 245792 | tf_op jit(solution)/shard_map/ppermute | solution.py:23
  667.8 25.3 %collective-permute-done.68 = bf16[64,1920]{1,0:T(8,128)(2,1)S(1)} collective-permute-done((bf16[64,1920]{1,0:T(8,128)(2,1)S(1)}, bf16[64,1920]{1,0:T(8,128)(2,1)S(1)}, u32[]{:S(2)}, u32[]{:S(2)}) %collective-permute-start.68) | collective-permute-done | bytes 245792 | tf_op jit(solution)/shard_map/ppermute | solution.py:23
  696.3 2.9 collective-permute-start.73
  699.4 4.9 collective-permute-done.90
  704.2 5.8 collective-permute-done.89
  711.8 8.6 %collective-permute-done.92 = bf16[64,3072]{1,0:T(8,128)(2,1)} collective-permute-done((bf16[64,3072]{1,0:T(8,128)(2,1)S(1)}, bf16[64,3072]{1,0:T(8,128)(2,1)}, u32[]{:S(2)}, u32[]{:S(2)}) %collective-permute-start.92) | collective-permute-done | bytes 393248 | tf_op jit(solution)/shard_map/ppermute | solution.py:18
  (826 shorter events, 281.9 us)
Async XLA Ops:
  5.8 34.2 %collective-permute-start = (bf16[64,512]{1,0:T(8,128)(2,1)}, bf16[64,512]{1,0:T(8,128)(2,1)}, u32[]{:S(2)}, u32[]{:S(2)}) collective-permute-start(bf16[64,512]{1,0:T(8,128)(2,1)} %constant_dynamic-slice_fusion.11), channel_id=1, source_target_pairs={{8,0},{16,8},{24,16},{0,24},{9,1},{17,9},{25,17},{1,25},{10,2},{18... | collective-permute-start | bytes 196616 | tf_op jit(solution)/shard_map/ppermute | solution.py:23
  9.0 47.5 %collective-permute-start.15 = (bf16[64,1920]{1,0:T(8,128)(2,1)}, bf16[64,1920]{1,0:T(8,128)(2,1)}, u32[]{:S(2)}, u32[]{:S(2)}) collective-permute-start(bf16[64,1920]{1,0:T(8,128)(2,1)} %constant_dynamic-slice_fusion.10), channel_id=1, source_target_pairs={{8,0},{16,8},{24,16},{0,24},{9,1},{17,9},{25,17},{1,25},{10,2},{18... | collective-permute-start | bytes 737288 | tf_op jit(solution)/shard_map/ppermute | solution.py:23
  13.3 33.4 %collective-permute-start.30 = (bf16[64,1024]{1,0:T(8,128)(2,1)}, bf16[64,1024]{1,0:T(8,128)(2,1)}, u32[]{:S(2)}, u32[]{:S(2)}) collective-permute-start(bf16[64,1024]{1,0:T(8,128)(2,1)} %fusion.125), channel_id=1, source_target_pairs={{8,0},{16,8},{24,16},{0,24},{9,1},{17,9},{25,17},{1,25},{10,2},{18... | collective-permute-start | bytes 393224 | tf_op jit(solution)/shard_map/ppermute | solution.py:23
  17.2 58.2 %collective-permute-start.37 = (bf16[64,3072]{1,0:T(8,128)(2,1)}, bf16[64,3072]{1,0:T(8,128)(2,1)}, u32[]{:S(2)}, u32[]{:S(2)}) collective-permute-start(bf16[64,3072]{1,0:T(8,128)(2,1)} %constant_dynamic-slice_fusion.9), channel_id=1, source_target_pairs={{8,0},{16,8},{24,16},{0,24},{9,1},{17,9},{25,17},{1,25},{10,2},{18... | collective-permute-start | bytes 1179656 | tf_op jit(solution)/shard_map/ppermute | solution.py:23
  51.5 8.3 %collective-permute-start.31 = (bf16[64,1024]{1,0:T(8,128)(2,1)}, bf16[64,1024]{1,0:T(8,128)(2,1)S(1)}, u32[]{:S(2)}, u32[]{:S(2)}) collective-permute-start(bf16[64,1024]{1,0:T(8,128)(2,1)} %collective-permute-done.30), channel_id=1, source_target_pairs={{8,0},{16,8},{24,16},{0,24},{9,1},{17,9},{25,17},{1,25},{10,2},{18... | collective-permute-start | bytes 393224 | tf_op jit(solution)/shard_map/ppermute | solution.py:23
  58.6 19.6 %collective-permute-start.16 = (bf16[64,1920]{1,0:T(8,128)(2,1)}, bf16[64,1920]{1,0:T(8,128)(2,1)S(1)}, u32[]{:S(2)}, u32[]{:S(2)}) collective-permute-start(bf16[64,1920]{1,0:T(8,128)(2,1)} %collective-permute-done.15), channel_id=1, source_target_pairs={{0,4},{2,6},{4,0},{6,2},{1,5},{3,7},{5,1},{7,3},{8,12},{10,14},{12... | collective-permute-start | bytes 737288 | tf_op jit(solution)/shard_map/ppermute | solution.py:18
  59.8 19.4 %collective-permute-start.17 = (bf16[64,1920]{1,0:T(8,128)(2,1)}, bf16[64,1920]{1,0:T(8,128)(2,1)S(1)}, u32[]{:S(2)}, u32[]{:S(2)}) collective-permute-start(bf16[64,1920]{1,0:T(8,128)(2,1)} %collective-permute-done.15), channel_id=1, source_target_pairs={{0,2},{2,0},{4,6},{6,4},{1,3},{3,1},{5,7},{7,5},{8,10},{10,8},{12,... | collective-permute-start | bytes 737288 | tf_op jit(solution)/shard_map/ppermute | solution.py:18
  61.0 21.8 %collective-permute-start.19 = (bf16[64,1920]{1,0:T(8,128)(2,1)}, bf16[64,1920]{1,0:T(8,128)(2,1)S(1)}, u32[]{:S(2)}, u32[]{:S(2)}) collective-permute-start(bf16[64,1920]{1,0:T(8,128)(2,1)} %collective-permute-done.15), channel_id=1, source_target_pairs={{8,0},{16,8},{24,16},{0,24},{9,1},{17,9},{25,17},{1,25},{10,2},{18... | collective-permute-start | bytes 737288 | tf_op jit(solution)/shard_map/ppermute | solution.py:23
  64.3 9.0 %collective-permute-start.32 = (bf16[64,1024]{1,0:T(8,128)(2,1)S(1)}, bf16[64,1024]{1,0:T(8,128)(2,1)S(1)}, u32[]{:S(2)}, u32[]{:S(2)}) collective-permute-start(bf16[64,1024]{1,0:T(8,128)(2,1)S(1)} %collective-permute-done.31), channel_id=1, source_target_pairs={{8,0},{16,8},{24,16},{0,24},{9,1},{17,9},{25,17},{1,25},{10,2},{18... | collective-permute-start | bytes 393224 | tf_op jit(solution)/shard_map/ppermute | solution.py:23
  75.4 9.3 %collective-permute-start.13 = (bf16[2,512,128]{2,1,0:T(8,128)(2,1)S(1)}, bf16[2,512,128]{2,1,0:T(8,128)(2,1)S(1)}, u32[]{:S(2)}, u32[]{:S(2)}) collective-permute-start(bf16[2,512,128]{2,1,0:T(8,128)(2,1)S(1)} %bitcast.675), channel_id=1, source_target_pairs={{0,2},{2,0},{4,6},{6,4},{1,3},{3,1},{5,7},{7,5},{8,10},{10,8},{12,... | collective-permute-start | bytes 786440 | tf_op jit(solution)/shard_map/ppermute | solution.py:18
  78.2 24.8 %collective-permute-start.33 = (bf16[3,64,1024]{2,1,0:T(8,128)(2,1)S(1)}, bf16[3,64,1024]{2,1,0:T(8,128)(2,1)S(1)}, u32[]{:S(2)}, u32[]{:S(2)}) collective-permute-start(bf16[3,64,1024]{2,1,0:T(8,128)(2,1)S(1)} %pad_maximum_fusion.10), channel_id=1, source_target_pairs={{0,4},{2,6},{4,0},{6,2},{1,5},{3,7},{5,1},{7,3},{8,12},{10,14},{12... | collective-permute-start | bytes 1179656 | tf_op jit(solution)/shard_map/ppermute | solution.py:18
  79.2 26.7 %collective-permute-start.34 = (bf16[3,64,1024]{2,1,0:T(8,128)(2,1)S(1)}, bf16[3,64,1024]{2,1,0:T(8,128)(2,1)S(1)}, u32[]{:S(2)}, u32[]{:S(2)}) collective-permute-start(bf16[3,64,1024]{2,1,0:T(8,128)(2,1)S(1)} %pad_maximum_fusion.10), channel_id=1, source_target_pairs={{0,2},{2,0},{4,6},{6,4},{1,3},{3,1},{5,7},{7,5},{8,10},{10,8},{12,... | collective-permute-start | bytes 1179656 | tf_op jit(solution)/shard_map/ppermute | solution.py:18
  82.9 25.3 %collective-permute-start.38 = (bf16[64,3072]{1,0:T(8,128)(2,1)}, bf16[64,3072]{1,0:T(8,128)(2,1)S(1)}, u32[]{:S(2)}, u32[]{:S(2)}) collective-permute-start(bf16[64,3072]{1,0:T(8,128)(2,1)} %collective-permute-done.37), channel_id=1, source_target_pairs={{8,0},{16,8},{24,16},{0,24},{9,1},{17,9},{25,17},{1,25},{10,2},{18... | collective-permute-start | bytes 1179656 | tf_op jit(solution)/shard_map/ppermute | solution.py:23
  84.7 10.0 %collective-permute-start.20 = (bf16[64,1920]{1,0:T(8,128)(2,1)S(1)}, bf16[64,1920]{1,0:T(8,128)(2,1)S(1)}, u32[]{:S(2)}, u32[]{:S(2)}) collective-permute-start(bf16[64,1920]{1,0:T(8,128)(2,1)S(1)} %collective-permute-done.19), channel_id=1, source_target_pairs={{0,4},{2,6},{4,0},{6,2},{1,5},{3,7},{5,1},{7,3},{8,12},{10,14},{12... | collective-permute-start | bytes 737288 | tf_op jit(solution)/shard_map/ppermute | solution.py:18
  84.7 12.0 %collective-permute-start.21 = (bf16[64,1920]{1,0:T(8,128)(2,1)S(1)}, bf16[64,1920]{1,0:T(8,128)(2,1)S(1)}, u32[]{:S(2)}, u32[]{:S(2)}) collective-permute-start(bf16[64,1920]{1,0:T(8,128)(2,1)S(1)} %collective-permute-done.19), channel_id=1, source_target_pairs={{0,2},{2,0},{4,6},{6,4},{1,3},{3,1},{5,7},{7,5},{8,10},{10,8},{12,... | collective-permute-start | bytes 737288 | tf_op jit(solution)/shard_map/ppermute | solution.py:18
  96.7 12.5 %collective-permute-start.14 = (bf16[2,512,128]{2,1,0:T(8,128)(2,1)S(1)}, bf16[2,512,128]{2,1,0:T(8,128)(2,1)S(1)}, u32[]{:S(2)}, u32[]{:S(2)}) collective-permute-start(bf16[2,512,128]{2,1,0:T(8,128)(2,1)S(1)} %collective-permute-done.12), channel_id=1, source_target_pairs={{0,2},{2,0},{4,6},{6,4},{1,3},{3,1},{5,7},{7,5},{8,10},{10,8},{12,... | collective-permute-start | bytes 786440 | tf_op jit(solution)/shard_map/ppermute | solution.py:18
  101.2 33.6 %collective-permute-start.22 = (bf16[64,1920]{1,0:T(8,128)(2,1)S(1)}, bf16[64,1920]{1,0:T(8,128)(2,1)S(1)}, u32[]{:S(2)}, u32[]{:S(2)}) collective-permute-start(bf16[64,1920]{1,0:T(8,128)(2,1)S(1)} %collective-permute-done.20), channel_id=1, source_target_pairs={{0,2},{2,0},{4,6},{6,4},{1,3},{3,1},{5,7},{7,5},{8,10},{10,8},{12,... | collective-permute-start | bytes 737288 | tf_op jit(solution)/shard_map/ppermute | solution.py:18
  103.0 31.8 %collective-permute-start.24 = (bf16[64,1920]{1,0:T(8,128)(2,1)S(1)}, bf16[64,1920]{1,0:T(8,128)(2,1)S(1)}, u32[]{:S(2)}, u32[]{:S(2)}) collective-permute-start(bf16[64,1920]{1,0:T(8,128)(2,1)S(1)} %collective-permute-done.23), channel_id=1, source_target_pairs={{0,4},{2,6},{4,0},{6,2},{1,5},{3,7},{5,1},{7,3},{8,12},{10,14},{12... | collective-permute-start | bytes 737288 | tf_op jit(solution)/shard_map/ppermute | solution.py:18
  105.9 29.1 %collective-permute-start.25 = (bf16[64,1920]{1,0:T(8,128)(2,1)S(1)}, bf16[64,1920]{1,0:T(8,128)(2,1)S(1)}, u32[]{:S(2)}, u32[]{:S(2)}) collective-permute-start(bf16[64,1920]{1,0:T(8,128)(2,1)S(1)} %collective-permute-done.23), channel_id=1, source_target_pairs={{0,2},{2,0},{4,6},{6,4},{1,3},{3,1},{5,7},{7,5},{8,10},{10,8},{12,... | collective-permute-start | bytes 737288 | tf_op jit(solution)/shard_map/ppermute | solution.py:18
  108.2 26.9 %collective-permute-start.35 = (bf16[3,64,1024]{2,1,0:T(8,128)(2,1)S(1)}, bf16[3,64,1024]{2,1,0:T(8,128)(2,1)S(1)}, u32[]{:S(2)}, u32[]{:S(2)}) collective-permute-start(bf16[3,64,1024]{2,1,0:T(8,128)(2,1)S(1)} %collective-permute-done.33), channel_id=1, source_target_pairs={{0,2},{2,0},{4,6},{6,4},{1,3},{3,1},{5,7},{7,5},{8,10},{10,8},{12,... | collective-permute-start | bytes 1179656 | tf_op jit(solution)/shard_map/ppermute | solution.py:18
  109.2 27.9 %collective-permute-start.39 = (bf16[64,3072]{1,0:T(8,128)(2,1)S(1)}, bf16[64,3072]{1,0:T(8,128)(2,1)S(1)}, u32[]{:S(2)}, u32[]{:S(2)}) collective-permute-start(bf16[64,3072]{1,0:T(8,128)(2,1)S(1)} %collective-permute-done.38), channel_id=1, source_target_pairs={{8,0},{16,8},{24,16},{0,24},{9,1},{17,9},{25,17},{1,25},{10,2},{18... | collective-permute-start | bytes 1179656 | tf_op jit(solution)/shard_map/ppermute | solution.py:23
  139.3 74.5 %collective-permute-start.40 = (bf16[3,64,3072]{2,1,0:T(8,128)(2,1)}, bf16[3,64,3072]{2,1,0:T(8,128)(2,1)}, u32[]{:S(2)}, u32[]{:S(2)}) collective-permute-start(bf16[3,64,3072]{2,1,0:T(8,128)(2,1)} %pad_maximum_fusion.8), channel_id=1, source_target_pairs={{0,4},{2,6},{4,0},{6,2},{1,5},{3,7},{5,1},{7,3},{8,12},{10,14},{12... | collective-permute-start | bytes 3538952 | tf_op jit(solution)/shard_map/ppermute | solution.py:18
  139.3 80.5 %collective-permute-start.41 = (bf16[3,64,3072]{2,1,0:T(8,128)(2,1)}, bf16[3,64,3072]{2,1,0:T(8,128)(2,1)}, u32[]{:S(2)}, u32[]{:S(2)}) collective-permute-start(bf16[3,64,3072]{2,1,0:T(8,128)(2,1)} %pad_maximum_fusion.8), channel_id=1, source_target_pairs={{0,2},{2,0},{4,6},{6,4},{1,3},{3,1},{5,7},{7,5},{8,10},{10,8},{12,... | collective-permute-start | bytes 3538952 | tf_op jit(solution)/shard_map/ppermute | solution.py:18
  176.9 12.4 %collective-permute-start.27 = (bf16[2,144,768]{2,1,0:T(8,128)(2,1)}, bf16[2,144,768]{2,1,0:T(8,128)(2,1)}, u32[]{:S(2)}, u32[]{:S(2)}) collective-permute-start(bf16[2,144,768]{2,1,0:T(8,128)(2,1)} %maximum_maximum_fusion.1), channel_id=1, source_target_pairs={{0,4},{2,6},{4,0},{6,2},{1,5},{3,7},{5,1},{7,3},{8,12},{10,14},{12... | collective-permute-start | bytes 1327112 | tf_op jit(solution)/shard_map/ppermute | solution.py:18
  179.4 11.7 %collective-permute-start.28 = (bf16[2,144,768]{2,1,0:T(8,128)(2,1)}, bf16[2,144,768]{2,1,0:T(8,128)(2,1)}, u32[]{:S(2)}, u32[]{:S(2)}) collective-permute-start(bf16[2,144,768]{2,1,0:T(8,128)(2,1)} %maximum_maximum_fusion.1), channel_id=1, source_target_pairs={{0,2},{2,0},{4,6},{6,4},{1,3},{3,1},{5,7},{7,5},{8,10},{10,8},{12,... | collective-permute-start | bytes 1327112 | tf_op jit(solution)/shard_map/ppermute | solution.py:18
  203.5 25.1 %collective-permute-start.36 = (bf16[512,1024]{1,0:T(8,128)(2,1)}, bf16[512,1024]{1,0:T(8,128)(2,1)}, u32[]{:S(2)}, u32[]{:S(2)}) collective-permute-start(bf16[512,1024]{1,0:T(8,128)(2,1)} %convolution_convert_fusion.5), channel_id=1, source_target_pairs={{0,1},{1,0},{2,3},{3,2},{4,5},{5,4},{6,7},{7,6},{8,9},{9,8},{10,11... | collective-permute-start | bytes 3145736 | tf_op jit(solution)/shard_map/ppermute | solution.py:112
  213.0 38.0 %collective-permute-start.44 = (bf16[512,1024]{1,0:T(8,128)(2,1)S(1)}, bf16[512,1024]{1,0:T(8,128)(2,1)S(1)}, u32[]{:S(2)}, u32[]{:S(2)}) collective-permute-start(bf16[512,1024]{1,0:T(8,128)(2,1)S(1)} %convolution_convert_fusion.3), channel_id=1, source_target_pairs={{0,1},{1,0},{2,3},{3,2},{4,5},{5,4},{6,7},{7,6},{8,9},{9,8},{10,11... | collective-permute-start | bytes 3145736 | tf_op jit(solution)/shard_map/ppermute | solution.py:112
  213.9 39.7 %collective-permute-start.42 = (bf16[3,64,3072]{2,1,0:T(8,128)(2,1)}, bf16[3,64,3072]{2,1,0:T(8,128)(2,1)S(1)}, u32[]{:S(2)}, u32[]{:S(2)}) collective-permute-start(bf16[3,64,3072]{2,1,0:T(8,128)(2,1)} %collective-permute-done.40), channel_id=1, source_target_pairs={{0,2},{2,0},{4,6},{6,4},{1,3},{3,1},{5,7},{7,5},{8,10},{10,8},{12,... | collective-permute-start | bytes 3538952 | tf_op jit(solution)/shard_map/ppermute | solution.py:18
  277.5 38.2 %collective-permute-start.46 = (bf16[512,1024]{1,0:T(8,128)(2,1)S(1)}, bf16[512,1024]{1,0:T(8,128)(2,1)}, u32[]{:S(2)}, u32[]{:S(2)}) collective-permute-start(bf16[512,1024]{1,0:T(8,128)(2,1)S(1)} %fusion.26), channel_id=1, source_target_pairs={{0,1},{1,0},{2,3},{3,2},{4,5},{5,4},{6,7},{7,6},{8,9},{9,8},{10,11... | collective-permute-start | bytes 3145736 | tf_op jit(solution)/shard_map/ppermute | solution.py:112
  293.6 30.5 %collective-permute-start.49 = (bf16[512,1024]{1,0:T(8,128)(2,1)}, bf16[512,1024]{1,0:T(8,128)(2,1)}, u32[]{:S(2)}, u32[]{:S(2)}) collective-permute-start(bf16[512,1024]{1,0:T(8,128)(2,1)} %fusion.29), channel_id=1, source_target_pairs={{0,1},{1,0},{2,3},{3,2},{4,5},{5,4},{6,7},{7,6},{8,9},{9,8},{10,11... | collective-permute-start | bytes 3145736 | tf_op jit(solution)/shard_map/ppermute | solution.py:112
  297.7 48.9 %collective-permute-start.45 = (bf16[512,1024]{1,0:T(8,128)(2,1)}, bf16[512,1024]{1,0:T(8,128)(2,1)}, u32[]{:S(2)}, u32[]{:S(2)}) collective-permute-start(bf16[512,1024]{1,0:T(8,128)(2,1)} %convolution_convert_fusion.2), channel_id=1, source_target_pairs={{0,1},{1,0},{2,3},{3,2},{4,5},{5,4},{6,7},{7,6},{8,9},{9,8},{10,11... | collective-permute-start | bytes 3145736 | tf_op jit(solution)/shard_map/ppermute | solution.py:112
  298.9 70.2 %collective-permute-start.43 = (bf16[512,1024]{1,0:T(8,128)(2,1)}, bf16[512,1024]{1,0:T(8,128)(2,1)}, u32[]{:S(2)}, u32[]{:S(2)}) collective-permute-start(bf16[512,1024]{1,0:T(8,128)(2,1)} %convolution_convert_fusion.4), channel_id=1, source_target_pairs={{0,1},{1,0},{2,3},{3,2},{4,5},{5,4},{6,7},{7,6},{8,9},{9,8},{10,11... | collective-permute-start | bytes 3145736 | tf_op jit(solution)/shard_map/ppermute | solution.py:112
  381.3 57.9 %collective-permute-start.50 = (bf16[2,128,768]{2,1,0:T(8,128)(2,1)}, bf16[2,128,768]{2,1,0:T(8,128)(2,1)}, u32[]{:S(2)}, u32[]{:S(2)}) collective-permute-start(bf16[2,128,768]{2,1,0:T(8,128)(2,1)} %pad_maximum_fusion.11), channel_id=1, source_target_pairs={{0,4},{2,6},{4,0},{6,2},{1,5},{3,7},{5,1},{7,3},{8,12},{10,14},{12... | collective-permute-start | bytes 1179656 | tf_op jit(solution)/shard_map/ppermute | solution.py:18
  382.5 59.6 %collective-permute-start.51 = (bf16[2,128,768]{2,1,0:T(8,128)(2,1)}, bf16[2,128,768]{2,1,0:T(8,128)(2,1)}, u32[]{:S(2)}, u32[]{:S(2)}) collective-permute-start(bf16[2,128,768]{2,1,0:T(8,128)(2,1)} %pad_maximum_fusion.11), channel_id=1, source_target_pairs={{0,2},{2,0},{4,6},{6,4},{1,3},{3,1},{5,7},{7,5},{8,10},{10,8},{12,... | collective-permute-start | bytes 1179656 | tf_op jit(solution)/shard_map/ppermute | solution.py:18
  406.2 29.0 %collective-permute-start.47 = (bf16[2,512,128]{2,1,0:T(8,128)(2,1)}, bf16[2,512,128]{2,1,0:T(8,128)(2,1)}, u32[]{:S(2)}, u32[]{:S(2)}) collective-permute-start(bf16[2,512,128]{2,1,0:T(8,128)(2,1)} %dynamic-slice_bitcast_fusion.8), channel_id=1, source_target_pairs={{0,2},{2,0},{4,6},{6,4},{1,3},{3,1},{5,7},{7,5},{8,10},{10,8},{12,... | collective-permute-start | bytes 786440 | tf_op jit(solution)/shard_map/ppermute | solution.py:18
  424.4 12.2 %collective-permute-start.54 = (bf16[2,512,128]{2,1,0:T(8,128)(2,1)}, bf16[2,512,128]{2,1,0:T(8,128)(2,1)}, u32[]{:S(2)}, u32[]{:S(2)}) collective-permute-start(bf16[2,512,128]{2,1,0:T(8,128)(2,1)} %dynamic-slice_bitcast_fusion.7), channel_id=1, source_target_pairs={{0,2},{2,0},{4,6},{6,4},{1,3},{3,1},{5,7},{7,5},{8,10},{10,8},{12,... | collective-permute-start | bytes 786440 | tf_op jit(solution)/shard_map/ppermute | solution.py:18
  432.2 92.2 %collective-permute-start.79 = (bf16[4,2,64,1024]{3,2,1,0:T(8,128)(2,1)}, bf16[4,2,64,1024]{3,2,1,0:T(8,128)(2,1)}, u32[]{:S(2)}, u32[]{:S(2)}) collective-permute-start(bf16[4,2,64,1024]{3,2,1,0:T(8,128)(2,1)} %dynamic-slice_bitcast_fusion.2), channel_id=1, source_target_pairs={{0,2},{2,0},{4,6},{6,4},{1,3},{3,1},{5,7},{7,5},{8,10},{10,8},{12,... | collective-permute-start | bytes 3145736 | tf_op jit(solution)/shard_map/ppermute | solution.py:18
  506.0 54.9 %collective-permute-start.53 = (bf16[512,1024]{1,0:T(8,128)(2,1)}, bf16[512,1024]{1,0:T(8,128)(2,1)}, u32[]{:S(2)}, u32[]{:S(2)}) collective-permute-start(bf16[512,1024]{1,0:T(8,128)(2,1)} %get-tuple-element.266), channel_id=1, source_target_pairs={{0,1},{1,0},{2,3},{3,2},{4,5},{5,4},{6,7},{7,6},{8,9},{9,8},{10,11... | collective-permute-start | bytes 3145736 | tf_op jit(solution)/shard_map/ppermute | solution.py:112
  517.5 43.5 %collective-permute-start.56 = (bf16[512,1024]{1,0:T(8,128)(2,1)S(1)}, bf16[512,1024]{1,0:T(8,128)(2,1)S(1)}, u32[]{:S(2)}, u32[]{:S(2)}) collective-permute-start(bf16[512,1024]{1,0:T(8,128)(2,1)S(1)} %get-tuple-element.268), channel_id=1, source_target_pairs={{0,1},{1,0},{2,3},{3,2},{4,5},{5,4},{6,7},{7,6},{8,9},{9,8},{10,11... | collective-permute-start | bytes 3145736 | tf_op jit(solution)/shard_map/ppermute | solution.py:112
  520.3 11.5 %collective-permute-start.77 = (f32[3,12]{1,0:T(4,128)S(1)}, f32[3,12]{1,0:T(4,128)S(1)}, u32[]{:S(2)}, u32[]{:S(2)}) collective-permute-start(f32[3,12]{1,0:T(4,128)S(1)} %fusion.197), channel_id=1, source_target_pairs={{0,8},{8,0},{16,24},{24,16},{1,9},{9,1},{17,25},{25,17},{2,10},{10... | collective-permute-start | bytes 440 | tf_op jit(solution)/shard_map/ppermute | solution.py:104
  526.1 12.1 %collective-permute-start.80 = (bf16[4,1,64,1024]{3,2,1,0:T(8,128)(2,1)S(1)}, bf16[4,1,64,1024]{3,2,1,0:T(8,128)(2,1)S(1)}, u32[]{:S(2)}, u32[]{:S(2)}) collective-permute-start(bf16[4,1,64,1024]{3,2,1,0:T(8,128)(2,1)S(1)} %constant_dynamic-slice_fusion.4), channel_id=1, source_target_pairs={{0,4},{2,6},{4,0},{6,2},{1,5},{3,7},{5,1},{7,3},{8,12},{10,14},{12... | collective-permute-start | bytes 1572872 | tf_op jit(solution)/shard_map/ppermute | solution.py:18
  531.8 9.2 %collective-permute-start.78 = (f32[3,12]{1,0:T(4,128)S(1)}, f32[3,12]{1,0:T(4,128)S(1)}, u32[]{:S(2)}, u32[]{:S(2)}) collective-permute-start(f32[3,12]{1,0:T(4,128)S(1)} %add.783), channel_id=1, source_target_pairs={{0,16},{8,24},{16,0},{24,8},{1,17},{9,25},{17,1},{25,9},{2,18},{10... | collective-permute-start | bytes 440 | tf_op jit(solution)/shard_map/ppermute | solution.py:104
  538.5 11.7 %collective-permute-start.82 = (bf16[64,1024]{1,0:T(8,128)(2,1)S(1)}, bf16[64,1024]{1,0:T(8,128)(2,1)S(1)}, u32[]{:S(2)}, u32[]{:S(2)}) collective-permute-start(bf16[64,1024]{1,0:T(8,128)(2,1)S(1)} %get-tuple-element.209), channel_id=1, source_target_pairs={{16,0},{24,8},{0,16},{8,24},{17,1},{25,9},{1,17},{9,25},{18,2},{26... | collective-permute-start | bytes 393224 | tf_op jit(solution)/shard_map/ppermute | solution.py:23
  541.0 12.4 %collective-permute-start.81 = (bf16[64,1024]{1,0:T(8,128)(2,1)S(1)}, bf16[64,1024]{1,0:T(8,128)(2,1)S(1)}, u32[]{:S(2)}, u32[]{:S(2)}) collective-permute-start(bf16[64,1024]{1,0:T(8,128)(2,1)S(1)} %get-tuple-element.207), channel_id=1, source_target_pairs={{8,0},{16,8},{24,16},{0,24},{9,1},{17,9},{25,17},{1,25},{10,2},{18... | collective-permute-start | bytes 393224 | tf_op jit(solution)/shard_map/ppermute | solution.py:23
  542.6 38.9 %collective-permute-start.87 = (bf16[4,2,64,3072]{3,2,1,0:T(8,128)(2,1)}, bf16[4,2,64,3072]{3,2,1,0:T(8,128)(2,1)}, u32[]{:S(2)}, u32[]{:S(2)}) collective-permute-start(bf16[4,2,64,3072]{3,2,1,0:T(8,128)(2,1)} %dynamic-slice_bitcast_fusion), channel_id=1, source_target_pairs={{0,2},{2,0},{4,6},{6,4},{1,3},{3,1},{5,7},{7,5},{8,10},{10,8},{12,... | collective-permute-start | bytes 9437192 | tf_op jit(solution)/shard_map/ppermute | solution.py:18
  550.2 52.4 %collective-permute-start.66 = (bf16[4,2,64,1920]{3,2,1,0:T(8,128)(2,1)}, bf16[4,2,64,1920]{3,2,1,0:T(8,128)(2,1)}, u32[]{:S(2)}, u32[]{:S(2)}) collective-permute-start(bf16[4,2,64,1920]{3,2,1,0:T(8,128)(2,1)} %dynamic-slice_bitcast_fusion.1), channel_id=1, source_target_pairs={{0,2},{2,0},{4,6},{6,4},{1,3},{3,1},{5,7},{7,5},{8,10},{10,8},{12,... | collective-permute-start | bytes 5898248 | tf_op jit(solution)/shard_map/ppermute | solution.py:18
  560.6 16.5 %collective-permute-start.86 = (bf16[64,1024]{1,0:T(8,128)(2,1)S(1)}, bf16[64,1024]{1,0:T(8,128)(2,1)}, u32[]{:S(2)}, u32[]{:S(2)}) collective-permute-start(bf16[64,1024]{1,0:T(8,128)(2,1)S(1)} %collective-permute-done.84), channel_id=1, source_target_pairs={{0,2},{2,0},{4,6},{6,4},{1,3},{3,1},{5,7},{7,5},{8,10},{10,8},{12,... | collective-permute-start | bytes 393224 | tf_op jit(solution)/shard_map/ppermute | solution.py:18
  570.0 10.2 %collective-permute-start.57 = (bf16[4,2,64,512]{3,2,1,0:T(8,128)(2,1)}, bf16[4,2,64,512]{3,2,1,0:T(8,128)(2,1)}, u32[]{:S(2)}, u32[]{:S(2)}) collective-permute-start(bf16[4,2,64,512]{3,2,1,0:T(8,128)(2,1)} %dynamic-slice_bitcast_fusion.3), channel_id=1, source_target_pairs={{0,2},{2,0},{4,6},{6,4},{1,3},{3,1},{5,7},{7,5},{8,10},{10,8},{12,... | collective-permute-start | bytes 1572872 | tf_op jit(solution)/shard_map/ppermute | solution.py:18
  581.4 7.6 %collective-permute-start.58 = (bf16[4,1,64,512]{3,2,1,0:T(8,128)(2,1)S(1)}, bf16[4,1,64,512]{3,2,1,0:T(8,128)(2,1)S(1)}, u32[]{:S(2)}, u32[]{:S(2)}) collective-permute-start(bf16[4,1,64,512]{3,2,1,0:T(8,128)(2,1)S(1)} %constant_dynamic-slice_fusion.6), channel_id=1, source_target_pairs={{0,4},{2,6},{4,0},{6,2},{1,5},{3,7},{5,1},{7,3},{8,12},{10,14},{12... | collective-permute-start | bytes 786440 | tf_op jit(solution)/shard_map/ppermute | solution.py:18
  593.5 46.7 %collective-permute-start.88 = (bf16[4,1,64,3072]{3,2,1,0:T(8,128)(2,1)}, bf16[4,1,64,3072]{3,2,1,0:T(8,128)(2,1)}, u32[]{:S(2)}, u32[]{:S(2)}) collective-permute-start(bf16[4,1,64,3072]{3,2,1,0:T(8,128)(2,1)} %constant_dynamic-slice_fusion.3), channel_id=1, source_target_pairs={{0,4},{2,6},{4,0},{6,2},{1,5},{3,7},{5,1},{7,3},{8,12},{10,14},{12... | collective-permute-start | bytes 4718600 | tf_op jit(solution)/shard_map/ppermute | solution.py:18
  600.4 28.7 %collective-permute-start.63 = (bf16[64,512]{1,0:T(8,128)(2,1)S(1)}, bf16[64,512]{1,0:T(8,128)(2,1)S(1)}, u32[]{:S(2)}, u32[]{:S(2)}) collective-permute-start(bf16[64,512]{1,0:T(8,128)(2,1)S(1)} %pad_maximum_fusion.17), channel_id=1, source_target_pairs={{0,4},{2,6},{4,0},{6,2},{1,5},{3,7},{5,1},{7,3},{8,12},{10,14},{12... | collective-permute-start | bytes 196616 | tf_op jit(solution)/shard_map/ppermute | solution.py:18
  600.6 33.9 %collective-permute-start.64 = (bf16[64,512]{1,0:T(8,128)(2,1)S(1)}, bf16[64,512]{1,0:T(8,128)(2,1)S(1)}, u32[]{:S(2)}, u32[]{:S(2)}) collective-permute-start(bf16[64,512]{1,0:T(8,128)(2,1)S(1)} %pad_maximum_fusion.17), channel_id=1, source_target_pairs={{0,2},{2,0},{4,6},{6,4},{1,3},{3,1},{5,7},{7,5},{8,10},{10,8},{12,... | collective-permute-start | bytes 196616 | tf_op jit(solution)/shard_map/ppermute | solution.py:18
  605.9 44.3 %collective-permute-start.67 = (bf16[4,1,64,1920]{3,2,1,0:T(8,128)(2,1)}, bf16[4,1,64,1920]{3,2,1,0:T(8,128)(2,1)}, u32[]{:S(2)}, u32[]{:S(2)}) collective-permute-start(bf16[4,1,64,1920]{3,2,1,0:T(8,128)(2,1)} %constant_dynamic-slice_fusion.5), channel_id=1, source_target_pairs={{0,4},{2,6},{4,0},{6,2},{1,5},{3,7},{5,1},{7,3},{8,12},{10,14},{12... | collective-permute-start | bytes 2949128 | tf_op jit(solution)/shard_map/ppermute | solution.py:18
  652.1 15.7 %collective-permute-start.69 = (bf16[64,1920]{1,0:T(8,128)(2,1)S(1)}, bf16[64,1920]{1,0:T(8,128)(2,1)S(1)}, u32[]{:S(2)}, u32[]{:S(2)}) collective-permute-start(bf16[64,1920]{1,0:T(8,128)(2,1)S(1)} %get-tuple-element.206), channel_id=1, source_target_pairs={{16,0},{24,8},{0,16},{8,24},{17,1},{25,9},{1,17},{9,25},{18,2},{26... | collective-permute-start | bytes 737288 | tf_op jit(solution)/shard_map/ppermute | solution.py:23
  654.8 38.4 %collective-permute-start.68 = (bf16[64,1920]{1,0:T(8,128)(2,1)S(1)}, bf16[64,1920]{1,0:T(8,128)(2,1)S(1)}, u32[]{:S(2)}, u32[]{:S(2)}) collective-permute-start(bf16[64,1920]{1,0:T(8,128)(2,1)S(1)} %get-tuple-element.204), channel_id=1, source_target_pairs={{8,0},{16,8},{24,16},{0,24},{9,1},{17,9},{25,17},{1,25},{10,2},{18... | collective-permute-start | bytes 737288 | tf_op jit(solution)/shard_map/ppermute | solution.py:23
  654.8 44.5 %collective-permute-start.91 = (bf16[64,3072]{1,0:T(8,128)(2,1)S(1)}, bf16[64,3072]{1,0:T(8,128)(2,1)S(1)}, u32[]{:S(2)}, u32[]{:S(2)}) collective-permute-start(bf16[64,3072]{1,0:T(8,128)(2,1)S(1)} %get-tuple-element.200), channel_id=1, source_target_pairs={{24,0},{0,8},{8,16},{16,24},{25,1},{1,9},{9,17},{17,25},{26,2},{2,... | collective-permute-start | bytes 1179656 | tf_op jit(solution)/shard_map/ppermute | solution.py:23
  656.4 47.9 %collective-permute-start.90 = (bf16[64,3072]{1,0:T(8,128)(2,1)S(1)}, bf16[64,3072]{1,0:T(8,128)(2,1)S(1)}, u32[]{:S(2)}, u32[]{:S(2)}) collective-permute-start(bf16[64,3072]{1,0:T(8,128)(2,1)S(1)} %get-tuple-element.201), channel_id=1, source_target_pairs={{16,0},{24,8},{0,16},{8,24},{17,1},{25,9},{1,17},{9,25},{18,2},{26... | collective-permute-start | bytes 1179656 | tf_op jit(solution)/shard_map/ppermute | solution.py:23
  658.2 51.9 %collective-permute-start.89 = (bf16[64,3072]{1,0:T(8,128)(2,1)S(1)}, bf16[64,3072]{1,0:T(8,128)(2,1)S(1)}, u32[]{:S(2)}, u32[]{:S(2)}) collective-permute-start(bf16[64,3072]{1,0:T(8,128)(2,1)S(1)} %get-tuple-element.199), channel_id=1, source_target_pairs={{8,0},{16,8},{24,16},{0,24},{9,1},{17,9},{25,17},{1,25},{10,2},{18... | collective-permute-start | bytes 1179656 | tf_op jit(solution)/shard_map/ppermute | solution.py:23
  696.2 15.5 %collective-permute-start.72 = (bf16[64,1920]{1,0:T(8,128)(2,1)S(1)}, bf16[64,1920]{1,0:T(8,128)(2,1)S(1)}, u32[]{:S(2)}, u32[]{:S(2)}) collective-permute-start(bf16[64,1920]{1,0:T(8,128)(2,1)S(1)} %pad_maximum_fusion.12), channel_id=1, source_target_pairs={{0,4},{2,6},{4,0},{6,2},{1,5},{3,7},{5,1},{7,3},{8,12},{10,14},{12... | collective-permute-start | bytes 737288 | tf_op jit(solution)/shard_map/ppermute | solution.py:18
  696.3 15.4 %collective-permute-start.73 = (bf16[64,1920]{1,0:T(8,128)(2,1)S(1)}, bf16[64,1920]{1,0:T(8,128)(2,1)S(1)}, u32[]{:S(2)}, u32[]{:S(2)}) collective-permute-start(bf16[64,1920]{1,0:T(8,128)(2,1)S(1)} %pad_maximum_fusion.12), channel_id=1, source_target_pairs={{0,2},{2,0},{4,6},{6,4},{1,3},{3,1},{5,7},{7,5},{8,10},{10,8},{12,... | collective-permute-start | bytes 737288 | tf_op jit(solution)/shard_map/ppermute | solution.py:18
  710.4 9.9 %collective-permute-start.92 = (bf16[64,3072]{1,0:T(8,128)(2,1)S(1)}, bf16[64,3072]{1,0:T(8,128)(2,1)}, u32[]{:S(2)}, u32[]{:S(2)}) collective-permute-start(bf16[64,3072]{1,0:T(8,128)(2,1)S(1)} %get-tuple-element.163), channel_id=1, source_target_pairs={{0,4},{2,6},{4,0},{6,2},{1,5},{3,7},{5,1},{7,3},{8,12},{10,14},{12... | collective-permute-start | bytes 1179656 | tf_op jit(solution)/shard_map/ppermute | solution.py:18
  710.5 12.6 %collective-permute-start.93 = (bf16[64,3072]{1,0:T(8,128)(2,1)S(1)}, bf16[64,3072]{1,0:T(8,128)(2,1)S(1)}, u32[]{:S(2)}, u32[]{:S(2)}) collective-permute-start(bf16[64,3072]{1,0:T(8,128)(2,1)S(1)} %get-tuple-element.163), channel_id=1, source_target_pairs={{0,2},{2,0},{4,6},{6,4},{1,3},{3,1},{5,7},{7,5},{8,10},{10,8},{12,... | collective-permute-start | bytes 1179656 | tf_op jit(solution)/shard_map/ppermute | solution.py:18
  711.7 11.5 %collective-permute-start.74 = (bf16[64,1920]{1,0:T(8,128)(2,1)S(1)}, bf16[64,1920]{1,0:T(8,128)(2,1)S(1)}, u32[]{:S(2)}, u32[]{:S(2)}) collective-permute-start(bf16[64,1920]{1,0:T(8,128)(2,1)S(1)} %collective-permute-done.72), channel_id=1, source_target_pairs={{0,2},{2,0},{4,6},{6,4},{1,3},{3,1},{5,7},{7,5},{8,10},{10,8},{12,... | collective-permute-start | bytes 737288 | tf_op jit(solution)/shard_map/ppermute | solution.py:18
  720.4 7.3 %collective-permute-start.94 = (bf16[64,3072]{1,0:T(8,128)(2,1)}, bf16[64,3072]{1,0:T(8,128)(2,1)}, u32[]{:S(2)}, u32[]{:S(2)}) collective-permute-start(bf16[64,3072]{1,0:T(8,128)(2,1)} %collective-permute-done.92), channel_id=1, source_target_pairs={{0,2},{2,0},{4,6},{6,4},{1,3},{3,1},{5,7},{7,5},{8,10},{10,8},{12,... | collective-permute-start | bytes 1179656 | tf_op jit(solution)/shard_map/ppermute | solution.py:18
  (204 other events, 1699.3 us)

commit v3 on v2

v3 whole, which is shorter than its diff:
```python
import jax
import jax.numpy as jnp
from jax import lax
from jax.experimental import pallas as pl
from jax.experimental.pallas import tpu as pltpu
from jax.sharding import PartitionSpec as P

HEAD_WIDTH = 64
EPSILON = 1e-06
LOW = jnp.bfloat16
F32 = jnp.float32
NEGATIVE = -1e30
PRECISE = lax.Precision.HIGHEST


def swap_context(x, bit):
    size = lax.axis_size("context")
    return lax.ppermute(x, "context", [(i, i ^ bit) for i in range(size)])


def from_next(x, axis, step=1):
    size = lax.axis_size(axis)
    return lax.ppermute(x, axis, [((i + step) % size, i) for i in range(size)])


def swap_tensor(x):
    size = lax.axis_size("tensor")
    return lax.ppermute(x, "tensor", [(i, (i + 1) % size) for i in range(size)])


def context_bits():
    size = lax.axis_size("context")
    return [1 << k for k in range(size.bit_length() - 1)]


def reverse_bits(index):
    bits = context_bits()
    return sum(((index // low) % 2) * high for low, high in zip(bits, reversed(bits)))


CHAIN = []
SCALE = 0.4e9


def anywhere(arrays):
    return [pl.BlockSpec(memory_space=pl.ANY)] * len(arrays)


def whole_spec(shape):
    return pl.BlockSpec(shape, lambda i: (0,) * len(shape))


def pair_spec(rows):
    return pl.BlockSpec((rows, 128), lambda i: (0, i))


SCALARS = pl.BlockSpec(memory_space=pltpu.SMEM)


def wait_for(*arrays):
    CHAIN.extend(arrays)


def launch(body, *, out_shape, in_specs, out_specs, name, us, grid=(1,), scratch_shapes=(), input_output_aliases=None):
    single = not isinstance(out_shape, tuple)
    outs = (out_shape,) if single else out_shape
    specs = [out_specs] if single else list(out_specs)

    def call(*args):
        waits = tuple(CHAIN)
        n_in, n_out = len(args), len(outs)
        at = n_in + len(waits)

        def run(*refs):
            body(*refs[:n_in], *refs[at : at + n_out], *refs[at + n_out + 1 :])

        made = pl.pallas_call(
            run,
            grid=grid,
            out_shape=outs + (jax.ShapeDtypeStruct((8, 128), F32),),
            in_specs=list(in_specs) + anywhere(waits),
            out_specs=specs + anywhere((0,)),
            scratch_shapes=list(scratch_shapes),
            input_output_aliases=input_output_aliases or {},
            compiler_params=pltpu.CompilerParams(vmem_limit_bytes=48 * 2**20),
            cost_estimate=pl.CostEstimate(flops=int(us * SCALE), bytes_accessed=1, transcendentals=0),
            name=name,
        )(*args, *waits)
        CHAIN[:] = made[-1:]
        return made[0] if single else made[:-1]

    return call


def column_block(cols):
    return next(blk for blk in (512, 256, 128) if cols % blk == 0)


def join(parts, axis_new):
    if axis_new:
        parts = [part[None] for part in parts]
    counts = [part.shape[0] for part in parts]
    shape = parts[0].shape[1:]
    cols = shape[-1]
    blk = column_block(cols)

    def spec(count):
        return pl.BlockSpec((count, *shape[:-1], blk), lambda j: (0,) * len(shape) + (j,))

    def body(*refs):
        at = 0
        for ref, count in zip(refs, counts):
            refs[-1][at : at + count] = ref[...]
            at += count

    return launch(
        body, grid=(cols // blk,), out_shape=jax.ShapeDtypeStruct((sum(counts), *shape), parts[0].dtype),
        in_specs=[spec(count) for count in counts], out_specs=spec(sum(counts)), name="join", us=2,
    )(*parts)


def send_near(own):
    return [from_next(own, "fsdp", k) for k in range(1, lax.axis_size("fsdp"))]


def far_bits():
    return list(reversed(context_bits()[1:]))


def spread_far(held):
    for bit in far_bits():
        held = join([held, swap_context(held, bit)], False)
    return held


def place_rows(place, shard, mine, other):
    nc, part, cols = shard.shape
    nf = lax.axis_size("fsdp")
    offsets = [reverse_bits(m) for m in range(nc)][: nc // 2]
    blk = column_block(cols)

    def body(place_ref, shard_ref, mine_ref, other_ref, out_ref):
        fi, ci = place_ref[0], place_ref[1]
        out_ref[fi] = shard_ref[...]
        for k in range(1, nf):
            z = lax.rem(fi + k, nf)
            for m, off in enumerate(offsets):
                at = m * (nf - 1) + k - 1
                out_ref[z, lax.bitwise_xor(ci, off)] = mine_ref[at]
                out_ref[z, lax.bitwise_xor(ci, off ^ 1)] = other_ref[at]

    def columns(*leading):
        return pl.BlockSpec((*leading, blk), lambda j: (0,) * len(leading) + (j,))

    count = mine.shape[0]
    full = launch(
        body,
        grid=(cols // blk,),
        out_shape=jax.ShapeDtypeStruct((nf, nc, part, cols), shard.dtype),
        in_specs=[SCALARS, columns(nc, part), columns(count, part), columns(count, part)],
        out_specs=columns(nf, nc, part),
        name="place_rows",
        us=cols / 600,
    )(place, shard, mine, other)
    return full.reshape(nf * nc * part, cols)


def place_blocks(place, mine, other):
    half, units, rows, cols = mine.shape
    nc = 2 * half
    offsets = [reverse_bits(m) for m in range(nc)][:half]

    def body(place_ref, mine_ref, other_ref, out_ref):
        ci = place_ref[1]
        for u in range(units):
            for m, off in enumerate(offsets):
                for ref, bit in ((mine_ref, 0), (other_ref, 1)):
                    at = pl.multiple_of(lax.bitwise_xor(ci, off ^ bit) * rows, rows)
                    out_ref[u, pl.ds(at, rows), :] = ref[m, u]

    return launch(
        body,
        out_shape=jax.ShapeDtypeStruct((units, nc * rows, cols), mine.dtype),
        in_specs=[SCALARS, whole_spec(mine.shape), whole_spec(other.shape)],
        out_specs=whole_spec((units, nc * rows, cols)),
        name="place_blocks",
        us=1,
    )(place, mine, other)


def at_offset(ref_pair, ci, k, nc):
    off = lax.bitwise_xor(ci, k)
    entry, weight, rest = 0, nc // 2, off
    half = lax.div(off, 2)
    width = nc // 2
    index, bit = 0, width // 2
    low = 1
    while bit:
        index = index + lax.rem(lax.div(half, low), 2) * bit
        bit, low = bit // 2, low * 2
    same = lax.rem(off, 2) == 0
    mine, other = ref_pair
    return index, same, mine, other


def chain_states(place, spans, state_dim, local=None, unit=None):
    half, units, height, width = spans[0].shape
    nc = 2 * half
    blk = column_block(width)
    count = units if local is None else 1
    extra = () if local is None else tuple(local)

    def body(place_ref, *refs):
        ci = place_ref[1]
        out_ref = refs[-1]
        for n in range(count):
            u = n if local is None else unit
            total = jnp.zeros((state_dim, blk), F32)
            for k in range(nc - 1) if local is None else range(nc - 1, 0, -1):
                index, same, mine, other = at_offset(refs[:2], ci, k, nc)
                passing = jnp.where(same, mine[index, u, state_dim:].astype(F32), other[index, u, state_dim:].astype(F32))
                if local is None:
                    term = jnp.where(same, mine[index, u, :state_dim].astype(F32), other[index, u, :state_dim].astype(F32))
                    active = k < ci
                else:
                    term = jnp.where(same, refs[2][index, 0].astype(F32), refs[3][index, 0].astype(F32))
                    active = k > ci
                new = (passing[0:1] + passing[1:2]) * total + term
                total = jnp.where(active, new, total)
            out_ref[n] = total.astype(LOW)

    def columns(shape):
        return pl.BlockSpec((*shape[:-1], blk), lambda j: (0,) * (len(shape) - 1) + (j,))

    out = (count, state_dim, width)
    return launch(
        body,
        grid=(width // blk,),
        out_shape=jax.ShapeDtypeStruct(out, LOW),
        in_specs=[SCALARS] + [columns(arr.shape) for arr in (*spans, *extra)],
        out_specs=columns(out),
        name="chain_states",
        us=1.2,
    )(place, *spans, *extra)


def outer(place, left, right, into, at, width):
    nf, nc = lax.axis_size("fsdp"), lax.axis_size("context")
    tokens, model = left.shape
    cols = right.shape[1]
    part = model // (nf * nc)
    blk = next(b for b in (512, 256, 128) if cols % b == 0 and at % b == 0)
    given = () if into is None else tuple(into)

    def body(place_ref, left_ref, right_ref, *rest):
        away_ref, keep_ref, turned, made = rest[-4:]

        @pl.when(pl.program_id(0) == 0)
        def _():
            turned[...] = left_ref[...].T

        made[...] = nn_dot(turned[...], right_ref[...])
        mine = lax.rem(place_ref[1], 2)
        for z in range(nf):
            for x in range(nc // 2):
                first = (z * nc + 2 * x) * part
                keep_ref[z, x] = made[pl.ds(pl.multiple_of(first + mine * part, part), part), :].astype(LOW)
                away_ref[z, x] = made[pl.ds(pl.multiple_of(first + (1 - mine) * part, part), part), :].astype(LOW)

    shape = jax.ShapeDtypeStruct((nf, nc // 2, part, width), LOW)
    spec = pl.BlockSpec((nf, nc // 2, part, blk), lambda j: (0, 0, 0, at // blk + j))
    return launch(
        body,
        grid=(cols // blk,),
        out_shape=(shape, shape),
        in_specs=[SCALARS, whole_spec((tokens, model)), pl.BlockSpec((tokens, blk), lambda j: (0, j))] + anywhere(given),
        out_specs=[spec, spec],
        input_output_aliases={3: 0, 4: 1} if given else {},
        scratch_shapes=[pltpu.VMEM((model, tokens), LOW), pltpu.VMEM((model, blk), F32)],
        name="outer",
        us=cols / 230,
    )(place, left, right, *given)


def split_sum(place, keep, got, bit):
    n, left, rows, cols = keep.shape
    blk = column_block(cols)

    def body(place_ref, keep_ref, got_ref, away_ref, stay_ref):
        mine = lax.rem(lax.div(place_ref[1], bit), 2)
        for z in range(n):
            for j in range(left // 2):
                for ref, b in ((stay_ref, mine), (away_ref, 1 - mine)):
                    i = 2 * j + b
                    ref[z, j] = (keep_ref[z, i].astype(F32) + got_ref[z, i].astype(F32)).astype(LOW)

    def spec(count):
        return pl.BlockSpec((n, count, rows, blk), lambda j: (0, 0, 0, j))

    shape = jax.ShapeDtypeStruct((n, left // 2, rows, cols), LOW)
    return launch(
        body, grid=(cols // blk,), out_shape=(shape, shape), in_specs=[SCALARS, spec(left), spec(left)],
        out_specs=[spec(left // 2)] * 2, name="split_sum", us=cols / 900,
    )(place, keep, got)


def split_fsdp(place, keep, got):
    nf, _, part, cols = keep.shape
    blk = column_block(cols)

    def body(place_ref, keep_ref, got_ref, *outs):
        for k in range(nf):
            z = lax.rem(place_ref[0] + (nf - k), nf)
            outs[k][...] = (keep_ref[z, 0].astype(F32) + got_ref[z, 0].astype(F32)).astype(LOW)

    spec = pl.BlockSpec((nf, 1, part, blk), lambda j: (0, 0, 0, j))
    return launch(
        body, grid=(cols // blk,), out_shape=(jax.ShapeDtypeStruct((part, cols), LOW),) * nf, in_specs=[SCALARS, spec, spec],
        out_specs=[pl.BlockSpec((part, blk), lambda j: (0, j))] * nf, name="split_fsdp", us=cols / 1200,
    )(place, keep, got)


def sum_parts(parts, shared=()):
    cols = parts[0].shape[1]
    blk = column_block(cols)

    def body(*refs):
        total = refs[0][...].astype(F32)
        for ref in refs[1:-1]:
            total = total + ref[...].astype(F32)
        refs[-1][...] = total.astype(LOW)

    spec = pl.BlockSpec((parts[0].shape[0], blk), lambda j: (0, j))
    total = launch(
        body, grid=(cols // blk,), out_shape=jax.ShapeDtypeStruct(parts[0].shape, LOW), in_specs=[spec] * len(parts),
        out_specs=spec, name="sum_parts", us=1.3,
    )(*parts)
    if shared:
        mid = total[:, shared[0] : shared[1]]
        mid = (mid.astype(F32) + swap_tensor(mid).astype(F32)).astype(LOW)
        total = jnp.concatenate([total[:, : shared[0]], mid, total[:, shared[1] :]], axis=1)
    return total


def share_rows(total):
    held = total[None]
    for bit in reversed(context_bits()):
        held = jnp.concatenate([held, swap_context(held, bit)])
    ci = lax.axis_index("context")
    order = [reverse_bits(k) ^ reverse_bits(ci) for k in range(lax.axis_size("context"))]
    rows = jnp.stack([lax.dynamic_index_in_dim(held, m, 0, keepdims=False) for m in order])
    return rows.astype(F32).reshape(-1, total.shape[1])


def reduce_far(place, keep, got, bits):
    for bit in bits:
        away, keep = split_sum(place, keep, got, bit)
        got = swap_context(away, bit)
    return keep, got


def all_sum(x):
    for bit in context_bits():
        x = x + swap_context(x, bit)
    size, bit = lax.axis_size("fsdp"), 1
    while bit < size:
        x = x + lax.ppermute(x, "fsdp", [(i, i ^ bit) for i in range(size)])
        bit *= 2
    return x


def tensor_sum(x):
    low = lax.reduce_precision(x, 8, 7).astype(LOW)
    return low.astype(F32) + swap_tensor(low).astype(F32)


def nt_dot(left, right):
    return lax.dot_general(left, right, (((1,), (1,)), ((), ())), preferred_element_type=F32)


def tn_dot(left, right):
    return lax.dot_general(left, right, (((0,), (0,)), ((), ())), preferred_element_type=F32)


def nn_dot(left, right):
    return jnp.dot(left, right, preferred_element_type=F32)


def document_start(lens_ref, unit, position):
    start, end = jnp.zeros_like(position), 0
    for d in range(lens_ref.shape[1]):
        end = end + lens_ref[unit, d]
        start = jnp.where(position >= end, end, start)
    return start


def lower_from(rows):
    u = lax.broadcasted_iota(jnp.int32, (rows, rows), 0)
    t = lax.broadcasted_iota(jnp.int32, (rows, rows), 1)
    return jnp.where(u <= t, 1.0, 0.0)


def project(place, lens, tokens, first, aux, q_dim, kv_dim, state, pairs):
    units = lens.shape[0]
    total, model = tokens.shape
    rows = total // units
    width = first.shape[1]
    at_b = q_dim + 2 * kv_dim
    at_dt = at_b + 2 * state

    def body(place_ref, lens_ref, x_ref, first_ref, aux_ref, n1_ref, q_ref, kv_ref, b_ref, c_ref, head_ref, gains_ref):
        unit = pl.program_id(0)

        @pl.when(unit == 0)
        def _():
            gains_ref[...] = first_ref[:, at_dt:].astype(F32).T[2 * pairs : 2 * pairs + 8]

        x = x_ref[...].astype(F32)
        scale = lax.rsqrt(jnp.mean(x * x, axis=1, keepdims=True) + EPSILON)
        n1_ref[...] = (x * scale * gains_ref[0:1, :]).astype(LOW)
        made = nn_dot(n1_ref[...], first_ref[...])
        q_ref[...] = (made[:, :q_dim].astype(LOW).astype(F32) * 0.125).astype(LOW)
        kv_ref[...] = made[:, q_dim:at_b].astype(LOW)
        b_ref[...] = made[:, at_b : at_b + state].astype(LOW)
        c_ref[...] = made[:, at_b + state : at_dt].astype(LOW)
        raw = made[:, at_dt:].T[:16] + aux_ref[:, 1:2]
        dt = jnp.maximum(raw, 0.0) + jnp.log1p(jnp.exp(-jnp.abs(raw)))
        decay = jnp.dot(-jnp.exp(aux_ref[:, 0:1]) * dt, lower_from(rows), precision=PRECISE, preferred_element_type=F32)
        base = place_ref[1] * rows
        position = base + lax.broadcasted_iota(jnp.int32, (1, rows), 1)
        carried = document_start(lens_ref, unit, position) < base
        closing = position >= document_start(lens_ref, unit, base + rows - 1)
        entering = jnp.where(carried, jnp.exp(decay), 0.0)
        leaving = jnp.where(closing, jnp.exp(decay[:, rows - 1 :] - decay), 0.0)
        for i in range(pairs):
            for at, value in enumerate((decay, dt, entering, leaving)):
                head_ref[i, 2 * at : 2 * at + 2, :] = value[2 * i : 2 * i + 2]

    def of_unit(cols):
        return pl.BlockSpec((rows, cols), lambda u: (u, 0))

    def made_as(cols):
        return jax.ShapeDtypeStruct((total, cols), LOW)

    return launch(
        body,
        grid=(units,),
        out_shape=(
            made_as(model), made_as(q_dim), made_as(2 * kv_dim), made_as(state), made_as(state),
            jax.ShapeDtypeStruct((units, pairs, 8, rows), F32), jax.ShapeDtypeStruct((8, model), F32),
        ),
        in_specs=[SCALARS, SCALARS, of_unit(model), whole_spec((model, width)), whole_spec((16, 2))],
        out_specs=[
            of_unit(model), of_unit(q_dim), of_unit(2 * kv_dim), of_unit(state), of_unit(state),
            pl.BlockSpec((None, pairs, 8, rows), lambda u: (u, 0, 0, 0)), whole_spec((8, model)),
        ],
        us=6.5, name="project",
    )(place, lens, tokens, first, aux)


def attention_forward(unit, place, lens, q, kv_all, into, width):
    units, length, _ = kv_all.shape
    rows, q_dim = q.shape[0] // units, q.shape[1]
    heads = q_dim // HEAD_WIDTH
    given = () if into is None else (into,)

    def body(place_ref, lens_ref, q_ref, kv_ref, *rest):
        o_ref, lse_ref, bias, top, low, acc = rest[-6:]
        top[...] = jnp.full_like(top, NEGATIVE)
        low[...] = jnp.zeros_like(low)
        acc[...] = jnp.zeros_like(acc)
        own = place_ref[1]
        base = own * rows
        start = document_start(lens_ref, unit, base + lax.broadcasted_iota(jnp.int32, (1, rows), 1))
        blocks = own - document_start(lens_ref, unit, base) // rows + 1

        def step(i, carry):
            j = own - i
            at = pl.multiple_of(j * rows, rows)
            keys = kv_ref[pl.ds(at, rows), :HEAD_WIDTH]
            turned = kv_ref[pl.ds(at, rows), :].astype(F32).T[HEAD_WIDTH:].astype(LOW)
            u = at + lax.broadcasted_iota(jnp.int32, (rows, rows), 0)
            t = base + lax.broadcasted_iota(jnp.int32, (rows, rows), 1)
            seen = (u <= t) & (u >= start)
            bias[...] = jnp.where(seen, 0.0, NEGATIVE)
            for h in range(heads):
                lanes = slice(h * HEAD_WIDTH, (h + 1) * HEAD_WIDTH)
                s = nt_dot(keys, q_ref[:, lanes]) + bias[...]
                before = top[h : h + 1, :]
                now = jnp.maximum(before, jnp.max(s, axis=0, keepdims=True))
                p = jnp.exp(s - now)
                scale = jnp.exp(before - now)
                top[h : h + 1, :] = now
                low[h : h + 1, :] = low[h : h + 1, :] * scale + jnp.sum(p, axis=0, keepdims=True)
                acc[lanes, :] = acc[lanes, :] * scale + nn_dot(turned, p.astype(LOW))
            return carry

        lax.fori_loop(0, blocks, step, 0)
        for h in range(heads):
            lanes = slice(h * HEAD_WIDTH, (h + 1) * HEAD_WIDTH)
            acc[lanes, :] = acc[lanes, :] / low[h : h + 1, :]
        o_ref[...] = acc[...].T.astype(LOW)
        lse_ref[...] = top[...] + jnp.log(low[...])

    return launch(
        body,
        grid=(1,),
        out_shape=(jax.ShapeDtypeStruct((units * rows, width), LOW), jax.ShapeDtypeStruct((8, rows), F32)),
        in_specs=[
            SCALARS, SCALARS, pl.BlockSpec((rows, q_dim), lambda i: (unit, 0)),
            pl.BlockSpec((None, length, 2 * HEAD_WIDTH), lambda i: (unit, 0, 0)),
        ] + anywhere(given),
        out_specs=[pl.BlockSpec((rows, q_dim), lambda i: (unit, 0)), whole_spec((8, rows))],
        input_output_aliases={4: 0} if given else {},
        scratch_shapes=[
            pltpu.VMEM((rows, rows), F32),
            pltpu.VMEM((8, rows), F32),
            pltpu.VMEM((8, rows), F32),
            pltpu.VMEM((q_dim, rows), F32),
        ],
        us=10.5, name="attention_forward",
    )(place, lens, q, kv_all, *given)


def attention_backward(unit, place, lens, q, dog, og, kv_all, lse):
    units, length, _ = kv_all.shape
    rows, q_dim = q.shape[0] // units, q.shape[1]
    heads = q_dim // HEAD_WIDTH
    half = (1, length // rows // 2, rows, 2 * HEAD_WIDTH)
    sub = min(256, rows)

    def body(place_ref, lens_ref, q_ref, do_ref, o_ref, kv_ref, lse_ref, *rest):
        dq_ref, away_ref, keep_ref, bias, dq_acc, delta = rest[-6:]
        own = place_ref[1]
        base = own * rows
        start = document_start(lens_ref, unit, base + lax.broadcasted_iota(jnp.int32, (1, rows), 1))
        blocks = own - document_start(lens_ref, unit, base) // rows + 1
        dq_acc[...] = jnp.zeros_like(dq_acc)
        away_ref[...] = jnp.zeros_like(away_ref)
        keep_ref[...] = jnp.zeros_like(keep_ref)
        both = do_ref[...].astype(F32) * o_ref[...].astype(F32)
        lane = lax.broadcasted_iota(jnp.int32, (rows, 128), 1)
        columns = jnp.zeros((rows, 128), F32)
        for h in range(heads):
            total = jnp.sum(both[:, h * HEAD_WIDTH : (h + 1) * HEAD_WIDTH], axis=1, keepdims=True)
            columns = jnp.where(lane == h, total, columns)
        delta[...] = columns.T[:8]

        def step(i, carry):
            j = own - i
            at = pl.multiple_of(j * rows, rows)
            u = at + lax.broadcasted_iota(jnp.int32, (rows, rows), 0)
            t = base + lax.broadcasted_iota(jnp.int32, (rows, rows), 1)
            seen = (u <= t) & (u >= start)
            bias[...] = jnp.where(seen, 0.0, NEGATIVE)
            for r in range(0, rows, sub):
                keys = kv_ref[pl.ds(pl.multiple_of(at + r, sub), sub), :HEAD_WIDTH]
                values = kv_ref[pl.ds(pl.multiple_of(at + r, sub), sub), HEAD_WIDTH:]
                dk = jnp.zeros((sub, HEAD_WIDTH), F32)
                dv = jnp.zeros((sub, HEAD_WIDTH), F32)
                for h in range(heads):
                    lanes = slice(h * HEAD_WIDTH, (h + 1) * HEAD_WIDTH)
                    q_h, do_h = q_ref[:, lanes], do_ref[:, lanes]
                    p = jnp.exp(nt_dot(keys, q_h) + (bias[r : r + sub, :] - lse_ref[h : h + 1, :]))
                    ds = (p * (nt_dot(values, do_h) - delta[h : h + 1, :])).astype(LOW)
                    dv = dv + nn_dot(p.astype(LOW), do_h)
                    dk = dk + nn_dot(ds, q_h)
                    dq_acc[:, lanes] = dq_acc[:, lanes] + tn_dot(ds, keys)
                dkv = jnp.concatenate([dk, dv], axis=1).astype(LOW)

                @pl.when(lax.rem(own - j, 2) == 0)
                def _():
                    keep_ref[0, j // 2, r : r + sub, :] = dkv

                @pl.when(lax.rem(own - j, 2) == 1)
                def _():
                    away_ref[0, j // 2, r : r + sub, :] = dkv
            return carry

        lax.fori_loop(0, blocks, step, 0)
        dq_ref[...] = (dq_acc[...] * 0.125).astype(LOW)

    return launch(
        body,
        out_shape=(jax.ShapeDtypeStruct((rows, q_dim), LOW),) + (jax.ShapeDtypeStruct(half, LOW),) * 2,
        grid=(1,),
        in_specs=[
            SCALARS, SCALARS, pl.BlockSpec((rows, q_dim), lambda i: (unit, 0)), whole_spec((rows, q_dim)),
            pl.BlockSpec((rows, q_dim), lambda i: (unit, 0)), pl.BlockSpec((None, length, 2 * HEAD_WIDTH), lambda i: (unit, 0, 0)),
            whole_spec((8, rows)),
        ],
        out_specs=[whole_spec((rows, q_dim)), whole_spec(half), whole_spec(half)],
        scratch_shapes=[
            pltpu.VMEM((rows, rows), F32),
            pltpu.VMEM((rows, q_dim), F32),
            pltpu.VMEM((8, rows), F32),
        ],
        us=17, name="attention_backward",
    )(place, lens, q, dog, og, kv_all, lse)


def halves(columns, first, lane):
    return jnp.where(lane < 64, columns[:, first : first + 1], columns[:, first + 1 : first + 2])


def mamba_state(unit, per_head, left, zx, right=None, first=0):
    _, pairs, _, rows = per_head.shape
    state = left.shape[1]
    rights = () if right is None else (right,)
    height = state if rights else state + 16

    def body(head_ref, left_ref, zx_ref, *rest):
        out_ref = rest[-1]
        lane = lax.broadcasted_iota(jnp.int32, (rows, 128), 1)
        turned = left_ref[...].astype(F32).T.astype(LOW)
        for i in range(pairs):
            lanes = slice(128 * i, 128 * (i + 1))
            by_col = head_ref[i].T
            if rights:
                z = zx_ref[:, 256 * i : 256 * i + 128].astype(F32)
                value = rest[0][:, first + 128 * i : first + 128 * (i + 1)].astype(F32) * z * jax.nn.sigmoid(z)
                weight = halves(by_col, 4, lane)
            else:
                value = zx_ref[:, 256 * i + 128 : 256 * (i + 1)].astype(F32)
                weight = halves(by_col, 2, lane) * halves(by_col, 6, lane)
                passing = halves(by_col[rows - 16 :], 4, lane[:16])[15:]
                high = passing.astype(LOW).astype(F32)
                row = lax.broadcasted_iota(jnp.int32, (16, 128), 0)
                out_ref[state:, lanes] = jnp.where(row == 0, high, jnp.where(row == 1, passing - high, 0.0)).astype(LOW)
            out_ref[:state, lanes] = nn_dot(turned, (value * weight).astype(LOW)).astype(LOW)

    return launch(
        body,
        grid=(1,),
        out_shape=jax.ShapeDtypeStruct((height, 128 * pairs), LOW),
        in_specs=[
            pl.BlockSpec((None, pairs, 8, rows), lambda i: (unit, 0, 0, 0)), pl.BlockSpec((rows, state), lambda i: (unit, 0)),
            pl.BlockSpec((rows, 256 * pairs), lambda i: (unit, 0)),
        ] + [whole_spec(r.shape) for r in rights],
        out_specs=whole_spec((height, 128 * pairs)),
        us=2, name="mamba_state",
    )(per_head, left, zx, *rights)


def same_document(place_ref, lens_ref, unit, rows, t_axis):
    base = place_ref[1] * rows
    shape = (1, rows) if t_axis else (rows, 1)
    start = document_start(lens_ref, unit, base + lax.broadcasted_iota(jnp.int32, shape, t_axis)) - base
    t = lax.broadcasted_iota(jnp.int32, (rows, rows), t_axis)
    u = lax.broadcasted_iota(jnp.int32, (rows, rows), 1 - t_axis)
    return (u <= t) & (u >= start)


def mamba_forward(unit, place, lens, per_head, zx, b, c, state_in, skip, into, first):
    _, pairs, _, rows = per_head.shape
    blk = min(256, rows)
    state = b.shape[1]

    def body(place_ref, lens_ref, head_ref, zx_ref, b_ref, c_ref, state_ref, skip_ref, *rest):
        g_ref, y_ref, inner, x_dt = rest[-4:]

        @pl.when(pl.program_id(0) == 0)
        def _():
            seen = same_document(place_ref, lens_ref, unit, rows, 0)
            inner[...] = jnp.where(seen, nt_dot(c_ref[...], b_ref[...]), 0.0)

        lane = lax.broadcasted_iota(jnp.int32, (rows, 128), 1)
        by_row = head_ref[...]
        by_col = by_row.T
        xs_f = zx_ref[:, 128:].astype(F32)
        x_dt[...] = (xs_f * halves(by_col, 2, lane)).astype(LOW)
        read = nn_dot(c_ref[...], state_ref[...]) * halves(by_col, 4, lane)
        for i in range(rows // blk):
            part = slice(i * blk, (i + 1) * blk)
            sums = []
            for h in range(2):
                total = None
                for j in range(i + 1):
                    other = slice(j * blk, (j + 1) * blk)
                    gap = by_col[part, h : h + 1] - by_row[h : h + 1, other]
                    kernel = jnp.exp(jnp.minimum(gap, 0.0)) * inner[part, other]
                    term = nn_dot(kernel.astype(LOW), x_dt[other, :])
                    total = term if total is None else total + term
                sums.append(total)
            y = jnp.where(lane[part] < 64, sums[0], sums[1]) + read[part]
            y_ref[part, :] = y
            z_f = zx_ref[part, :128].astype(F32)
            g_ref[part, :] = ((y + skip_ref[...] * xs_f[part]) * z_f * jax.nn.sigmoid(z_f)).astype(LOW)

    return launch(
        body,
        grid=(pairs,),
        out_shape=(jax.ShapeDtypeStruct(into.shape, LOW), jax.ShapeDtypeStruct((rows, 128 * pairs), F32)),
        in_specs=[
            SCALARS, SCALARS, pl.BlockSpec((None, None, 8, rows), lambda i: (unit, i, 0, 0)), pl.BlockSpec((rows, 256), lambda i: (unit, i)),
            pl.BlockSpec((rows, state), lambda i: (unit, 0)), pl.BlockSpec((rows, state), lambda i: (unit, 0)),
            pl.BlockSpec((None, state, 128), lambda i: (unit, 0, i)), pair_spec(1),
        ] + anywhere((into,)),
        out_specs=[pl.BlockSpec((rows, 128), lambda i: (unit, first // 128 + i)), pair_spec(rows)],
        input_output_aliases={8: 0},
        scratch_shapes=[pltpu.VMEM((rows, rows), F32), pltpu.VMEM((rows, 128), LOW)],
        us=7.5, name="mamba_forward",
    )(place, lens, per_head, zx, b, c, state_in, skip, into)


def mamba_backward(unit, place, lens, per_head, zx, y, dog, first, b, c, state_in, later, skip, aux, into):
    _, pairs, _, rows = per_head.shape
    blk = min(256, rows)
    state = b.shape[1]
    given = () if into is None else tuple(into)

    def body(place_ref, lens_ref, head_ref, zx_ref, y_ref, dg_ref, b_ref, c_ref, state_ref, later_ref, skip_ref, aux_ref, *rest):
        dzx_ref, dbc_ref, grads_ref, inner, d_inner, dy_low, x_low, db, dc, stats = rest[-10:]
        pair = pl.program_id(0)

        @pl.when(pair == 0)
        def _():
            seen = same_document(place_ref, lens_ref, unit, rows, 1)
            inner[...] = jnp.where(seen, nt_dot(b_ref[...], c_ref[...]), 0.0)
            d_inner[...] = jnp.zeros_like(d_inner)
            db[...] = jnp.zeros_like(db)
            dc[...] = jnp.zeros_like(dc)

        lane = lax.broadcasted_iota(jnp.int32, (rows, 128), 1)
        by_row = head_ref[pair]
        by_col = by_row.T
        xs_f = zx_ref[:, 128:].astype(F32)
        z_f = zx_ref[:, :128].astype(F32)
        sig = jax.nn.sigmoid(z_f)
        d_gate = dg_ref[...].astype(F32)
        d_y = d_gate * z_f * sig
        y_core = y_ref[...]
        dzx_ref[:, :128] = (d_gate * (y_core + skip_ref[...] * xs_f) * sig * (1.0 + z_f * (1.0 - sig))).astype(LOW)
        dy_low[...] = d_y.astype(LOW)
        dt = halves(by_col, 2, lane)
        x_dt = xs_f * dt
        x_low[...] = x_dt.astype(LOW)
        closing = halves(by_col, 6, lane)
        from_later = nn_dot(b_ref[...], later_ref[...]) * closing
        db[...] += nt_dot((x_dt * closing).astype(LOW), later_ref[...])
        dc[...] += nt_dot((d_y * halves(by_col, 4, lane)).astype(LOW), state_ref[...])
        count = rows // blk
        columns = jnp.zeros((rows, 128), F32)
        d_x_parts = []
        for j in range(count):
            part = slice(j * blk, (j + 1) * blk)
            sums = []
            for h in range(2):
                own = (lane[part] < 64) if h == 0 else (lane[part] >= 64)
                x_h = jnp.where(own, x_low[part, :].astype(F32), 0.0).astype(LOW)
                total = None
                for i in range(j, count):
                    other = slice(i * blk, (i + 1) * blk)
                    gap = by_row[h : h + 1, other] - by_col[part, h : h + 1]
                    decay = jnp.exp(jnp.minimum(gap, 0.0))
                    term = nn_dot((decay * inner[part, other]).astype(LOW), dy_low[other, :])
                    total = term if total is None else total + term
                    d_inner[part, other] += decay * nt_dot(x_h, dy_low[other, :])
                sums.append(total)
            d_x_parts.append(jnp.where(lane[part] < 64, sums[0], sums[1]))
        d_x = jnp.concatenate(d_x_parts, axis=0) if count > 1 else d_x_parts[0]
        d_x = d_x + from_later
        dzx_ref[:, 128:] = (d_x * dt + skip_ref[...] * d_y).astype(LOW)
        rounded_x = x_low[...].astype(F32)
        rounded_dy = dy_low[...].astype(F32)
        carried_back = jnp.sum(later_ref[...].astype(F32) * state_ref[...].astype(F32), axis=0, keepdims=True)
        row = lax.broadcasted_iota(jnp.int32, (rows, 1), 0)
        for at, value in enumerate((d_x * xs_f, rounded_dy * y_core - rounded_x * d_x, rounded_x * from_later, d_y * xs_f)):
            for h in range(2):
                own = (lane < 64) if h == 0 else (lane >= 64)
                total = jnp.sum(jnp.where(own, value, 0.0), axis=1, keepdims=True)
                if at == 2:
                    own = (lane[:1] < 64) if h == 0 else (lane[:1] >= 64)
                    passed = jnp.sum(jnp.where(own, carried_back, 0.0), axis=1, keepdims=True)
                    total = total + jnp.where(row == rows - 1, passed * by_row[4 + h : 5 + h, rows - 1 :], 0.0)
                columns = jnp.where(lane == 2 * at + h, total, columns)
        stats[pair] = columns.T[:8]

        @pl.when(pair == pairs - 1)
        def _():
            seen = same_document(place_ref, lens_ref, unit, rows, 1)
            low = jnp.where(seen, d_inner[...], 0.0).astype(LOW)
            dbc_ref[:, :state] = (db[...] + nn_dot(low, c_ref[...])).astype(LOW)
            dbc_ref[:, state : 2 * state] = (dc[...] + tn_dot(low, b_ref[...])).astype(LOW)

            def heads_of(ref, at):
                blank = jnp.zeros((16 - 2 * pairs, rows), F32)
                parts = [ref[i, 2 * at : 2 * at + 2, :] for i in range(pairs)]
                return jnp.concatenate(parts + [blank] * (2 * pairs < 16), axis=0)

            dt = heads_of(head_ref, 1)
            rate = -jnp.exp(aux_ref[:, 0:1])
            position = lax.broadcasted_iota(jnp.int32, (1, rows), 1)
            d_end = jnp.sum(heads_of(stats, 2), axis=1, keepdims=True)
            d_decay = heads_of(stats, 1) + jnp.where(position == rows - 1, d_end, 0.0)
            d_rate = lax.dot_general(
                d_decay, lower_from(rows), (((1,), (1,)), ((), ())), precision=PRECISE, preferred_element_type=F32)
            d_raw = (heads_of(stats, 0) + rate * d_rate) * (1.0 - jnp.exp(-dt))
            turned = jnp.concatenate([d_raw, jnp.zeros((112, rows), F32)], axis=0).T
            dbc_ref[:, 2 * state : 2 * state + 128] = turned.astype(LOW)
            dbc_ref[:, 2 * state + 128 :] = jnp.zeros((rows, 128), LOW)
            lanes = lax.broadcasted_iota(jnp.int32, (16, 128), 1)
            sums = jnp.zeros((16, 128), F32)
            for at, value in enumerate((d_rate * rate * dt, d_raw, heads_of(stats, 3))):
                sums = jnp.where(lanes == at, jnp.sum(value, axis=1, keepdims=True), sums)
            grads_ref[...] = sums

    total = zx.shape[0]
    return launch(
        body,
        grid=(pairs,),
        out_shape=(
            jax.ShapeDtypeStruct(zx.shape, LOW), jax.ShapeDtypeStruct((total, 2 * state + 256), LOW),
            jax.ShapeDtypeStruct((16, 128), F32),
        ),
        in_specs=[
            SCALARS, SCALARS, pl.BlockSpec((None, pairs, 8, rows), lambda i: (unit, 0, 0, 0)),
            pl.BlockSpec((rows, 256), lambda i: (unit, i)), pair_spec(rows),
            pl.BlockSpec((rows, 128), lambda i: (0, first // 128 + i)),
            pl.BlockSpec((rows, state), lambda i: (unit, 0)), pl.BlockSpec((rows, state), lambda i: (unit, 0)),
            pl.BlockSpec((None, state, 128), lambda i: (unit, 0, i)), pair_spec(state), pair_spec(1), whole_spec((16, 2)),
        ] + anywhere(given),
        out_specs=[
            pl.BlockSpec((rows, 256), lambda i: (unit, i)), pl.BlockSpec((rows, 2 * state + 256), lambda i: (unit, 0)),
            whole_spec((16, 128)),
        ],
        input_output_aliases={12: 0, 13: 1} if given else {},
        scratch_shapes=[
            pltpu.VMEM((rows, rows), F32), pltpu.VMEM((rows, rows), F32), pltpu.VMEM((rows, 128), LOW), pltpu.VMEM((rows, 128), LOW),
            pltpu.VMEM((rows, state), F32), pltpu.VMEM((rows, state), F32), pltpu.VMEM((pairs, 8, rows), F32),
        ],
        us=16.3, name="mamba_backward",
    )(place, lens, per_head, zx, y, dog, b, c, state_in, later, skip, aux, *given)


def feed_forward(unit, x, ours, theirs, gains, dy, weights, into):
    rows, model = ours.shape
    total = x.shape[0]
    hidden = weights.shape[1] // 3
    blk = min(256, hidden)
    count = hidden // blk
    given = () if into is None else tuple(into)

    def body(x_ref, ours_ref, theirs_ref, gains_ref, dy_ref, ab_ref, down_ref, *rest):
        h1_ref, n2_ref, f_ref, dab_ref, dn2_ref, dn2_acc = rest[-6:]

        @pl.when(pl.program_id(0) == 0)
        def _():
            h1 = x_ref[...].astype(F32) + (ours_ref[...].astype(F32) + theirs_ref[...].astype(F32))
            scale = lax.rsqrt(jnp.mean(h1 * h1, axis=1, keepdims=True) + EPSILON)
            h1_ref[...] = h1
            n2_ref[...] = (h1 * scale * gains_ref[1:2, :]).astype(LOW)

        ab = nn_dot(n2_ref[...], ab_ref[...])
        a, b = ab[:, :blk], ab[:, blk:]
        sig = jax.nn.sigmoid(a)
        silu = a * sig
        f = (silu * b).astype(LOW)
        f_ref[...] = f
        df = nn_dot(dy_ref[...], down_ref[...])
        dab_ref[:, :blk] = (df * b * sig * (1.0 + a * (1.0 - sig))).astype(LOW)
        dab_ref[:, blk:] = (df * silu).astype(LOW)
        dn2 = nt_dot(dab_ref[...], ab_ref[...])

        @pl.when(pl.program_id(0) == 0)
        def _():
            dn2_acc[...] = dn2

        @pl.when(pl.program_id(0) > 0)
        def _():
            dn2_acc[...] += dn2

        @pl.when(pl.program_id(0) == count - 1)
        def _():
            dn2_ref[...] = dn2_acc[...].astype(LOW)

    at_unit = pl.BlockSpec((rows, model), lambda j: (unit, 0))
    return launch(
        body,
        grid=(count,),
        out_shape=(
            jax.ShapeDtypeStruct((total, model), F32), jax.ShapeDtypeStruct((total, model), LOW),
            jax.ShapeDtypeStruct((total, hidden), LOW), jax.ShapeDtypeStruct((total, 2 * hidden), LOW),
            jax.ShapeDtypeStruct((rows, model), LOW),
        ),
        in_specs=[
            at_unit, whole_spec((rows, model)), whole_spec((rows, model)), whole_spec((8, model)), at_unit,
            pl.BlockSpec((model, 2 * blk), lambda j: (0, j)), pl.BlockSpec((model, blk), lambda j: (0, 2 * count + j)),
        ] + anywhere(given),
        out_specs=[
            at_unit, at_unit, pl.BlockSpec((rows, blk), lambda j: (unit, j)), pl.BlockSpec((rows, 2 * blk), lambda j: (unit, j)),
            whole_spec((rows, model)),
        ],
        input_output_aliases={7: 0, 8: 1, 9: 2, 10: 3} if given else {},
        scratch_shapes=[pltpu.VMEM((rows, model), F32)],
        us=14, name="feed_forward",
    )(x, ours, theirs, gains, dy, weights, weights, *given)


def feed_forward_out(f, weights):
    total, hidden = f.shape
    model = weights.shape[0]
    blk = min(512, total)

    def body(f_ref, down_ref, *rest):
        rest[-1][...] = nt_dot(f_ref[...], down_ref[...]).astype(LOW)

    return launch(
        body,
        grid=(total // blk,),
        out_shape=jax.ShapeDtypeStruct((total, model), LOW),
        in_specs=[pl.BlockSpec((blk, hidden), lambda i: (i, 0)), pl.BlockSpec((model, hidden), lambda i: (0, 2))],
        out_specs=pl.BlockSpec((blk, model), lambda i: (i, 0)),
        us=5, name="feed_forward_out",
    )(f, weights)


def norm_gradient(hidden, gain, d_normed):
    inv = lax.rsqrt(jnp.mean(hidden * hidden, axis=1, keepdims=True) + EPSILON)
    weighted = gain * d_normed
    mean = jnp.mean(weighted * hidden, axis=1, keepdims=True)
    normed = hidden * inv
    return inv * weighted - normed * (inv * inv * mean), jnp.sum(d_normed * normed, axis=0, keepdims=True)


def middle_backward(unit, h1, ours, theirs, gains, dy, third, into):
    rows, model = ours.shape
    width = third.shape[1]
    given = () if into is None else (into,)

    def body(h1_ref, ours_ref, theirs_ref, gains_ref, dy_ref, third_ref, *rest):
        dm_ref, dh_ref, dog_ref, sum_ref = rest[-4:]
        dn2 = ours_ref[...].astype(F32) + theirs_ref[...].astype(F32)
        dh, terms = norm_gradient(h1_ref[...], gains_ref[1:2, :], dn2)
        dh = dh + dy_ref[...].astype(F32)
        dh_ref[...] = dh
        dm = dh.astype(LOW)
        dm_ref[...] = dm
        dog_ref[...] = nn_dot(dm, third_ref[...]).astype(LOW)
        sum_ref[...] = jnp.broadcast_to(terms, sum_ref.shape)

    at_unit = pl.BlockSpec((rows, model), lambda i: (unit, 0))
    full = whole_spec((rows, model))
    return launch(
        body,
        grid=(1,),
        out_shape=(
            jax.ShapeDtypeStruct(h1.shape, LOW), jax.ShapeDtypeStruct((rows, model), F32),
            jax.ShapeDtypeStruct((rows, width), LOW), jax.ShapeDtypeStruct((8, model), F32),
        ),
        in_specs=[at_unit, full, full, whole_spec((8, model)), at_unit, whole_spec((model, width))] + anywhere(given),
        out_specs=[at_unit, full, whole_spec((rows, width)), whole_spec((8, model))],
        input_output_aliases={6: 0} if given else {},
        us=5.4, name="middle_backward",
    )(h1, ours, theirs, gains, dy, third, *given)


def input_backward(unit, dq, keep, got, dbc, dzx, first, second, x, into):
    rows, q_dim = dq.shape
    model = first.shape[0]
    blk = 256 if model % 256 == 0 else model
    rest_width = dbc.shape[1]
    width = q_dim + keep.shape[-1]
    rest = first.shape[1] - width
    given = () if into is None else (into,)

    def body(dq_ref, keep_ref, got_ref, dbc_ref, dzx_ref, first_ref, second_ref, x_ref, *others):
        dqkv_ref, part_ref, sum_ref, inv = others[-4:]
        j = pl.program_id(0)

        @pl.when(j == 0)
        def _():
            x = x_ref[...].astype(F32)
            scale = lax.rsqrt(jnp.mean(x * x, axis=1, keepdims=True) + EPSILON)
            inv[...] = jnp.broadcast_to(scale, inv.shape)
            dqkv_ref[:, :q_dim] = dq_ref[...]
            dqkv_ref[:, q_dim:] = (keep_ref[0, 0].astype(F32) + got_ref[0, 0].astype(F32)).astype(LOW)

        part = nt_dot(dqkv_ref[...], first_ref[:, :width]) + nt_dot(dbc_ref[:, :rest], first_ref[:, width:])
        part = part + nt_dot(dzx_ref[...], second_ref[...])
        part_ref[...] = part.astype(LOW)
        x = x_ref[:, pl.ds(pl.multiple_of(j * blk, blk), blk)].astype(F32)
        terms = jnp.sum(part * x * inv[:, :1], axis=0, keepdims=True)
        sum_ref[...] = jnp.broadcast_to(terms, sum_ref.shape)

    return launch(
        body,
        grid=(model // blk,),
        out_shape=(
            jax.ShapeDtypeStruct((x.shape[0], width), LOW), jax.ShapeDtypeStruct((rows, model), LOW), jax.ShapeDtypeStruct((8, model), F32),
        ),
        in_specs=[
            whole_spec((rows, q_dim)), whole_spec(keep.shape), whole_spec(keep.shape), pl.BlockSpec((rows, rest_width), lambda j: (unit, 0)),
            pl.BlockSpec((rows, dzx.shape[1]), lambda j: (unit, 0)), pl.BlockSpec((blk, first.shape[1]), lambda j: (j, 0)),
            pl.BlockSpec((blk, second.shape[1]), lambda j: (j, 0)), pl.BlockSpec((rows, model), lambda j: (unit, 0)),
        ] + anywhere(given),
        out_specs=[
            pl.BlockSpec((rows, width), lambda j: (unit, 0)), pl.BlockSpec((rows, blk), lambda j: (0, j)),
            pl.BlockSpec((8, blk), lambda j: (0, j)),
        ],
        input_output_aliases={8: 0} if given else {},
        scratch_shapes=[pltpu.VMEM((rows, 128), F32)],
        us=6.5, name="input_backward",
    )(dq, keep, got, dbc, dzx, first, second, x, *given)


def finish(unit, x, ours, theirs, gains, dh, into):
    rows, model = ours.shape
    given = () if into is None else (into,)

    def body(x_ref, ours_ref, theirs_ref, gains_ref, dh_ref, *rest):
        dn1 = ours_ref[...].astype(F32) + theirs_ref[...].astype(F32)
        dx, _ = norm_gradient(x_ref[...].astype(F32), gains_ref[0:1, :], dn1)
        rest[-1][...] = dx + dh_ref[...]

    at_unit = pl.BlockSpec((rows, model), lambda i: (unit, 0))
    full = whole_spec((rows, model))
    return launch(
        body,
        grid=(1,),
        out_shape=jax.ShapeDtypeStruct(x.shape, F32),
        in_specs=[at_unit, full, full, whole_spec((8, model)), full] + anywhere(given),
        out_specs=at_unit,
        input_output_aliases={5: 0} if given else {},
        us=4.2, name="finish",
    )(x, ours, theirs, gains, dh, *given)


def pack(place, parts, cols, name):
    arrays = []
    for arr, *_ in parts:
        if not any(arr is other for other in arrays):
            arrays.append(arr)
    where = [next(i for i, other in enumerate(arrays) if other is part[0]) for part in parts]
    nc = lax.axis_size("context")
    rows = arrays[0].shape[1] if parts[0][4] else arrays[0].shape[0]
    filled = max(part[1] + part[2] for part in parts)

    def body(place_ref, *refs):
        out_ref, own_ref = refs[-2:]
        if filled < cols:
            start = filled - filled % 128
            out_ref[:, start:] = jnp.zeros((rows, cols - start), LOW)
        for n, (_, at, width, first, turned) in zip(where, parts):
            if turned:
                out_ref[:, at : at + width] = refs[n][...].T
            else:
                out_ref[:, at : at + width] = refs[n][:, first : first + width]
        own_ref[...] = out_ref[pl.ds(pl.multiple_of(place_ref[1] * (rows // nc), rows // nc), rows // nc), :]

    return launch(
        body, out_shape=(jax.ShapeDtypeStruct((rows, cols), LOW), jax.ShapeDtypeStruct((rows // nc, cols), LOW)),
        in_specs=[SCALARS] + [whole_spec(arr.shape) for arr in arrays],
        out_specs=[whole_spec((rows, cols)), whole_spec((rows // nc, cols))], name=name, us=2,
    )(place, *arrays)


def emit(place, held, got, outs, name):
    half, part, cols = held.shape
    nc = 2 * half
    rows = nc * part
    offsets = [reverse_bits(m) for m in range(nc)][:half]
    widths = [sum(width for _, width in pieces) for pieces, _ in outs]

    def body(place_ref, held_ref, got_ref, *refs):
        whole = refs[-1]
        ci = place_ref[1]
        for m, off in enumerate(offsets):
            for ref, bit in ((held_ref, 0), (got_ref, 1)):
                at = pl.multiple_of(lax.bitwise_xor(ci, off ^ bit) * part, part)
                whole[pl.ds(at, part), :] = ref[m].astype(F32)
        for ref, (pieces, turned) in zip(refs, outs):
            to = 0
            for first, width in pieces:
                if turned:
                    ref[to : to + width, :] = whole[:, first : first + width].T
                else:
                    ref[:, to : to + width] = whole[:, first : first + width]
                to += width

    shapes = [(width, rows) if turned else (rows, width) for width, (_, turned) in zip(widths, outs)]
    return launch(
        body, out_shape=tuple(jax.ShapeDtypeStruct(shape, F32) for shape in shapes),
        in_specs=[SCALARS, whole_spec(held.shape), whole_spec(held.shape)], out_specs=[whole_spec(shape) for shape in shapes],
        scratch_shapes=[pltpu.VMEM((rows, cols), F32)], name=name, us=3,
    )(place, held, got)


def close_forward(h1, ours, theirs):
    total, model = h1.shape
    blk = min(256, total)

    def body(h1_ref, ours_ref, theirs_ref, out_ref):
        out_ref[...] = (h1_ref[...] + (ours_ref[...].astype(F32) + theirs_ref[...].astype(F32))).astype(LOW)

    spec = pl.BlockSpec((blk, model), lambda i: (i, 0))
    return launch(
        body, grid=(total // blk,), out_shape=jax.ShapeDtypeStruct((total, model), LOW), in_specs=[spec] * 3, out_specs=spec,
        name="close_forward", us=4,
    )(h1, ours, theirs)


def project_mixer(n1, second):
    tokens, model = n1.shape
    cols = second.shape[1]
    blk = column_block(cols)

    def body(n1_ref, second_ref, out_ref):
        out_ref[...] = nn_dot(n1_ref[...], second_ref[...]).astype(LOW)

    return launch(
        body, grid=(cols // blk,), out_shape=jax.ShapeDtypeStruct((tokens, cols), LOW),
        in_specs=[whole_spec((tokens, model)), pl.BlockSpec((model, blk), lambda j: (0, j))],
        out_specs=pl.BlockSpec((tokens, blk), lambda j: (0, j)), name="project_mixer", us=5,
    )(n1, second)


def mixer_out(unit, og, third, rows):
    width = og.shape[1]
    model = third.shape[0]
    blk = column_block(model)

    def body(og_ref, third_ref, out_ref):
        out_ref[...] = nt_dot(og_ref[...], third_ref[...]).astype(LOW)

    return launch(
        body, grid=(model // blk,), out_shape=jax.ShapeDtypeStruct((rows, model), LOW),
        in_specs=[pl.BlockSpec((rows, width), lambda j: (unit, 0)), pl.BlockSpec((blk, width), lambda j: (j, 0))],
        out_specs=pl.BlockSpec((rows, blk), lambda j: (0, j)), name="mixer_out", us=2,
    )(og, third)


def turns(first, second, width):
    count = first.shape[-1] // width
    parts = [arr[..., width * i : width * (i + 1)] for i in range(count) for arr in (first, second)]
    return jnp.concatenate(parts, axis=-1)


def unturned(mixed, width, which):
    count = mixed.shape[-1] // (2 * width)
    return jnp.concatenate([mixed[..., width * (2 * i + which) : width * (2 * i + which + 1)] for i in range(count)], axis=-1)


def per_device(
    tokens, cotangent, doc_lengths, mixer_gain, w_query, key_matrix, value_matrix, mamba_gate_weight,
    mamba_input_weight, w_bproj, w_cproj, w_dt, a_log, dt_bias, d_skip, w_attn_out, w_mixer_out,
    ffn_gain, w_gate, w_up, w_down,
):
    CHAIN.clear()
    micro_count, seq_count, block_len, model_dim = tokens.shape
    rows_here = mixer_gain.shape[0]
    heads = w_dt.shape[1]
    ssm_dim = mamba_gate_weight.shape[1]
    head_dim = ssm_dim // heads
    q_dim = w_query.shape[1]
    kv_dim = key_matrix.shape[1]
    state_dim = w_bproj.shape[1]
    ff_dim = w_gate.shape[1]
    ff_blk = min(256, ff_dim)
    ci = lax.axis_index("context")
    nc = lax.axis_size("context")
    full_len = nc * block_len
    units = micro_count * seq_count
    pairs = heads // 2
    tokens_here = units * block_len
    at_b = q_dim + 2 * kv_dim
    at_c = at_b + state_dim
    at_dt = at_c + state_dim
    at_gain = at_dt + heads
    first_width = at_gain + 2 + -(at_gain + 2) % 128

    place = jnp.stack([lax.axis_index("fsdp"), ci]).astype(jnp.int32)
    at_k, at_v = q_dim, q_dim + kv_dim
    two = 2 * head_dim
    first, own_first = pack(
        place,
        [(w_query, 0, q_dim, 0, False), (key_matrix, at_k, kv_dim, 0, False), (value_matrix, at_v, kv_dim, 0, False),
         (w_bproj, at_b, state_dim, 0, False), (w_cproj, at_c, state_dim, 0, False), (w_dt, at_dt, heads, 0, False),
         (jnp.stack([mixer_gain, ffn_gain], axis=1), at_gain, 2, 0, False)],
        first_width, "pack_first")
    near_first = send_near(own_first)
    second, own_second = pack(
        place,
        [(arr, (2 * i + n) * two, two, i * two, False)
         for i in range(pairs) for n, arr in enumerate((mamba_gate_weight, mamba_input_weight))],
        2 * ssm_dim, "pack_second")
    third, own_third = pack(
        place, [(w_attn_out, 0, q_dim, 0, True), (w_mixer_out, q_dim, ssm_dim, 0, True)], q_dim + ssm_dim, "pack_third")
    fourth, own_fourth = pack(
        place,
        [(arr, (2 * i + n) * ff_blk, ff_blk, i * ff_blk, False) for i in range(ff_dim // ff_blk) for n, arr in enumerate((w_gate, w_up))]
        + [(w_down, 2 * ff_dim, ff_dim, 0, True)],
        3 * ff_dim, "pack_fourth")
    lens = doc_lengths.reshape(units, -1)
    aux = jnp.pad(jnp.stack([a_log, dt_bias], axis=1), ((0, 16 - heads), (0, 0)))
    skip_row = jnp.repeat(d_skip, head_dim)[None]
    tokens = tokens.reshape(tokens_here, model_dim)
    cotangent = cotangent.reshape(tokens_here, model_dim)
    width = q_dim + ssm_dim

    def placed(shard, mine, other):
        return place_rows(place, shard.reshape(nc, -1, shard.shape[1]), mine, other)

    held_first = join(near_first, True)
    wait_for(held_first)
    near_second = send_near(own_second)
    held_first = spread_far(held_first)
    core_first = swap_context(held_first, 1)
    first = placed(first, held_first, core_first)
    wait_for(*near_second)
    n1, q, kv, b, c, per_head, gains = project(place, lens, tokens, first, aux, q_dim, kv_dim, state_dim, pairs)
    kv = kv.reshape(1, units, block_len, 2 * kv_dim)
    kv_far = [swap_context(kv, bit) for bit in far_bits()[:1]]
    held_second = join(near_second, True)
    near_third = send_near(own_third)
    kv_held = join([kv, *kv_far], False)
    for bit in far_bits()[1:]:
        kv_held = join([kv_held, swap_context(kv_held, bit)], False)
    kv_all = place_blocks(place, kv_held, swap_context(kv_held, 1))
    wait_for(*near_third)
    og, lse = None, [None] * units
    og, lse[0] = attention_forward(0, place, lens, q, kv_all, og, width)
    near_fourth = send_near(own_fourth)
    held_second = spread_far(held_second)
    held_third = join(near_third, True)
    second = placed(second, held_second, swap_context(held_second, 1))
    zx = project_mixer(n1, second)
    span = join([mamba_state(u, per_head, b, zx) for u in range(units)], True)[None]
    span_far = [swap_context(span, bit) for bit in far_bits()[:1]]
    held_fourth = join(near_fourth, True)
    for u in range(1, units):
        og, lse[u] = attention_forward(u, place, lens, q, kv_all, og, width)
    span = join([span, *span_far], False)
    for bit in far_bits()[1:]:
        span = join([span, swap_context(span, bit)], False)
    spans = (span, swap_context(span, 1))
    held_third = spread_far(held_third)
    core_third = swap_context(held_third, 1)
    state = chain_states(place, spans, state_dim)
    third = placed(third, held_third, core_third)
    og, y_u = mamba_forward(0, place, lens, per_head, zx, b, c, state, skip_row, og, q_dim)
    y, ours = [y_u], [mixer_out(0, og, third, block_len)]
    theirs = [swap_tensor(ours[0])]
    held_fourth = spread_far(held_fourth)
    core_fourth = swap_context(held_fourth, 1)
    for u in range(1, units):
        og, y_u = mamba_forward(u, place, lens, per_head, zx, b, c, state, skip_row, og, q_dim)
        y.append(y_u)
        ours.append(mixer_out(u, og, third, block_len))
        theirs.append(swap_tensor(ours[u]))
    fourth = placed(fourth, held_fourth, core_fourth)

    stacked, dn2, dn2_theirs = None, [], []
    for u in range(units):
        *stacked, dn2_u = feed_forward(u, tokens, ours[u], theirs[u], gains, cotangent, fourth, stacked)
        dn2.append(dn2_u)
        dn2_theirs.append(swap_tensor(dn2_u))
    h1, n2, f, dab = stacked
    wide = 3 * ff_dim
    away, keep_fourth = outer(place, n2, dab, None, 0, wide)
    wait_for(dn2_theirs[0])
    away, keep_fourth = outer(place, cotangent, f, (away, keep_fourth), 2 * ff_dim, wide)
    got_fourth = swap_context(away, 1)

    dm, dh, dog, d_span, local = None, [], [], [], []
    g_gain_two = 0.0
    d_second, dq, dkv, head_grads = None, [None] * units, [None] * units, 0.0
    bits = context_bits()[1:]

    def open_backward(u, dm):
        dm, dh_u, dog_u, terms = middle_backward(u, h1, dn2[u], dn2_theirs[u], gains, cotangent, third, dm)
        dh.append(dh_u)
        dog.append(dog_u)
        local.append(mamba_state(u, per_head, c, zx, dog_u, q_dim)[None, None])
        return dm, terms[0]

    def attend_back(u):
        dq[u], away, keep = attention_backward(u, place, lens, q, dog[u], og, kv_all, lse[u])
        return keep, swap_context(away, 1)

    def close_states(u):
        held = spread_far(local[u])
        return held, swap_context(held, 1)

    def to_owners(keep, got):
        own, *away = split_fsdp(place, keep, got)
        return [own] + [from_next(arr, "fsdp", k + 1) for k, arr in enumerate(away)]

    def share(total):
        held = spread_far(total[None])
        return held, swap_context(held, 1)

    for u in range(units - 1):
        dm, terms = open_backward(u, dm)
        g_gain_two = g_gain_two + terms
        kept = attend_back(u)
        pair = close_states(u)
        if u == 0:
            keep_fourth, got_fourth = reduce_far(place, keep_fourth, got_fourth, bits)
        dkv[u] = reduce_far(place, *kept, bits)
        d_span.append(chain_states(place, spans, state_dim, pair, u)[0])
    dm, terms = open_backward(units - 1, dm)
    g_gain_two = g_gain_two + terms
    ff = feed_forward_out(f, fourth)
    ff_theirs = swap_tensor(ff)
    wide = q_dim + ssm_dim
    away, keep_third = outer(place, dm, og, None, 0, wide)
    got_third = swap_context(away, 1)
    for u in range(units):
        if u == units - 1:
            pair = close_states(u)
            keep_third, got_third = reduce_far(place, keep_third, got_third, bits)
            parts_fourth = to_owners(keep_fourth, got_fourth)
            d_span.append(chain_states(place, spans, state_dim, pair, u)[0])
        *d_second, grads_u = mamba_backward(
            u, place, lens, per_head, zx, y[u], dog[u], q_dim, b, c, state, d_span[u], skip_row, aux, d_second)
        head_grads = head_grads + grads_u
    dzx, dbc = d_second
    at_rest = 2 * ssm_dim
    wide = at_rest + dbc.shape[1]
    pair = outer(place, n1, dzx, None, 0, wide)
    wait_for(*parts_fourth)
    away, keep_second = outer(place, n1, dbc, pair, at_rest, wide)
    got_second = swap_context(away, 1)
    parts_third = to_owners(keep_third, got_third)
    parts, parts_theirs, g_gain_one, dqkv = [None] * units, [None] * units, 0.0, None

    def close_backward(u, dqkv):
        dqkv, parts[u], terms = input_backward(u, dq[u], *dkv[u], dbc, dzx, first, second, tokens, dqkv)
        parts_theirs[u] = swap_tensor(parts[u])
        return dqkv, terms[0]

    for u in range(units - 1):
        dqkv, terms = close_backward(u, dqkv)
        g_gain_one = g_gain_one + terms
    g_fourth = sum_parts(parts_fourth)
    keep_second, got_second = reduce_far(place, keep_second, got_second, bits)
    kept = attend_back(units - 1)
    head_grads = all_sum(head_grads[:heads, :3])
    dkv[units - 1] = reduce_far(place, *kept, bits)
    g_third = sum_parts(parts_third)
    layer_out = close_forward(h1, ff, ff_theirs)
    dqkv, terms = close_backward(units - 1, dqkv)
    g_gain_one = g_gain_one + terms
    g_gains = jnp.pad(jnp.stack([g_gain_one, g_gain_two], axis=1).astype(LOW), ((0, 0), (0, 126)))
    wide = at_b + 128
    away, keep_first = outer(place, n1, dqkv, None, 0, wide)
    g_gains = g_gains.reshape((lax.axis_size("fsdp"), nc // 2, 2, -1, 128))
    mine = ci % 2
    away = away.at[..., at_b:].set(lax.dynamic_index_in_dim(g_gains, 1 - mine, 2, keepdims=False))
    keep_first = keep_first.at[..., at_b:].set(lax.dynamic_index_in_dim(g_gains, mine, 2, keepdims=False))
    got_first = swap_context(away, 1)
    parts_second = to_owners(keep_second, got_second)
    keep_first, got_first = reduce_far(place, keep_first, got_first, bits)
    fourth_pair = share(g_fourth)
    third_pair = share(g_third)
    parts_first = to_owners(keep_first, got_first)
    input_grads = None
    for u in range(units - 1):
        input_grads = finish(u, tokens, parts[u], parts_theirs[u], gains, dh[u], input_grads)

    def columns(first, width, turned=False):
        return [(first, width)], turned

    def in_turns(which, width, total):
        return [(width * (2 * i + which), width) for i in range(total // width)], False

    g_gate, g_up, g_down = emit(
        place, *fourth_pair,
        [in_turns(0, ff_blk, ff_dim), in_turns(1, ff_blk, ff_dim), columns(2 * ff_dim, ff_dim, True)], "emit_fourth")
    g_attn, g_mixer = emit(place, *third_pair, [columns(0, q_dim, True), columns(q_dim, ssm_dim, True)], "emit_third")
    g_second = sum_parts(parts_second, (at_rest, at_rest + 2 * state_dim))
    g_first = sum_parts(parts_first)
    lane = jnp.arange(128)[None]
    g_gains = g_first[:, at_b:]
    g_gains = jnp.where(lane == 0, (g_gains.astype(F32) + swap_tensor(g_gains).astype(F32)).astype(LOW), g_gains)
    g_first = jnp.concatenate([g_first[:, :at_b], g_gains], axis=1)
    u = units - 1
    input_grads = finish(u, tokens, parts[u], parts_theirs[u], gains, dh[u], input_grads)
    g_z, g_x, g_b, g_c, g_dt = emit(
        place, *share(g_second),
        [in_turns(0, two, ssm_dim), in_turns(1, two, ssm_dim), columns(at_rest, state_dim),
         columns(at_rest + state_dim, state_dim), columns(at_rest + 2 * state_dim, heads)], "emit_second")
    g_q, g_k, g_v, g_gains = emit(
        place, *share(g_first),
        [columns(0, q_dim), columns(at_k, kv_dim), columns(at_v, kv_dim), columns(at_b, 128)], "emit_first")
    shape = (micro_count, seq_count, block_len, model_dim)
    return (
        layer_out.reshape(shape), input_grads.reshape(shape), g_gains[:, 0], g_q, g_k, g_v, g_z, g_x, g_b, g_c, g_dt,
        head_grads[:, 0], head_grads[:, 1], head_grads[:, 2], g_attn, g_mixer, g_gains[:, 1], g_gate, g_up, g_down,
    )


def solution(mesh):
    rows, cols = P("fsdp", "tensor"), P("tensor", "fsdp")
    acts = P(None, "fsdp", "context", None)
    return jax.shard_map(
        per_device,
        mesh=mesh,
        in_specs=(
            acts, acts, P(None, "fsdp", None), P("fsdp"), rows, rows, rows, rows, rows, P("fsdp", None),
            P("fsdp", None), rows, P("tensor"), P("tensor"), P("tensor"), cols, cols, P("fsdp"), rows, rows, cols,
        ),
        out_specs=(
            acts, acts, P("fsdp"), rows, rows, rows, rows, rows, P("fsdp", None), P("fsdp", None), rows,
            P("tensor"), P("tensor"), P("tensor"), cols, cols, P("fsdp"), rows, rows, cols,
        ),
        check_vma=False,
    )
```

time: 743 us -> 568 us (0.76)
  the two profiles are of different devices: /device:TPU:11 before, /device:TPU:0 now
where the time goes in v3:
time: 568 us; the launch traced here: 562 us
  Pallas kernels  248 us (44%)
  waiting for transfers between devices  157 us (28%)
  starting transfers between devices  114 us (20%)
  local copies, waits for them, and re-layouts  39.1 us (7%)
    pallas_call x79, Pallas kernels, call(): pl.pallas_call(run, grid=grid, out_shape=outs + (jax.ShapeDtypeStruct((8,...  248 us
    ppermute x38, waiting for transfers between devices, swap_context(): return lax.ppermute(x, 'context', [(i, i ^ bit) for i in range(size)])  76.3 us
    ppermute x38, starting transfers between devices, swap_context(): return lax.ppermute(x, 'context', [(i, i ^ bit) for i in range(size)])  65 us
    ppermute x24, waiting for transfers between devices, from_next(): return lax.ppermute(x, axis, [((i + step) % size, i) for i in range(size)])  58.3 us
    unnamed x243, local copies, waits for them, and re-layouts  35.6 us
    ppermute x24, starting transfers between devices, from_next(): return lax.ppermute(x, axis, [((i + step) % size, i) for i in range(size)])  33 us
    ppermute x9, waiting for transfers between devices, swap_tensor(): return lax.ppermute(x, 'tensor', [(i, (i + 1) % size) for i in range(size)])  17.6 us
    ppermute x9, starting transfers between devices, swap_tensor(): return lax.ppermute(x, 'tensor', [(i, (i + 1) % size) for i in range(size)])  12 us
  transfers between devices with their start and end apart: 73, of which 31 were waited for; matrix products, arithmetic and copies ran while one was open for 1% of the time, Pallas kernels for 40%

profile of v3, /device:TPU:0, one launch (start us, length us, event | category | flops | bytes accessed | tf_op | source)
XLA Modules:
  0.0 561.6 jit_solution(16021010401199306844)
XLA Ops:
  8.9 5.0 collective-permute-start
  19.5 3.2 collective-permute-done.1
  24.5 7.0 %collective-permute-done.3.refs_1_ = bf16[3,64,768]{2,1,0:T(8,128)(2,1)S(1)} collective-permute-done((bf16[3,64,768]{2,1,0:T(8,128)(2,1)S(1)}, bf16[3,64,768]{2,1,0:T(8,128)(2,1)S(1)}, u32[]{:S(2)}, u32[]{:S(2)}) %collective-permute-start.3) | collective-permute-done | bytes 294944 | tf_op jit(solution)/shard_map/ppermute | solution.py:18
  39.0 12.9 %collective-permute-done.6.refs_7_ = bf16[64,1536]{1,0:T(8,128)(2,1)S(1)} collective-permute-done((bf16[64,1536]{1,0:T(8,128)(2,1)S(1)}, bf16[64,1536]{1,0:T(8,128)(2,1)S(1)}, u32[]{:S(2)}, u32[]{:S(2)}) %collective-permute-start.6) | collective-permute-done | bytes 196640 | tf_op jit(solution)/shard_map/ppermute | solution.py:23
  51.9 5.9 %project.1 = (bf16[1024,1024]{1,0:T(8,128)(2,1)S(1)}, bf16[1024,256]{1,0:T(8,128)(2,1)S(1)}, bf16[1024,128]{1,0:T(8,128)(2,1)S(1)}, bf16[1024,128]{1,0:T(8,128)(...) custom-call(s32[2]{0:T(128)S(1)} %pad_add_fusion.refs_0_, ...), custom_call_target="tpu_custom_call" | custom-call | flops 2600000000 | bytes 1 | tf_op jit(solution)/shard_map/project/pallas_call | solution.py:77
  59.6 6.4 %collective-permute-done.9.refs_1_ = bf16[1,2,512,128]{3,2,1,0:T(8,128)(2,1)S(1)} collective-permute-done((bf16[1,2,512,128]{3,2,1,0:T(8,128)(2,1)S(1)}, bf16[1,2,512,128]{3,2,1,0:T(8,128)(2,1)S(1)}, u32[]{:S(2)}, u32[]{:S(2)}) %collective-permute-start.9) | collective-permute-done | bytes 262176 | tf_op jit(solution)/shard_map/ppermute | solution.py:18
  73.9 7.5 %collective-permute-done.12.refs_6_ = bf16[64,1024]{1,0:T(8,128)(2,1)S(1)} collective-permute-done((bf16[64,1024]{1,0:T(8,128)(2,1)S(1)}, bf16[64,1024]{1,0:T(8,128)(2,1)S(1)}, u32[]{:S(2)}, u32[]{:S(2)}) %collective-permute-start.12) | collective-permute-done | bytes 131104 | tf_op jit(solution)/shard_map/ppermute | solution.py:23
  81.4 3.1 attention_forward.2
  88.8 2.2 collective-permute-start.18
  91.2 5.4 collective-permute-start.20
  96.5 2.8 place_rows.5
  99.3 5.2 project_mixer.1
  104.5 2.5 mamba_state.4
  107.0 2.5 mamba_state.5
  109.9 13.8 %collective-permute-done.17 = bf16[64,3072]{1,0:T(8,128)(2,1)S(1)} collective-permute-done((bf16[64,3072]{1,0:T(8,128)(2,1)}, bf16[64,3072]{1,0:T(8,128)(2,1)S(1)}, u32[]{:S(2)}, u32[]{:S(2)}) %collective-permute-start.17) | collective-permute-done | bytes 393248 | tf_op jit(solution)/shard_map/ppermute | solution.py:23
  123.6 2.3 join.24
  125.9 3.4 attention_forward.3
  133.1 10.0 %collective-permute-start.22 = (bf16[3,64,3072]{2,1,0:T(8,128)(2,1)}, bf16[3,64,3072]{2,1,0:T(8,128)(2,1)}, u32[]{:S(2)}, u32[]{:S(2)}) collective-permute-start(bf16[3,64,3072]{2,1,0:T(8,128)(2,1)} %get-tuple-element.332.refs_0_), channel_id=1, source_target_pairs={{0,4},{2,6},{4,0},{6,2},{1,5},{3,7},{5,1},{7,3},{8,12},{10,14},{12... | collective-permute-start | bytes 3538952 | tf_op jit(solution)/shard_map/ppermute | solution.py:18
  149.4 7.5 %mamba_forward.2 = (bf16[1024,1024]{1,0:T(8,128)(2,1)S(1)}, f32[512,768]{1,0:T(8,128)S(1)}, f32[8,128]{1,0:T(8,128)S(1)}) custom-call(s32[2]{0:T(128)S(1)} %pad_add_fusion.refs_0_, s32[2,4]{1,0:T(2,128)S(1)} %bitcast.106, f32[2,6,8,512]{3,2,1,0:T(8,128)S(1)} %get-tuple-element.288.refs_0_.refs_2_, ...), custom_call_target="tpu_custom_call", output_to_operand_aliasing={{0}: (8, {})} | custom-call | flops 3000000000 | bytes 1 | tf_op jit(solution)/shard_map/mamba_forward/pallas_call | solution.py:77
  158.6 11.1 %collective-permute-done.22.refs_1_ = bf16[3,64,3072]{2,1,0:T(8,128)(2,1)} collective-permute-done((bf16[3,64,3072]{2,1,0:T(8,128)(2,1)}, bf16[3,64,3072]{2,1,0:T(8,128)(2,1)}, u32[]{:S(2)}, u32[]{:S(2)}) %collective-permute-start.22) | collective-permute-done | bytes 1179680 | tf_op jit(solution)/shard_map/ppermute | solution.py:18
  169.6 3.5 join.27
  174.8 7.3 %mamba_forward.3 = (bf16[1024,1024]{1,0:T(8,128)(2,1)S(1)}, f32[512,768]{1,0:T(8,128)S(1)}, f32[8,128]{1,0:T(8,128)S(1)}) custom-call(s32[2]{0:T(128)S(1)} %pad_add_fusion.refs_0_, s32[2,4]{1,0:T(2,128)S(1)} %bitcast.107, f32[2,6,8,512]{3,2,1,0:T(8,128)S(1)} %get-tuple-element.288.refs_0_.refs_2_, ...), custom_call_target="tpu_custom_call", output_to_operand_aliasing={{0}: (8, {})} | custom-call | flops 3000000000 | bytes 1 | tf_op jit(solution)/shard_map/mamba_forward/pallas_call | solution.py:77
  184.8 5.9 %place_rows.7 = (bf16[4,4,64,3072]{3,2,1,0:T(8,128)(2,1)}, f32[8,128]{1,0:T(8,128)S(1)}) custom-call(s32[2]{0:T(128)S(1)} %pad_add_fusion.refs_0_, bf16[4,64,3072]{2,1,0:T(8,128)(2,1)S(1)} %bitcast.112, bf16[6,64,3072]{2,1,0:T(8,128)(2,1)S(1)} %get-tuple-element.342.refs_2_, bf16[6,64,3072]{2,1,0:T(8,128)(2,1)} %collective-permute-done.24.refs_3_, ...), custom_call_target="tpu_custom_call" | custom-call | flops 2048000000 | bytes 1 | tf_op jit(solution)/shard_map/place_rows/pallas_call | solution.py:77
  190.7 8.6 %collective-permute-done.25.refs_2_ = bf16[512,1024]{1,0:T(8,128)(2,1)S(1)} collective-permute-done((bf16[512,1024]{1,0:T(8,128)(2,1)S(1)}, bf16[512,1024]{1,0:T(8,128)(2,1)S(1)}, u32[]{:S(2)}, u32[]{:S(2)}) %collective-permute-start.25) | collective-permute-done | bytes 1048608 | tf_op jit(solution)/shard_map/ppermute | solution.py:28
  201.5 13.6 %feed_forward.2 = (f32[1024,1024]{1,0:T(8,128)}, bf16[1024,1024]{1,0:T(8,128)(2,1)S(1)}, bf16[1024,1024]{1,0:T(8,128)(2,1)}, bf16[1024,2048]{1,0:T(8,128)(2,1)},...) custom-call(bf16[1024,1024]{1,0:T(8,128)(2,1)} %bitcast.57, bf16[512,1024]{1,0:T(8,128)(2,1)S(1)} %get-tuple-element.345.refs_1_, ...), custom_call_target="tpu_custom_call" | custom-call | flops 5600000000 | bytes 1 | tf_op jit(solution)/shard_map/feed_forward/pallas_call | solution.py:77
  216.6 5.1 collective-permute-done.23.refs_2_
  221.7 14.0 %feed_forward.3 = (f32[1024,1024]{1,0:T(8,128)}, bf16[1024,1024]{1,0:T(8,128)(2,1)S(1)}, bf16[1024,1024]{1,0:T(8,128)(2,1)}, bf16[1024,2048]{1,0:T(8,128)(2,1)},...) custom-call(bf16[1024,1024]{1,0:T(8,128)(2,1)} %bitcast.58, ...), custom_call_target="tpu_custom_call", output_to_operand_aliasing={{0}: (7, {}), {1}: (8, {}), {2}: (9, {}), {3}: (10, {})} | custom-call | flops 5600000000 | bytes 1 | tf_op jit(solution)/shard_map/feed_forward/pallas_call | solution.py:77
  235.8 8.8 %outer.6 = (bf16[4,2,64,3072]{3,2,1,0:T(8,128)(2,1)S(1)}, bf16[4,2,64,3072]{3,2,1,0:T(8,128)(2,1)}, f32[8,128]{1,0:T(8,128)S(1)}) custom-call(s32[2]{0:T(128)S(1)} %pad_add_fusion.refs_0_, bf16[1024,1024]{1,0:T(8,128)(2,1)S(1)} %get-tuple-element.356.refs_1_, bf16[1024,2048]{1,0:T(8,128)(2,1)} %get-tuple-element.357.refs_2_, ...), custom_call_target="tpu_custom_call" | custom-call | flops 3561739008 | bytes 1 | tf_op jit(solution)/shard_map/outer/pallas_call | solution.py:77
  246.3 5.7 %outer.7 = (bf16[4,2,64,3072]{3,2,1,0:T(8,128)(2,1)}, bf16[4,2,64,3072]{3,2,1,0:T(8,128)(2,1)}, f32[8,128]{1,0:T(8,128)S(1)}) custom-call(s32[2]{0:T(128)S(1)} %pad_add_fusion.refs_0_, bf16[1024,1024]{1,0:T(8,128)(2,1)S(1)} %bitcast.71, bf16[1024,1024]{1,0:T(8,128)(2,1)S(1)} %copy-done.5, ...), custom_call_target="tpu_custom_call", output_to_operand_aliasing={{0}: (3, {}), {1}: (4, {})} | custom-call | flops 1780869504 | bytes 1 | tf_op jit(solution)/shard_map/outer/pallas_call | solution.py:77
  253.5 5.4 middle_backward.2
  263.7 5.2 attention_backward.2
  269.3 4.0 collective-permute-start.29
  273.4 5.8 %split_sum.6 = (bf16[4,1,64,3072]{3,2,1,0:T(8,128)(2,1)}, bf16[4,1,64,3072]{3,2,1,0:T(8,128)(2,1)S(1)}, f32[8,128]{1,0:T(8,128)S(1)}) custom-call(s32[2]{0:T(128)S(1)} %pad_add_fusion.refs_0_, bf16[4,2,64,3072]{3,2,1,0:T(8,128)(2,1)} %get-tuple-element.373.refs_1_, bf16[4,2,64,3072]{3,2,1,0:T(8,128)(2,1)} %collective-permute-done.31.refs_2_, ...), custom_call_target="tpu_custom_call" | custom-call | flops 1365333376 | bytes 1 | tf_op jit(solution)/shard_map/split_sum/pallas_call | solution.py:77
  280.4 8.3 %collective-permute-start.37 = (bf16[4,1,64,3072]{3,2,1,0:T(8,128)(2,1)}, bf16[4,1,64,3072]{3,2,1,0:T(8,128)(2,1)}, u32[]{:S(2)}, u32[]{:S(2)}) collective-permute-start(bf16[4,1,64,3072]{3,2,1,0:T(8,128)(2,1)} %get-tuple-element.398), channel_id=1, source_target_pairs={{0,4},{2,6},{4,0},{6,2},{1,5},{3,7},{5,1},{7,3},{8,12},{10,14},{12... | collective-permute-start | bytes 4718600 | tf_op jit(solution)/shard_map/ppermute | solution.py:18
  291.0 5.9 %middle_backward.3 = (bf16[1024,1024]{1,0:T(8,128)(2,1)S(1)}, f32[512,1024]{1,0:T(8,128)}, bf16[512,1024]{1,0:T(8,128)(2,1)S(1)}, f32[8,1024]{1,0:T(8,128)S(1)}, f32[8,128]{1,0:T(8,128)S(1)}) custom-call(f32[1024,1024]{1,0:T(8,128)} %get-tuple-element.352.refs_0_, bf16[512,1024]{1,0:T(8,128)(2,1)} %get-tuple-element.354.refs_1_, ...), custom_call_target="tpu_custom_call", output_to_operand_aliasing={{0}: (6, {})} | custom-call | flops 2160000000 | bytes 1 | tf_op jit(solution)/shard_map/middle_backward/pallas_call | solution.py:77
  298.6 4.3 feed_forward_out.1
  303.1 5.0 outer.8
  308.7 16.3 %mamba_backward.2 = (bf16[1024,1536]{1,0:T(8,128)(2,1)}, bf16[1024,512]{1,0:T(8,128)(2,1)S(1)}, f32[16,128]{1,0:T(8,128)S(1)}, f32[8,128]{1,0:T(8,128)S(1)}) custom-call(s32[2]{0:T(128)S(1)} %pad_add_fusion.refs_0_, s32[2,4]{1,0:T(2,128)S(1)} %bitcast.109, f32[2,6,8,512]{3,2,1,0:T(8,128)S(1)} %get-tuple-element.288.refs_0_.refs_2_, ...), custom_call_target="tpu_custom_call" | custom-call | flops 6520000000 | bytes 1 | tf_op jit(solution)/shard_map/mamba_backward/pallas_call | solution.py:77
  325.0 3.0 collective-permute-done.34.refs_1_
  330.9 3.4 split_fsdp.4
  340.7 16.2 %mamba_backward.3 = (bf16[1024,1536]{1,0:T(8,128)(2,1)}, bf16[1024,512]{1,0:T(8,128)(2,1)S(1)}, f32[16,128]{1,0:T(8,128)S(1)}, f32[8,128]{1,0:T(8,128)S(1)}) custom-call(s32[2]{0:T(128)S(1)} %pad_add_fusion.refs_0_, s32[2,4]{1,0:T(2,128)S(1)} %bitcast.110, ...), custom_call_target="tpu_custom_call", output_to_operand_aliasing={{0}: (12, {}), {1}: (13, {})} | custom-call | flops 6520000000 | bytes 1 | tf_op jit(solution)/shard_map/mamba_backward/pallas_call | solution.py:77
  356.9 7.1 %outer.9 = (bf16[4,2,64,2048]{3,2,1,0:T(8,128)(2,1)S(1)}, bf16[4,2,64,2048]{3,2,1,0:T(8,128)(2,1)S(1)}, f32[8,128]{1,0:T(8,128)S(1)}) custom-call(s32[2]{0:T(128)S(1)} %pad_add_fusion.refs_0_, bf16[1024,1024]{1,0:T(8,128)(2,1)} %copy-done.12, bf16[1024,1536]{1,0:T(8,128)(2,1)} %get-tuple-element.406.refs_2_.refs_4_, f32[8,128]{1,0:T(8,128)S(1)} %get-tuple-element.407.refs_3_), custom_call_target="tpu_custom_call" | custom-call | flops 2671304448 | bytes 1 | tf_op jit(solution)/shard_map/outer/pallas_call | solution.py:77
  365.4 5.7 %collective-permute-done.39.refs_8_.refs_2_ = bf16[64,3072]{1,0:T(8,128)(2,1)S(1)} collective-permute-done((bf16[64,3072]{1,0:T(8,128)(2,1)S(1)}, bf16[64,3072]{1,0:T(8,128)(2,1)S(1)}, u32[]{:S(2)}, u32[]{:S(2)}) %collective-permute-start.39) | collective-permute-done | bytes 393248 | tf_op jit(solution)/shard_map/ppermute | solution.py:23
  371.1 4.1 outer.10
  377.8 12.7 %collective-permute-done.35.refs_2_ = bf16[4,1,64,1024]{3,2,1,0:T(8,128)(2,1)S(1)} collective-permute-done((bf16[4,1,64,1024]{3,2,1,0:T(8,128)(2,1)S(1)}, bf16[4,1,64,1024]{3,2,1,0:T(8,128)(2,1)S(1)}, u32[]{:S(2)}, u32[]{:S(2)}) %collective-permute-start.35) | collective-permute-done | bytes 524320 | tf_op jit(solution)/shard_map/ppermute | solution.py:18
  392.6 6.5 %input_backward.2 = (bf16[1024,384]{1,0:T(8,128)(2,1)S(1)}, bf16[512,1024]{1,0:T(8,128)(2,1)S(1)}, f32[8,1024]{1,0:T(8,128)S(1)}, f32[8,128]{1,0:T(8,128)S(1)}) custom-call(bf16[512,256]{1,0:T(8,128)(2,1)S(1)} %copy-done.56, bf16[1,1,512,128]{3,2,1,0:T(8,128)(2,1)S(1)} %get-tuple-element.424.refs_1_, ...), custom_call_target="tpu_custom_call" | custom-call | flops 2600000000 | bytes 1 | tf_op jit(solution)/shard_map/input_backward/pallas_call | solution.py:77
  401.1 3.0 split_sum.9
  406.0 6.1 %attention_backward.3 = (bf16[512,256]{1,0:T(8,128)(2,1)S(1)}, bf16[1,2,512,128]{3,2,1,0:T(8,128)(2,1)}, bf16[1,2,512,128]{3,2,1,0:T(8,128)(2,1)S(1)}, f32[8,128]{1,0:T(8,128)S(1)}) custom-call(s32[2]{0:T(128)S(1)} %pad_add_fusion.refs_0_, s32[2,4]{1,0:T(2,128)S(1)} %bitcast.111, bf16[1024,256]{1,0:T(8,128)(2,1)S(1)} %copy-done.112, ...), custom_call_target="tpu_custom_call" | custom-call | flops 6800000000 | bytes 1 | tf_op jit(solution)/shard_map/attention_backward/pallas_call | solution.py:77
  413.5 3.4 collective-permute-start.46
  421.0 9.7 %collective-permute-start.51 = (bf16[4,1,64,2048]{3,2,1,0:T(8,128)(2,1)}, bf16[4,1,64,2048]{3,2,1,0:T(8,128)(2,1)}, u32[]{:S(2)}, u32[]{:S(2)}) collective-permute-start(bf16[4,1,64,2048]{3,2,1,0:T(8,128)(2,1)} %copy-done.63), channel_id=1, source_target_pairs={{0,4},{2,6},{4,0},{6,2},{1,5},{3,7},{5,1},{7,3},{8,12},{10,14},{12... | collective-permute-start | bytes 3145736 | tf_op jit(solution)/shard_map/ppermute | solution.py:18
  433.9 4.9 close_forward.1
  438.8 17.3 %collective-permute-done.47.refs_2_ = bf16[1,1,512,128]{3,2,1,0:T(8,128)(2,1)S(1)} collective-permute-done((bf16[1,1,512,128]{3,2,1,0:T(8,128)(2,1)S(1)}, bf16[1,1,512,128]{3,2,1,0:T(8,128)(2,1)S(1)}, u32[]{:S(2)}, u32[]{:S(2)}) %collective-permute-start.47) | collective-permute-done | bytes 131104 | tf_op jit(solution)/shard_map/ppermute | solution.py:18
  456.2 6.5 %input_backward.3 = (bf16[1024,384]{1,0:T(8,128)(2,1)S(1)}, bf16[512,1024]{1,0:T(8,128)(2,1)S(1)}, f32[8,1024]{1,0:T(8,128)S(1)}, f32[8,128]{1,0:T(8,128)S(1)}) custom-call(bf16[512,256]{1,0:T(8,128)(2,1)S(1)} %copy-done.52, bf16[1,1,512,128]{3,2,1,0:T(8,128)(2,1)S(1)} %get-tuple-element.437.refs_1_, ...), custom_call_target="tpu_custom_call", output_to_operand_aliasing={{0}: (8, {})} | custom-call | flops 2600000000 | bytes 1 | tf_op jit(solution)/shard_map/input_backward/pallas_call | solution.py:77
  466.0 3.6 outer.11
  473.1 2.3 split_fsdp.6
  476.1 5.2 collective-permute-done.54.refs_1_
  483.8 9.4 %collective-permute-done.53.refs_1_ = bf16[1,64,1024]{2,1,0:T(8,128)(2,1)S(1)} collective-permute-done((bf16[1,64,1024]{2,1,0:T(8,128)(2,1)S(1)}, bf16[1,64,1024]{2,1,0:T(8,128)(2,1)S(1)}, u32[]{:S(2)}, u32[]{:S(2)}) %collective-permute-start.53) | collective-permute-done | bytes 131104 | tf_op jit(solution)/shard_map/ppermute | solution.py:18
  497.9 4.0 finish.2
  503.5 2.7 emit_fourth.1
  508.1 11.0 %collective-permute-done.59.refs_2_ = bf16[64,2048]{1,0:T(8,128)(2,1)S(1)} collective-permute-done((bf16[64,2048]{1,0:T(8,128)(2,1)S(1)}, bf16[64,2048]{1,0:T(8,128)(2,1)S(1)}, u32[]{:S(2)}, u32[]{:S(2)}) %collective-permute-start.59) | collective-permute-done | bytes 262176 | tf_op jit(solution)/shard_map/ppermute | solution.py:23
  521.0 2.9 collective-permute-start.56
  523.9 2.3 collective-permute-start.57
  530.3 3.9 finish.3
  553.5 2.6 collective-permute-done.72
  (435 shorter events, 146.9 us)
Async XLA Ops:
  8.9 10.6 %collective-permute-start = (bf16[64,768]{1,0:T(8,128)(2,1)S(1)}, bf16[64,768]{1,0:T(8,128)(2,1)S(1)}, u32[]{:S(2)}, u32[]{:S(2)}) collective-permute-start(bf16[64,768]{1,0:T(8,128)(2,1)S(1)} %get-tuple-element.276), channel_id=1, source_target_pairs={{8,0},{16,8},{24,16},{0,24},{9,1},{17,9},{25,17},{1,25},{10,2},{18... | collective-permute-start | bytes 294920 | tf_op jit(solution)/shard_map/ppermute | solution.py:23
  14.0 8.7 %collective-permute-start.1 = (bf16[64,768]{1,0:T(8,128)(2,1)S(1)}, bf16[64,768]{1,0:T(8,128)(2,1)S(1)}, u32[]{:S(2)}, u32[]{:S(2)}) collective-permute-start(bf16[64,768]{1,0:T(8,128)(2,1)S(1)} %get-tuple-element.276), channel_id=1, source_target_pairs={{16,0},{24,8},{0,16},{8,24},{17,1},{25,9},{1,17},{9,25},{18,2},{26... | collective-permute-start | bytes 294920 | tf_op jit(solution)/shard_map/ppermute | solution.py:23
  14.0 8.7 %collective-permute-start.2 = (bf16[64,768]{1,0:T(8,128)(2,1)S(1)}, bf16[64,768]{1,0:T(8,128)(2,1)S(1)}, u32[]{:S(2)}, u32[]{:S(2)}) collective-permute-start(bf16[64,768]{1,0:T(8,128)(2,1)S(1)} %get-tuple-element.276), channel_id=1, source_target_pairs={{24,0},{0,8},{8,16},{16,24},{25,1},{1,9},{9,17},{17,25},{26,2},{2,... | collective-permute-start | bytes 294920 | tf_op jit(solution)/shard_map/ppermute | solution.py:23
  22.9 8.5 %collective-permute-start.3 = (bf16[3,64,768]{2,1,0:T(8,128)(2,1)S(1)}, bf16[3,64,768]{2,1,0:T(8,128)(2,1)S(1)}, u32[]{:S(2)}, u32[]{:S(2)}) collective-permute-start(bf16[3,64,768]{2,1,0:T(8,128)(2,1)S(1)} %get-tuple-element.281.refs_0_.refs_3_), channel_id=1, source_target_pairs={{0,4},{2,6},{4,0},{6,2},{1,5},{3,7},{5,1},{7,3},{8,12},{10,14},{12... | collective-permute-start | bytes 884744 | tf_op jit(solution)/shard_map/ppermute | solution.py:18
  31.7 7.3 %collective-permute-start.5 = (bf16[64,1536]{1,0:T(8,128)(2,1)S(1)}, bf16[64,1536]{1,0:T(8,128)(2,1)S(1)}, u32[]{:S(2)}, u32[]{:S(2)}) collective-permute-start(bf16[64,1536]{1,0:T(8,128)(2,1)S(1)} %get-tuple-element.287), channel_id=1, source_target_pairs={{8,0},{16,8},{24,16},{0,24},{9,1},{17,9},{25,17},{1,25},{10,2},{18... | collective-permute-start | bytes 589832 | tf_op jit(solution)/shard_map/ppermute | solution.py:23
  32.3 19.5 %collective-permute-start.6 = (bf16[64,1536]{1,0:T(8,128)(2,1)S(1)}, bf16[64,1536]{1,0:T(8,128)(2,1)S(1)}, u32[]{:S(2)}, u32[]{:S(2)}) collective-permute-start(bf16[64,1536]{1,0:T(8,128)(2,1)S(1)} %get-tuple-element.287), channel_id=1, source_target_pairs={{16,0},{24,8},{0,16},{8,24},{17,1},{25,9},{1,17},{9,25},{18,2},{26... | collective-permute-start | bytes 589832 | tf_op jit(solution)/shard_map/ppermute | solution.py:23
  33.8 18.1 %collective-permute-start.7 = (bf16[64,1536]{1,0:T(8,128)(2,1)S(1)}, bf16[64,1536]{1,0:T(8,128)(2,1)S(1)}, u32[]{:S(2)}, u32[]{:S(2)}) collective-permute-start(bf16[64,1536]{1,0:T(8,128)(2,1)S(1)} %get-tuple-element.287), channel_id=1, source_target_pairs={{24,0},{0,8},{8,16},{16,24},{25,1},{1,9},{9,17},{17,25},{26,2},{2,... | collective-permute-start | bytes 589832 | tf_op jit(solution)/shard_map/ppermute | solution.py:23
  57.8 8.1 %collective-permute-start.9 = (bf16[1,2,512,128]{3,2,1,0:T(8,128)(2,1)S(1)}, bf16[1,2,512,128]{3,2,1,0:T(8,128)(2,1)S(1)}, u32[]{:S(2)}, u32[]{:S(2)}) collective-permute-start(bf16[1,2,512,128]{3,2,1,0:T(8,128)(2,1)S(1)} %bitcast.82), channel_id=1, source_target_pairs={{0,4},{2,6},{4,0},{6,2},{1,5},{3,7},{5,1},{7,3},{8,12},{10,14},{12... | collective-permute-start | bytes 786440 | tf_op jit(solution)/shard_map/ppermute | solution.py:18
  66.1 18.4 %collective-permute-start.8 = (bf16[3,64,1536]{2,1,0:T(8,128)(2,1)S(1)}, bf16[3,64,1536]{2,1,0:T(8,128)(2,1)S(1)}, u32[]{:S(2)}, u32[]{:S(2)}) collective-permute-start(bf16[3,64,1536]{2,1,0:T(8,128)(2,1)S(1)} %get-tuple-element.292.refs_0_), channel_id=1, source_target_pairs={{0,4},{2,6},{4,0},{6,2},{1,5},{3,7},{5,1},{7,3},{8,12},{10,14},{12... | collective-permute-start | bytes 1769480 | tf_op jit(solution)/shard_map/ppermute | solution.py:18
  67.7 6.2 %collective-permute-start.11 = (bf16[64,1024]{1,0:T(8,128)(2,1)S(1)}, bf16[64,1024]{1,0:T(8,128)(2,1)S(1)}, u32[]{:S(2)}, u32[]{:S(2)}) collective-permute-start(bf16[64,1024]{1,0:T(8,128)(2,1)S(1)} %get-tuple-element.300), channel_id=1, source_target_pairs={{8,0},{16,8},{24,16},{0,24},{9,1},{17,9},{25,17},{1,25},{10,2},{18... | collective-permute-start | bytes 393224 | tf_op jit(solution)/shard_map/ppermute | solution.py:23
  67.7 13.7 %collective-permute-start.12 = (bf16[64,1024]{1,0:T(8,128)(2,1)S(1)}, bf16[64,1024]{1,0:T(8,128)(2,1)S(1)}, u32[]{:S(2)}, u32[]{:S(2)}) collective-permute-start(bf16[64,1024]{1,0:T(8,128)(2,1)S(1)} %get-tuple-element.300), channel_id=1, source_target_pairs={{16,0},{24,8},{0,16},{8,24},{17,1},{25,9},{1,17},{9,25},{18,2},{26... | collective-permute-start | bytes 393224 | tf_op jit(solution)/shard_map/ppermute | solution.py:23
  69.1 12.3 %collective-permute-start.13 = (bf16[64,1024]{1,0:T(8,128)(2,1)S(1)}, bf16[64,1024]{1,0:T(8,128)(2,1)S(1)}, u32[]{:S(2)}, u32[]{:S(2)}) collective-permute-start(bf16[64,1024]{1,0:T(8,128)(2,1)S(1)} %get-tuple-element.300), channel_id=1, source_target_pairs={{24,0},{0,8},{8,16},{16,24},{25,1},{1,9},{9,17},{17,25},{26,2},{2,... | collective-permute-start | bytes 393224 | tf_op jit(solution)/shard_map/ppermute | solution.py:23
  84.9 11.6 %collective-permute-start.14 = (bf16[6,64,1536]{2,1,0:T(8,128)(2,1)S(1)}, bf16[6,64,1536]{2,1,0:T(8,128)(2,1)S(1)}, u32[]{:S(2)}, u32[]{:S(2)}) collective-permute-start(bf16[6,64,1536]{2,1,0:T(8,128)(2,1)S(1)} %get-tuple-element.302.refs_2_), channel_id=1, source_target_pairs={{0,2},{2,0},{4,6},{6,4},{1,3},{3,1},{5,7},{7,5},{8,10},{10,8},{12,... | collective-permute-start | bytes 3538952 | tf_op jit(solution)/shard_map/ppermute | solution.py:18
  87.0 22.9 %collective-permute-start.16 = (bf16[64,3072]{1,0:T(8,128)(2,1)}, bf16[64,3072]{1,0:T(8,128)(2,1)S(1)}, u32[]{:S(2)}, u32[]{:S(2)}) collective-permute-start(bf16[64,3072]{1,0:T(8,128)(2,1)} %get-tuple-element.317), channel_id=1, source_target_pairs={{8,0},{16,8},{24,16},{0,24},{9,1},{17,9},{25,17},{1,25},{10,2},{18... | collective-permute-start | bytes 1179656 | tf_op jit(solution)/shard_map/ppermute | solution.py:23
  87.0 36.6 %collective-permute-start.17 = (bf16[64,3072]{1,0:T(8,128)(2,1)}, bf16[64,3072]{1,0:T(8,128)(2,1)S(1)}, u32[]{:S(2)}, u32[]{:S(2)}) collective-permute-start(bf16[64,3072]{1,0:T(8,128)(2,1)} %get-tuple-element.317), channel_id=1, source_target_pairs={{16,0},{24,8},{0,16},{8,24},{17,1},{25,9},{1,17},{9,25},{18,2},{26... | collective-permute-start | bytes 1179656 | tf_op jit(solution)/shard_map/ppermute | solution.py:23
  88.8 34.8 %collective-permute-start.18 = (bf16[64,3072]{1,0:T(8,128)(2,1)}, bf16[64,3072]{1,0:T(8,128)(2,1)S(1)}, u32[]{:S(2)}, u32[]{:S(2)}) collective-permute-start(bf16[64,3072]{1,0:T(8,128)(2,1)} %get-tuple-element.317), channel_id=1, source_target_pairs={{24,0},{0,8},{8,16},{16,24},{25,1},{1,9},{9,17},{17,25},{26,2},{2,... | collective-permute-start | bytes 1179656 | tf_op jit(solution)/shard_map/ppermute | solution.py:23
  91.2 40.5 %collective-permute-start.20 = (bf16[3,64,1024]{2,1,0:T(8,128)(2,1)S(1)}, bf16[3,64,1024]{2,1,0:T(8,128)(2,1)S(1)}, u32[]{:S(2)}, u32[]{:S(2)}) collective-permute-start(bf16[3,64,1024]{2,1,0:T(8,128)(2,1)S(1)} %get-tuple-element.322.refs_0_), channel_id=1, source_target_pairs={{0,4},{2,6},{4,0},{6,2},{1,5},{3,7},{5,1},{7,3},{8,12},{10,14},{12... | collective-permute-start | bytes 1179656 | tf_op jit(solution)/shard_map/ppermute | solution.py:18
  109.7 19.6 %collective-permute-start.15 = (bf16[1,2,144,768]{3,2,1,0:T(8,128)(2,1)S(1)}, bf16[1,2,144,768]{3,2,1,0:T(8,128)(2,1)S(1)}, u32[]{:S(2)}, u32[]{:S(2)}) collective-permute-start(bf16[1,2,144,768]{3,2,1,0:T(8,128)(2,1)S(1)} %bitcast.75), channel_id=1, source_target_pairs={{0,4},{2,6},{4,0},{6,2},{1,5},{3,7},{5,1},{7,3},{8,12},{10,14},{12... | collective-permute-start | bytes 1327112 | tf_op jit(solution)/shard_map/ppermute | solution.py:18
  129.6 13.6 %collective-permute-start.19 = (bf16[2,2,144,768]{3,2,1,0:T(8,128)(2,1)S(1)}, bf16[2,2,144,768]{3,2,1,0:T(8,128)(2,1)S(1)}, u32[]{:S(2)}, u32[]{:S(2)}) collective-permute-start(bf16[2,2,144,768]{3,2,1,0:T(8,128)(2,1)S(1)} %get-tuple-element.321.refs_1_), channel_id=1, source_target_pairs={{0,2},{2,0},{4,6},{6,4},{1,3},{3,1},{5,7},{7,5},{8,10},{10,8},{12,... | collective-permute-start | bytes 2654216 | tf_op jit(solution)/shard_map/ppermute | solution.py:18
  132.6 14.0 %collective-permute-start.21 = (bf16[6,64,1024]{2,1,0:T(8,128)(2,1)}, bf16[6,64,1024]{2,1,0:T(8,128)(2,1)}, u32[]{:S(2)}, u32[]{:S(2)}) collective-permute-start(bf16[6,64,1024]{2,1,0:T(8,128)(2,1)} %get-tuple-element.328.refs_2_), channel_id=1, source_target_pairs={{0,2},{2,0},{4,6},{6,4},{1,3},{3,1},{5,7},{7,5},{8,10},{10,8},{12,... | collective-permute-start | bytes 2359304 | tf_op jit(solution)/shard_map/ppermute | solution.py:18
  133.1 36.6 %collective-permute-start.22 = (bf16[3,64,3072]{2,1,0:T(8,128)(2,1)}, bf16[3,64,3072]{2,1,0:T(8,128)(2,1)}, u32[]{:S(2)}, u32[]{:S(2)}) collective-permute-start(bf16[3,64,3072]{2,1,0:T(8,128)(2,1)} %get-tuple-element.332.refs_0_), channel_id=1, source_target_pairs={{0,4},{2,6},{4,0},{6,2},{1,5},{3,7},{5,1},{7,3},{8,12},{10,14},{12... | collective-permute-start | bytes 3538952 | tf_op jit(solution)/shard_map/ppermute | solution.py:18
  173.2 11.2 %collective-permute-start.24 = (bf16[6,64,3072]{2,1,0:T(8,128)(2,1)S(1)}, bf16[6,64,3072]{2,1,0:T(8,128)(2,1)}, u32[]{:S(2)}, u32[]{:S(2)}) collective-permute-start(bf16[6,64,3072]{2,1,0:T(8,128)(2,1)S(1)} %get-tuple-element.342.refs_2_), channel_id=1, source_target_pairs={{0,2},{2,0},{4,6},{6,4},{1,3},{3,1},{5,7},{7,5},{8,10},{10,8},{12,... | collective-permute-start | bytes 7077896 | tf_op jit(solution)/shard_map/ppermute | solution.py:18
  173.2 26.0 %collective-permute-start.25 = (bf16[512,1024]{1,0:T(8,128)(2,1)S(1)}, bf16[512,1024]{1,0:T(8,128)(2,1)S(1)}, u32[]{:S(2)}, u32[]{:S(2)}) collective-permute-start(bf16[512,1024]{1,0:T(8,128)(2,1)S(1)} %get-tuple-element.345.refs_1_), channel_id=1, source_target_pairs={{0,1},{1,0},{2,3},{3,2},{4,5},{5,4},{6,7},{7,6},{8,9},{9,8},{10,11... | collective-permute-start | bytes 3145736 | tf_op jit(solution)/shard_map/ppermute | solution.py:28
  183.8 37.9 %collective-permute-start.23 = (bf16[512,1024]{1,0:T(8,128)(2,1)S(1)}, bf16[512,1024]{1,0:T(8,128)(2,1)S(1)}, u32[]{:S(2)}, u32[]{:S(2)}) collective-permute-start(bf16[512,1024]{1,0:T(8,128)(2,1)S(1)} %get-tuple-element.339.refs_1_), channel_id=1, source_target_pairs={{0,1},{1,0},{2,3},{3,2},{4,5},{5,4},{6,7},{7,6},{8,9},{9,8},{10,11... | collective-permute-start | bytes 3145736 | tf_op jit(solution)/shard_map/ppermute | solution.py:28
  215.1 31.1 %collective-permute-start.27 = (bf16[512,1024]{1,0:T(8,128)(2,1)S(1)}, bf16[512,1024]{1,0:T(8,128)(2,1)S(1)}, u32[]{:S(2)}, u32[]{:S(2)}) collective-permute-start(bf16[512,1024]{1,0:T(8,128)(2,1)S(1)} %get-tuple-element.355.refs_1_), channel_id=1, source_target_pairs={{0,1},{1,0},{2,3},{3,2},{4,5},{5,4},{6,7},{7,6},{8,9},{9,8},{10,11... | collective-permute-start | bytes 3145736 | tf_op jit(solution)/shard_map/ppermute | solution.py:28
  251.9 21.4 %collective-permute-start.31 = (bf16[4,2,64,3072]{3,2,1,0:T(8,128)(2,1)}, bf16[4,2,64,3072]{3,2,1,0:T(8,128)(2,1)}, u32[]{:S(2)}, u32[]{:S(2)}) collective-permute-start(bf16[4,2,64,3072]{3,2,1,0:T(8,128)(2,1)} %get-tuple-element.374), channel_id=1, source_target_pairs={{0,2},{2,0},{4,6},{6,4},{1,3},{3,1},{5,7},{7,5},{8,10},{10,8},{12,... | collective-permute-start | bytes 9437192 | tf_op jit(solution)/shard_map/ppermute | solution.py:18
  251.9 39.1 %collective-permute-start.26 = (bf16[512,1024]{1,0:T(8,128)(2,1)}, bf16[512,1024]{1,0:T(8,128)(2,1)}, u32[]{:S(2)}, u32[]{:S(2)}) collective-permute-start(bf16[512,1024]{1,0:T(8,128)(2,1)} %get-tuple-element.354.refs_1_), channel_id=1, source_target_pairs={{0,1},{1,0},{2,3},{3,2},{4,5},{5,4},{6,7},{7,6},{8,9},{9,8},{10,11... | collective-permute-start | bytes 3145736 | tf_op jit(solution)/shard_map/ppermute | solution.py:28
  261.9 7.1 %collective-permute-start.28 = (bf16[1,1,128,768]{3,2,1,0:T(8,128)(2,1)S(1)}, bf16[1,1,128,768]{3,2,1,0:T(8,128)(2,1)S(1)}, u32[]{:S(2)}, u32[]{:S(2)}) collective-permute-start(bf16[1,1,128,768]{3,2,1,0:T(8,128)(2,1)S(1)} %bitcast.93), channel_id=1, source_target_pairs={{0,4},{2,6},{4,0},{6,2},{1,5},{3,7},{5,1},{7,3},{8,12},{10,14},{12... | collective-permute-start | bytes 589832 | tf_op jit(solution)/shard_map/ppermute | solution.py:18
  269.3 20.0 %collective-permute-start.29 = (bf16[2,1,128,768]{3,2,1,0:T(8,128)(2,1)S(1)}, bf16[2,1,128,768]{3,2,1,0:T(8,128)(2,1)S(1)}, u32[]{:S(2)}, u32[]{:S(2)}) collective-permute-start(bf16[2,1,128,768]{3,2,1,0:T(8,128)(2,1)S(1)} %get-tuple-element.370.refs_3_), channel_id=1, source_target_pairs={{0,2},{2,0},{4,6},{6,4},{1,3},{3,1},{5,7},{7,5},{8,10},{10,8},{12,... | collective-permute-start | bytes 1179656 | tf_op jit(solution)/shard_map/ppermute | solution.py:18
  273.3 15.3 %collective-permute-start.30 = (bf16[1,2,512,128]{3,2,1,0:T(8,128)(2,1)S(1)}, bf16[1,2,512,128]{3,2,1,0:T(8,128)(2,1)S(1)}, u32[]{:S(2)}, u32[]{:S(2)}) collective-permute-start(bf16[1,2,512,128]{3,2,1,0:T(8,128)(2,1)S(1)} %get-tuple-element.372), channel_id=1, source_target_pairs={{0,2},{2,0},{4,6},{6,4},{1,3},{3,1},{5,7},{7,5},{8,10},{10,8},{12,... | collective-permute-start | bytes 786440 | tf_op jit(solution)/shard_map/ppermute | solution.py:18
  280.4 50.5 %collective-permute-start.37 = (bf16[4,1,64,3072]{3,2,1,0:T(8,128)(2,1)}, bf16[4,1,64,3072]{3,2,1,0:T(8,128)(2,1)}, u32[]{:S(2)}, u32[]{:S(2)}) collective-permute-start(bf16[4,1,64,3072]{3,2,1,0:T(8,128)(2,1)} %get-tuple-element.398), channel_id=1, source_target_pairs={{0,4},{2,6},{4,0},{6,2},{1,5},{3,7},{5,1},{7,3},{8,12},{10,14},{12... | collective-permute-start | bytes 4718600 | tf_op jit(solution)/shard_map/ppermute | solution.py:18
  308.1 20.2 %collective-permute-start.33 = (bf16[4,2,64,1024]{3,2,1,0:T(8,128)(2,1)S(1)}, bf16[4,2,64,1024]{3,2,1,0:T(8,128)(2,1)S(1)}, u32[]{:S(2)}, u32[]{:S(2)}) collective-permute-start(bf16[4,2,64,1024]{3,2,1,0:T(8,128)(2,1)S(1)} %get-tuple-element.386), channel_id=1, source_target_pairs={{0,2},{2,0},{4,6},{6,4},{1,3},{3,1},{5,7},{7,5},{8,10},{10,8},{12,... | collective-permute-start | bytes 3145736 | tf_op jit(solution)/shard_map/ppermute | solution.py:18
  308.5 19.6 %collective-permute-start.34 = (bf16[1,1,128,768]{3,2,1,0:T(8,128)(2,1)S(1)}, bf16[1,1,128,768]{3,2,1,0:T(8,128)(2,1)S(1)}, u32[]{:S(2)}, u32[]{:S(2)}) collective-permute-start(bf16[1,1,128,768]{3,2,1,0:T(8,128)(2,1)S(1)} %bitcast.90), channel_id=1, source_target_pairs={{0,4},{2,6},{4,0},{6,2},{1,5},{3,7},{5,1},{7,3},{8,12},{10,14},{12... | collective-permute-start | bytes 589832 | tf_op jit(solution)/shard_map/ppermute | solution.py:18
  328.2 9.8 %collective-permute-start.36 = (bf16[2,1,128,768]{3,2,1,0:T(8,128)(2,1)S(1)}, bf16[2,1,128,768]{3,2,1,0:T(8,128)(2,1)S(1)}, u32[]{:S(2)}, u32[]{:S(2)}) collective-permute-start(bf16[2,1,128,768]{3,2,1,0:T(8,128)(2,1)S(1)} %get-tuple-element.396.refs_3_), channel_id=1, source_target_pairs={{0,2},{2,0},{4,6},{6,4},{1,3},{3,1},{5,7},{7,5},{8,10},{10,8},{12,... | collective-permute-start | bytes 1179656 | tf_op jit(solution)/shard_map/ppermute | solution.py:18
  334.3 31.0 %collective-permute-start.38 = (bf16[64,3072]{1,0:T(8,128)(2,1)S(1)}, bf16[64,3072]{1,0:T(8,128)(2,1)S(1)}, u32[]{:S(2)}, u32[]{:S(2)}) collective-permute-start(bf16[64,3072]{1,0:T(8,128)(2,1)S(1)} %get-tuple-element.412), channel_id=1, source_target_pairs={{8,0},{16,8},{24,16},{0,24},{9,1},{17,9},{25,17},{1,25},{10,2},{18... | collective-permute-start | bytes 1179656 | tf_op jit(solution)/shard_map/ppermute | solution.py:23
  334.4 36.6 %collective-permute-start.39 = (bf16[64,3072]{1,0:T(8,128)(2,1)S(1)}, bf16[64,3072]{1,0:T(8,128)(2,1)S(1)}, u32[]{:S(2)}, u32[]{:S(2)}) collective-permute-start(bf16[64,3072]{1,0:T(8,128)(2,1)S(1)} %get-tuple-element.413), channel_id=1, source_target_pairs={{16,0},{24,8},{0,16},{8,24},{17,1},{25,9},{1,17},{9,25},{18,2},{26... | collective-permute-start | bytes 1179656 | tf_op jit(solution)/shard_map/ppermute | solution.py:23
  336.1 35.0 %collective-permute-start.40 = (bf16[64,3072]{1,0:T(8,128)(2,1)S(1)}, bf16[64,3072]{1,0:T(8,128)(2,1)S(1)}, u32[]{:S(2)}, u32[]{:S(2)}) collective-permute-start(bf16[64,3072]{1,0:T(8,128)(2,1)S(1)} %get-tuple-element.414), channel_id=1, source_target_pairs={{24,0},{0,8},{8,16},{16,24},{25,1},{1,9},{9,17},{17,25},{26,2},{2,... | collective-permute-start | bytes 1179656 | tf_op jit(solution)/shard_map/ppermute | solution.py:23
  375.2 25.4 %collective-permute-start.44 = (bf16[4,2,64,2048]{3,2,1,0:T(8,128)(2,1)S(1)}, bf16[4,2,64,2048]{3,2,1,0:T(8,128)(2,1)}, u32[]{:S(2)}, u32[]{:S(2)}) collective-permute-start(bf16[4,2,64,2048]{3,2,1,0:T(8,128)(2,1)S(1)} %get-tuple-element.422), channel_id=1, source_target_pairs={{0,2},{2,0},{4,6},{6,4},{1,3},{3,1},{5,7},{7,5},{8,10},{10,8},{12,... | collective-permute-start | bytes 6291464 | tf_op jit(solution)/shard_map/ppermute | solution.py:18
  375.2 58.6 %collective-permute-start.32 = (bf16[1024,1024]{1,0:T(8,128)(2,1)S(1)}, bf16[1024,1024]{1,0:T(8,128)(2,1)}, u32[]{:S(2)}, u32[]{:S(2)}) collective-permute-start(bf16[1024,1024]{1,0:T(8,128)(2,1)S(1)} %get-tuple-element.382.refs_1_), channel_id=1, source_target_pairs={{0,1},{1,0},{2,3},{3,2},{4,5},{5,4},{6,7},{7,6},{8,9},{9,8},{10,11... | collective-permute-start | bytes 6291464 | tf_op jit(solution)/shard_map/ppermute | solution.py:28
  375.8 14.8 %collective-permute-start.35 = (bf16[4,1,64,1024]{3,2,1,0:T(8,128)(2,1)S(1)}, bf16[4,1,64,1024]{3,2,1,0:T(8,128)(2,1)S(1)}, u32[]{:S(2)}, u32[]{:S(2)}) collective-permute-start(bf16[4,1,64,1024]{3,2,1,0:T(8,128)(2,1)S(1)} %copy-done.72), channel_id=1, source_target_pairs={{0,4},{2,6},{4,0},{6,2},{1,5},{3,7},{5,1},{7,3},{8,12},{10,14},{12... | collective-permute-start | bytes 1572872 | tf_op jit(solution)/shard_map/ppermute | solution.py:18
  377.6 15.0 %collective-permute-start.45 = (bf16[1,1,512,128]{3,2,1,0:T(8,128)(2,1)S(1)}, bf16[1,1,512,128]{3,2,1,0:T(8,128)(2,1)S(1)}, u32[]{:S(2)}, u32[]{:S(2)}) collective-permute-start(bf16[1,1,512,128]{3,2,1,0:T(8,128)(2,1)S(1)} %copy-done.83), channel_id=1, source_target_pairs={{0,4},{2,6},{4,0},{6,2},{1,5},{3,7},{5,1},{7,3},{8,12},{10,14},{12... | collective-permute-start | bytes 393224 | tf_op jit(solution)/shard_map/ppermute | solution.py:18
  413.5 7.4 %collective-permute-start.46 = (bf16[1,2,512,128]{3,2,1,0:T(8,128)(2,1)}, bf16[1,2,512,128]{3,2,1,0:T(8,128)(2,1)}, u32[]{:S(2)}, u32[]{:S(2)}) collective-permute-start(bf16[1,2,512,128]{3,2,1,0:T(8,128)(2,1)} %get-tuple-element.431), channel_id=1, source_target_pairs={{0,2},{2,0},{4,6},{6,4},{1,3},{3,1},{5,7},{7,5},{8,10},{10,8},{12,... | collective-permute-start | bytes 786440 | tf_op jit(solution)/shard_map/ppermute | solution.py:18
  416.9 15.7 %collective-permute-start.41 = (bf16[64,1024]{1,0:T(8,128)(2,1)S(1)}, bf16[64,1024]{1,0:T(8,128)(2,1)S(1)}, u32[]{:S(2)}, u32[]{:S(2)}) collective-permute-start(bf16[64,1024]{1,0:T(8,128)(2,1)S(1)} %copy-done.85), channel_id=1, source_target_pairs={{8,0},{16,8},{24,16},{0,24},{9,1},{17,9},{25,17},{1,25},{10,2},{18... | collective-permute-start | bytes 393224 | tf_op jit(solution)/shard_map/ppermute | solution.py:23
  416.9 15.8 %collective-permute-start.42 = (bf16[64,1024]{1,0:T(8,128)(2,1)}, bf16[64,1024]{1,0:T(8,128)(2,1)S(1)}, u32[]{:S(2)}, u32[]{:S(2)}) collective-permute-start(bf16[64,1024]{1,0:T(8,128)(2,1)} %get-tuple-element.418), channel_id=1, source_target_pairs={{16,0},{24,8},{0,16},{8,24},{17,1},{25,9},{1,17},{9,25},{18,2},{26... | collective-permute-start | bytes 393224 | tf_op jit(solution)/shard_map/ppermute | solution.py:23
  418.1 14.6 %collective-permute-start.43 = (bf16[64,1024]{1,0:T(8,128)(2,1)}, bf16[64,1024]{1,0:T(8,128)(2,1)S(1)}, u32[]{:S(2)}, u32[]{:S(2)}) collective-permute-start(bf16[64,1024]{1,0:T(8,128)(2,1)} %get-tuple-element.419), channel_id=1, source_target_pairs={{24,0},{0,8},{8,16},{16,24},{25,1},{1,9},{9,17},{17,25},{26,2},{2,... | collective-permute-start | bytes 393224 | tf_op jit(solution)/shard_map/ppermute | solution.py:23
  421.0 52.1 %collective-permute-start.51 = (bf16[4,1,64,2048]{3,2,1,0:T(8,128)(2,1)}, bf16[4,1,64,2048]{3,2,1,0:T(8,128)(2,1)}, u32[]{:S(2)}, u32[]{:S(2)}) collective-permute-start(bf16[4,1,64,2048]{3,2,1,0:T(8,128)(2,1)} %copy-done.63), channel_id=1, source_target_pairs={{0,4},{2,6},{4,0},{6,2},{1,5},{3,7},{5,1},{7,3},{8,12},{10,14},{12... | collective-permute-start | bytes 3145736 | tf_op jit(solution)/shard_map/ppermute | solution.py:18
  432.6 23.5 %collective-permute-start.47 = (bf16[1,1,512,128]{3,2,1,0:T(8,128)(2,1)S(1)}, bf16[1,1,512,128]{3,2,1,0:T(8,128)(2,1)S(1)}, u32[]{:S(2)}, u32[]{:S(2)}) collective-permute-start(bf16[1,1,512,128]{3,2,1,0:T(8,128)(2,1)S(1)} %get-tuple-element.438), channel_id=1, source_target_pairs={{0,4},{2,6},{4,0},{6,2},{1,5},{3,7},{5,1},{7,3},{8,12},{10,14},{12... | collective-permute-start | bytes 393224 | tf_op jit(solution)/shard_map/ppermute | solution.py:18
  469.7 5.8 %collective-permute-start.50 = (bf16[4,2,64,512]{3,2,1,0:T(8,128)(2,1)S(1)}, bf16[4,2,64,512]{3,2,1,0:T(8,128)(2,1)S(1)}, u32[]{:S(2)}, u32[]{:S(2)}) collective-permute-start(bf16[4,2,64,512]{3,2,1,0:T(8,128)(2,1)S(1)} %get-tuple-element.573), channel_id=1, source_target_pairs={{0,2},{2,0},{4,6},{6,4},{1,3},{3,1},{5,7},{7,5},{8,10},{10,8},{12,... | collective-permute-start | bytes 1572872 | tf_op jit(solution)/shard_map/ppermute | solution.py:18
  469.8 11.5 %collective-permute-start.54 = (bf16[1,64,3072]{2,1,0:T(8,128)(2,1)S(1)}, bf16[1,64,3072]{2,1,0:T(8,128)(2,1)S(1)}, u32[]{:S(2)}, u32[]{:S(2)}) collective-permute-start(bf16[1,64,3072]{2,1,0:T(8,128)(2,1)S(1)} %bitcast.77), channel_id=1, source_target_pairs={{0,4},{2,6},{4,0},{6,2},{1,5},{3,7},{5,1},{7,3},{8,12},{10,14},{12... | collective-permute-start | bytes 1179656 | tf_op jit(solution)/shard_map/ppermute | solution.py:18
  471.6 25.2 %collective-permute-start.49 = (bf16[512,1024]{1,0:T(8,128)(2,1)S(1)}, bf16[512,1024]{1,0:T(8,128)(2,1)S(1)}, u32[]{:S(2)}, u32[]{:S(2)}) collective-permute-start(bf16[512,1024]{1,0:T(8,128)(2,1)S(1)} %copy-done.36), channel_id=1, source_target_pairs={{0,1},{1,0},{2,3},{3,2},{4,5},{5,4},{6,7},{7,6},{8,9},{9,8},{10,11... | collective-permute-start | bytes 3145736 | tf_op jit(solution)/shard_map/ppermute | solution.py:28
  481.6 20.4 %collective-permute-start.62 = (bf16[2,64,3072]{2,1,0:T(8,128)(2,1)S(1)}, bf16[2,64,3072]{2,1,0:T(8,128)(2,1)S(1)}, u32[]{:S(2)}, u32[]{:S(2)}) collective-permute-start(bf16[2,64,3072]{2,1,0:T(8,128)(2,1)S(1)} %get-tuple-element.475.refs_1_), channel_id=1, source_target_pairs={{0,2},{2,0},{4,6},{6,4},{1,3},{3,1},{5,7},{7,5},{8,10},{10,8},{12,... | collective-permute-start | bytes 2359304 | tf_op jit(solution)/shard_map/ppermute | solution.py:18
  481.7 13.9 %collective-permute-start.52 = (bf16[4,1,64,512]{3,2,1,0:T(8,128)(2,1)S(1)}, bf16[4,1,64,512]{3,2,1,0:T(8,128)(2,1)S(1)}, u32[]{:S(2)}, u32[]{:S(2)}) collective-permute-start(bf16[4,1,64,512]{3,2,1,0:T(8,128)(2,1)S(1)} %get-tuple-element.458), channel_id=1, source_target_pairs={{0,4},{2,6},{4,0},{6,2},{1,5},{3,7},{5,1},{7,3},{8,12},{10,14},{12... | collective-permute-start | bytes 786440 | tf_op jit(solution)/shard_map/ppermute | solution.py:18
  483.5 9.7 %collective-permute-start.53 = (bf16[1,64,1024]{2,1,0:T(8,128)(2,1)S(1)}, bf16[1,64,1024]{2,1,0:T(8,128)(2,1)S(1)}, u32[]{:S(2)}, u32[]{:S(2)}) collective-permute-start(bf16[1,64,1024]{2,1,0:T(8,128)(2,1)S(1)} %bitcast.95), channel_id=1, source_target_pairs={{0,4},{2,6},{4,0},{6,2},{1,5},{3,7},{5,1},{7,3},{8,12},{10,14},{12... | collective-permute-start | bytes 393224 | tf_op jit(solution)/shard_map/ppermute | solution.py:18
  493.3 12.9 %collective-permute-start.61 = (bf16[2,64,1024]{2,1,0:T(8,128)(2,1)S(1)}, bf16[2,64,1024]{2,1,0:T(8,128)(2,1)S(1)}, u32[]{:S(2)}, u32[]{:S(2)}) collective-permute-start(bf16[2,64,1024]{2,1,0:T(8,128)(2,1)S(1)} %get-tuple-element.474.refs_1_), channel_id=1, source_target_pairs={{0,2},{2,0},{4,6},{6,4},{1,3},{3,1},{5,7},{7,5},{8,10},{10,8},{12,... | collective-permute-start | bytes 786440 | tf_op jit(solution)/shard_map/ppermute | solution.py:18
  493.4 14.7 %collective-permute-start.58 = (bf16[64,2048]{1,0:T(8,128)(2,1)S(1)}, bf16[64,2048]{1,0:T(8,128)(2,1)S(1)}, u32[]{:S(2)}, u32[]{:S(2)}) collective-permute-start(bf16[64,2048]{1,0:T(8,128)(2,1)S(1)} %get-tuple-element.471), channel_id=1, source_target_pairs={{8,0},{16,8},{24,16},{0,24},{9,1},{17,9},{25,17},{1,25},{10,2},{18... | collective-permute-start | bytes 786440 | tf_op jit(solution)/shard_map/ppermute | solution.py:23
  495.6 23.4 %collective-permute-start.59 = (bf16[64,2048]{1,0:T(8,128)(2,1)S(1)}, bf16[64,2048]{1,0:T(8,128)(2,1)S(1)}, u32[]{:S(2)}, u32[]{:S(2)}) collective-permute-start(bf16[64,2048]{1,0:T(8,128)(2,1)S(1)} %get-tuple-element.472), channel_id=1, source_target_pairs={{16,0},{24,8},{0,16},{8,24},{17,1},{25,9},{1,17},{9,25},{18,2},{26... | collective-permute-start | bytes 786440 | tf_op jit(solution)/shard_map/ppermute | solution.py:23
  496.8 22.2 %collective-permute-start.60 = (bf16[64,2048]{1,0:T(8,128)(2,1)S(1)}, bf16[64,2048]{1,0:T(8,128)(2,1)S(1)}, u32[]{:S(2)}, u32[]{:S(2)}) collective-permute-start(bf16[64,2048]{1,0:T(8,128)(2,1)S(1)} %get-tuple-element.473), channel_id=1, source_target_pairs={{24,0},{0,8},{8,16},{16,24},{25,1},{1,9},{9,17},{17,25},{26,2},{2,... | collective-permute-start | bytes 786440 | tf_op jit(solution)/shard_map/ppermute | solution.py:23
  501.9 28.3 %collective-permute-start.48 = (bf16[512,1024]{1,0:T(8,128)(2,1)S(1)}, bf16[512,1024]{1,0:T(8,128)(2,1)S(1)}, u32[]{:S(2)}, u32[]{:S(2)}) collective-permute-start(bf16[512,1024]{1,0:T(8,128)(2,1)S(1)} %copy-done.32), channel_id=1, source_target_pairs={{0,1},{1,0},{2,3},{3,2},{4,5},{5,4},{6,7},{7,6},{8,9},{9,8},{10,11... | collective-permute-start | bytes 3145736 | tf_op jit(solution)/shard_map/ppermute | solution.py:28
  519.4 7.9 %collective-permute-start.65 = (bf16[64,256]{1,0:T(8,128)(2,1)S(1)}, bf16[64,256]{1,0:T(8,128)(2,1)S(1)}, u32[]{:S(2)}, u32[]{:S(2)}) collective-permute-start(bf16[64,256]{1,0:T(8,128)(2,1)S(1)} %get-tuple-element.571), channel_id=1, source_target_pairs={{0,1},{1,0},{2,3},{3,2},{4,5},{5,4},{6,7},{7,6},{8,9},{9,8},{10,11... | collective-permute-start | bytes 98312 | tf_op jit(solution)/shard_map/ppermute | solution.py:28
  521.0 8.2 %collective-permute-start.55 = (bf16[64,512]{1,0:T(8,128)(2,1)S(1)}, bf16[64,512]{1,0:T(8,128)(2,1)S(1)}, u32[]{:S(2)}, u32[]{:S(2)}) collective-permute-start(bf16[64,512]{1,0:T(8,128)(2,1)S(1)} %get-tuple-element.467), channel_id=1, source_target_pairs={{8,0},{16,8},{24,16},{0,24},{9,1},{17,9},{25,17},{1,25},{10,2},{18... | collective-permute-start | bytes 196616 | tf_op jit(solution)/shard_map/ppermute | solution.py:23
  521.0 8.3 %collective-permute-start.56 = (bf16[64,512]{1,0:T(8,128)(2,1)S(1)}, bf16[64,512]{1,0:T(8,128)(2,1)S(1)}, u32[]{:S(2)}, u32[]{:S(2)}) collective-permute-start(bf16[64,512]{1,0:T(8,128)(2,1)S(1)} %get-tuple-element.468), channel_id=1, source_target_pairs={{16,0},{24,8},{0,16},{8,24},{17,1},{25,9},{1,17},{9,25},{18,2},{26... | collective-permute-start | bytes 196616 | tf_op jit(solution)/shard_map/ppermute | solution.py:23
  523.9 6.3 %collective-permute-start.57 = (bf16[64,512]{1,0:T(8,128)(2,1)S(1)}, bf16[64,512]{1,0:T(8,128)(2,1)S(1)}, u32[]{:S(2)}, u32[]{:S(2)}) collective-permute-start(bf16[64,512]{1,0:T(8,128)(2,1)S(1)} %get-tuple-element.469), channel_id=1, source_target_pairs={{24,0},{0,8},{8,16},{16,24},{25,1},{1,9},{9,17},{17,25},{26,2},{2,... | collective-permute-start | bytes 196616 | tf_op jit(solution)/shard_map/ppermute | solution.py:23
  527.4 7.0 %collective-permute-start.66 = (bf16[1,64,2048]{2,1,0:T(8,128)(2,1)S(1)}, bf16[1,64,2048]{2,1,0:T(8,128)(2,1)S(1)}, u32[]{:S(2)}, u32[]{:S(2)}) collective-permute-start(bf16[1,64,2048]{2,1,0:T(8,128)(2,1)S(1)} %maximum_bitcast_fusion.refs_0_), channel_id=1, source_target_pairs={{0,4},{2,6},{4,0},{6,2},{1,5},{3,7},{5,1},{7,3},{8,12},{10,14},{12... | collective-permute-start | bytes 786440 | tf_op jit(solution)/shard_map/ppermute | solution.py:18
  542.8 14.7 %collective-permute-start.68 = (bf16[2,64,512]{2,1,0:T(8,128)(2,1)S(1)}, bf16[2,64,512]{2,1,0:T(8,128)(2,1)S(1)}, u32[]{:S(2)}, u32[]{:S(2)}) collective-permute-start(bf16[2,64,512]{2,1,0:T(8,128)(2,1)S(1)} %get-tuple-element.488.refs_1_), channel_id=1, source_target_pairs={{0,2},{2,0},{4,6},{6,4},{1,3},{3,1},{5,7},{7,5},{8,10},{10,8},{12,... | collective-permute-start | bytes 393224 | tf_op jit(solution)/shard_map/ppermute | solution.py:18
  (127 other events, 1061.6 us)

commit v4 on v3

--- a/solution.py
+++ b/solution.py
@@ -82,7 +82,7 @@
             out_specs=specs + anywhere((0,)),
             scratch_shapes=list(scratch_shapes),
             input_output_aliases=input_output_aliases or {},
-            compiler_params=pltpu.CompilerParams(vmem_limit_bytes=48 * 2**20),
+            compiler_params=pltpu.CompilerParams(vmem_limit_bytes=(60 if name.startswith("pack") else 18 if name in ("feed_forward", "outer") else 10) * 2**20),
             cost_estimate=pl.CostEstimate(flops=int(us * SCALE), bytes_accessed=1, transcendentals=0),
             name=name,
         )(*args, *waits)
@@ -96,7 +96,7 @@
     return next(blk for blk in (512, 256, 128) if cols % blk == 0)
 
 
-def join(parts, axis_new):
+def join(parts, axis_new, splits=1):
     if axis_new:
         parts = [part[None] for part in parts]
     counts = [part.shape[0] for part in parts]
@@ -108,28 +108,41 @@
         return pl.BlockSpec((count, *shape[:-1], blk), lambda j: (0,) * len(shape) + (j,))
 
     def body(*refs):
+        outs = refs[len(counts) :]
+        width = blk // len(outs)
         at = 0
         for ref, count in zip(refs, counts):
-            refs[-1][at : at + count] = ref[...]
+            for n, out in enumerate(outs):
+                out[at : at + count] = ref[..., n * width : (n + 1) * width]
             at += count
 
+    if splits > 1:
+        blk = cols
+        out = (sum(counts), *shape[:-1], cols // splits)
+        return launch(
+            body, out_shape=(jax.ShapeDtypeStruct(out, parts[0].dtype),) * splits, in_specs=[spec(count) for count in counts],
+            out_specs=[whole_spec(out)] * splits, name="join", us=3,
+        )(*parts)
     return launch(
         body, grid=(cols // blk,), out_shape=jax.ShapeDtypeStruct((sum(counts), *shape), parts[0].dtype),
         in_specs=[spec(count) for count in counts], out_specs=spec(sum(counts)), name="join", us=2,
     )(*parts)
 
 
-def send_near(own):
-    return [from_next(own, "fsdp", k) for k in range(1, lax.axis_size("fsdp"))]
+def send_near(own, ring=False):
+    got = []
+    for k in range(1, lax.axis_size("fsdp")):
+        got.append(from_next(got[-1] if ring and got else own, "fsdp", 1 if ring else k))
+    return got
 
 
 def far_bits():
     return list(reversed(context_bits()[1:]))
 
 
-def spread_far(held):
+def spread_far(held, splits=1):
     for bit in far_bits():
-        held = join([held, swap_context(held, bit)], False)
+        held = join([held, swap_context(held, bit)], False, splits if bit == far_bits()[-1] else 1)
     return held
 
 
@@ -137,31 +150,42 @@
     nc, part, cols = shard.shape
     nf = lax.axis_size("fsdp")
     offsets = [reverse_bits(m) for m in range(nc)][: nc // 2]
-    blk = column_block(cols)
-
-    def body(place_ref, shard_ref, mine_ref, other_ref, out_ref):
+    pieces = len(mine)
+    blk = column_block(cols // pieces)
+    steps = cols // pieces // blk
+
+    def body(place_ref, shard_ref, *refs):
+        out_ref = refs[-1]
         fi, ci = place_ref[0], place_ref[1]
         out_ref[fi] = shard_ref[...]
-        for k in range(1, nf):
-            z = lax.rem(fi + k, nf)
-            for m, off in enumerate(offsets):
-                at = m * (nf - 1) + k - 1
-                out_ref[z, lax.bitwise_xor(ci, off)] = mine_ref[at]
-                out_ref[z, lax.bitwise_xor(ci, off ^ 1)] = other_ref[at]
+
+        def fill(mine_ref, other_ref):
+            for k in range(1, nf):
+                z = lax.rem(fi + k, nf)
+                for m, off in enumerate(offsets):
+                    at = m * (nf - 1) + k - 1
+                    out_ref[z, lax.bitwise_xor(ci, off)] = mine_ref[at]
+                    out_ref[z, lax.bitwise_xor(ci, off ^ 1)] = other_ref[at]
+
+        for n in range(pieces):
+            pl.when(pl.program_id(0) // steps == n)(lambda n=n: fill(refs[n], refs[pieces + n]))
 
     def columns(*leading):
         return pl.BlockSpec((*leading, blk), lambda j: (0,) * len(leading) + (j,))
 
-    count = mine.shape[0]
+    def piece(n):
+        return pl.BlockSpec((count, part, blk), lambda j: (0, 0, jnp.clip(j - n * steps, 0, steps - 1)))
+
+    count = mine[0].shape[0]
     full = launch(
         body,
         grid=(cols // blk,),
         out_shape=jax.ShapeDtypeStruct((nf, nc, part, cols), shard.dtype),
-        in_specs=[SCALARS, columns(nc, part), columns(count, part), columns(count, part)],
+        in_specs=[SCALARS, columns(nc, part)] + [piece(n) for n in range(pieces)] * 2,
         out_specs=columns(nf, nc, part),
         name="place_rows",
         us=cols / 600,
-    )(place, shard, mine, other)
+    )(place, shard, *mine, *other)
     return full.reshape(nf * nc * part, cols)
 
 
@@ -244,13 +268,14 @@
     )(place, *spans, *extra)
 
 
-def outer(place, left, right, into, at, width):
+def outer(place, left, right, into, at, width, last=None):
     nf, nc = lax.axis_size("fsdp"), lax.axis_size("context")
     tokens, model = left.shape
     cols = right.shape[1]
     part = model // (nf * nc)
     blk = next(b for b in (512, 256, 128) if cols % b == 0 and at % b == 0)
     given = () if into is None else tuple(into)
+    lasts = () if last is None else (last,)
 
     def body(place_ref, left_ref, right_ref, *rest):
         away_ref, keep_ref, turned, made = rest[-4:]
@@ -260,6 +285,13 @@
             turned[...] = left_ref[...].T
 
         made[...] = nn_dot(turned[...], right_ref[...])
+        if lasts:
+
+            @pl.when(pl.program_id(0) == cols // blk - 1)
+            def _():
+                for top in range(0, model, part):
+                    made[top : top + 8, blk - 128 :] = rest[len(given)][...]
+
         mine = lax.rem(place_ref[1], 2)
         for z in range(nf):
             for x in range(nc // 2):
@@ -273,13 +305,14 @@
         body,
         grid=(cols // blk,),
         out_shape=(shape, shape),
-        in_specs=[SCALARS, whole_spec((tokens, model)), pl.BlockSpec((tokens, blk), lambda j: (0, j))] + anywhere(given),
+        in_specs=[SCALARS, whole_spec((tokens, model)), pl.BlockSpec((tokens, blk), lambda j: (0, j))]
+        + anywhere(given) + [whole_spec((8, 128)) for _ in lasts],
         out_specs=[spec, spec],
         input_output_aliases={3: 0, 4: 1} if given else {},
         scratch_shapes=[pltpu.VMEM((model, tokens), LOW), pltpu.VMEM((model, blk), F32)],
         name="outer",
         us=cols / 230,
-    )(place, left, right, *given)
+    )(place, left, right, *given, *lasts)
 
 
 def split_sum(place, keep, got, bit):
@@ -320,21 +353,56 @@
     )(place, keep, got)
 
 
-def sum_parts(parts, shared=()):
+def ring_step(got, own):
+    part, cols = own.shape
+    blk = column_block(cols)
+
+    def body(got_ref, own_ref, out_ref):
+        out_ref[...] = (got_ref[...].astype(F32) + own_ref[...].astype(F32)).astype(LOW)
+
+    spec = pl.BlockSpec((part, blk), lambda j: (0, j))
+    return launch(
+        body, grid=(cols // blk,), out_shape=jax.ShapeDtypeStruct((part, cols), LOW), in_specs=[spec, spec], out_specs=spec,
+        name="ring_step", us=1,
+    )(got, own)
+
+
+def share_columns(total, first, last):
+    mid = total[:, first:last]
+    mid = (mid.astype(F32) + swap_tensor(mid).astype(F32)).astype(LOW)
+    return jnp.concatenate([total[:, :first], mid, total[:, last:]], axis=1)
+
+
+def sum_parts(parts, shared=(), ordered=None):
     cols = parts[0].shape[1]
     blk = column_block(cols)
+    given = () if ordered is None else (ordered,)
+    nf = len(parts)
 
     def body(*refs):
-        total = refs[0][...].astype(F32)
-        for ref in refs[1:-1]:
+        some = refs[len(given) : -1]
+        total = some[0][...].astype(F32)
+        for ref in some[1:]:
             total = total + ref[...].astype(F32)
         refs[-1][...] = total.astype(LOW)
+        if given:
+
+            @pl.when(pl.program_id(0) == cols // blk - 1)
+            def _():
+                total = None
+                for z in range(nf):
+                    k = lax.rem(z + nf - refs[0][0], nf)
+                    value = some[0][:, blk - 128 :].astype(F32)
+                    for n in range(1, nf):
+                        value = jnp.where(k == n, some[n][:, blk - 128 :].astype(F32), value)
+                    total = value if total is None else total + value
+                refs[-1][:, blk - 128 :] = total.astype(LOW)
 
     spec = pl.BlockSpec((parts[0].shape[0], blk), lambda j: (0, j))
     total = launch(
-        body, grid=(cols // blk,), out_shape=jax.ShapeDtypeStruct(parts[0].shape, LOW), in_specs=[spec] * len(parts),
-        out_specs=spec, name="sum_parts", us=1.3,
-    )(*parts)
+        body, grid=(cols // blk,), out_shape=jax.ShapeDtypeStruct(parts[0].shape, LOW),
+        in_specs=[SCALARS] * len(given) + [spec] * nf, out_specs=spec, name="sum_parts", us=1.3,
+    )(*given, *parts)
     if shared:
         mid = total[:, shared[0] : shared[1]]
         mid = (mid.astype(F32) + swap_tensor(mid).astype(F32)).astype(LOW)
@@ -357,21 +425,6 @@
         away, keep = split_sum(place, keep, got, bit)
         got = swap_context(away, bit)
     return keep, got
-
-
-def all_sum(x):
-    for bit in context_bits():
-        x = x + swap_context(x, bit)
-    size, bit = lax.axis_size("fsdp"), 1
-    while bit < size:
-        x = x + lax.ppermute(x, "fsdp", [(i, i ^ bit) for i in range(size)])
-        bit *= 2
-    return x
-
-
-def tensor_sum(x):
-    low = lax.reduce_precision(x, 8, 7).astype(LOW)
-    return low.astype(F32) + swap_tensor(low).astype(F32)
 
 
 def nt_dot(left, right):
@@ -1043,7 +1096,7 @@
             out_ref[:, start:] = jnp.zeros((rows, cols - start), LOW)
         for n, (_, at, width, first, turned) in zip(where, parts):
             if turned:
-                out_ref[:, at : at + width] = refs[n][...].T
+                out_ref[:, at : at + width] = refs[n][...].astype(F32).T.astype(LOW)
             else:
                 out_ref[:, at : at + width] = refs[n][:, first : first + width]
         own_ref[...] = out_ref[pl.ds(pl.multiple_of(place_ref[1] * (rows // nc), rows // nc), rows // nc), :]
@@ -1056,7 +1109,11 @@
 
 
 def emit(place, held, got, outs, name):
-    half, part, cols = held.shape
+    half, part, _ = held.shape
+    low = min(first for pieces, _ in outs for first, _ in pieces)
+    low -= low % 128
+    cols = max(first + width for pieces, _ in outs for first, width in pieces) - low
+    cols += -cols % 128
     nc = 2 * half
     rows = nc * part
     offsets = [reverse_bits(m) for m in range(nc)][:half]
@@ -1068,14 +1125,14 @@
         for m, off in enumerate(offsets):
             for ref, bit in ((held_ref, 0), (got_ref, 1)):
                 at = pl.multiple_of(lax.bitwise_xor(ci, off ^ bit) * part, part)
-                whole[pl.ds(at, part), :] = ref[m].astype(F32)
+                whole[pl.ds(at, part), :] = ref[m, :, low : low + cols].astype(F32)
         for ref, (pieces, turned) in zip(refs, outs):
             to = 0
             for first, width in pieces:
                 if turned:
-                    ref[to : to + width, :] = whole[:, first : first + width].T
+                    ref[to : to + width, :] = whole[:, first - low : first - low + width].T
                 else:
-                    ref[:, to : to + width] = whole[:, first : first + width]
+                    ref[:, to : to + width] = whole[:, first - low : first - low + width]
                 to += width
 
     shapes = [(width, rows) if turned else (rows, width) for width, (_, turned) in zip(widths, outs)]
@@ -1174,9 +1231,9 @@
     two = 2 * head_dim
     first, own_first = pack(
         place,
-        [(w_query, 0, q_dim, 0, False), (key_matrix, at_k, kv_dim, 0, False), (value_matrix, at_v, kv_dim, 0, False),
-         (w_bproj, at_b, state_dim, 0, False), (w_cproj, at_c, state_dim, 0, False), (w_dt, at_dt, heads, 0, False),
-         (jnp.stack([mixer_gain, ffn_gain], axis=1), at_gain, 2, 0, False)],
+        [(w_query, 0, q_dim, 0, False), (key_matrix.T, at_k, kv_dim, 0, True), (value_matrix.T, at_v, kv_dim, 0, True),
+         (w_bproj, at_b, state_dim, 0, False), (w_cproj, at_c, state_dim, 0, False), (w_dt.T, at_dt, heads, 0, True),
+         (jnp.stack([mixer_gain, ffn_gain]), at_gain, 2, 0, True)],
         first_width, "pack_first")
     near_first = send_near(own_first)
     second, own_second = pack(
@@ -1199,56 +1256,59 @@
     width = q_dim + ssm_dim
 
     def placed(shard, mine, other):
-        return place_rows(place, shard.reshape(nc, -1, shard.shape[1]), mine, other)
+        return place_rows(place, shard.reshape(nc, -1, shard.shape[1]), [mine], [other])
 
     held_first = join(near_first, True)
-    wait_for(held_first)
     near_second = send_near(own_second)
+    wait_for(*near_second)
     held_first = spread_far(held_first)
     core_first = swap_context(held_first, 1)
+    held_second = join(near_second, True)
     first = placed(first, held_first, core_first)
-    wait_for(*near_second)
     n1, q, kv, b, c, per_head, gains = project(place, lens, tokens, first, aux, q_dim, kv_dim, state_dim, pairs)
     kv = kv.reshape(1, units, block_len, 2 * kv_dim)
     kv_far = [swap_context(kv, bit) for bit in far_bits()[:1]]
-    held_second = join(near_second, True)
     near_third = send_near(own_third)
+    near_fourth = send_near(own_fourth, True)
+    wait_for(*near_third)
     kv_held = join([kv, *kv_far], False)
     for bit in far_bits()[1:]:
         kv_held = join([kv_held, swap_context(kv_held, bit)], False)
-    kv_all = place_blocks(place, kv_held, swap_context(kv_held, 1))
-    wait_for(*near_third)
-    og, lse = None, [None] * units
-    og, lse[0] = attention_forward(0, place, lens, q, kv_all, og, width)
-    near_fourth = send_near(own_fourth)
+    kv_core = swap_context(kv_held, 1)
     held_second = spread_far(held_second)
+    core_second = swap_context(held_second, 1)
+    kv_all = place_blocks(place, kv_held, kv_core)
     held_third = join(near_third, True)
-    second = placed(second, held_second, swap_context(held_second, 1))
+    wait_for(near_fourth[0])
+    second = placed(second, held_second, core_second)
     zx = project_mixer(n1, second)
     span = join([mamba_state(u, per_head, b, zx) for u in range(units)], True)[None]
     span_far = [swap_context(span, bit) for bit in far_bits()[:1]]
-    held_fourth = join(near_fourth, True)
-    for u in range(1, units):
-        og, lse[u] = attention_forward(u, place, lens, q, kv_all, og, width)
+    og, lse = None, [None] * units
+    wait_for(*near_fourth[1:2])
+    og, lse[0] = attention_forward(0, place, lens, q, kv_all, og, width)
     span = join([span, *span_far], False)
     for bit in far_bits()[1:]:
         span = join([span, swap_context(span, bit)], False)
     spans = (span, swap_context(span, 1))
+    wait_for(*near_fourth[2:])
     held_third = spread_far(held_third)
     core_third = swap_context(held_third, 1)
+    held_fourth = join(near_fourth, True)
     state = chain_states(place, spans, state_dim)
     third = placed(third, held_third, core_third)
     og, y_u = mamba_forward(0, place, lens, per_head, zx, b, c, state, skip_row, og, q_dim)
     y, ours = [y_u], [mixer_out(0, og, third, block_len)]
     theirs = [swap_tensor(ours[0])]
-    held_fourth = spread_far(held_fourth)
-    core_fourth = swap_context(held_fourth, 1)
     for u in range(1, units):
+        og, lse[u] = attention_forward(u, place, lens, q, kv_all, og, width)
         og, y_u = mamba_forward(u, place, lens, per_head, zx, b, c, state, skip_row, og, q_dim)
         y.append(y_u)
         ours.append(mixer_out(u, og, third, block_len))
         theirs.append(swap_tensor(ours[u]))
-    fourth = placed(fourth, held_fourth, core_fourth)
+    held_fourth = spread_far(held_fourth, 3)
+    fourth = place_rows(
+        place, fourth.reshape(nc, -1, fourth.shape[1]), held_fourth, [swap_context(arr, 1) for arr in held_fourth])
 
     stacked, dn2, dn2_theirs = None, [], []
     for u in range(units):
@@ -1303,26 +1363,22 @@
     g_gain_two = g_gain_two + terms
     ff = feed_forward_out(f, fourth)
     ff_theirs = swap_tensor(ff)
-    wide = q_dim + ssm_dim
-    away, keep_third = outer(place, dm, og, None, 0, wide)
-    got_third = swap_context(away, 1)
+    at_zx = q_dim + ssm_dim
+    at_rest = at_zx + 2 * ssm_dim
+    wide = wide_second = at_rest + 2 * state_dim + 256
+    pair_second = outer(place, dm, og, None, 0, wide)
     for u in range(units):
         if u == units - 1:
             pair = close_states(u)
-            keep_third, got_third = reduce_far(place, keep_third, got_third, bits)
             parts_fourth = to_owners(keep_fourth, got_fourth)
             d_span.append(chain_states(place, spans, state_dim, pair, u)[0])
         *d_second, grads_u = mamba_backward(
             u, place, lens, per_head, zx, y[u], dog[u], q_dim, b, c, state, d_span[u], skip_row, aux, d_second)
         head_grads = head_grads + grads_u
     dzx, dbc = d_second
-    at_rest = 2 * ssm_dim
-    wide = at_rest + dbc.shape[1]
-    pair = outer(place, n1, dzx, None, 0, wide)
-    wait_for(*parts_fourth)
-    away, keep_second = outer(place, n1, dbc, pair, at_rest, wide)
+    pair_second = outer(place, n1, dzx, pair_second, at_zx, wide)
+    away, keep_second = outer(place, n1, dbc, pair_second, at_rest, wide)
     got_second = swap_context(away, 1)
-    parts_third = to_owners(keep_third, got_third)
     parts, parts_theirs, g_gain_one, dqkv = [None] * units, [None] * units, 0.0, None
 
     def close_backward(u, dqkv):
@@ -1333,61 +1389,70 @@
     for u in range(units - 1):
         dqkv, terms = close_backward(u, dqkv)
         g_gain_one = g_gain_one + terms
-    g_fourth = sum_parts(parts_fourth)
     keep_second, got_second = reduce_far(place, keep_second, got_second, bits)
     kept = attend_back(units - 1)
-    head_grads = all_sum(head_grads[:heads, :3])
+    g_fourth = sum_parts(parts_fourth)
     dkv[units - 1] = reduce_far(place, *kept, bits)
-    g_third = sum_parts(parts_third)
+    own_second, *below = split_fsdp(place, keep_second, got_second)
+    chunks = below[::-1]
+    ring = from_next(chunks[0], "fsdp")
     layer_out = close_forward(h1, ff, ff_theirs)
+    fourth_held = spread_far(g_fourth[None])
+    fourth_core = swap_context(fourth_held, 1)
+    nf = lax.axis_size("fsdp")
+    for k in range(1, nf - 2):
+        ring = from_next(ring_step(ring, chunks[k]), "fsdp")
     dqkv, terms = close_backward(units - 1, dqkv)
     g_gain_one = g_gain_one + terms
-    g_gains = jnp.pad(jnp.stack([g_gain_one, g_gain_two], axis=1).astype(LOW), ((0, 0), (0, 126)))
+    nf = lax.axis_size("fsdp")
+    part = model_dim // (nf * nc)
+    head_grads = jnp.tile(jnp.pad(head_grads[:16, :3], ((0, part - 16), (0, 0))), (nf * nc, 1))
+    g_gains = jnp.concatenate([jnp.stack([g_gain_one, g_gain_two], axis=1), head_grads], axis=1).astype(LOW)
+    g_gains = jnp.pad(g_gains, ((0, 0), (0, 123)))
     wide = at_b + 128
     away, keep_first = outer(place, n1, dqkv, None, 0, wide)
-    g_gains = g_gains.reshape((lax.axis_size("fsdp"), nc // 2, 2, -1, 128))
+    g_gains = g_gains.reshape((nf, nc // 2, 2, -1, 128))
     mine = ci % 2
     away = away.at[..., at_b:].set(lax.dynamic_index_in_dim(g_gains, 1 - mine, 2, keepdims=False))
     keep_first = keep_first.at[..., at_b:].set(lax.dynamic_index_in_dim(g_gains, mine, 2, keepdims=False))
     got_first = swap_context(away, 1)
-    parts_second = to_owners(keep_second, got_second)
-    keep_first, got_first = reduce_far(place, keep_first, got_first, bits)
-    fourth_pair = share(g_fourth)
-    third_pair = share(g_third)
-    parts_first = to_owners(keep_first, got_first)
+    if nf > 2:
+        ring = from_next(ring_step(ring, chunks[nf - 2]), "fsdp")
     input_grads = None
     for u in range(units - 1):
         input_grads = finish(u, tokens, parts[u], parts_theirs[u], gains, dh[u], input_grads)
+    keep_first, got_first = reduce_far(place, keep_first, got_first, bits)
 
     def columns(first, width, turned=False):
         return [(first, width)], turned
 
-    def in_turns(which, width, total):
-        return [(width * (2 * i + which), width) for i in range(total // width)], False
+    def in_turns(which, width, total, first=0):
+        return [(first + width * (2 * i + which), width) for i in range(total // width)], False
 
     g_gate, g_up, g_down = emit(
-        place, *fourth_pair,
+        place, fourth_held, fourth_core,
         [in_turns(0, ff_blk, ff_dim), in_turns(1, ff_blk, ff_dim), columns(2 * ff_dim, ff_dim, True)], "emit_fourth")
-    g_attn, g_mixer = emit(place, *third_pair, [columns(0, q_dim, True), columns(q_dim, ssm_dim, True)], "emit_third")
-    g_second = sum_parts(parts_second, (at_rest, at_rest + 2 * state_dim))
-    g_first = sum_parts(parts_first)
-    lane = jnp.arange(128)[None]
-    g_gains = g_first[:, at_b:]
-    g_gains = jnp.where(lane == 0, (g_gains.astype(F32) + swap_tensor(g_gains).astype(F32)).astype(LOW), g_gains)
-    g_first = jnp.concatenate([g_first[:, :at_b], g_gains], axis=1)
+    parts_first = to_owners(keep_first, got_first)
+    g_second = share_columns(ring_step(ring, own_second), at_rest, at_rest + 2 * state_dim)
     u = units - 1
     input_grads = finish(u, tokens, parts[u], parts_theirs[u], gains, dh[u], input_grads)
-    g_z, g_x, g_b, g_c, g_dt = emit(
-        place, *share(g_second),
-        [in_turns(0, two, ssm_dim), in_turns(1, two, ssm_dim), columns(at_rest, state_dim),
-         columns(at_rest + state_dim, state_dim), columns(at_rest + 2 * state_dim, heads)], "emit_second")
+    g_first = share_columns(sum_parts(parts_first, (), place), at_b, at_b + 1)
+    last_held = spread_far(jnp.concatenate([g_second, g_first], axis=1)[None])
+    last_core = swap_context(last_held, 1)
+    at_last = wide_second
+    outs = [
+        columns(0, q_dim, True), columns(q_dim, ssm_dim, True), in_turns(0, two, ssm_dim, at_zx), in_turns(1, two, ssm_dim, at_zx),
+        columns(at_rest, state_dim), columns(at_rest + state_dim, state_dim), columns(at_rest + 2 * state_dim, heads, True)]
+    g_attn, g_mixer, g_z, g_x, g_b, g_c, g_dt = emit(place, last_held, last_core, outs, "emit_second")
     g_q, g_k, g_v, g_gains = emit(
-        place, *share(g_first),
-        [columns(0, q_dim), columns(at_k, kv_dim), columns(at_v, kv_dim), columns(at_b, 128)], "emit_first")
+        place, last_held, last_core,
+        [columns(at_last, q_dim), columns(at_last + at_k, kv_dim, True), columns(at_last + at_v, kv_dim, True),
+         columns(at_last + at_b, 16, True)], "emit_first")
+    head_grads = g_gains[2:5]
     shape = (micro_count, seq_count, block_len, model_dim)
     return (
-        layer_out.reshape(shape), input_grads.reshape(shape), g_gains[:, 0], g_q, g_k, g_v, g_z, g_x, g_b, g_c, g_dt,
-        head_grads[:, 0], head_grads[:, 1], head_grads[:, 2], g_attn, g_mixer, g_gains[:, 1], g_gate, g_up, g_down,
+        layer_out.reshape(shape), input_grads.reshape(shape), g_gains[0], g_q, g_k.T, g_v.T, g_z, g_x, g_b, g_c, g_dt.T,
+        head_grads[0, :heads], head_grads[1, :heads], head_grads[2, :heads], g_attn, g_mixer, g_gains[1], g_gate, g_up, g_down,
     )
 
 

time: 568 us -> 464 us (0.82)
  starting transfers between devices: 114 us -> 71.7 us
  waiting for transfers between devices: 157 us -> 123 us
  Pallas kernels: 248 us -> 223 us
    ppermute x38 -> x32, starting transfers between devices: 65 us -> 32.9 us  [swap_context(): return lax.ppermute(x, 'context', [(i, i ^ bit) for i in range(size)])]
    ppermute x38 -> x32, waiting for transfers between devices: 76.3 us -> 44.5 us  [swap_context(): return lax.ppermute(x, 'context', [(i, i ^ bit) for i in range(size)])]
    pallas_call x79 -> x75, Pallas kernels: 248 us -> 223 us  [call(): pl.pallas_call(run, grid=grid, out_shape=outs + (jax.ShapeDtypeStruct((8,...]
    unnamed x243 -> x190, local copies, waits for them, and re-layouts: 35.6 us -> 30.2 us
    ppermute x24 -> x21, starting transfers between devices: 33 us -> 28.3 us  [from_next(): return lax.ppermute(x, axis, [((i + step) % size, i) for i in range(size)])]
    ppermute x24 -> x21, waiting for transfers between devices: 58.3 us -> 57.4 us  [from_next(): return lax.ppermute(x, axis, [((i + step) % size, i) for i in range(size)])]
  transfers between devices with their start and end apart: 73 -> 62, of which waited for: 31 -> 26; matrix products, arithmetic and copies ran while one was open for 1% -> 0% of each run, Pallas kernels for 40% -> 41%
where the time goes in v4:
time: 464 us; the launch traced here: 455 us
  Pallas kernels  223 us (48%)
  waiting for transfers between devices  123 us (27%)
  starting transfers between devices  71.7 us (15%)
  local copies, waits for them, and re-layouts  33.6 us (7%)
    pallas_call x75, Pallas kernels, call(): pl.pallas_call(run, grid=grid, out_shape=outs + (jax.ShapeDtypeStruct((8,...  223 us
    ppermute x21, waiting for transfers between devices, from_next(): return lax.ppermute(x, axis, [((i + step) % size, i) for i in range(size)])  57.4 us
    ppermute x32, waiting for transfers between devices, swap_context(): return lax.ppermute(x, 'context', [(i, i ^ bit) for i in range(size)])  44.5 us
    ppermute x32, starting transfers between devices, swap_context(): return lax.ppermute(x, 'context', [(i, i ^ bit) for i in range(size)])  32.9 us
    unnamed x190, local copies, waits for them, and re-layouts  30.2 us
    ppermute x21, starting transfers between devices, from_next(): return lax.ppermute(x, axis, [((i + step) % size, i) for i in range(size)])  28.3 us
    ppermute x9, waiting for transfers between devices, swap_tensor(): return lax.ppermute(x, 'tensor', [(i, (i + 1) % size) for i in range(size)])  20.9 us
    ppermute x9, starting transfers between devices, swap_tensor(): return lax.ppermute(x, 'tensor', [(i, (i + 1) % size) for i in range(size)])  10.5 us
  transfers between devices with their start and end apart: 62, of which 26 were waited for; matrix products, arithmetic and copies ran while one was open for 0% of the time, Pallas kernels for 41%

profile of v4, /device:TPU:0, one launch (start us, length us, event | category | flops | bytes accessed | tf_op | source)
XLA Modules:
  0.0 455.1 jit_solution(1385590407672308042)
XLA Ops:
  5.1 3.0 collective-permute-start.2
  11.2 2.2 pack_second.1
  15.5 2.9 pack_fourth.1
  25.0 4.0 collective-permute-done.4.refs_3_
  29.0 11.2 %collective-permute-done.5.refs_4_ = bf16[64,1536]{1,0:T(8,128)(2,1)S(1)} collective-permute-done((bf16[64,1536]{1,0:T(8,128)(2,1)S(1)}, bf16[64,1536]{1,0:T(8,128)(2,1)S(1)}, u32[]{:S(2)}, u32[]{:S(2)}) %collective-permute-start.5) | collective-permute-done | bytes 196640 | tf_op jit(solution)/shard_map/ppermute | solution.py:23
  47.7 5.1 %project.1 = (bf16[1024,1024]{1,0:T(8,128)(2,1)S(1)}, bf16[1024,256]{1,0:T(8,128)(2,1)S(1)}, bf16[1024,128]{1,0:T(8,128)(2,1)S(1)}, bf16[1024,128]{1,0:T(8,128)(...) custom-call(s32[2]{0:T(128)S(1)} %copy-done.46, ...), custom_call_target="tpu_custom_call" | custom-call | flops 2600000000 | bytes 1 | tf_op jit(solution)/shard_map/project/pallas_call | solution.py:77
  55.5 2.2 collective-permute-start.11
  60.2 9.4 %collective-permute-done.11.refs_4_ = bf16[64,1024]{1,0:T(8,128)(2,1)S(1)} collective-permute-done((bf16[64,1024]{1,0:T(8,128)(2,1)S(1)}, bf16[64,1024]{1,0:T(8,128)(2,1)S(1)}, u32[]{:S(2)}, u32[]{:S(2)}) %collective-permute-start.11) | collective-permute-done | bytes 131104 | tf_op jit(solution)/shard_map/ppermute | solution.py:23
  70.6 11.0 %collective-permute-done.15.refs_5_ = bf16[64,3072]{1,0:T(8,128)(2,1)S(1)} collective-permute-done((bf16[64,3072]{1,0:T(8,128)(2,1)S(1)}, bf16[64,3072]{1,0:T(8,128)(2,1)S(1)}, u32[]{:S(2)}, u32[]{:S(2)}) %collective-permute-start.15) | collective-permute-done | bytes 393248 | tf_op jit(solution)/shard_map/ppermute | solution.py:23
  86.1 4.2 project_mixer.1
  90.3 2.5 mamba_state.4
  92.9 2.5 mamba_state.5
  97.9 3.3 attention_forward.2
  101.8 7.0 %collective-permute-done.16.refs_1_ = bf16[1,2,144,768]{3,2,1,0:T(8,128)(2,1)S(1)} collective-permute-done((bf16[1,2,144,768]{3,2,1,0:T(8,128)(2,1)S(1)}, bf16[1,2,144,768]{3,2,1,0:T(8,128)(2,1)S(1)}, u32[]{:S(2)}, u32[]{:S(2)}) %collective-permute-start.16) | collective-permute-done | bytes 442400 | tf_op jit(solution)/shard_map/ppermute | solution.py:18
  109.2 6.2 %collective-permute-done.20.refs_1_ = bf16[3,64,1024]{2,1,0:T(8,128)(2,1)S(1)} collective-permute-done((bf16[3,64,1024]{2,1,0:T(8,128)(2,1)S(1)}, bf16[3,64,1024]{2,1,0:T(8,128)(2,1)S(1)}, u32[]{:S(2)}, u32[]{:S(2)}) %collective-permute-start.20) | collective-permute-done | bytes 393248 | tf_op jit(solution)/shard_map/ppermute | solution.py:18
  120.7 2.5 chain_states.3
  124.9 7.0 %mamba_forward.2 = (bf16[1024,1024]{1,0:T(8,128)(2,1)S(1)}, f32[512,768]{1,0:T(8,128)S(1)}, f32[8,128]{1,0:T(8,128)S(1)}) custom-call(s32[2]{0:T(128)S(1)} %copy-done.46, s32[2,4]{1,0:T(2,128)S(1)} %bitcast.123, f32[2,6,8,512]{3,2,1,0:T(8,128)S(1)} %get-tuple-element.280.refs_0_.refs_2_, ...), custom_call_target="tpu_custom_call", output_to_operand_aliasing={{0}: (8, {})} | custom-call | flops 3000000000 | bytes 1 | tf_op jit(solution)/shard_map/mamba_forward/pallas_call | solution.py:77
  135.1 3.3 attention_forward.3
  138.4 7.0 %mamba_forward.3 = (bf16[1024,1024]{1,0:T(8,128)(2,1)S(1)}, f32[512,768]{1,0:T(8,128)S(1)}, f32[8,128]{1,0:T(8,128)S(1)}) custom-call(s32[2]{0:T(128)S(1)} %copy-done.46, s32[2,4]{1,0:T(2,128)S(1)} %bitcast.125, f32[2,6,8,512]{3,2,1,0:T(8,128)S(1)} %get-tuple-element.280.refs_0_.refs_2_, ...), custom_call_target="tpu_custom_call", output_to_operand_aliasing={{0}: (8, {})} | custom-call | flops 3000000000 | bytes 1 | tf_op jit(solution)/shard_map/mamba_forward/pallas_call | solution.py:77
  153.7 2.4 place_rows.7
  156.1 3.4 collective-permute-done.27.refs_2_
  159.5 10.9 %feed_forward.2 = (f32[1024,1024]{1,0:T(8,128)S(1)}, bf16[1024,1024]{1,0:T(8,128)(2,1)S(1)}, bf16[1024,1024]{1,0:T(8,128)(2,1)S(1)}, bf16[1024,2048]{1,0:T(8,128...) custom-call(bf16[1024,1024]{1,0:T(8,128)(2,1)S(1)} %bitcast.74, ...), custom_call_target="tpu_custom_call" | custom-call | flops 5600000000 | bytes 1 | tf_op jit(solution)/shard_map/feed_forward/pallas_call | solution.py:77
  172.0 10.0 %collective-permute-done.22.refs_2_ = bf16[512,1024]{1,0:T(8,128)(2,1)S(1)} collective-permute-done((bf16[512,1024]{1,0:T(8,128)(2,1)S(1)}, bf16[512,1024]{1,0:T(8,128)(2,1)S(1)}, u32[]{:S(2)}, u32[]{:S(2)}) %collective-permute-start.22) | collective-permute-done | bytes 1048608 | tf_op jit(solution)/shard_map/ppermute | solution.py:28
  182.0 11.8 %feed_forward.3 = (f32[1024,1024]{1,0:T(8,128)S(1)}, bf16[1024,1024]{1,0:T(8,128)(2,1)S(1)}, bf16[1024,1024]{1,0:T(8,128)(2,1)S(1)}, bf16[1024,2048]{1,0:T(8,128...) custom-call(bf16[1024,1024]{1,0:T(8,128)(2,1)S(1)} %bitcast.75, ...), custom_call_target="tpu_custom_call", output_to_operand_aliasing={{0}: (7, {}), {1}: (8, {}), {2}: (9, {}), {3}: (10, {})} | custom-call | flops 5600000000 | bytes 1 | tf_op jit(solution)/shard_map/feed_forward/pallas_call | solution.py:77
  193.8 7.5 %outer.6 = (bf16[4,2,64,3072]{3,2,1,0:T(8,128)(2,1)S(1)}, bf16[4,2,64,3072]{3,2,1,0:T(8,128)(2,1)S(1)}, f32[8,128]{1,0:T(8,128)S(1)}) custom-call(s32[2]{0:T(128)S(1)} %copy-done.46, bf16[1024,1024]{1,0:T(8,128)(2,1)S(1)} %get-tuple-element.349.refs_1_, bf16[1024,2048]{1,0:T(8,128)(2,1)S(1)} %get-tuple-element.350.refs_2_, ...), custom_call_target="tpu_custom_call" | custom-call | flops 3561739008 | bytes 1 | tf_op jit(solution)/shard_map/outer/pallas_call | solution.py:77
  201.3 2.5 collective-permute-done.29.refs_6_.refs_2_
  203.8 4.7 %outer.7 = (bf16[4,2,64,3072]{3,2,1,0:T(8,128)(2,1)S(1)}, bf16[4,2,64,3072]{3,2,1,0:T(8,128)(2,1)S(1)}, f32[8,128]{1,0:T(8,128)S(1)}) custom-call(s32[2]{0:T(128)S(1)} %copy-done.46, bf16[1024,1024]{1,0:T(8,128)(2,1)S(1)} %bitcast.86, bf16[1024,1024]{1,0:T(8,128)(2,1)S(1)} %get-tuple-element.346.refs_2_.refs_0_, ...), custom_call_target="tpu_custom_call", output_to_operand_aliasing={{0}: (3, {}), {1}: (4, {})} | custom-call | flops 1780869504 | bytes 1 | tf_op jit(solution)/shard_map/outer/pallas_call | solution.py:77
  210.1 2.2 middle_backward.2
  215.6 5.2 %attention_backward.2 = (bf16[512,256]{1,0:T(8,128)(2,1)S(1)}, bf16[1,2,512,128]{3,2,1,0:T(8,128)(2,1)S(1)}, bf16[1,2,512,128]{3,2,1,0:T(8,128)(2,1)S(1)}, f32[8,128]{1,0:T(8,128)S(1)}) custom-call(s32[2]{0:T(128)S(1)} %copy-done.46, s32[2,4]{1,0:T(2,128)S(1)} %bitcast.126, bf16[1024,256]{1,0:T(8,128)(2,1)S(1)} %copy-done.84, ...), custom_call_target="tpu_custom_call" | custom-call | flops 6800000000 | bytes 1 | tf_op jit(solution)/shard_map/attention_backward/pallas_call | solution.py:77
  221.5 3.6 collective-permute-start.31
  227.2 8.9 %collective-permute-start.37 = (bf16[4,1,64,3072]{3,2,1,0:T(8,128)(2,1)S(1)}, bf16[4,1,64,3072]{3,2,1,0:T(8,128)(2,1)S(1)}, u32[]{:S(2)}, u32[]{:S(2)}) collective-permute-start(bf16[4,1,64,3072]{3,2,1,0:T(8,128)(2,1)S(1)} %get-tuple-element.386), channel_id=1, source_target_pairs={{0,4},{2,6},{4,0},{6,2},{1,5},{3,7},{5,1},{7,3},{8,12},{10,14},{12... | collective-permute-start | bytes 4718600 | tf_op jit(solution)/shard_map/ppermute | solution.py:18
  236.7 2.2 chain_states.4
  239.0 3.4 middle_backward.3
  244.3 3.7 feed_forward_out.1
  248.0 4.3 outer.8
  252.3 15.5 %mamba_backward.2 = (bf16[1024,1536]{1,0:T(8,128)(2,1)S(1)}, bf16[1024,512]{1,0:T(8,128)(2,1)S(1)}, f32[16,128]{1,0:T(8,128)S(1)}, f32[8,128]{1,0:T(8,128)S(1)}) custom-call(s32[2]{0:T(128)S(1)} %copy-done.46, s32[2,4]{1,0:T(2,128)S(1)} %bitcast.127, f32[2,6,8,512]{3,2,1,0:T(8,128)S(1)} %get-tuple-element.280.refs_0_.refs_2_, ...), custom_call_target="tpu_custom_call" | custom-call | flops 6520000000 | bytes 1 | tf_op jit(solution)/shard_map/mamba_backward/pallas_call | solution.py:77
  267.8 7.4 %collective-permute-done.35.refs_1_ = bf16[1,1,128,768]{3,2,1,0:T(8,128)(2,1)S(1)} collective-permute-done((bf16[1,1,128,768]{3,2,1,0:T(8,128)(2,1)S(1)}, bf16[1,1,128,768]{3,2,1,0:T(8,128)(2,1)S(1)}, u32[]{:S(2)}, u32[]{:S(2)}) %collective-permute-start.35) | collective-permute-done | bytes 196640 | tf_op jit(solution)/shard_map/ppermute | solution.py:18
  279.2 2.3 chain_states.5
  281.6 15.8 %mamba_backward.3 = (bf16[1024,1536]{1,0:T(8,128)(2,1)S(1)}, bf16[1024,512]{1,0:T(8,128)(2,1)S(1)}, f32[16,128]{1,0:T(8,128)S(1)}, f32[8,128]{1,0:T(8,128)S(1)}) custom-call(s32[2]{0:T(128)S(1)} %copy-done.46, s32[2,4]{1,0:T(2,128)S(1)} %bitcast.128, ...), custom_call_target="tpu_custom_call", output_to_operand_aliasing={{0}: (12, {}), {1}: (13, {})} | custom-call | flops 6520000000 | bytes 1 | tf_op jit(solution)/shard_map/mamba_backward/pallas_call | solution.py:77
  297.4 5.9 %outer.9 = (bf16[4,2,64,3072]{3,2,1,0:T(8,128)(2,1)S(1)}, bf16[4,2,64,3072]{3,2,1,0:T(8,128)(2,1)S(1)}, f32[8,128]{1,0:T(8,128)S(1)}) custom-call(s32[2]{0:T(128)S(1)} %copy-done.46, bf16[1024,1024]{1,0:T(8,128)(2,1)S(1)} %copy-done.9, bf16[1024,1536]{1,0:T(8,128)(2,1)S(1)} %get-tuple-element.394.refs_2_.refs_4_, ...), custom_call_target="tpu_custom_call", output_to_operand_aliasing={{0}: (3, {}), {1}: (4, {})} | custom-call | flops 2671304448 | bytes 1 | tf_op jit(solution)/shard_map/outer/pallas_call | solution.py:77
  308.3 3.2 collective-permute-done.39.refs_2_
  311.5 4.3 input_backward.2
  316.8 3.5 split_sum.7
  330.3 5.4 %attention_backward.3 = (bf16[512,256]{1,0:T(8,128)(2,1)S(1)}, bf16[1,2,512,128]{3,2,1,0:T(8,128)(2,1)S(1)}, bf16[1,2,512,128]{3,2,1,0:T(8,128)(2,1)S(1)}, f32[8,128]{1,0:T(8,128)S(1)}) custom-call(s32[2]{0:T(128)S(1)} %copy-done.46, s32[2,4]{1,0:T(2,128)S(1)} %bitcast.129, bf16[1024,256]{1,0:T(8,128)(2,1)S(1)} %copy-done.85, ...), custom_call_target="tpu_custom_call" | custom-call | flops 6800000000 | bytes 1 | tf_op jit(solution)/shard_map/attention_backward/pallas_call | solution.py:77
  336.4 2.5 collective-permute-start.41
  338.9 18.8 %collective-permute-done.43.refs_2_ = bf16[64,3072]{1,0:T(8,128)(2,1)S(1)} collective-permute-done((bf16[64,3072]{1,0:T(8,128)(2,1)}, bf16[64,3072]{1,0:T(8,128)(2,1)S(1)}, u32[]{:S(2)}, u32[]{:S(2)}) %collective-permute-start.43) | collective-permute-done | bytes 393248 | tf_op jit(solution)/shard_map/ppermute | solution.py:23
  361.5 4.5 split_fsdp.4
  370.7 2.2 copy-done.1
  372.9 5.0 %close_forward.1 = (bf16[1024,1024]{1,0:T(8,128)(2,1)}, f32[8,128]{1,0:T(8,128)S(1)}) custom-call(f32[1024,1024]{1,0:T(8,128)S(1)} %copy-done.1, bf16[1024,1024]{1,0:T(8,128)(2,1)} %get-tuple-element.375.refs_1_, bf16[1024,1024]{1,0:T(8,128)(2,1)} %collective-permute-done.34.refs_2_, f32[8,128]{1,0:T(8,128)S(1)} %get-tuple-element.421.refs_3_), custom_call_target="tpu_custom_call" | custom-call | flops 1600000000 | bytes 1 | tf_op jit(solution)/shard_map/close_forward/pallas_call | solution.py:77
  377.9 4.6 %join.28 = (bf16[2,64,3072]{2,1,0:T(8,128)(2,1)}, f32[8,128]{1,0:T(8,128)S(1)}) custom-call(bf16[1,64,3072]{2,1,0:T(8,128)(2,1)} %bitcast.40.refs_0_, bf16[1,64,3072]{2,1,0:T(8,128)(2,1)} %collective-permute-done.47.refs_1_, f32[8,128]{1,0:T(8,128)S(1)} %get-tuple-element.430.refs_2_), custom_call_target="tpu_custom_call" | custom-call | flops 800000000 | bytes 1 | tf_op jit(solution)/shard_map/join/pallas_call | solution.py:77
  382.5 2.7 ring_step.3
  386.0 4.3 input_backward.3
  392.4 3.8 collective-permute-start.50
  399.0 3.6 outer.11
  405.9 4.2 collective-permute-start.51
  410.1 3.6 finish.2
  414.8 3.6 emit_fourth.1
  418.5 3.7 collective-permute-done.53.refs_2_
  426.8 2.3 collective-permute-done.55
  429.1 2.4 finish.3
  433.8 2.7 collective-permute-done.59
  437.0 9.7 %collective-permute-done.60.refs_1_ = bf16[1,64,3584]{2,1,0:T(8,128)(2,1)S(1)} collective-permute-done((bf16[1,64,3584]{2,1,0:T(8,128)(2,1)S(1)}, bf16[1,64,3584]{2,1,0:T(8,128)(2,1)S(1)}, u32[]{:S(2)}, u32[]{:S(2)}) %collective-permute-start.60) | collective-permute-done | bytes 458784 | tf_op jit(solution)/shard_map/ppermute | solution.py:18
  447.2 2.5 collective-permute-done.61.refs_2_
  449.6 2.5 emit_second.1
  (355 shorter events, 116.7 us)
Async XLA Ops:
  5.1 13.3 %collective-permute-start.2 = (bf16[64,768]{1,0:T(8,128)(2,1)}, bf16[64,768]{1,0:T(8,128)(2,1)S(1)}, u32[]{:S(2)}, u32[]{:S(2)}) collective-permute-start(bf16[64,768]{1,0:T(8,128)(2,1)} %get-tuple-element.267), channel_id=1, source_target_pairs={{24,0},{0,8},{8,16},{16,24},{25,1},{1,9},{9,17},{17,25},{26,2},{2,... | collective-permute-start | bytes 294920 | tf_op jit(solution)/shard_map/ppermute | solution.py:23
  8.2 10.3 %collective-permute-start = (bf16[64,768]{1,0:T(8,128)(2,1)}, bf16[64,768]{1,0:T(8,128)(2,1)S(1)}, u32[]{:S(2)}, u32[]{:S(2)}) collective-permute-start(bf16[64,768]{1,0:T(8,128)(2,1)} %get-tuple-element.267), channel_id=1, source_target_pairs={{8,0},{16,8},{24,16},{0,24},{9,1},{17,9},{25,17},{1,25},{10,2},{18... | collective-permute-start | bytes 294920 | tf_op jit(solution)/shard_map/ppermute | solution.py:23
  10.2 9.3 %collective-permute-start.1 = (bf16[64,768]{1,0:T(8,128)(2,1)}, bf16[64,768]{1,0:T(8,128)(2,1)S(1)}, u32[]{:S(2)}, u32[]{:S(2)}) collective-permute-start(bf16[64,768]{1,0:T(8,128)(2,1)} %get-tuple-element.267), channel_id=1, source_target_pairs={{16,0},{24,8},{0,16},{8,24},{17,1},{25,9},{1,17},{9,25},{18,2},{26... | collective-permute-start | bytes 294920 | tf_op jit(solution)/shard_map/ppermute | solution.py:23
  20.4 19.8 %collective-permute-start.3 = (bf16[3,64,768]{2,1,0:T(8,128)(2,1)S(1)}, bf16[3,64,768]{2,1,0:T(8,128)(2,1)S(1)}, u32[]{:S(2)}, u32[]{:S(2)}) collective-permute-start(bf16[3,64,768]{2,1,0:T(8,128)(2,1)S(1)} %get-tuple-element.272.refs_0_), channel_id=1, source_target_pairs={{0,4},{2,6},{4,0},{6,2},{1,5},{3,7},{5,1},{7,3},{8,12},{10,14},{12... | collective-permute-start | bytes 884744 | tf_op jit(solution)/shard_map/ppermute | solution.py:18
  21.9 7.1 %collective-permute-start.4 = (bf16[64,1536]{1,0:T(8,128)(2,1)S(1)}, bf16[64,1536]{1,0:T(8,128)(2,1)S(1)}, u32[]{:S(2)}, u32[]{:S(2)}) collective-permute-start(bf16[64,1536]{1,0:T(8,128)(2,1)S(1)} %copy-done.93), channel_id=1, source_target_pairs={{8,0},{16,8},{24,16},{0,24},{9,1},{17,9},{25,17},{1,25},{10,2},{18... | collective-permute-start | bytes 589832 | tf_op jit(solution)/shard_map/ppermute | solution.py:23
  23.6 16.6 %collective-permute-start.5 = (bf16[64,1536]{1,0:T(8,128)(2,1)S(1)}, bf16[64,1536]{1,0:T(8,128)(2,1)S(1)}, u32[]{:S(2)}, u32[]{:S(2)}) collective-permute-start(bf16[64,1536]{1,0:T(8,128)(2,1)S(1)} %copy-done.93), channel_id=1, source_target_pairs={{16,0},{24,8},{0,16},{8,24},{17,1},{25,9},{1,17},{9,25},{18,2},{26... | collective-permute-start | bytes 589832 | tf_op jit(solution)/shard_map/ppermute | solution.py:23
  23.9 16.3 %collective-permute-start.6 = (bf16[64,1536]{1,0:T(8,128)(2,1)S(1)}, bf16[64,1536]{1,0:T(8,128)(2,1)S(1)}, u32[]{:S(2)}, u32[]{:S(2)}) collective-permute-start(bf16[64,1536]{1,0:T(8,128)(2,1)S(1)} %copy-done.93), channel_id=1, source_target_pairs={{24,0},{0,8},{8,16},{16,24},{25,1},{1,9},{9,17},{17,25},{26,2},{2,... | collective-permute-start | bytes 589832 | tf_op jit(solution)/shard_map/ppermute | solution.py:23
  40.4 4.1 collective-permute-start.7
  43.9 25.7 %collective-permute-start.8 = (bf16[3,64,1536]{2,1,0:T(8,128)(2,1)S(1)}, bf16[3,64,1536]{2,1,0:T(8,128)(2,1)S(1)}, u32[]{:S(2)}, u32[]{:S(2)}) collective-permute-start(bf16[3,64,1536]{2,1,0:T(8,128)(2,1)S(1)} %get-tuple-element.283.refs_0_), channel_id=1, source_target_pairs={{0,4},{2,6},{4,0},{6,2},{1,5},{3,7},{5,1},{7,3},{8,12},{10,14},{12... | collective-permute-start | bytes 1769480 | tf_op jit(solution)/shard_map/ppermute | solution.py:18
  53.6 84.8 %copy-start.40 = (bf16[1024,128]{1,0:T(8,128)(2,1)}, bf16[1024,128]{1,0:T(8,128)(2,1)S(1)}, u32[]{:S(2)}) copy-start(bf16[1024,128]{1,0:T(8,128)(2,1)S(1)} %get-tuple-element.297.refs_1_.refs_4_.refs_6_) | copy-start | bytes 786436
  53.6 16.0 %collective-permute-start.9 = (bf16[1,2,512,128]{3,2,1,0:T(8,128)(2,1)S(1)}, bf16[1,2,512,128]{3,2,1,0:T(8,128)(2,1)S(1)}, u32[]{:S(2)}, u32[]{:S(2)}) collective-permute-start(bf16[1,2,512,128]{3,2,1,0:T(8,128)(2,1)S(1)} %bitcast.102), channel_id=1, source_target_pairs={{0,4},{2,6},{4,0},{6,2},{1,5},{3,7},{5,1},{7,3},{8,12},{10,14},{12... | collective-permute-start | bytes 786440 | tf_op jit(solution)/shard_map/ppermute | solution.py:18
  55.1 5.1 %collective-permute-start.10 = (bf16[64,1024]{1,0:T(8,128)(2,1)S(1)}, bf16[64,1024]{1,0:T(8,128)(2,1)S(1)}, u32[]{:S(2)}, u32[]{:S(2)}) collective-permute-start(bf16[64,1024]{1,0:T(8,128)(2,1)S(1)} %copy-done.94), channel_id=1, source_target_pairs={{8,0},{16,8},{24,16},{0,24},{9,1},{17,9},{25,17},{1,25},{10,2},{18... | collective-permute-start | bytes 393224 | tf_op jit(solution)/shard_map/ppermute | solution.py:23
  55.5 14.0 %collective-permute-start.11 = (bf16[64,1024]{1,0:T(8,128)(2,1)S(1)}, bf16[64,1024]{1,0:T(8,128)(2,1)S(1)}, u32[]{:S(2)}, u32[]{:S(2)}) collective-permute-start(bf16[64,1024]{1,0:T(8,128)(2,1)S(1)} %copy-done.94), channel_id=1, source_target_pairs={{16,0},{24,8},{0,16},{8,24},{17,1},{25,9},{1,17},{9,25},{18,2},{26... | collective-permute-start | bytes 393224 | tf_op jit(solution)/shard_map/ppermute | solution.py:23
  57.7 11.8 %collective-permute-start.12 = (bf16[64,1024]{1,0:T(8,128)(2,1)S(1)}, bf16[64,1024]{1,0:T(8,128)(2,1)S(1)}, u32[]{:S(2)}, u32[]{:S(2)}) collective-permute-start(bf16[64,1024]{1,0:T(8,128)(2,1)S(1)} %copy-done.94), channel_id=1, source_target_pairs={{24,0},{0,8},{8,16},{16,24},{25,1},{1,9},{9,17},{17,25},{26,2},{2,... | collective-permute-start | bytes 393224 | tf_op jit(solution)/shard_map/ppermute | solution.py:23
  69.9 14.6 %collective-permute-start.13 = (bf16[6,64,1536]{2,1,0:T(8,128)(2,1)S(1)}, bf16[6,64,1536]{2,1,0:T(8,128)(2,1)S(1)}, u32[]{:S(2)}, u32[]{:S(2)}) collective-permute-start(bf16[6,64,1536]{2,1,0:T(8,128)(2,1)S(1)} %get-tuple-element.288.refs_2_), channel_id=1, source_target_pairs={{0,2},{2,0},{4,6},{6,4},{1,3},{3,1},{5,7},{7,5},{8,10},{10,8},{12,... | collective-permute-start | bytes 3538952 | tf_op jit(solution)/shard_map/ppermute | solution.py:18
  70.0 13.7 %collective-permute-start.14 = (bf16[2,2,512,128]{3,2,1,0:T(8,128)(2,1)S(1)}, bf16[2,2,512,128]{3,2,1,0:T(8,128)(2,1)S(1)}, u32[]{:S(2)}, u32[]{:S(2)}) collective-permute-start(bf16[2,2,512,128]{3,2,1,0:T(8,128)(2,1)S(1)} %get-tuple-element.289.refs_1_), channel_id=1, source_target_pairs={{0,2},{2,0},{4,6},{6,4},{1,3},{3,1},{5,7},{7,5},{8,10},{10,8},{12,... | collective-permute-start | bytes 1572872 | tf_op jit(solution)/shard_map/ppermute | solution.py:18
  70.6 11.0 %collective-permute-start.15 = (bf16[64,3072]{1,0:T(8,128)(2,1)S(1)}, bf16[64,3072]{1,0:T(8,128)(2,1)S(1)}, u32[]{:S(2)}, u32[]{:S(2)}) collective-permute-start(bf16[64,3072]{1,0:T(8,128)(2,1)S(1)} %copy-done.92), channel_id=1, source_target_pairs={{8,0},{16,8},{24,16},{0,24},{9,1},{17,9},{25,17},{1,25},{10,2},{18... | collective-permute-start | bytes 1179656 | tf_op jit(solution)/shard_map/ppermute | solution.py:23
  81.6 14.7 %collective-permute-start.17 = (bf16[64,3072]{1,0:T(8,128)(2,1)S(1)}, bf16[64,3072]{1,0:T(8,128)(2,1)S(1)}, u32[]{:S(2)}, u32[]{:S(2)}) collective-permute-start(bf16[64,3072]{1,0:T(8,128)(2,1)S(1)} %collective-permute-done.15.refs_5_), channel_id=1, source_target_pairs={{8,0},{16,8},{24,16},{0,24},{9,1},{17,9},{25,17},{1,25},{10,2},{18... | collective-permute-start | bytes 1179656 | tf_op jit(solution)/shard_map/ppermute | solution.py:23
  95.6 13.2 %collective-permute-start.16 = (bf16[1,2,144,768]{3,2,1,0:T(8,128)(2,1)S(1)}, bf16[1,2,144,768]{3,2,1,0:T(8,128)(2,1)S(1)}, u32[]{:S(2)}, u32[]{:S(2)}) collective-permute-start(bf16[1,2,144,768]{3,2,1,0:T(8,128)(2,1)S(1)} %bitcast.97), channel_id=1, source_target_pairs={{0,4},{2,6},{4,0},{6,2},{1,5},{3,7},{5,1},{7,3},{8,12},{10,14},{12... | collective-permute-start | bytes 1327112 | tf_op jit(solution)/shard_map/ppermute | solution.py:18
  96.3 12.8 %collective-permute-start.19 = (bf16[64,3072]{1,0:T(8,128)(2,1)S(1)}, bf16[64,3072]{1,0:T(8,128)(2,1)S(1)}, u32[]{:S(2)}, u32[]{:S(2)}) collective-permute-start(bf16[64,3072]{1,0:T(8,128)(2,1)S(1)} %collective-permute-done.17.refs_5_), channel_id=1, source_target_pairs={{8,0},{16,8},{24,16},{0,24},{9,1},{17,9},{25,17},{1,25},{10,2},{18... | collective-permute-start | bytes 1179656 | tf_op jit(solution)/shard_map/ppermute | solution.py:23
  96.5 18.9 %collective-permute-start.20 = (bf16[3,64,1024]{2,1,0:T(8,128)(2,1)S(1)}, bf16[3,64,1024]{2,1,0:T(8,128)(2,1)S(1)}, u32[]{:S(2)}, u32[]{:S(2)}) collective-permute-start(bf16[3,64,1024]{2,1,0:T(8,128)(2,1)S(1)} %get-tuple-element.310.refs_0_), channel_id=1, source_target_pairs={{0,4},{2,6},{4,0},{6,2},{1,5},{3,7},{5,1},{7,3},{8,12},{10,14},{12... | collective-permute-start | bytes 1179656 | tf_op jit(solution)/shard_map/ppermute | solution.py:18
  109.1 127.6 %copy-start.22 = (bf16[2,2,144,768]{3,2,1,0:T(8,128)(2,1)}, bf16[2,2,144,768]{3,2,1,0:T(8,128)(2,1)S(1)}, u32[]{:S(2)}) copy-start(bf16[2,2,144,768]{3,2,1,0:T(8,128)(2,1)S(1)} %get-tuple-element.309.refs_1_) | copy-start | bytes 2654212
  109.1 11.6 %collective-permute-start.18 = (bf16[2,2,144,768]{3,2,1,0:T(8,128)(2,1)S(1)}, bf16[2,2,144,768]{3,2,1,0:T(8,128)(2,1)}, u32[]{:S(2)}, u32[]{:S(2)}) collective-permute-start(bf16[2,2,144,768]{3,2,1,0:T(8,128)(2,1)S(1)} %get-tuple-element.309.refs_1_), channel_id=1, source_target_pairs={{0,2},{2,0},{4,6},{6,4},{1,3},{3,1},{5,7},{7,5},{8,10},{10,8},{12,... | collective-permute-start | bytes 2654216 | tf_op jit(solution)/shard_map/ppermute | solution.py:18
  116.4 6.8 %collective-permute-start.21 = (bf16[6,64,1024]{2,1,0:T(8,128)(2,1)}, bf16[6,64,1024]{2,1,0:T(8,128)(2,1)}, u32[]{:S(2)}, u32[]{:S(2)}) collective-permute-start(bf16[6,64,1024]{2,1,0:T(8,128)(2,1)} %get-tuple-element.317.refs_2_), channel_id=1, source_target_pairs={{0,2},{2,0},{4,6},{6,4},{1,3},{3,1},{5,7},{7,5},{8,10},{10,8},{12,... | collective-permute-start | bytes 2359304 | tf_op jit(solution)/shard_map/ppermute | solution.py:18
  119.9 28.4 %collective-permute-start.23 = (bf16[3,64,3072]{2,1,0:T(8,128)(2,1)S(1)}, bf16[3,64,3072]{2,1,0:T(8,128)(2,1)S(1)}, u32[]{:S(2)}, u32[]{:S(2)}) collective-permute-start(bf16[3,64,3072]{2,1,0:T(8,128)(2,1)S(1)} %get-tuple-element.331.refs_0_), channel_id=1, source_target_pairs={{0,4},{2,6},{4,0},{6,2},{1,5},{3,7},{5,1},{7,3},{8,12},{10,14},{12... | collective-permute-start | bytes 3538952 | tf_op jit(solution)/shard_map/ppermute | solution.py:18
  133.5 26.1 %collective-permute-start.27 = (bf16[512,1024]{1,0:T(8,128)(2,1)S(1)}, bf16[512,1024]{1,0:T(8,128)(2,1)S(1)}, u32[]{:S(2)}, u32[]{:S(2)}) collective-permute-start(bf16[512,1024]{1,0:T(8,128)(2,1)S(1)} %get-tuple-element.338.refs_1_), channel_id=1, source_target_pairs={{0,1},{1,0},{2,3},{3,2},{4,5},{5,4},{6,7},{7,6},{8,9},{9,8},{10,11... | collective-permute-start | bytes 3145736 | tf_op jit(solution)/shard_map/ppermute | solution.py:28
  148.5 2.9 collective-permute-start.24
  149.6 3.0 collective-permute-start.25
  149.6 4.1 collective-permute-start.26
  150.1 31.9 %collective-permute-start.22 = (bf16[512,1024]{1,0:T(8,128)(2,1)S(1)}, bf16[512,1024]{1,0:T(8,128)(2,1)S(1)}, u32[]{:S(2)}, u32[]{:S(2)}) collective-permute-start(bf16[512,1024]{1,0:T(8,128)(2,1)S(1)} %get-tuple-element.328.refs_1_), channel_id=1, source_target_pairs={{0,1},{1,0},{2,3},{3,2},{4,5},{5,4},{6,7},{7,6},{8,9},{9,8},{10,11... | collective-permute-start | bytes 3145736 | tf_op jit(solution)/shard_map/ppermute | solution.py:28
  170.4 33.3 %collective-permute-start.29 = (bf16[512,1024]{1,0:T(8,128)(2,1)S(1)}, bf16[512,1024]{1,0:T(8,128)(2,1)S(1)}, u32[]{:S(2)}, u32[]{:S(2)}) collective-permute-start(bf16[512,1024]{1,0:T(8,128)(2,1)S(1)} %get-tuple-element.348.refs_1_), channel_id=1, source_target_pairs={{0,1},{1,0},{2,3},{3,2},{4,5},{5,4},{6,7},{7,6},{8,9},{9,8},{10,11... | collective-permute-start | bytes 3145736 | tf_op jit(solution)/shard_map/ppermute | solution.py:28
  208.5 16.7 %collective-permute-start.33 = (bf16[4,2,64,3072]{3,2,1,0:T(8,128)(2,1)S(1)}, bf16[4,2,64,3072]{3,2,1,0:T(8,128)(2,1)S(1)}, u32[]{:S(2)}, u32[]{:S(2)}) collective-permute-start(bf16[4,2,64,3072]{3,2,1,0:T(8,128)(2,1)S(1)} %get-tuple-element.367), channel_id=1, source_target_pairs={{0,2},{2,0},{4,6},{6,4},{1,3},{3,1},{5,7},{7,5},{8,10},{10,8},{12,... | collective-permute-start | bytes 9437192 | tf_op jit(solution)/shard_map/ppermute | solution.py:18
  208.5 30.4 %collective-permute-start.28 = (bf16[512,1024]{1,0:T(8,128)(2,1)}, bf16[512,1024]{1,0:T(8,128)(2,1)S(1)}, u32[]{:S(2)}, u32[]{:S(2)}) collective-permute-start(bf16[512,1024]{1,0:T(8,128)(2,1)} %get-tuple-element.347.refs_1_), channel_id=1, source_target_pairs={{0,1},{1,0},{2,3},{3,2},{4,5},{5,4},{6,7},{7,6},{8,9},{9,8},{10,11... | collective-permute-start | bytes 3145736 | tf_op jit(solution)/shard_map/ppermute | solution.py:28
  214.1 7.0 %collective-permute-start.30 = (bf16[1,1,128,768]{3,2,1,0:T(8,128)(2,1)S(1)}, bf16[1,1,128,768]{3,2,1,0:T(8,128)(2,1)S(1)}, u32[]{:S(2)}, u32[]{:S(2)}) collective-permute-start(bf16[1,1,128,768]{3,2,1,0:T(8,128)(2,1)S(1)} %bitcast.113), channel_id=1, source_target_pairs={{0,4},{2,6},{4,0},{6,2},{1,5},{3,7},{5,1},{7,3},{8,12},{10,14},{12... | collective-permute-start | bytes 589832 | tf_op jit(solution)/shard_map/ppermute | solution.py:18
  221.5 15.2 %collective-permute-start.31 = (bf16[2,1,128,768]{3,2,1,0:T(8,128)(2,1)S(1)}, bf16[2,1,128,768]{3,2,1,0:T(8,128)(2,1)S(1)}, u32[]{:S(2)}, u32[]{:S(2)}) collective-permute-start(bf16[2,1,128,768]{3,2,1,0:T(8,128)(2,1)S(1)} %get-tuple-element.363.refs_3_), channel_id=1, source_target_pairs={{0,2},{2,0},{4,6},{6,4},{1,3},{3,1},{5,7},{7,5},{8,10},{10,8},{12,... | collective-permute-start | bytes 1179656 | tf_op jit(solution)/shard_map/ppermute | solution.py:18
  225.1 11.0 %collective-permute-start.32 = (bf16[1,2,512,128]{3,2,1,0:T(8,128)(2,1)S(1)}, bf16[1,2,512,128]{3,2,1,0:T(8,128)(2,1)S(1)}, u32[]{:S(2)}, u32[]{:S(2)}) collective-permute-start(bf16[1,2,512,128]{3,2,1,0:T(8,128)(2,1)S(1)} %get-tuple-element.365), channel_id=1, source_target_pairs={{0,2},{2,0},{4,6},{6,4},{1,3},{3,1},{5,7},{7,5},{8,10},{10,8},{12,... | collective-permute-start | bytes 786440 | tf_op jit(solution)/shard_map/ppermute | solution.py:18
  227.2 48.3 %collective-permute-start.37 = (bf16[4,1,64,3072]{3,2,1,0:T(8,128)(2,1)S(1)}, bf16[4,1,64,3072]{3,2,1,0:T(8,128)(2,1)S(1)}, u32[]{:S(2)}, u32[]{:S(2)}) collective-permute-start(bf16[4,1,64,3072]{3,2,1,0:T(8,128)(2,1)S(1)} %get-tuple-element.386), channel_id=1, source_target_pairs={{0,4},{2,6},{4,0},{6,2},{1,5},{3,7},{5,1},{7,3},{8,12},{10,14},{12... | collective-permute-start | bytes 4718600 | tf_op jit(solution)/shard_map/ppermute | solution.py:18
  244.2 31.1 %collective-permute-start.35 = (bf16[1,1,128,768]{3,2,1,0:T(8,128)(2,1)S(1)}, bf16[1,1,128,768]{3,2,1,0:T(8,128)(2,1)S(1)}, u32[]{:S(2)}, u32[]{:S(2)}) collective-permute-start(bf16[1,1,128,768]{3,2,1,0:T(8,128)(2,1)S(1)} %bitcast.110), channel_id=1, source_target_pairs={{0,4},{2,6},{4,0},{6,2},{1,5},{3,7},{5,1},{7,3},{8,12},{10,14},{12... | collective-permute-start | bytes 589832 | tf_op jit(solution)/shard_map/ppermute | solution.py:18
  275.4 3.8 collective-permute-start.36
  305.3 11.5 %collective-permute-start.38 = (bf16[4,2,64,3072]{3,2,1,0:T(8,128)(2,1)S(1)}, bf16[4,2,64,3072]{3,2,1,0:T(8,128)(2,1)S(1)}, u32[]{:S(2)}, u32[]{:S(2)}) collective-permute-start(bf16[4,2,64,3072]{3,2,1,0:T(8,128)(2,1)S(1)} %get-tuple-element.402), channel_id=1, source_target_pairs={{0,2},{2,0},{4,6},{6,4},{1,3},{3,1},{5,7},{7,5},{8,10},{10,8},{12,... | collective-permute-start | bytes 9437192 | tf_op jit(solution)/shard_map/ppermute | solution.py:18
  306.0 5.5 %collective-permute-start.39 = (bf16[1,1,512,128]{3,2,1,0:T(8,128)(2,1)S(1)}, bf16[1,1,512,128]{3,2,1,0:T(8,128)(2,1)S(1)}, u32[]{:S(2)}, u32[]{:S(2)}) collective-permute-start(bf16[1,1,512,128]{3,2,1,0:T(8,128)(2,1)S(1)} %get-tuple-element.405), channel_id=1, source_target_pairs={{0,4},{2,6},{4,0},{6,2},{1,5},{3,7},{5,1},{7,3},{8,12},{10,14},{12... | collective-permute-start | bytes 393224 | tf_op jit(solution)/shard_map/ppermute | solution.py:18
  307.8 63.0 %collective-permute-start.34 = (bf16[1024,1024]{1,0:T(8,128)(2,1)}, bf16[1024,1024]{1,0:T(8,128)(2,1)}, u32[]{:S(2)}, u32[]{:S(2)}) collective-permute-start(bf16[1024,1024]{1,0:T(8,128)(2,1)} %get-tuple-element.375.refs_1_), channel_id=1, source_target_pairs={{0,1},{1,0},{2,3},{3,2},{4,5},{5,4},{6,7},{7,6},{8,9},{9,8},{10,11... | collective-permute-start | bytes 6291464 | tf_op jit(solution)/shard_map/ppermute | solution.py:28
  321.4 40.1 %collective-permute-start.40 = (bf16[4,1,64,3072]{3,2,1,0:T(8,128)(2,1)}, bf16[4,1,64,3072]{3,2,1,0:T(8,128)(2,1)}, u32[]{:S(2)}, u32[]{:S(2)}) collective-permute-start(bf16[4,1,64,3072]{3,2,1,0:T(8,128)(2,1)} %get-tuple-element.409), channel_id=1, source_target_pairs={{0,4},{2,6},{4,0},{6,2},{1,5},{3,7},{5,1},{7,3},{8,12},{10,14},{12... | collective-permute-start | bytes 4718600 | tf_op jit(solution)/shard_map/ppermute | solution.py:18
  323.1 13.3 %collective-permute-start.42 = (bf16[64,3072]{1,0:T(8,128)(2,1)}, bf16[64,3072]{1,0:T(8,128)(2,1)S(1)}, u32[]{:S(2)}, u32[]{:S(2)}) collective-permute-start(bf16[64,3072]{1,0:T(8,128)(2,1)} %copy-done.51), channel_id=1, source_target_pairs={{8,0},{16,8},{24,16},{0,24},{9,1},{17,9},{25,17},{1,25},{10,2},{18... | collective-permute-start | bytes 1179656 | tf_op jit(solution)/shard_map/ppermute | solution.py:23
  323.6 34.2 %collective-permute-start.43 = (bf16[64,3072]{1,0:T(8,128)(2,1)}, bf16[64,3072]{1,0:T(8,128)(2,1)S(1)}, u32[]{:S(2)}, u32[]{:S(2)}) collective-permute-start(bf16[64,3072]{1,0:T(8,128)(2,1)} %copy-done.50), channel_id=1, source_target_pairs={{16,0},{24,8},{0,16},{8,24},{17,1},{25,9},{1,17},{9,25},{18,2},{26... | collective-permute-start | bytes 1179656 | tf_op jit(solution)/shard_map/ppermute | solution.py:23
  324.2 33.5 %collective-permute-start.44 = (bf16[64,3072]{1,0:T(8,128)(2,1)}, bf16[64,3072]{1,0:T(8,128)(2,1)S(1)}, u32[]{:S(2)}, u32[]{:S(2)}) collective-permute-start(bf16[64,3072]{1,0:T(8,128)(2,1)} %copy-done.49), channel_id=1, source_target_pairs={{24,0},{0,8},{8,16},{16,24},{25,1},{1,9},{9,17},{17,25},{26,2},{2,... | collective-permute-start | bytes 1179656 | tf_op jit(solution)/shard_map/ppermute | solution.py:23
  336.4 23.8 %collective-permute-start.41 = (bf16[1,2,512,128]{3,2,1,0:T(8,128)(2,1)S(1)}, bf16[1,2,512,128]{3,2,1,0:T(8,128)(2,1)S(1)}, u32[]{:S(2)}, u32[]{:S(2)}) collective-permute-start(bf16[1,2,512,128]{3,2,1,0:T(8,128)(2,1)S(1)} %get-tuple-element.413), channel_id=1, source_target_pairs={{0,2},{2,0},{4,6},{6,4},{1,3},{3,1},{5,7},{7,5},{8,10},{10,8},{12,... | collective-permute-start | bytes 786440 | tf_op jit(solution)/shard_map/ppermute | solution.py:18
  359.9 18.0 %collective-permute-start.47 = (bf16[1,64,3072]{2,1,0:T(8,128)(2,1)}, bf16[1,64,3072]{2,1,0:T(8,128)(2,1)}, u32[]{:S(2)}, u32[]{:S(2)}) collective-permute-start(bf16[1,64,3072]{2,1,0:T(8,128)(2,1)} %bitcast.40.refs_0_), channel_id=1, source_target_pairs={{0,4},{2,6},{4,0},{6,2},{1,5},{3,7},{5,1},{7,3},{8,12},{10,14},{12... | collective-permute-start | bytes 1179656 | tf_op jit(solution)/shard_map/ppermute | solution.py:18
  368.3 14.2 %collective-permute-start.46 = (bf16[64,3072]{1,0:T(8,128)(2,1)}, bf16[64,3072]{1,0:T(8,128)(2,1)}, u32[]{:S(2)}, u32[]{:S(2)}) collective-permute-start(bf16[64,3072]{1,0:T(8,128)(2,1)} %get-tuple-element.427), channel_id=1, source_target_pairs={{8,0},{16,8},{24,16},{0,24},{9,1},{17,9},{25,17},{1,25},{10,2},{18... | collective-permute-start | bytes 1179656 | tf_op jit(solution)/shard_map/ppermute | solution.py:23
  368.5 41.7 %collective-permute-start.49 = (bf16[512,1024]{1,0:T(8,128)(2,1)}, bf16[512,1024]{1,0:T(8,128)(2,1)}, u32[]{:S(2)}, u32[]{:S(2)}) collective-permute-start(bf16[512,1024]{1,0:T(8,128)(2,1)} %copy-done.36), channel_id=1, source_target_pairs={{0,1},{1,0},{2,3},{3,2},{4,5},{5,4},{6,7},{7,6},{8,9},{9,8},{10,11... | collective-permute-start | bytes 3145736 | tf_op jit(solution)/shard_map/ppermute | solution.py:28
  369.0 17.0 %collective-permute-start.45 = (bf16[1,1,512,128]{3,2,1,0:T(8,128)(2,1)}, bf16[1,1,512,128]{3,2,1,0:T(8,128)(2,1)S(1)}, u32[]{:S(2)}, u32[]{:S(2)}) collective-permute-start(bf16[1,1,512,128]{3,2,1,0:T(8,128)(2,1)} %copy-done.65), channel_id=1, source_target_pairs={{0,4},{2,6},{4,0},{6,2},{1,5},{3,7},{5,1},{7,3},{8,12},{10,14},{12... | collective-permute-start | bytes 393224 | tf_op jit(solution)/shard_map/ppermute | solution.py:18
  382.5 32.3 %collective-permute-start.54 = (bf16[2,64,3072]{2,1,0:T(8,128)(2,1)}, bf16[2,64,3072]{2,1,0:T(8,128)(2,1)}, u32[]{:S(2)}, u32[]{:S(2)}) collective-permute-start(bf16[2,64,3072]{2,1,0:T(8,128)(2,1)} %get-tuple-element.457.refs_1_), channel_id=1, source_target_pairs={{0,2},{2,0},{4,6},{6,4},{1,3},{3,1},{5,7},{7,5},{8,10},{10,8},{12,... | collective-permute-start | bytes 2359304 | tf_op jit(solution)/shard_map/ppermute | solution.py:18
  392.4 13.2 %collective-permute-start.50 = (bf16[64,3072]{1,0:T(8,128)(2,1)}, bf16[64,3072]{1,0:T(8,128)(2,1)S(1)}, u32[]{:S(2)}, u32[]{:S(2)}) collective-permute-start(bf16[64,3072]{1,0:T(8,128)(2,1)} %copy-done.56), channel_id=1, source_target_pairs={{8,0},{16,8},{24,16},{0,24},{9,1},{17,9},{25,17},{1,25},{10,2},{18... | collective-permute-start | bytes 1179656 | tf_op jit(solution)/shard_map/ppermute | solution.py:23
  402.7 11.0 %collective-permute-start.52 = (bf16[4,2,64,512]{3,2,1,0:T(8,128)(2,1)S(1)}, bf16[4,2,64,512]{3,2,1,0:T(8,128)(2,1)S(1)}, u32[]{:S(2)}, u32[]{:S(2)}) collective-permute-start(bf16[4,2,64,512]{3,2,1,0:T(8,128)(2,1)S(1)} %get-tuple-element.570), channel_id=1, source_target_pairs={{0,2},{2,0},{4,6},{6,4},{1,3},{3,1},{5,7},{7,5},{8,10},{10,8},{12,... | collective-permute-start | bytes 1572872 | tf_op jit(solution)/shard_map/ppermute | solution.py:18
  403.1 26.0 %collective-permute-start.48 = (bf16[512,1024]{1,0:T(8,128)(2,1)S(1)}, bf16[512,1024]{1,0:T(8,128)(2,1)S(1)}, u32[]{:S(2)}, u32[]{:S(2)}) collective-permute-start(bf16[512,1024]{1,0:T(8,128)(2,1)S(1)} %copy-done.33), channel_id=1, source_target_pairs={{0,1},{1,0},{2,3},{3,2},{4,5},{5,4},{6,7},{7,6},{8,9},{9,8},{10,11... | collective-permute-start | bytes 3145736 | tf_op jit(solution)/shard_map/ppermute | solution.py:28
  405.9 16.9 %collective-permute-start.51 = (bf16[64,3072]{1,0:T(8,128)(2,1)S(1)}, bf16[64,3072]{1,0:T(8,128)(2,1)S(1)}, u32[]{:S(2)}, u32[]{:S(2)}) collective-permute-start(bf16[64,3072]{1,0:T(8,128)(2,1)S(1)} %get-tuple-element.444), channel_id=1, source_target_pairs={{8,0},{16,8},{24,16},{0,24},{9,1},{17,9},{25,17},{1,25},{10,2},{18... | collective-permute-start | bytes 1179656 | tf_op jit(solution)/shard_map/ppermute | solution.py:23
  414.4 7.7 %collective-permute-start.53 = (bf16[4,1,64,512]{3,2,1,0:T(8,128)(2,1)S(1)}, bf16[4,1,64,512]{3,2,1,0:T(8,128)(2,1)S(1)}, u32[]{:S(2)}, u32[]{:S(2)}) collective-permute-start(bf16[4,1,64,512]{3,2,1,0:T(8,128)(2,1)S(1)} %get-tuple-element.456), channel_id=1, source_target_pairs={{0,4},{2,6},{4,0},{6,2},{1,5},{3,7},{5,1},{7,3},{8,12},{10,14},{12... | collective-permute-start | bytes 786440 | tf_op jit(solution)/shard_map/ppermute | solution.py:18
  423.1 6.0 %collective-permute-start.55 = (bf16[64,256]{1,0:T(8,128)(2,1)S(1)}, bf16[64,256]{1,0:T(8,128)(2,1)S(1)}, u32[]{:S(2)}, u32[]{:S(2)}) collective-permute-start(bf16[64,256]{1,0:T(8,128)(2,1)S(1)} %get-tuple-element.569), channel_id=1, source_target_pairs={{0,1},{1,0},{2,3},{3,2},{4,5},{5,4},{6,7},{7,6},{8,9},{9,8},{10,11... | collective-permute-start | bytes 98312 | tf_op jit(solution)/shard_map/ppermute | solution.py:28
  424.7 6.8 %collective-permute-start.56 = (bf16[64,512]{1,0:T(8,128)(2,1)S(1)}, bf16[64,512]{1,0:T(8,128)(2,1)S(1)}, u32[]{:S(2)}, u32[]{:S(2)}) collective-permute-start(bf16[64,512]{1,0:T(8,128)(2,1)S(1)} %get-tuple-element.465), channel_id=1, source_target_pairs={{8,0},{16,8},{24,16},{0,24},{9,1},{17,9},{25,17},{1,25},{10,2},{18... | collective-permute-start | bytes 196616 | tf_op jit(solution)/shard_map/ppermute | solution.py:23
  425.1 6.4 %collective-permute-start.57 = (bf16[64,512]{1,0:T(8,128)(2,1)S(1)}, bf16[64,512]{1,0:T(8,128)(2,1)S(1)}, u32[]{:S(2)}, u32[]{:S(2)}) collective-permute-start(bf16[64,512]{1,0:T(8,128)(2,1)S(1)} %get-tuple-element.466), channel_id=1, source_target_pairs={{16,0},{24,8},{0,16},{8,24},{17,1},{25,9},{1,17},{9,25},{18,2},{26... | collective-permute-start | bytes 196616 | tf_op jit(solution)/shard_map/ppermute | solution.py:23
  425.1 7.0 %collective-permute-start.58 = (bf16[64,512]{1,0:T(8,128)(2,1)S(1)}, bf16[64,512]{1,0:T(8,128)(2,1)S(1)}, u32[]{:S(2)}, u32[]{:S(2)}) collective-permute-start(bf16[64,512]{1,0:T(8,128)(2,1)S(1)} %get-tuple-element.467), channel_id=1, source_target_pairs={{24,0},{0,8},{8,16},{16,24},{25,1},{1,9},{9,17},{17,25},{26,2},{2,... | collective-permute-start | bytes 196616 | tf_op jit(solution)/shard_map/ppermute | solution.py:23
  432.7 3.8 collective-permute-start.59
  436.7 10.1 %collective-permute-start.60 = (bf16[1,64,3584]{2,1,0:T(8,128)(2,1)S(1)}, bf16[1,64,3584]{2,1,0:T(8,128)(2,1)S(1)}, u32[]{:S(2)}, u32[]{:S(2)}) collective-permute-start(bf16[1,64,3584]{2,1,0:T(8,128)(2,1)S(1)} %bitcast.95), channel_id=1, source_target_pairs={{0,4},{2,6},{4,0},{6,2},{1,5},{3,7},{5,1},{7,3},{8,12},{10,14},{12... | collective-permute-start | bytes 1376264 | tf_op jit(solution)/shard_map/ppermute | solution.py:18
  447.1 2.5 collective-permute-start.61
  (93 other events, 663.3 us)

commit v5 on v4

--- a/solution.py
+++ b/solution.py
@@ -1376,6 +1376,7 @@
             u, place, lens, per_head, zx, y[u], dog[u], q_dim, b, c, state, d_span[u], skip_row, aux, d_second)
         head_grads = head_grads + grads_u
     dzx, dbc = d_second
+    wait_for(ff_theirs)
     pair_second = outer(place, n1, dzx, pair_second, at_zx, wide)
     away, keep_second = outer(place, n1, dbc, pair_second, at_rest, wide)
     got_second = swap_context(away, 1)
@@ -1391,12 +1392,13 @@
         g_gain_one = g_gain_one + terms
     keep_second, got_second = reduce_far(place, keep_second, got_second, bits)
     kept = attend_back(units - 1)
+    wait_for(*parts_theirs[: units - 1])
+    layer_out = close_forward(h1, ff, ff_theirs)
     g_fourth = sum_parts(parts_fourth)
     dkv[units - 1] = reduce_far(place, *kept, bits)
     own_second, *below = split_fsdp(place, keep_second, got_second)
     chunks = below[::-1]
     ring = from_next(chunks[0], "fsdp")
-    layer_out = close_forward(h1, ff, ff_theirs)
     fourth_held = spread_far(g_fourth[None])
     fourth_core = swap_context(fourth_held, 1)
     nf = lax.axis_size("fsdp")
@@ -1406,6 +1408,7 @@
     g_gain_one = g_gain_one + terms
     nf = lax.axis_size("fsdp")
     part = model_dim // (nf * nc)
+    g_gain_one = g_gain_one + swap_tensor(g_gain_one)
     head_grads = jnp.tile(jnp.pad(head_grads[:16, :3], ((0, part - 16), (0, 0))), (nf * nc, 1))
     g_gains = jnp.concatenate([jnp.stack([g_gain_one, g_gain_two], axis=1), head_grads], axis=1).astype(LOW)
     g_gains = jnp.pad(g_gains, ((0, 0), (0, 123)))
@@ -1429,14 +1432,15 @@
     def in_turns(which, width, total, first=0):
         return [(first + width * (2 * i + which), width) for i in range(total // width)], False
 
+    wait_for(parts_theirs[units - 1])
     g_gate, g_up, g_down = emit(
         place, fourth_held, fourth_core,
         [in_turns(0, ff_blk, ff_dim), in_turns(1, ff_blk, ff_dim), columns(2 * ff_dim, ff_dim, True)], "emit_fourth")
     parts_first = to_owners(keep_first, got_first)
     g_second = share_columns(ring_step(ring, own_second), at_rest, at_rest + 2 * state_dim)
+    g_first = sum_parts(parts_first, (), place)
     u = units - 1
     input_grads = finish(u, tokens, parts[u], parts_theirs[u], gains, dh[u], input_grads)
-    g_first = share_columns(sum_parts(parts_first, (), place), at_b, at_b + 1)
     last_held = spread_far(jnp.concatenate([g_second, g_first], axis=1)[None])
     last_core = swap_context(last_held, 1)
     at_last = wide_second

time: 464 us -> 458 us (0.987)
  local copies, waits for them, and re-layouts: 33.6 us -> 27.6 us
    ppermute x9, waiting for transfers between devices: 20.9 us -> 29.2 us  [swap_tensor(): return lax.ppermute(x, 'tensor', [(i, (i + 1) % size) for i in range(size)])]
    ppermute x32, waiting for transfers between devices: 44.5 us -> 37.2 us  [swap_context(): return lax.ppermute(x, 'context', [(i, i ^ bit) for i in range(size)])]
    unnamed x190 -> x184, local copies, waits for them, and re-layouts: 30.2 us -> 23.2 us
  transfers between devices with their start and end apart: 62 -> 62, of which waited for: 26 -> 29; matrix products, arithmetic and copies ran while one was open for 0% -> 1% of each run, Pallas kernels for 41% -> 45%
where the time goes in v5:
time: 458 us; the launch traced here: 449 us
  Pallas kernels  227 us (50%)
  waiting for transfers between devices  120 us (26%)
  starting transfers between devices  69.1 us (15%)
  local copies, waits for them, and re-layouts  27.6 us (6%)
    pallas_call x75, Pallas kernels, call(): pl.pallas_call(run, grid=grid, out_shape=outs + (jax.ShapeDtypeStruct((8,...  227 us
    ppermute x21, waiting for transfers between devices, from_next(): return lax.ppermute(x, axis, [((i + step) % size, i) for i in range(size)])  53.9 us
    ppermute x32, waiting for transfers between devices, swap_context(): return lax.ppermute(x, 'context', [(i, i ^ bit) for i in range(size)])  37.2 us
    ppermute x32, starting transfers between devices, swap_context(): return lax.ppermute(x, 'context', [(i, i ^ bit) for i in range(size)])  32.3 us
    ppermute x9, waiting for transfers between devices, swap_tensor(): return lax.ppermute(x, 'tensor', [(i, (i + 1) % size) for i in range(size)])  29.2 us
    ppermute x21, starting transfers between devices, from_next(): return lax.ppermute(x, axis, [((i + step) % size, i) for i in range(size)])  27.9 us
    unnamed x184, local copies, waits for them, and re-layouts  23.2 us
  transfers between devices with their start and end apart: 62, of which 29 were waited for; matrix products, arithmetic and copies ran while one was open for 1% of the time, Pallas kernels for 45%

profile of v5, /device:TPU:0, one launch (start us, length us, event | category | flops | bytes accessed | tf_op | source)
XLA Modules:
  0.0 448.9 jit_solution(969476083295057182)
XLA Ops:
  5.1 3.0 collective-permute-start.2
  11.2 2.2 pack_second.1
  15.5 2.9 pack_fourth.1
  25.0 4.0 collective-permute-done.4.refs_3_
  29.0 11.2 %collective-permute-done.5.refs_4_ = bf16[64,1536]{1,0:T(8,128)(2,1)S(1)} collective-permute-done((bf16[64,1536]{1,0:T(8,128)(2,1)S(1)}, bf16[64,1536]{1,0:T(8,128)(2,1)S(1)}, u32[]{:S(2)}, u32[]{:S(2)}) %collective-permute-start.5) | collective-permute-done | bytes 196640 | tf_op jit(solution)/shard_map/ppermute | solution.py:23
  44.0 2.3 place_rows.4
  46.4 5.1 %project.1 = (bf16[1024,1024]{1,0:T(8,128)(2,1)S(1)}, bf16[1024,256]{1,0:T(8,128)(2,1)S(1)}, bf16[1024,128]{1,0:T(8,128)(2,1)S(1)}, bf16[1024,128]{1,0:T(8,128)(...) custom-call(s32[2]{0:T(128)S(1)} %copy-done.50, ...), custom_call_target="tpu_custom_call" | custom-call | flops 2600000000 | bytes 1 | tf_op jit(solution)/shard_map/project/pallas_call | solution.py:77
  52.6 2.2 collective-permute-start.11
  57.4 9.4 %collective-permute-done.11.refs_4_ = bf16[64,1024]{1,0:T(8,128)(2,1)S(1)} collective-permute-done((bf16[64,1024]{1,0:T(8,128)(2,1)S(1)}, bf16[64,1024]{1,0:T(8,128)(2,1)S(1)}, u32[]{:S(2)}, u32[]{:S(2)}) %collective-permute-start.11) | collective-permute-done | bytes 131104 | tf_op jit(solution)/shard_map/ppermute | solution.py:23
  67.8 11.0 %collective-permute-done.15.refs_5_ = bf16[64,3072]{1,0:T(8,128)(2,1)S(1)} collective-permute-done((bf16[64,3072]{1,0:T(8,128)(2,1)S(1)}, bf16[64,3072]{1,0:T(8,128)(2,1)S(1)}, u32[]{:S(2)}, u32[]{:S(2)}) %collective-permute-start.15) | collective-permute-done | bytes 393248 | tf_op jit(solution)/shard_map/ppermute | solution.py:23
  83.4 4.2 project_mixer.1
  87.6 2.5 mamba_state.4
  90.1 2.5 mamba_state.5
  95.0 3.3 attention_forward.2
  98.3 7.6 %collective-permute-done.16.refs_1_ = bf16[1,2,144,768]{3,2,1,0:T(8,128)(2,1)S(1)} collective-permute-done((bf16[1,2,144,768]{3,2,1,0:T(8,128)(2,1)S(1)}, bf16[1,2,144,768]{3,2,1,0:T(8,128)(2,1)S(1)}, u32[]{:S(2)}, u32[]{:S(2)}) %collective-permute-start.16) | collective-permute-done | bytes 442400 | tf_op jit(solution)/shard_map/ppermute | solution.py:18
  106.3 6.2 %collective-permute-done.20.refs_1_ = bf16[3,64,1024]{2,1,0:T(8,128)(2,1)S(1)} collective-permute-done((bf16[3,64,1024]{2,1,0:T(8,128)(2,1)S(1)}, bf16[3,64,1024]{2,1,0:T(8,128)(2,1)S(1)}, u32[]{:S(2)}, u32[]{:S(2)}) %collective-permute-start.20) | collective-permute-done | bytes 393248 | tf_op jit(solution)/shard_map/ppermute | solution.py:18
  118.6 2.5 chain_states.3
  122.9 7.0 %mamba_forward.2 = (bf16[1024,1024]{1,0:T(8,128)(2,1)S(1)}, f32[512,768]{1,0:T(8,128)S(1)}, f32[8,128]{1,0:T(8,128)S(1)}) custom-call(s32[2]{0:T(128)S(1)} %copy-done.50, s32[2,4]{1,0:T(2,128)S(1)} %bitcast.121, f32[2,6,8,512]{3,2,1,0:T(8,128)S(1)} %get-tuple-element.280.refs_0_.refs_2_, ...), custom_call_target="tpu_custom_call", output_to_operand_aliasing={{0}: (8, {})} | custom-call | flops 3000000000 | bytes 1 | tf_op jit(solution)/shard_map/mamba_forward/pallas_call | solution.py:77
  133.1 3.3 attention_forward.3
  136.4 7.0 %mamba_forward.3 = (bf16[1024,1024]{1,0:T(8,128)(2,1)S(1)}, f32[512,768]{1,0:T(8,128)S(1)}, f32[8,128]{1,0:T(8,128)S(1)}) custom-call(s32[2]{0:T(128)S(1)} %copy-done.50, s32[2,4]{1,0:T(2,128)S(1)} %bitcast.123, f32[2,6,8,512]{3,2,1,0:T(8,128)S(1)} %get-tuple-element.280.refs_0_.refs_2_, ...), custom_call_target="tpu_custom_call", output_to_operand_aliasing={{0}: (8, {})} | custom-call | flops 3000000000 | bytes 1 | tf_op jit(solution)/shard_map/mamba_forward/pallas_call | solution.py:77
  151.7 2.4 place_rows.7
  154.1 3.5 collective-permute-done.27.refs_2_
  157.5 10.8 %feed_forward.2 = (f32[1024,1024]{1,0:T(8,128)S(1)}, bf16[1024,1024]{1,0:T(8,128)(2,1)S(1)}, bf16[1024,1024]{1,0:T(8,128)(2,1)S(1)}, bf16[1024,2048]{1,0:T(8,128...) custom-call(bf16[1024,1024]{1,0:T(8,128)(2,1)S(1)} %bitcast.74, ...), custom_call_target="tpu_custom_call" | custom-call | flops 5600000000 | bytes 1 | tf_op jit(solution)/shard_map/feed_forward/pallas_call | solution.py:77
  170.0 10.0 %collective-permute-done.22.refs_2_ = bf16[512,1024]{1,0:T(8,128)(2,1)S(1)} collective-permute-done((bf16[512,1024]{1,0:T(8,128)(2,1)S(1)}, bf16[512,1024]{1,0:T(8,128)(2,1)S(1)}, u32[]{:S(2)}, u32[]{:S(2)}) %collective-permute-start.22) | collective-permute-done | bytes 1048608 | tf_op jit(solution)/shard_map/ppermute | solution.py:28
  180.0 11.8 %feed_forward.3 = (f32[1024,1024]{1,0:T(8,128)S(1)}, bf16[1024,1024]{1,0:T(8,128)(2,1)S(1)}, bf16[1024,1024]{1,0:T(8,128)(2,1)S(1)}, bf16[1024,2048]{1,0:T(8,128...) custom-call(bf16[1024,1024]{1,0:T(8,128)(2,1)S(1)} %bitcast.75, ...), custom_call_target="tpu_custom_call", output_to_operand_aliasing={{0}: (7, {}), {1}: (8, {}), {2}: (9, {}), {3}: (10, {})} | custom-call | flops 5600000000 | bytes 1 | tf_op jit(solution)/shard_map/feed_forward/pallas_call | solution.py:77
  191.8 7.5 %outer.6 = (bf16[4,2,64,3072]{3,2,1,0:T(8,128)(2,1)S(1)}, bf16[4,2,64,3072]{3,2,1,0:T(8,128)(2,1)S(1)}, f32[8,128]{1,0:T(8,128)S(1)}) custom-call(s32[2]{0:T(128)S(1)} %copy-done.50, bf16[1024,1024]{1,0:T(8,128)(2,1)S(1)} %get-tuple-element.349.refs_1_, bf16[1024,2048]{1,0:T(8,128)(2,1)S(1)} %get-tuple-element.350.refs_2_, ...), custom_call_target="tpu_custom_call" | custom-call | flops 3561739008 | bytes 1 | tf_op jit(solution)/shard_map/outer/pallas_call | solution.py:77
  199.2 2.5 collective-permute-done.29.refs_6_.refs_2_
  201.8 4.7 %outer.7 = (bf16[4,2,64,3072]{3,2,1,0:T(8,128)(2,1)S(1)}, bf16[4,2,64,3072]{3,2,1,0:T(8,128)(2,1)S(1)}, f32[8,128]{1,0:T(8,128)S(1)}) custom-call(s32[2]{0:T(128)S(1)} %copy-done.50, bf16[1024,1024]{1,0:T(8,128)(2,1)S(1)} %bitcast.86, bf16[1024,1024]{1,0:T(8,128)(2,1)S(1)} %get-tuple-element.346.refs_2_.refs_0_, ...), custom_call_target="tpu_custom_call", output_to_operand_aliasing={{0}: (3, {}), {1}: (4, {})} | custom-call | flops 1780869504 | bytes 1 | tf_op jit(solution)/shard_map/outer/pallas_call | solution.py:77
  212.5 5.2 %attention_backward.2 = (bf16[512,256]{1,0:T(8,128)(2,1)S(1)}, bf16[1,2,512,128]{3,2,1,0:T(8,128)(2,1)S(1)}, bf16[1,2,512,128]{3,2,1,0:T(8,128)(2,1)S(1)}, f32[8,128]{1,0:T(8,128)S(1)}) custom-call(s32[2]{0:T(128)S(1)} %copy-done.50, s32[2,4]{1,0:T(2,128)S(1)} %bitcast.124, bf16[1024,256]{1,0:T(8,128)(2,1)S(1)} %copy-done.81, ...), custom_call_target="tpu_custom_call" | custom-call | flops 6800000000 | bytes 1 | tf_op jit(solution)/shard_map/attention_backward/pallas_call | solution.py:77
  219.2 3.1 collective-permute-start.31
  224.4 9.1 %collective-permute-start.37 = (bf16[4,1,64,3072]{3,2,1,0:T(8,128)(2,1)S(1)}, bf16[4,1,64,3072]{3,2,1,0:T(8,128)(2,1)S(1)}, u32[]{:S(2)}, u32[]{:S(2)}) collective-permute-start(bf16[4,1,64,3072]{3,2,1,0:T(8,128)(2,1)S(1)} %get-tuple-element.387), channel_id=1, source_target_pairs={{0,4},{2,6},{4,0},{6,2},{1,5},{3,7},{5,1},{7,3},{8,12},{10,14},{12... | collective-permute-start | bytes 4718600 | tf_op jit(solution)/shard_map/ppermute | solution.py:18
  234.2 2.2 chain_states.4
  236.4 3.3 middle_backward.3
  241.7 2.7 feed_forward_out.1
  245.0 4.3 outer.8
  249.3 15.5 %mamba_backward.2 = (bf16[1024,1536]{1,0:T(8,128)(2,1)S(1)}, bf16[1024,512]{1,0:T(8,128)(2,1)S(1)}, f32[16,128]{1,0:T(8,128)S(1)}, f32[8,128]{1,0:T(8,128)S(1)}) custom-call(s32[2]{0:T(128)S(1)} %copy-done.50, s32[2,4]{1,0:T(2,128)S(1)} %bitcast.125, f32[2,6,8,512]{3,2,1,0:T(8,128)S(1)} %get-tuple-element.280.refs_0_.refs_2_, ...), custom_call_target="tpu_custom_call" | custom-call | flops 6520000000 | bytes 1 | tf_op jit(solution)/shard_map/mamba_backward/pallas_call | solution.py:77
  264.9 7.8 %collective-permute-done.35.refs_1_ = bf16[1,1,128,768]{3,2,1,0:T(8,128)(2,1)S(1)} collective-permute-done((bf16[1,1,128,768]{3,2,1,0:T(8,128)(2,1)S(1)}, bf16[1,1,128,768]{3,2,1,0:T(8,128)(2,1)S(1)}, u32[]{:S(2)}, u32[]{:S(2)}) %collective-permute-start.35) | collective-permute-done | bytes 196640 | tf_op jit(solution)/shard_map/ppermute | solution.py:18
  275.9 2.5 chain_states.5
  278.4 15.8 %mamba_backward.3 = (bf16[1024,1536]{1,0:T(8,128)(2,1)S(1)}, bf16[1024,512]{1,0:T(8,128)(2,1)S(1)}, f32[16,128]{1,0:T(8,128)S(1)}, f32[8,128]{1,0:T(8,128)S(1)}) custom-call(s32[2]{0:T(128)S(1)} %copy-done.50, s32[2,4]{1,0:T(2,128)S(1)} %bitcast.126, ...), custom_call_target="tpu_custom_call", output_to_operand_aliasing={{0}: (12, {}), {1}: (13, {})} | custom-call | flops 6520000000 | bytes 1 | tf_op jit(solution)/shard_map/mamba_backward/pallas_call | solution.py:77
  294.2 5.9 %outer.9 = (bf16[4,2,64,3072]{3,2,1,0:T(8,128)(2,1)S(1)}, bf16[4,2,64,3072]{3,2,1,0:T(8,128)(2,1)S(1)}, f32[8,128]{1,0:T(8,128)S(1)}) custom-call(s32[2]{0:T(128)S(1)} %copy-done.50, bf16[1024,1024]{1,0:T(8,128)(2,1)S(1)} %copy-done.9, bf16[1024,1536]{1,0:T(8,128)(2,1)S(1)} %get-tuple-element.395.refs_2_.refs_4_, ...), custom_call_target="tpu_custom_call", output_to_operand_aliasing={{0}: (3, {}), {1}: (4, {})} | custom-call | flops 2671304448 | bytes 1 | tf_op jit(solution)/shard_map/outer/pallas_call | solution.py:77
  304.6 3.7 collective-permute-done.39.refs_2_
  308.4 4.7 %input_backward.2 = (bf16[1024,384]{1,0:T(8,128)(2,1)S(1)}, bf16[512,1024]{1,0:T(8,128)(2,1)}, f32[8,1024]{1,0:T(8,128)S(1)}, f32[8,128]{1,0:T(8,128)S(1)}) custom-call(bf16[512,256]{1,0:T(8,128)(2,1)S(1)} %get-tuple-element.404.refs_0_, bf16[1,1,512,128]{3,2,1,0:T(8,128)(2,1)S(1)} %get-tuple-element.405.refs_1_, ...), custom_call_target="tpu_custom_call" | custom-call | flops 2600000000 | bytes 1 | tf_op jit(solution)/shard_map/input_backward/pallas_call | solution.py:77
  313.1 3.5 split_sum.7
  327.1 5.4 %attention_backward.3 = (bf16[512,256]{1,0:T(8,128)(2,1)S(1)}, bf16[1,2,512,128]{3,2,1,0:T(8,128)(2,1)S(1)}, bf16[1,2,512,128]{3,2,1,0:T(8,128)(2,1)S(1)}, f32[8,128]{1,0:T(8,128)S(1)}) custom-call(s32[2]{0:T(128)S(1)} %copy-done.50, s32[2,4]{1,0:T(2,128)S(1)} %bitcast.127, bf16[1024,256]{1,0:T(8,128)(2,1)S(1)} %copy-done.82, ...), custom_call_target="tpu_custom_call" | custom-call | flops 6800000000 | bytes 1 | tf_op jit(solution)/shard_map/attention_backward/pallas_call | solution.py:77
  332.6 11.3 %collective-permute-done.40.refs_4_.refs_2_ = bf16[512,1024]{1,0:T(8,128)(2,1)} collective-permute-done((bf16[512,1024]{1,0:T(8,128)(2,1)}, bf16[512,1024]{1,0:T(8,128)(2,1)}, u32[]{:S(2)}, u32[]{:S(2)}) %collective-permute-start.40) | collective-permute-done | bytes 1048608 | tf_op jit(solution)/shard_map/ppermute | solution.py:28
  346.6 7.7 %collective-permute-done.43.refs_2_ = bf16[64,3072]{1,0:T(8,128)(2,1)S(1)} collective-permute-done((bf16[64,3072]{1,0:T(8,128)(2,1)}, bf16[64,3072]{1,0:T(8,128)(2,1)S(1)}, u32[]{:S(2)}, u32[]{:S(2)}) %collective-permute-start.43) | collective-permute-done | bytes 393248 | tf_op jit(solution)/shard_map/ppermute | solution.py:23
  354.3 2.2 sum_parts.2
  358.0 4.5 %split_fsdp.4 = (bf16[64,3072]{1,0:T(8,128)(2,1)S(1)}, bf16[64,3072]{1,0:T(8,128)(2,1)S(1)}, bf16[64,3072]{1,0:T(8,128)(2,1)S(1)}, bf16[64,3072]{1,0:T(8,128)(2,1)}, f32[8,128]{1,0:T(8,128)S(1)}) custom-call(s32[2]{0:T(128)S(1)} %copy-done.50, bf16[4,1,64,3072]{3,2,1,0:T(8,128)(2,1)S(1)} %copy-done.53, ...), custom_call_target="tpu_custom_call" | custom-call | flops 1024000000 | bytes 1 | tf_op jit(solution)/shard_map/split_fsdp/pallas_call | solution.py:77
  367.3 4.6 %join.28 = (bf16[2,64,3072]{2,1,0:T(8,128)(2,1)}, f32[8,128]{1,0:T(8,128)S(1)}) custom-call(bf16[1,64,3072]{2,1,0:T(8,128)(2,1)} %bitcast.40.refs_0_, bf16[1,64,3072]{2,1,0:T(8,128)(2,1)} %collective-permute-done.48.refs_1_, f32[8,128]{1,0:T(8,128)S(1)} %get-tuple-element.431.refs_2_), custom_call_target="tpu_custom_call" | custom-call | flops 800000000 | bytes 1 | tf_op jit(solution)/shard_map/join/pallas_call | solution.py:77
  371.8 2.7 collective-permute-done.47.refs_0_
  375.5 3.9 ring_step.3
  384.3 4.7 %input_backward.3 = (bf16[1024,384]{1,0:T(8,128)(2,1)S(1)}, bf16[512,1024]{1,0:T(8,128)(2,1)}, f32[8,1024]{1,0:T(8,128)S(1)}, f32[8,128]{1,0:T(8,128)S(1)}) custom-call(bf16[512,256]{1,0:T(8,128)(2,1)S(1)} %copy-done.47, bf16[1,1,512,128]{3,2,1,0:T(8,128)(2,1)S(1)} %get-tuple-element.422.refs_1_, ...), custom_call_target="tpu_custom_call", output_to_operand_aliasing={{0}: (8, {})} | custom-call | flops 2600000000 | bytes 1 | tf_op jit(solution)/shard_map/input_backward/pallas_call | solution.py:77
  391.3 2.5 collective-permute-start.50
  394.4 3.6 outer.11
  403.2 2.7 ring_step.4
  405.9 3.6 collective-permute-start.58
  409.5 4.0 finish.2
  417.6 3.6 emit_fourth.1
  422.9 2.3 collective-permute-start.55
  427.9 2.5 collective-permute-done.56.refs_3_
  433.7 3.6 finish.3
  437.3 3.2 collective-permute-done.60.refs_1_
  440.9 2.5 collective-permute-done.61.refs_2_
  443.3 2.5 emit_second.1
  (347 shorter events, 121.1 us)
Async XLA Ops:
  5.1 13.3 %collective-permute-start.2 = (bf16[64,768]{1,0:T(8,128)(2,1)}, bf16[64,768]{1,0:T(8,128)(2,1)S(1)}, u32[]{:S(2)}, u32[]{:S(2)}) collective-permute-start(bf16[64,768]{1,0:T(8,128)(2,1)} %get-tuple-element.267), channel_id=1, source_target_pairs={{24,0},{0,8},{8,16},{16,24},{25,1},{1,9},{9,17},{17,25},{26,2},{2,... | collective-permute-start | bytes 294920 | tf_op jit(solution)/shard_map/ppermute | solution.py:23
  8.2 10.3 %collective-permute-start = (bf16[64,768]{1,0:T(8,128)(2,1)}, bf16[64,768]{1,0:T(8,128)(2,1)S(1)}, u32[]{:S(2)}, u32[]{:S(2)}) collective-permute-start(bf16[64,768]{1,0:T(8,128)(2,1)} %get-tuple-element.267), channel_id=1, source_target_pairs={{8,0},{16,8},{24,16},{0,24},{9,1},{17,9},{25,17},{1,25},{10,2},{18... | collective-permute-start | bytes 294920 | tf_op jit(solution)/shard_map/ppermute | solution.py:23
  10.2 9.3 %collective-permute-start.1 = (bf16[64,768]{1,0:T(8,128)(2,1)}, bf16[64,768]{1,0:T(8,128)(2,1)S(1)}, u32[]{:S(2)}, u32[]{:S(2)}) collective-permute-start(bf16[64,768]{1,0:T(8,128)(2,1)} %get-tuple-element.267), channel_id=1, source_target_pairs={{16,0},{24,8},{0,16},{8,24},{17,1},{25,9},{1,17},{9,25},{18,2},{26... | collective-permute-start | bytes 294920 | tf_op jit(solution)/shard_map/ppermute | solution.py:23
  20.4 19.8 %collective-permute-start.3 = (bf16[3,64,768]{2,1,0:T(8,128)(2,1)S(1)}, bf16[3,64,768]{2,1,0:T(8,128)(2,1)S(1)}, u32[]{:S(2)}, u32[]{:S(2)}) collective-permute-start(bf16[3,64,768]{2,1,0:T(8,128)(2,1)S(1)} %get-tuple-element.272.refs_0_), channel_id=1, source_target_pairs={{0,4},{2,6},{4,0},{6,2},{1,5},{3,7},{5,1},{7,3},{8,12},{10,14},{12... | collective-permute-start | bytes 884744 | tf_op jit(solution)/shard_map/ppermute | solution.py:18
  21.9 7.1 %collective-permute-start.4 = (bf16[64,1536]{1,0:T(8,128)(2,1)S(1)}, bf16[64,1536]{1,0:T(8,128)(2,1)S(1)}, u32[]{:S(2)}, u32[]{:S(2)}) collective-permute-start(bf16[64,1536]{1,0:T(8,128)(2,1)S(1)} %copy-done.90), channel_id=1, source_target_pairs={{8,0},{16,8},{24,16},{0,24},{9,1},{17,9},{25,17},{1,25},{10,2},{18... | collective-permute-start | bytes 589832 | tf_op jit(solution)/shard_map/ppermute | solution.py:23
  23.6 16.6 %collective-permute-start.5 = (bf16[64,1536]{1,0:T(8,128)(2,1)S(1)}, bf16[64,1536]{1,0:T(8,128)(2,1)S(1)}, u32[]{:S(2)}, u32[]{:S(2)}) collective-permute-start(bf16[64,1536]{1,0:T(8,128)(2,1)S(1)} %copy-done.90), channel_id=1, source_target_pairs={{16,0},{24,8},{0,16},{8,24},{17,1},{25,9},{1,17},{9,25},{18,2},{26... | collective-permute-start | bytes 589832 | tf_op jit(solution)/shard_map/ppermute | solution.py:23
  23.9 16.3 %collective-permute-start.6 = (bf16[64,1536]{1,0:T(8,128)(2,1)S(1)}, bf16[64,1536]{1,0:T(8,128)(2,1)S(1)}, u32[]{:S(2)}, u32[]{:S(2)}) collective-permute-start(bf16[64,1536]{1,0:T(8,128)(2,1)S(1)} %copy-done.90), channel_id=1, source_target_pairs={{24,0},{0,8},{8,16},{16,24},{25,1},{1,9},{9,17},{17,25},{26,2},{2,... | collective-permute-start | bytes 589832 | tf_op jit(solution)/shard_map/ppermute | solution.py:23
  41.6 2.3 collective-permute-start.7
  42.0 24.8 %collective-permute-start.8 = (bf16[3,64,1536]{2,1,0:T(8,128)(2,1)S(1)}, bf16[3,64,1536]{2,1,0:T(8,128)(2,1)S(1)}, u32[]{:S(2)}, u32[]{:S(2)}) collective-permute-start(bf16[3,64,1536]{2,1,0:T(8,128)(2,1)S(1)} %get-tuple-element.283.refs_0_), channel_id=1, source_target_pairs={{0,4},{2,6},{4,0},{6,2},{1,5},{3,7},{5,1},{7,3},{8,12},{10,14},{12... | collective-permute-start | bytes 1769480 | tf_op jit(solution)/shard_map/ppermute | solution.py:18
  51.6 15.2 %collective-permute-start.9 = (bf16[1,2,512,128]{3,2,1,0:T(8,128)(2,1)S(1)}, bf16[1,2,512,128]{3,2,1,0:T(8,128)(2,1)S(1)}, u32[]{:S(2)}, u32[]{:S(2)}) collective-permute-start(bf16[1,2,512,128]{3,2,1,0:T(8,128)(2,1)S(1)} %bitcast.100), channel_id=1, source_target_pairs={{0,4},{2,6},{4,0},{6,2},{1,5},{3,7},{5,1},{7,3},{8,12},{10,14},{12... | collective-permute-start | bytes 786440 | tf_op jit(solution)/shard_map/ppermute | solution.py:18
  52.2 5.2 %collective-permute-start.10 = (bf16[64,1024]{1,0:T(8,128)(2,1)S(1)}, bf16[64,1024]{1,0:T(8,128)(2,1)S(1)}, u32[]{:S(2)}, u32[]{:S(2)}) collective-permute-start(bf16[64,1024]{1,0:T(8,128)(2,1)S(1)} %copy-done.91), channel_id=1, source_target_pairs={{8,0},{16,8},{24,16},{0,24},{9,1},{17,9},{25,17},{1,25},{10,2},{18... | collective-permute-start | bytes 393224 | tf_op jit(solution)/shard_map/ppermute | solution.py:23
  52.6 14.2 %collective-permute-start.11 = (bf16[64,1024]{1,0:T(8,128)(2,1)S(1)}, bf16[64,1024]{1,0:T(8,128)(2,1)S(1)}, u32[]{:S(2)}, u32[]{:S(2)}) collective-permute-start(bf16[64,1024]{1,0:T(8,128)(2,1)S(1)} %copy-done.91), channel_id=1, source_target_pairs={{16,0},{24,8},{0,16},{8,24},{17,1},{25,9},{1,17},{9,25},{18,2},{26... | collective-permute-start | bytes 393224 | tf_op jit(solution)/shard_map/ppermute | solution.py:23
  54.9 11.9 %collective-permute-start.12 = (bf16[64,1024]{1,0:T(8,128)(2,1)S(1)}, bf16[64,1024]{1,0:T(8,128)(2,1)S(1)}, u32[]{:S(2)}, u32[]{:S(2)}) collective-permute-start(bf16[64,1024]{1,0:T(8,128)(2,1)S(1)} %copy-done.91), channel_id=1, source_target_pairs={{24,0},{0,8},{8,16},{16,24},{25,1},{1,9},{9,17},{17,25},{26,2},{2,... | collective-permute-start | bytes 393224 | tf_op jit(solution)/shard_map/ppermute | solution.py:23
  67.2 14.6 %collective-permute-start.13 = (bf16[6,64,1536]{2,1,0:T(8,128)(2,1)S(1)}, bf16[6,64,1536]{2,1,0:T(8,128)(2,1)S(1)}, u32[]{:S(2)}, u32[]{:S(2)}) collective-permute-start(bf16[6,64,1536]{2,1,0:T(8,128)(2,1)S(1)} %get-tuple-element.288.refs_2_), channel_id=1, source_target_pairs={{0,2},{2,0},{4,6},{6,4},{1,3},{3,1},{5,7},{7,5},{8,10},{10,8},{12,... | collective-permute-start | bytes 3538952 | tf_op jit(solution)/shard_map/ppermute | solution.py:18
  67.3 13.7 %collective-permute-start.14 = (bf16[2,2,512,128]{3,2,1,0:T(8,128)(2,1)S(1)}, bf16[2,2,512,128]{3,2,1,0:T(8,128)(2,1)S(1)}, u32[]{:S(2)}, u32[]{:S(2)}) collective-permute-start(bf16[2,2,512,128]{3,2,1,0:T(8,128)(2,1)S(1)} %get-tuple-element.289.refs_1_), channel_id=1, source_target_pairs={{0,2},{2,0},{4,6},{6,4},{1,3},{3,1},{5,7},{7,5},{8,10},{10,8},{12,... | collective-permute-start | bytes 1572872 | tf_op jit(solution)/shard_map/ppermute | solution.py:18
  67.8 11.0 %collective-permute-start.15 = (bf16[64,3072]{1,0:T(8,128)(2,1)S(1)}, bf16[64,3072]{1,0:T(8,128)(2,1)S(1)}, u32[]{:S(2)}, u32[]{:S(2)}) collective-permute-start(bf16[64,3072]{1,0:T(8,128)(2,1)S(1)} %copy-done.89), channel_id=1, source_target_pairs={{8,0},{16,8},{24,16},{0,24},{9,1},{17,9},{25,17},{1,25},{10,2},{18... | collective-permute-start | bytes 1179656 | tf_op jit(solution)/shard_map/ppermute | solution.py:23
  78.9 15.4 %collective-permute-start.17 = (bf16[64,3072]{1,0:T(8,128)(2,1)S(1)}, bf16[64,3072]{1,0:T(8,128)(2,1)S(1)}, u32[]{:S(2)}, u32[]{:S(2)}) collective-permute-start(bf16[64,3072]{1,0:T(8,128)(2,1)S(1)} %collective-permute-done.15.refs_5_), channel_id=1, source_target_pairs={{8,0},{16,8},{24,16},{0,24},{9,1},{17,9},{25,17},{1,25},{10,2},{18... | collective-permute-start | bytes 1179656 | tf_op jit(solution)/shard_map/ppermute | solution.py:23
  92.8 13.2 %collective-permute-start.16 = (bf16[1,2,144,768]{3,2,1,0:T(8,128)(2,1)S(1)}, bf16[1,2,144,768]{3,2,1,0:T(8,128)(2,1)S(1)}, u32[]{:S(2)}, u32[]{:S(2)}) collective-permute-start(bf16[1,2,144,768]{3,2,1,0:T(8,128)(2,1)S(1)} %bitcast.95), channel_id=1, source_target_pairs={{0,4},{2,6},{4,0},{6,2},{1,5},{3,7},{5,1},{7,3},{8,12},{10,14},{12... | collective-permute-start | bytes 1327112 | tf_op jit(solution)/shard_map/ppermute | solution.py:18
  94.3 12.0 %collective-permute-start.19 = (bf16[64,3072]{1,0:T(8,128)(2,1)S(1)}, bf16[64,3072]{1,0:T(8,128)(2,1)S(1)}, u32[]{:S(2)}, u32[]{:S(2)}) collective-permute-start(bf16[64,3072]{1,0:T(8,128)(2,1)S(1)} %collective-permute-done.17.refs_5_), channel_id=1, source_target_pairs={{8,0},{16,8},{24,16},{0,24},{9,1},{17,9},{25,17},{1,25},{10,2},{18... | collective-permute-start | bytes 1179656 | tf_op jit(solution)/shard_map/ppermute | solution.py:23
  94.5 18.1 %collective-permute-start.20 = (bf16[3,64,1024]{2,1,0:T(8,128)(2,1)S(1)}, bf16[3,64,1024]{2,1,0:T(8,128)(2,1)S(1)}, u32[]{:S(2)}, u32[]{:S(2)}) collective-permute-start(bf16[3,64,1024]{2,1,0:T(8,128)(2,1)S(1)} %get-tuple-element.310.refs_0_), channel_id=1, source_target_pairs={{0,4},{2,6},{4,0},{6,2},{1,5},{3,7},{5,1},{7,3},{8,12},{10,14},{12... | collective-permute-start | bytes 1179656 | tf_op jit(solution)/shard_map/ppermute | solution.py:18
  106.2 128.0 %copy-start.24 = (bf16[2,2,144,768]{3,2,1,0:T(8,128)(2,1)}, bf16[2,2,144,768]{3,2,1,0:T(8,128)(2,1)S(1)}, u32[]{:S(2)}) copy-start(bf16[2,2,144,768]{3,2,1,0:T(8,128)(2,1)S(1)} %get-tuple-element.309.refs_1_) | copy-start | bytes 2654212
  106.2 12.4 %collective-permute-start.18 = (bf16[2,2,144,768]{3,2,1,0:T(8,128)(2,1)S(1)}, bf16[2,2,144,768]{3,2,1,0:T(8,128)(2,1)}, u32[]{:S(2)}, u32[]{:S(2)}) collective-permute-start(bf16[2,2,144,768]{3,2,1,0:T(8,128)(2,1)S(1)} %get-tuple-element.309.refs_1_), channel_id=1, source_target_pairs={{0,2},{2,0},{4,6},{6,4},{1,3},{3,1},{5,7},{7,5},{8,10},{10,8},{12,... | collective-permute-start | bytes 2654216 | tf_op jit(solution)/shard_map/ppermute | solution.py:18
  113.5 7.7 %collective-permute-start.21 = (bf16[6,64,1024]{2,1,0:T(8,128)(2,1)}, bf16[6,64,1024]{2,1,0:T(8,128)(2,1)}, u32[]{:S(2)}, u32[]{:S(2)}) collective-permute-start(bf16[6,64,1024]{2,1,0:T(8,128)(2,1)} %get-tuple-element.317.refs_2_), channel_id=1, source_target_pairs={{0,2},{2,0},{4,6},{6,4},{1,3},{3,1},{5,7},{7,5},{8,10},{10,8},{12,... | collective-permute-start | bytes 2359304 | tf_op jit(solution)/shard_map/ppermute | solution.py:18
  117.1 28.4 %collective-permute-start.23 = (bf16[3,64,3072]{2,1,0:T(8,128)(2,1)S(1)}, bf16[3,64,3072]{2,1,0:T(8,128)(2,1)S(1)}, u32[]{:S(2)}, u32[]{:S(2)}) collective-permute-start(bf16[3,64,3072]{2,1,0:T(8,128)(2,1)S(1)} %get-tuple-element.331.refs_0_), channel_id=1, source_target_pairs={{0,4},{2,6},{4,0},{6,2},{1,5},{3,7},{5,1},{7,3},{8,12},{10,14},{12... | collective-permute-start | bytes 3538952 | tf_op jit(solution)/shard_map/ppermute | solution.py:18
  131.5 26.1 %collective-permute-start.27 = (bf16[512,1024]{1,0:T(8,128)(2,1)S(1)}, bf16[512,1024]{1,0:T(8,128)(2,1)S(1)}, u32[]{:S(2)}, u32[]{:S(2)}) collective-permute-start(bf16[512,1024]{1,0:T(8,128)(2,1)S(1)} %get-tuple-element.338.refs_1_), channel_id=1, source_target_pairs={{0,1},{1,0},{2,3},{3,2},{4,5},{5,4},{6,7},{7,6},{8,9},{9,8},{10,11... | collective-permute-start | bytes 3145736 | tf_op jit(solution)/shard_map/ppermute | solution.py:28
  145.7 3.8 collective-permute-start.24
  147.5 3.0 collective-permute-start.25
  147.6 4.1 collective-permute-start.26
  148.1 31.9 %collective-permute-start.22 = (bf16[512,1024]{1,0:T(8,128)(2,1)S(1)}, bf16[512,1024]{1,0:T(8,128)(2,1)S(1)}, u32[]{:S(2)}, u32[]{:S(2)}) collective-permute-start(bf16[512,1024]{1,0:T(8,128)(2,1)S(1)} %get-tuple-element.328.refs_1_), channel_id=1, source_target_pairs={{0,1},{1,0},{2,3},{3,2},{4,5},{5,4},{6,7},{7,6},{8,9},{9,8},{10,11... | collective-permute-start | bytes 3145736 | tf_op jit(solution)/shard_map/ppermute | solution.py:28
  168.4 33.4 %collective-permute-start.29 = (bf16[512,1024]{1,0:T(8,128)(2,1)S(1)}, bf16[512,1024]{1,0:T(8,128)(2,1)S(1)}, u32[]{:S(2)}, u32[]{:S(2)}) collective-permute-start(bf16[512,1024]{1,0:T(8,128)(2,1)S(1)} %get-tuple-element.348.refs_1_), channel_id=1, source_target_pairs={{0,1},{1,0},{2,3},{3,2},{4,5},{5,4},{6,7},{7,6},{8,9},{9,8},{10,11... | collective-permute-start | bytes 3145736 | tf_op jit(solution)/shard_map/ppermute | solution.py:28
  191.8 44.6 %copy-start = (f32[1024,1024]{1,0:T(8,128)}, f32[1024,1024]{1,0:T(8,128)S(1)}, u32[]{:S(2)}) copy-start(f32[1024,1024]{1,0:T(8,128)S(1)} %get-tuple-element.345.refs_0_) | copy-start | bytes 12582916
  206.5 15.9 %collective-permute-start.33 = (bf16[4,2,64,3072]{3,2,1,0:T(8,128)(2,1)S(1)}, bf16[4,2,64,3072]{3,2,1,0:T(8,128)(2,1)S(1)}, u32[]{:S(2)}, u32[]{:S(2)}) collective-permute-start(bf16[4,2,64,3072]{3,2,1,0:T(8,128)(2,1)S(1)} %get-tuple-element.367), channel_id=1, source_target_pairs={{0,2},{2,0},{4,6},{6,4},{1,3},{3,1},{5,7},{7,5},{8,10},{10,8},{12,... | collective-permute-start | bytes 9437192 | tf_op jit(solution)/shard_map/ppermute | solution.py:18
  206.5 29.9 %collective-permute-start.28 = (bf16[512,1024]{1,0:T(8,128)(2,1)}, bf16[512,1024]{1,0:T(8,128)(2,1)S(1)}, u32[]{:S(2)}, u32[]{:S(2)}) collective-permute-start(bf16[512,1024]{1,0:T(8,128)(2,1)} %get-tuple-element.347.refs_1_), channel_id=1, source_target_pairs={{0,1},{1,0},{2,3},{3,2},{4,5},{5,4},{6,7},{7,6},{8,9},{9,8},{10,11... | collective-permute-start | bytes 3145736 | tf_op jit(solution)/shard_map/ppermute | solution.py:28
  211.9 7.0 %collective-permute-start.30 = (bf16[1,1,128,768]{3,2,1,0:T(8,128)(2,1)S(1)}, bf16[1,1,128,768]{3,2,1,0:T(8,128)(2,1)S(1)}, u32[]{:S(2)}, u32[]{:S(2)}) collective-permute-start(bf16[1,1,128,768]{3,2,1,0:T(8,128)(2,1)S(1)} %bitcast.111), channel_id=1, source_target_pairs={{0,4},{2,6},{4,0},{6,2},{1,5},{3,7},{5,1},{7,3},{8,12},{10,14},{12... | collective-permute-start | bytes 589832 | tf_op jit(solution)/shard_map/ppermute | solution.py:18
  219.2 14.9 %collective-permute-start.31 = (bf16[2,1,128,768]{3,2,1,0:T(8,128)(2,1)S(1)}, bf16[2,1,128,768]{3,2,1,0:T(8,128)(2,1)S(1)}, u32[]{:S(2)}, u32[]{:S(2)}) collective-permute-start(bf16[2,1,128,768]{3,2,1,0:T(8,128)(2,1)S(1)} %get-tuple-element.363.refs_3_), channel_id=1, source_target_pairs={{0,2},{2,0},{4,6},{6,4},{1,3},{3,1},{5,7},{7,5},{8,10},{10,8},{12,... | collective-permute-start | bytes 1179656 | tf_op jit(solution)/shard_map/ppermute | solution.py:18
  222.3 11.2 %collective-permute-start.32 = (bf16[1,2,512,128]{3,2,1,0:T(8,128)(2,1)S(1)}, bf16[1,2,512,128]{3,2,1,0:T(8,128)(2,1)S(1)}, u32[]{:S(2)}, u32[]{:S(2)}) collective-permute-start(bf16[1,2,512,128]{3,2,1,0:T(8,128)(2,1)S(1)} %get-tuple-element.365), channel_id=1, source_target_pairs={{0,2},{2,0},{4,6},{6,4},{1,3},{3,1},{5,7},{7,5},{8,10},{10,8},{12,... | collective-permute-start | bytes 786440 | tf_op jit(solution)/shard_map/ppermute | solution.py:18
  224.4 48.6 %collective-permute-start.37 = (bf16[4,1,64,3072]{3,2,1,0:T(8,128)(2,1)S(1)}, bf16[4,1,64,3072]{3,2,1,0:T(8,128)(2,1)S(1)}, u32[]{:S(2)}, u32[]{:S(2)}) collective-permute-start(bf16[4,1,64,3072]{3,2,1,0:T(8,128)(2,1)S(1)} %get-tuple-element.387), channel_id=1, source_target_pairs={{0,4},{2,6},{4,0},{6,2},{1,5},{3,7},{5,1},{7,3},{8,12},{10,14},{12... | collective-permute-start | bytes 4718600 | tf_op jit(solution)/shard_map/ppermute | solution.py:18
  244.4 49.8 %collective-permute-start.34 = (bf16[1024,1024]{1,0:T(8,128)(2,1)S(1)}, bf16[1024,1024]{1,0:T(8,128)(2,1)S(1)}, u32[]{:S(2)}, u32[]{:S(2)}) collective-permute-start(bf16[1024,1024]{1,0:T(8,128)(2,1)S(1)} %get-tuple-element.375.refs_1_), channel_id=1, source_target_pairs={{0,1},{1,0},{2,3},{3,2},{4,5},{5,4},{6,7},{7,6},{8,9},{9,8},{10,11... | collective-permute-start | bytes 6291464 | tf_op jit(solution)/shard_map/ppermute | solution.py:28
  245.0 27.7 %collective-permute-start.35 = (bf16[1,1,128,768]{3,2,1,0:T(8,128)(2,1)S(1)}, bf16[1,1,128,768]{3,2,1,0:T(8,128)(2,1)S(1)}, u32[]{:S(2)}, u32[]{:S(2)}) collective-permute-start(bf16[1,1,128,768]{3,2,1,0:T(8,128)(2,1)S(1)} %bitcast.106), channel_id=1, source_target_pairs={{0,4},{2,6},{4,0},{6,2},{1,5},{3,7},{5,1},{7,3},{8,12},{10,14},{12... | collective-permute-start | bytes 589832 | tf_op jit(solution)/shard_map/ppermute | solution.py:18
  272.9 3.0 collective-permute-start.36
  302.1 11.0 %collective-permute-start.38 = (bf16[4,2,64,3072]{3,2,1,0:T(8,128)(2,1)S(1)}, bf16[4,2,64,3072]{3,2,1,0:T(8,128)(2,1)S(1)}, u32[]{:S(2)}, u32[]{:S(2)}) collective-permute-start(bf16[4,2,64,3072]{3,2,1,0:T(8,128)(2,1)S(1)} %get-tuple-element.403), channel_id=1, source_target_pairs={{0,2},{2,0},{4,6},{6,4},{1,3},{3,1},{5,7},{7,5},{8,10},{10,8},{12,... | collective-permute-start | bytes 9437192 | tf_op jit(solution)/shard_map/ppermute | solution.py:18
  302.9 5.5 %collective-permute-start.39 = (bf16[1,1,512,128]{3,2,1,0:T(8,128)(2,1)S(1)}, bf16[1,1,512,128]{3,2,1,0:T(8,128)(2,1)S(1)}, u32[]{:S(2)}, u32[]{:S(2)}) collective-permute-start(bf16[1,1,512,128]{3,2,1,0:T(8,128)(2,1)S(1)} %get-tuple-element.406), channel_id=1, source_target_pairs={{0,4},{2,6},{4,0},{6,2},{1,5},{3,7},{5,1},{7,3},{8,12},{10,14},{12... | collective-permute-start | bytes 393224 | tf_op jit(solution)/shard_map/ppermute | solution.py:18
  317.8 40.2 %collective-permute-start.46 = (bf16[4,1,64,3072]{3,2,1,0:T(8,128)(2,1)}, bf16[4,1,64,3072]{3,2,1,0:T(8,128)(2,1)}, u32[]{:S(2)}, u32[]{:S(2)}) collective-permute-start(bf16[4,1,64,3072]{3,2,1,0:T(8,128)(2,1)} %get-tuple-element.426), channel_id=1, source_target_pairs={{0,4},{2,6},{4,0},{6,2},{1,5},{3,7},{5,1},{7,3},{8,12},{10,14},{12... | collective-permute-start | bytes 4718600 | tf_op jit(solution)/shard_map/ppermute | solution.py:18
  319.5 24.3 %collective-permute-start.40 = (bf16[512,1024]{1,0:T(8,128)(2,1)}, bf16[512,1024]{1,0:T(8,128)(2,1)}, u32[]{:S(2)}, u32[]{:S(2)}) collective-permute-start(bf16[512,1024]{1,0:T(8,128)(2,1)} %get-tuple-element.411.refs_1_), channel_id=1, source_target_pairs={{0,1},{1,0},{2,3},{3,2},{4,5},{5,4},{6,7},{7,6},{8,9},{9,8},{10,11... | collective-permute-start | bytes 3145736 | tf_op jit(solution)/shard_map/ppermute | solution.py:28
  320.0 26.6 %collective-permute-start.42 = (bf16[64,3072]{1,0:T(8,128)(2,1)}, bf16[64,3072]{1,0:T(8,128)(2,1)S(1)}, u32[]{:S(2)}, u32[]{:S(2)}) collective-permute-start(bf16[64,3072]{1,0:T(8,128)(2,1)} %copy-done.57), channel_id=1, source_target_pairs={{8,0},{16,8},{24,16},{0,24},{9,1},{17,9},{25,17},{1,25},{10,2},{18... | collective-permute-start | bytes 1179656 | tf_op jit(solution)/shard_map/ppermute | solution.py:23
  320.4 33.8 %collective-permute-start.43 = (bf16[64,3072]{1,0:T(8,128)(2,1)}, bf16[64,3072]{1,0:T(8,128)(2,1)S(1)}, u32[]{:S(2)}, u32[]{:S(2)}) collective-permute-start(bf16[64,3072]{1,0:T(8,128)(2,1)} %copy-done.56), channel_id=1, source_target_pairs={{16,0},{24,8},{0,16},{8,24},{17,1},{25,9},{1,17},{9,25},{18,2},{26... | collective-permute-start | bytes 1179656 | tf_op jit(solution)/shard_map/ppermute | solution.py:23
  321.1 33.2 %collective-permute-start.44 = (bf16[64,3072]{1,0:T(8,128)(2,1)}, bf16[64,3072]{1,0:T(8,128)(2,1)S(1)}, u32[]{:S(2)}, u32[]{:S(2)}) collective-permute-start(bf16[64,3072]{1,0:T(8,128)(2,1)} %copy-done.55), channel_id=1, source_target_pairs={{24,0},{0,8},{8,16},{16,24},{25,1},{1,9},{9,17},{17,25},{26,2},{2,... | collective-permute-start | bytes 1179656 | tf_op jit(solution)/shard_map/ppermute | solution.py:23
  343.8 12.9 %collective-permute-start.41 = (bf16[1,2,512,128]{3,2,1,0:T(8,128)(2,1)S(1)}, bf16[1,2,512,128]{3,2,1,0:T(8,128)(2,1)S(1)}, u32[]{:S(2)}, u32[]{:S(2)}) collective-permute-start(bf16[1,2,512,128]{3,2,1,0:T(8,128)(2,1)S(1)} %get-tuple-element.415), channel_id=1, source_target_pairs={{0,2},{2,0},{4,6},{6,4},{1,3},{3,1},{5,7},{7,5},{8,10},{10,8},{12,... | collective-permute-start | bytes 786440 | tf_op jit(solution)/shard_map/ppermute | solution.py:18
  356.4 10.8 %collective-permute-start.48 = (bf16[1,64,3072]{2,1,0:T(8,128)(2,1)}, bf16[1,64,3072]{2,1,0:T(8,128)(2,1)}, u32[]{:S(2)}, u32[]{:S(2)}) collective-permute-start(bf16[1,64,3072]{2,1,0:T(8,128)(2,1)} %bitcast.40.refs_0_), channel_id=1, source_target_pairs={{0,4},{2,6},{4,0},{6,2},{1,5},{3,7},{5,1},{7,3},{8,12},{10,14},{12... | collective-permute-start | bytes 1179656 | tf_op jit(solution)/shard_map/ppermute | solution.py:18
  364.7 9.8 %collective-permute-start.47 = (bf16[64,3072]{1,0:T(8,128)(2,1)}, bf16[64,3072]{1,0:T(8,128)(2,1)}, u32[]{:S(2)}, u32[]{:S(2)}) collective-permute-start(bf16[64,3072]{1,0:T(8,128)(2,1)} %get-tuple-element.428), channel_id=1, source_target_pairs={{8,0},{16,8},{24,16},{0,24},{9,1},{17,9},{25,17},{1,25},{10,2},{18... | collective-permute-start | bytes 1179656 | tf_op jit(solution)/shard_map/ppermute | solution.py:23
  364.7 14.7 %collective-permute-start.45 = (bf16[1,1,512,128]{3,2,1,0:T(8,128)(2,1)}, bf16[1,1,512,128]{3,2,1,0:T(8,128)(2,1)S(1)}, u32[]{:S(2)}, u32[]{:S(2)}) collective-permute-start(bf16[1,1,512,128]{3,2,1,0:T(8,128)(2,1)} %get-tuple-element.423), channel_id=1, source_target_pairs={{0,4},{2,6},{4,0},{6,2},{1,5},{3,7},{5,1},{7,3},{8,12},{10,14},{12... | collective-permute-start | bytes 393224 | tf_op jit(solution)/shard_map/ppermute | solution.py:18
  371.8 43.9 %collective-permute-start.54 = (bf16[2,64,3072]{2,1,0:T(8,128)(2,1)}, bf16[2,64,3072]{2,1,0:T(8,128)(2,1)}, u32[]{:S(2)}, u32[]{:S(2)}) collective-permute-start(bf16[2,64,3072]{2,1,0:T(8,128)(2,1)} %get-tuple-element.455.refs_1_), channel_id=1, source_target_pairs={{0,2},{2,0},{4,6},{6,4},{1,3},{3,1},{5,7},{7,5},{8,10},{10,8},{12,... | collective-permute-start | bytes 2359304 | tf_op jit(solution)/shard_map/ppermute | solution.py:18
  389.8 9.8 %collective-permute-start.51 = (f32[1024]{0:T(1024)S(1)}, f32[1024]{0:T(1024)S(1)}, u32[]{:S(2)}, u32[]{:S(2)}) collective-permute-start(f32[1024]{0:T(1024)S(1)} %bitcast.134), channel_id=1, source_target_pairs={{0,1},{1,0},{2,3},{3,2},{4,5},{5,4},{6,7},{7,6},{8,9},{9,8},{10,11... | collective-permute-start | bytes 12296 | tf_op jit(solution)/shard_map/ppermute | solution.py:28
  391.3 10.9 %collective-permute-start.50 = (bf16[64,3072]{1,0:T(8,128)(2,1)}, bf16[64,3072]{1,0:T(8,128)(2,1)}, u32[]{:S(2)}, u32[]{:S(2)}) collective-permute-start(bf16[64,3072]{1,0:T(8,128)(2,1)} %get-tuple-element.437), channel_id=1, source_target_pairs={{8,0},{16,8},{24,16},{0,24},{9,1},{17,9},{25,17},{1,25},{10,2},{18... | collective-permute-start | bytes 1179656 | tf_op jit(solution)/shard_map/ppermute | solution.py:23
  393.9 23.8 %collective-permute-start.49 = (bf16[512,1024]{1,0:T(8,128)(2,1)}, bf16[512,1024]{1,0:T(8,128)(2,1)S(1)}, u32[]{:S(2)}, u32[]{:S(2)}) collective-permute-start(bf16[512,1024]{1,0:T(8,128)(2,1)} %get-tuple-element.434.refs_1_), channel_id=1, source_target_pairs={{0,1},{1,0},{2,3},{3,2},{4,5},{5,4},{6,7},{7,6},{8,9},{9,8},{10,11... | collective-permute-start | bytes 3145736 | tf_op jit(solution)/shard_map/ppermute | solution.py:28
  400.7 12.8 %collective-permute-start.52 = (bf16[4,2,64,512]{3,2,1,0:T(8,128)(2,1)}, bf16[4,2,64,512]{3,2,1,0:T(8,128)(2,1)S(1)}, u32[]{:S(2)}, u32[]{:S(2)}) collective-permute-start(bf16[4,2,64,512]{3,2,1,0:T(8,128)(2,1)} %get-tuple-element.570), channel_id=1, source_target_pairs={{0,2},{2,0},{4,6},{6,4},{1,3},{3,1},{5,7},{7,5},{8,10},{10,8},{12,... | collective-permute-start | bytes 1572872 | tf_op jit(solution)/shard_map/ppermute | solution.py:18
  405.9 16.0 %collective-permute-start.58 = (bf16[64,3072]{1,0:T(8,128)(2,1)S(1)}, bf16[64,3072]{1,0:T(8,128)(2,1)S(1)}, u32[]{:S(2)}, u32[]{:S(2)}) collective-permute-start(bf16[64,3072]{1,0:T(8,128)(2,1)S(1)} %get-tuple-element.462), channel_id=1, source_target_pairs={{8,0},{16,8},{24,16},{0,24},{9,1},{17,9},{25,17},{1,25},{10,2},{18... | collective-permute-start | bytes 1179656 | tf_op jit(solution)/shard_map/ppermute | solution.py:23
  414.2 7.1 %collective-permute-start.53 = (bf16[4,1,64,512]{3,2,1,0:T(8,128)(2,1)S(1)}, bf16[4,1,64,512]{3,2,1,0:T(8,128)(2,1)S(1)}, u32[]{:S(2)}, u32[]{:S(2)}) collective-permute-start(bf16[4,1,64,512]{3,2,1,0:T(8,128)(2,1)S(1)} %get-tuple-element.454), channel_id=1, source_target_pairs={{0,4},{2,6},{4,0},{6,2},{1,5},{3,7},{5,1},{7,3},{8,12},{10,14},{12... | collective-permute-start | bytes 786440 | tf_op jit(solution)/shard_map/ppermute | solution.py:18
  422.3 4.2 collective-permute-start.59
  422.9 5.0 %collective-permute-start.55 = (bf16[64,512]{1,0:T(8,128)(2,1)S(1)}, bf16[64,512]{1,0:T(8,128)(2,1)S(1)}, u32[]{:S(2)}, u32[]{:S(2)}) collective-permute-start(bf16[64,512]{1,0:T(8,128)(2,1)S(1)} %get-tuple-element.459), channel_id=1, source_target_pairs={{8,0},{16,8},{24,16},{0,24},{9,1},{17,9},{25,17},{1,25},{10,2},{18... | collective-permute-start | bytes 196616 | tf_op jit(solution)/shard_map/ppermute | solution.py:23
  425.2 5.2 %collective-permute-start.56 = (bf16[64,512]{1,0:T(8,128)(2,1)S(1)}, bf16[64,512]{1,0:T(8,128)(2,1)S(1)}, u32[]{:S(2)}, u32[]{:S(2)}) collective-permute-start(bf16[64,512]{1,0:T(8,128)(2,1)S(1)} %get-tuple-element.460), channel_id=1, source_target_pairs={{16,0},{24,8},{0,16},{8,24},{17,1},{25,9},{1,17},{9,25},{18,2},{26... | collective-permute-start | bytes 196616 | tf_op jit(solution)/shard_map/ppermute | solution.py:23
  425.2 6.1 %collective-permute-start.57 = (bf16[64,512]{1,0:T(8,128)(2,1)S(1)}, bf16[64,512]{1,0:T(8,128)(2,1)S(1)}, u32[]{:S(2)}, u32[]{:S(2)}) collective-permute-start(bf16[64,512]{1,0:T(8,128)(2,1)S(1)} %get-tuple-element.461), channel_id=1, source_target_pairs={{24,0},{0,8},{8,16},{16,24},{25,1},{1,9},{9,17},{17,25},{26,2},{2,... | collective-permute-start | bytes 196616 | tf_op jit(solution)/shard_map/ppermute | solution.py:23
  431.9 8.5 %collective-permute-start.60 = (bf16[1,64,3584]{2,1,0:T(8,128)(2,1)S(1)}, bf16[1,64,3584]{2,1,0:T(8,128)(2,1)S(1)}, u32[]{:S(2)}, u32[]{:S(2)}) collective-permute-start(bf16[1,64,3584]{2,1,0:T(8,128)(2,1)S(1)} %maximum_bitcast_fusion.refs_0_), channel_id=1, source_target_pairs={{0,4},{2,6},{4,0},{6,2},{1,5},{3,7},{5,1},{7,3},{8,12},{10,14},{12... | collective-permute-start | bytes 1376264 | tf_op jit(solution)/shard_map/ppermute | solution.py:18
  440.8 2.5 collective-permute-start.61
  (90 other events, 684.1 us)

commit v6 on v5

--- a/solution.py
+++ b/solution.py
@@ -1366,9 +1366,9 @@
     at_zx = q_dim + ssm_dim
     at_rest = at_zx + 2 * ssm_dim
     wide = wide_second = at_rest + 2 * state_dim + 256
-    pair_second = outer(place, dm, og, None, 0, wide)
     for u in range(units):
         if u == units - 1:
+            pair_second = outer(place, dm, og, None, 0, wide)
             pair = close_states(u)
             parts_fourth = to_owners(keep_fourth, got_fourth)
             d_span.append(chain_states(place, spans, state_dim, pair, u)[0])

time: 458 us -> 458 us (level)
  no operation moved by 1% of the time
where the time goes in v6:
time: 458 us; the launch traced here: 449 us
  Pallas kernels  227 us (50%)
  waiting for transfers between devices  121 us (26%)
  starting transfers between devices  69.1 us (15%)
  local copies, waits for them, and re-layouts  27.3 us (6%)
    pallas_call x75, Pallas kernels, call(): pl.pallas_call(run, grid=grid, out_shape=outs + (jax.ShapeDtypeStruct((8,...  227 us
    ppermute x21, waiting for transfers between devices, from_next(): return lax.ppermute(x, axis, [((i + step) % size, i) for i in range(size)])  53.9 us
    ppermute x32, waiting for transfers between devices, swap_context(): return lax.ppermute(x, 'context', [(i, i ^ bit) for i in range(size)])  37.5 us
    ppermute x32, starting transfers between devices, swap_context(): return lax.ppermute(x, 'context', [(i, i ^ bit) for i in range(size)])  32.3 us
    ppermute x9, waiting for transfers between devices, swap_tensor(): return lax.ppermute(x, 'tensor', [(i, (i + 1) % size) for i in range(size)])  29.2 us
    ppermute x21, starting transfers between devices, from_next(): return lax.ppermute(x, axis, [((i + step) % size, i) for i in range(size)])  27.9 us
    unnamed x184, local copies, waits for them, and re-layouts  22.8 us
  transfers between devices with their start and end apart: 62, of which 29 were waited for; matrix products, arithmetic and copies ran while one was open for 1% of the time, Pallas kernels for 45%

profile of v6, /device:TPU:0, one launch (start us, length us, event | category | flops | bytes accessed | tf_op | source)
XLA Modules:
  0.0 448.9 jit_solution(4980505092926056661)
XLA Ops:
  5.1 3.0 collective-permute-start.2
  11.2 2.2 pack_second.1
  15.5 2.9 pack_fourth.1
  25.0 4.0 collective-permute-done.4.refs_3_
  29.0 11.2 %collective-permute-done.5.refs_4_ = bf16[64,1536]{1,0:T(8,128)(2,1)S(1)} collective-permute-done((bf16[64,1536]{1,0:T(8,128)(2,1)S(1)}, bf16[64,1536]{1,0:T(8,128)(2,1)S(1)}, u32[]{:S(2)}, u32[]{:S(2)}) %collective-permute-start.5) | collective-permute-done | bytes 196640 | tf_op jit(solution)/shard_map/ppermute | solution.py:23
  44.0 2.3 place_rows.4
  46.4 5.1 %project.1 = (bf16[1024,1024]{1,0:T(8,128)(2,1)S(1)}, bf16[1024,256]{1,0:T(8,128)(2,1)S(1)}, bf16[1024,128]{1,0:T(8,128)(2,1)S(1)}, bf16[1024,128]{1,0:T(8,128)(...) custom-call(s32[2]{0:T(128)S(1)} %copy-done.48, ...), custom_call_target="tpu_custom_call" | custom-call | flops 2600000000 | bytes 1 | tf_op jit(solution)/shard_map/project/pallas_call | solution.py:77
  52.6 2.2 collective-permute-start.11
  57.4 9.4 %collective-permute-done.11.refs_4_ = bf16[64,1024]{1,0:T(8,128)(2,1)S(1)} collective-permute-done((bf16[64,1024]{1,0:T(8,128)(2,1)S(1)}, bf16[64,1024]{1,0:T(8,128)(2,1)S(1)}, u32[]{:S(2)}, u32[]{:S(2)}) %collective-permute-start.11) | collective-permute-done | bytes 131104 | tf_op jit(solution)/shard_map/ppermute | solution.py:23
  67.8 11.0 %collective-permute-done.15.refs_5_ = bf16[64,3072]{1,0:T(8,128)(2,1)S(1)} collective-permute-done((bf16[64,3072]{1,0:T(8,128)(2,1)S(1)}, bf16[64,3072]{1,0:T(8,128)(2,1)S(1)}, u32[]{:S(2)}, u32[]{:S(2)}) %collective-permute-start.15) | collective-permute-done | bytes 393248 | tf_op jit(solution)/shard_map/ppermute | solution.py:23
  83.4 4.2 project_mixer.1
  87.6 2.5 mamba_state.4
  90.1 2.5 mamba_state.5
  95.0 3.3 attention_forward.2
  98.3 7.6 %collective-permute-done.16.refs_1_ = bf16[1,2,144,768]{3,2,1,0:T(8,128)(2,1)S(1)} collective-permute-done((bf16[1,2,144,768]{3,2,1,0:T(8,128)(2,1)S(1)}, bf16[1,2,144,768]{3,2,1,0:T(8,128)(2,1)S(1)}, u32[]{:S(2)}, u32[]{:S(2)}) %collective-permute-start.16) | collective-permute-done | bytes 442400 | tf_op jit(solution)/shard_map/ppermute | solution.py:18
  106.3 6.2 %collective-permute-done.20.refs_1_ = bf16[3,64,1024]{2,1,0:T(8,128)(2,1)S(1)} collective-permute-done((bf16[3,64,1024]{2,1,0:T(8,128)(2,1)S(1)}, bf16[3,64,1024]{2,1,0:T(8,128)(2,1)S(1)}, u32[]{:S(2)}, u32[]{:S(2)}) %collective-permute-start.20) | collective-permute-done | bytes 393248 | tf_op jit(solution)/shard_map/ppermute | solution.py:18
  118.6 2.5 chain_states.3
  122.9 7.0 %mamba_forward.2 = (bf16[1024,1024]{1,0:T(8,128)(2,1)S(1)}, f32[512,768]{1,0:T(8,128)S(1)}, f32[8,128]{1,0:T(8,128)S(1)}) custom-call(s32[2]{0:T(128)S(1)} %copy-done.48, s32[2,4]{1,0:T(2,128)S(1)} %bitcast.121, f32[2,6,8,512]{3,2,1,0:T(8,128)S(1)} %get-tuple-element.280.refs_0_.refs_2_, ...), custom_call_target="tpu_custom_call", output_to_operand_aliasing={{0}: (8, {})} | custom-call | flops 3000000000 | bytes 1 | tf_op jit(solution)/shard_map/mamba_forward/pallas_call | solution.py:77
  133.1 3.3 attention_forward.3
  136.4 7.0 %mamba_forward.3 = (bf16[1024,1024]{1,0:T(8,128)(2,1)S(1)}, f32[512,768]{1,0:T(8,128)S(1)}, f32[8,128]{1,0:T(8,128)S(1)}) custom-call(s32[2]{0:T(128)S(1)} %copy-done.48, s32[2,4]{1,0:T(2,128)S(1)} %bitcast.123, f32[2,6,8,512]{3,2,1,0:T(8,128)S(1)} %get-tuple-element.280.refs_0_.refs_2_, ...), custom_call_target="tpu_custom_call", output_to_operand_aliasing={{0}: (8, {})} | custom-call | flops 3000000000 | bytes 1 | tf_op jit(solution)/shard_map/mamba_forward/pallas_call | solution.py:77
  151.7 2.4 place_rows.7
  154.1 3.5 collective-permute-done.27.refs_2_
  157.6 10.8 %feed_forward.2 = (f32[1024,1024]{1,0:T(8,128)S(1)}, bf16[1024,1024]{1,0:T(8,128)(2,1)S(1)}, bf16[1024,1024]{1,0:T(8,128)(2,1)S(1)}, bf16[1024,2048]{1,0:T(8,128...) custom-call(bf16[1024,1024]{1,0:T(8,128)(2,1)S(1)} %bitcast.74, ...), custom_call_target="tpu_custom_call" | custom-call | flops 5600000000 | bytes 1 | tf_op jit(solution)/shard_map/feed_forward/pallas_call | solution.py:77
  170.0 10.0 %collective-permute-done.22.refs_2_ = bf16[512,1024]{1,0:T(8,128)(2,1)S(1)} collective-permute-done((bf16[512,1024]{1,0:T(8,128)(2,1)S(1)}, bf16[512,1024]{1,0:T(8,128)(2,1)S(1)}, u32[]{:S(2)}, u32[]{:S(2)}) %collective-permute-start.22) | collective-permute-done | bytes 1048608 | tf_op jit(solution)/shard_map/ppermute | solution.py:28
  180.0 11.8 %feed_forward.3 = (f32[1024,1024]{1,0:T(8,128)S(1)}, bf16[1024,1024]{1,0:T(8,128)(2,1)S(1)}, bf16[1024,1024]{1,0:T(8,128)(2,1)S(1)}, bf16[1024,2048]{1,0:T(8,128...) custom-call(bf16[1024,1024]{1,0:T(8,128)(2,1)S(1)} %bitcast.75, ...), custom_call_target="tpu_custom_call", output_to_operand_aliasing={{0}: (7, {}), {1}: (8, {}), {2}: (9, {}), {3}: (10, {})} | custom-call | flops 5600000000 | bytes 1 | tf_op jit(solution)/shard_map/feed_forward/pallas_call | solution.py:77
  191.8 7.5 %outer.6 = (bf16[4,2,64,3072]{3,2,1,0:T(8,128)(2,1)S(1)}, bf16[4,2,64,3072]{3,2,1,0:T(8,128)(2,1)S(1)}, f32[8,128]{1,0:T(8,128)S(1)}) custom-call(s32[2]{0:T(128)S(1)} %copy-done.48, bf16[1024,1024]{1,0:T(8,128)(2,1)S(1)} %get-tuple-element.349.refs_1_, bf16[1024,2048]{1,0:T(8,128)(2,1)S(1)} %get-tuple-element.350.refs_2_, ...), custom_call_target="tpu_custom_call" | custom-call | flops 3561739008 | bytes 1 | tf_op jit(solution)/shard_map/outer/pallas_call | solution.py:77
  199.3 2.5 collective-permute-done.29.refs_6_.refs_2_
  201.8 4.7 %outer.7 = (bf16[4,2,64,3072]{3,2,1,0:T(8,128)(2,1)S(1)}, bf16[4,2,64,3072]{3,2,1,0:T(8,128)(2,1)S(1)}, f32[8,128]{1,0:T(8,128)S(1)}) custom-call(s32[2]{0:T(128)S(1)} %copy-done.48, bf16[1024,1024]{1,0:T(8,128)(2,1)S(1)} %bitcast.86, bf16[1024,1024]{1,0:T(8,128)(2,1)S(1)} %get-tuple-element.346.refs_2_.refs_0_, ...), custom_call_target="tpu_custom_call", output_to_operand_aliasing={{0}: (3, {}), {1}: (4, {})} | custom-call | flops 1780869504 | bytes 1 | tf_op jit(solution)/shard_map/outer/pallas_call | solution.py:77
  212.5 5.2 %attention_backward.2 = (bf16[512,256]{1,0:T(8,128)(2,1)S(1)}, bf16[1,2,512,128]{3,2,1,0:T(8,128)(2,1)S(1)}, bf16[1,2,512,128]{3,2,1,0:T(8,128)(2,1)S(1)}, f32[8,128]{1,0:T(8,128)S(1)}) custom-call(s32[2]{0:T(128)S(1)} %copy-done.48, s32[2,4]{1,0:T(2,128)S(1)} %bitcast.124, bf16[1024,256]{1,0:T(8,128)(2,1)S(1)} %copy-done.81, ...), custom_call_target="tpu_custom_call" | custom-call | flops 6800000000 | bytes 1 | tf_op jit(solution)/shard_map/attention_backward/pallas_call | solution.py:77
  219.2 3.1 collective-permute-start.31
  224.4 9.1 %collective-permute-start.37 = (bf16[4,1,64,3072]{3,2,1,0:T(8,128)(2,1)S(1)}, bf16[4,1,64,3072]{3,2,1,0:T(8,128)(2,1)S(1)}, u32[]{:S(2)}, u32[]{:S(2)}) collective-permute-start(bf16[4,1,64,3072]{3,2,1,0:T(8,128)(2,1)S(1)} %get-tuple-element.387), channel_id=1, source_target_pairs={{0,4},{2,6},{4,0},{6,2},{1,5},{3,7},{5,1},{7,3},{8,12},{10,14},{12... | collective-permute-start | bytes 4718600 | tf_op jit(solution)/shard_map/ppermute | solution.py:18
  234.2 2.2 chain_states.4
  236.4 3.3 middle_backward.3
  241.4 2.7 feed_forward_out.1
  244.8 15.5 %mamba_backward.2 = (bf16[1024,1536]{1,0:T(8,128)(2,1)S(1)}, bf16[1024,512]{1,0:T(8,128)(2,1)S(1)}, f32[16,128]{1,0:T(8,128)S(1)}, f32[8,128]{1,0:T(8,128)S(1)}) custom-call(s32[2]{0:T(128)S(1)} %copy-done.48, s32[2,4]{1,0:T(2,128)S(1)} %bitcast.125, f32[2,6,8,512]{3,2,1,0:T(8,128)S(1)} %get-tuple-element.280.refs_0_.refs_2_, ...), custom_call_target="tpu_custom_call" | custom-call | flops 6520000000 | bytes 1 | tf_op jit(solution)/shard_map/mamba_backward/pallas_call | solution.py:77
  260.3 4.3 outer.8
  264.6 8.1 %collective-permute-done.35.refs_1_ = bf16[1,1,128,768]{3,2,1,0:T(8,128)(2,1)S(1)} collective-permute-done((bf16[1,1,128,768]{3,2,1,0:T(8,128)(2,1)S(1)}, bf16[1,1,128,768]{3,2,1,0:T(8,128)(2,1)S(1)}, u32[]{:S(2)}, u32[]{:S(2)}) %collective-permute-start.35) | collective-permute-done | bytes 196640 | tf_op jit(solution)/shard_map/ppermute | solution.py:18
  275.9 2.5 chain_states.5
  278.4 15.8 %mamba_backward.3 = (bf16[1024,1536]{1,0:T(8,128)(2,1)S(1)}, bf16[1024,512]{1,0:T(8,128)(2,1)S(1)}, f32[16,128]{1,0:T(8,128)S(1)}, f32[8,128]{1,0:T(8,128)S(1)}) custom-call(s32[2]{0:T(128)S(1)} %copy-done.48, s32[2,4]{1,0:T(2,128)S(1)} %bitcast.126, ...), custom_call_target="tpu_custom_call", output_to_operand_aliasing={{0}: (12, {}), {1}: (13, {})} | custom-call | flops 6520000000 | bytes 1 | tf_op jit(solution)/shard_map/mamba_backward/pallas_call | solution.py:77
  294.3 5.9 %outer.9 = (bf16[4,2,64,3072]{3,2,1,0:T(8,128)(2,1)S(1)}, bf16[4,2,64,3072]{3,2,1,0:T(8,128)(2,1)S(1)}, f32[8,128]{1,0:T(8,128)S(1)}) custom-call(s32[2]{0:T(128)S(1)} %copy-done.48, bf16[1024,1024]{1,0:T(8,128)(2,1)S(1)} %copy-done.9, bf16[1024,1536]{1,0:T(8,128)(2,1)S(1)} %get-tuple-element.395.refs_2_.refs_4_, ...), custom_call_target="tpu_custom_call", output_to_operand_aliasing={{0}: (3, {}), {1}: (4, {})} | custom-call | flops 2671304448 | bytes 1 | tf_op jit(solution)/shard_map/outer/pallas_call | solution.py:77
  304.6 3.7 collective-permute-done.39.refs_2_
  308.4 4.7 %input_backward.2 = (bf16[1024,384]{1,0:T(8,128)(2,1)S(1)}, bf16[512,1024]{1,0:T(8,128)(2,1)}, f32[8,1024]{1,0:T(8,128)S(1)}, f32[8,128]{1,0:T(8,128)S(1)}) custom-call(bf16[512,256]{1,0:T(8,128)(2,1)S(1)} %get-tuple-element.404.refs_0_, bf16[1,1,512,128]{3,2,1,0:T(8,128)(2,1)S(1)} %get-tuple-element.405.refs_1_, ...), custom_call_target="tpu_custom_call" | custom-call | flops 2600000000 | bytes 1 | tf_op jit(solution)/shard_map/input_backward/pallas_call | solution.py:77
  313.1 3.5 split_sum.7
  327.2 5.4 %attention_backward.3 = (bf16[512,256]{1,0:T(8,128)(2,1)S(1)}, bf16[1,2,512,128]{3,2,1,0:T(8,128)(2,1)S(1)}, bf16[1,2,512,128]{3,2,1,0:T(8,128)(2,1)S(1)}, f32[8,128]{1,0:T(8,128)S(1)}) custom-call(s32[2]{0:T(128)S(1)} %copy-done.48, s32[2,4]{1,0:T(2,128)S(1)} %bitcast.127, bf16[1024,256]{1,0:T(8,128)(2,1)S(1)} %copy-done.82, ...), custom_call_target="tpu_custom_call" | custom-call | flops 6800000000 | bytes 1 | tf_op jit(solution)/shard_map/attention_backward/pallas_call | solution.py:77
  332.6 11.3 %collective-permute-done.40.refs_4_.refs_2_ = bf16[512,1024]{1,0:T(8,128)(2,1)} collective-permute-done((bf16[512,1024]{1,0:T(8,128)(2,1)}, bf16[512,1024]{1,0:T(8,128)(2,1)}, u32[]{:S(2)}, u32[]{:S(2)}) %collective-permute-start.40) | collective-permute-done | bytes 1048608 | tf_op jit(solution)/shard_map/ppermute | solution.py:28
  346.6 7.7 %collective-permute-done.43.refs_2_ = bf16[64,3072]{1,0:T(8,128)(2,1)S(1)} collective-permute-done((bf16[64,3072]{1,0:T(8,128)(2,1)}, bf16[64,3072]{1,0:T(8,128)(2,1)S(1)}, u32[]{:S(2)}, u32[]{:S(2)}) %collective-permute-start.43) | collective-permute-done | bytes 393248 | tf_op jit(solution)/shard_map/ppermute | solution.py:23
  354.3 2.2 sum_parts.2
  358.0 4.5 %split_fsdp.4 = (bf16[64,3072]{1,0:T(8,128)(2,1)S(1)}, bf16[64,3072]{1,0:T(8,128)(2,1)S(1)}, bf16[64,3072]{1,0:T(8,128)(2,1)S(1)}, bf16[64,3072]{1,0:T(8,128)(2,1)}, f32[8,128]{1,0:T(8,128)S(1)}) custom-call(s32[2]{0:T(128)S(1)} %copy-done.48, bf16[4,1,64,3072]{3,2,1,0:T(8,128)(2,1)S(1)} %copy-done.51, ...), custom_call_target="tpu_custom_call" | custom-call | flops 1024000000 | bytes 1 | tf_op jit(solution)/shard_map/split_fsdp/pallas_call | solution.py:77
  367.3 4.6 %join.28 = (bf16[2,64,3072]{2,1,0:T(8,128)(2,1)}, f32[8,128]{1,0:T(8,128)S(1)}) custom-call(bf16[1,64,3072]{2,1,0:T(8,128)(2,1)} %bitcast.40.refs_0_, bf16[1,64,3072]{2,1,0:T(8,128)(2,1)} %collective-permute-done.48.refs_1_, f32[8,128]{1,0:T(8,128)S(1)} %get-tuple-element.431.refs_2_), custom_call_target="tpu_custom_call" | custom-call | flops 800000000 | bytes 1 | tf_op jit(solution)/shard_map/join/pallas_call | solution.py:77
  371.9 2.7 collective-permute-done.47.refs_0_
  375.6 3.9 ring_step.3
  384.3 4.7 %input_backward.3 = (bf16[1024,384]{1,0:T(8,128)(2,1)S(1)}, bf16[512,1024]{1,0:T(8,128)(2,1)}, f32[8,1024]{1,0:T(8,128)S(1)}, f32[8,128]{1,0:T(8,128)S(1)}) custom-call(bf16[512,256]{1,0:T(8,128)(2,1)S(1)} %copy-done.45, bf16[1,1,512,128]{3,2,1,0:T(8,128)(2,1)S(1)} %get-tuple-element.422.refs_1_, ...), custom_call_target="tpu_custom_call", output_to_operand_aliasing={{0}: (8, {})} | custom-call | flops 2600000000 | bytes 1 | tf_op jit(solution)/shard_map/input_backward/pallas_call | solution.py:77
  391.4 2.5 collective-permute-start.50
  394.4 3.6 outer.11
  403.2 2.7 ring_step.4
  405.9 3.6 collective-permute-start.58
  409.5 4.0 finish.2
  417.7 3.6 emit_fourth.1
  422.9 2.3 collective-permute-start.55
  427.9 2.5 collective-permute-done.56.refs_3_
  433.8 3.6 finish.3
  437.3 3.2 collective-permute-done.60.refs_1_
  440.9 2.5 collective-permute-done.61.refs_2_
  443.4 2.5 emit_second.1
  (347 shorter events, 120.7 us)
Async XLA Ops:
  5.1 13.3 %collective-permute-start.2 = (bf16[64,768]{1,0:T(8,128)(2,1)}, bf16[64,768]{1,0:T(8,128)(2,1)S(1)}, u32[]{:S(2)}, u32[]{:S(2)}) collective-permute-start(bf16[64,768]{1,0:T(8,128)(2,1)} %get-tuple-element.267), channel_id=1, source_target_pairs={{24,0},{0,8},{8,16},{16,24},{25,1},{1,9},{9,17},{17,25},{26,2},{2,... | collective-permute-start | bytes 294920 | tf_op jit(solution)/shard_map/ppermute | solution.py:23
  8.2 10.3 %collective-permute-start = (bf16[64,768]{1,0:T(8,128)(2,1)}, bf16[64,768]{1,0:T(8,128)(2,1)S(1)}, u32[]{:S(2)}, u32[]{:S(2)}) collective-permute-start(bf16[64,768]{1,0:T(8,128)(2,1)} %get-tuple-element.267), channel_id=1, source_target_pairs={{8,0},{16,8},{24,16},{0,24},{9,1},{17,9},{25,17},{1,25},{10,2},{18... | collective-permute-start | bytes 294920 | tf_op jit(solution)/shard_map/ppermute | solution.py:23
  10.2 9.3 %collective-permute-start.1 = (bf16[64,768]{1,0:T(8,128)(2,1)}, bf16[64,768]{1,0:T(8,128)(2,1)S(1)}, u32[]{:S(2)}, u32[]{:S(2)}) collective-permute-start(bf16[64,768]{1,0:T(8,128)(2,1)} %get-tuple-element.267), channel_id=1, source_target_pairs={{16,0},{24,8},{0,16},{8,24},{17,1},{25,9},{1,17},{9,25},{18,2},{26... | collective-permute-start | bytes 294920 | tf_op jit(solution)/shard_map/ppermute | solution.py:23
  20.4 19.8 %collective-permute-start.3 = (bf16[3,64,768]{2,1,0:T(8,128)(2,1)S(1)}, bf16[3,64,768]{2,1,0:T(8,128)(2,1)S(1)}, u32[]{:S(2)}, u32[]{:S(2)}) collective-permute-start(bf16[3,64,768]{2,1,0:T(8,128)(2,1)S(1)} %get-tuple-element.272.refs_0_), channel_id=1, source_target_pairs={{0,4},{2,6},{4,0},{6,2},{1,5},{3,7},{5,1},{7,3},{8,12},{10,14},{12... | collective-permute-start | bytes 884744 | tf_op jit(solution)/shard_map/ppermute | solution.py:18
  21.9 7.1 %collective-permute-start.4 = (bf16[64,1536]{1,0:T(8,128)(2,1)S(1)}, bf16[64,1536]{1,0:T(8,128)(2,1)S(1)}, u32[]{:S(2)}, u32[]{:S(2)}) collective-permute-start(bf16[64,1536]{1,0:T(8,128)(2,1)S(1)} %copy-done.90), channel_id=1, source_target_pairs={{8,0},{16,8},{24,16},{0,24},{9,1},{17,9},{25,17},{1,25},{10,2},{18... | collective-permute-start | bytes 589832 | tf_op jit(solution)/shard_map/ppermute | solution.py:23
  23.6 16.6 %collective-permute-start.5 = (bf16[64,1536]{1,0:T(8,128)(2,1)S(1)}, bf16[64,1536]{1,0:T(8,128)(2,1)S(1)}, u32[]{:S(2)}, u32[]{:S(2)}) collective-permute-start(bf16[64,1536]{1,0:T(8,128)(2,1)S(1)} %copy-done.90), channel_id=1, source_target_pairs={{16,0},{24,8},{0,16},{8,24},{17,1},{25,9},{1,17},{9,25},{18,2},{26... | collective-permute-start | bytes 589832 | tf_op jit(solution)/shard_map/ppermute | solution.py:23
  23.9 16.3 %collective-permute-start.6 = (bf16[64,1536]{1,0:T(8,128)(2,1)S(1)}, bf16[64,1536]{1,0:T(8,128)(2,1)S(1)}, u32[]{:S(2)}, u32[]{:S(2)}) collective-permute-start(bf16[64,1536]{1,0:T(8,128)(2,1)S(1)} %copy-done.90), channel_id=1, source_target_pairs={{24,0},{0,8},{8,16},{16,24},{25,1},{1,9},{9,17},{17,25},{26,2},{2,... | collective-permute-start | bytes 589832 | tf_op jit(solution)/shard_map/ppermute | solution.py:23
  41.6 2.3 collective-permute-start.7
  42.0 24.8 %collective-permute-start.8 = (bf16[3,64,1536]{2,1,0:T(8,128)(2,1)S(1)}, bf16[3,64,1536]{2,1,0:T(8,128)(2,1)S(1)}, u32[]{:S(2)}, u32[]{:S(2)}) collective-permute-start(bf16[3,64,1536]{2,1,0:T(8,128)(2,1)S(1)} %get-tuple-element.283.refs_0_), channel_id=1, source_target_pairs={{0,4},{2,6},{4,0},{6,2},{1,5},{3,7},{5,1},{7,3},{8,12},{10,14},{12... | collective-permute-start | bytes 1769480 | tf_op jit(solution)/shard_map/ppermute | solution.py:18
  51.6 15.2 %collective-permute-start.9 = (bf16[1,2,512,128]{3,2,1,0:T(8,128)(2,1)S(1)}, bf16[1,2,512,128]{3,2,1,0:T(8,128)(2,1)S(1)}, u32[]{:S(2)}, u32[]{:S(2)}) collective-permute-start(bf16[1,2,512,128]{3,2,1,0:T(8,128)(2,1)S(1)} %bitcast.100), channel_id=1, source_target_pairs={{0,4},{2,6},{4,0},{6,2},{1,5},{3,7},{5,1},{7,3},{8,12},{10,14},{12... | collective-permute-start | bytes 786440 | tf_op jit(solution)/shard_map/ppermute | solution.py:18
  52.2 5.2 %collective-permute-start.10 = (bf16[64,1024]{1,0:T(8,128)(2,1)S(1)}, bf16[64,1024]{1,0:T(8,128)(2,1)S(1)}, u32[]{:S(2)}, u32[]{:S(2)}) collective-permute-start(bf16[64,1024]{1,0:T(8,128)(2,1)S(1)} %copy-done.91), channel_id=1, source_target_pairs={{8,0},{16,8},{24,16},{0,24},{9,1},{17,9},{25,17},{1,25},{10,2},{18... | collective-permute-start | bytes 393224 | tf_op jit(solution)/shard_map/ppermute | solution.py:23
  52.6 14.2 %collective-permute-start.11 = (bf16[64,1024]{1,0:T(8,128)(2,1)S(1)}, bf16[64,1024]{1,0:T(8,128)(2,1)S(1)}, u32[]{:S(2)}, u32[]{:S(2)}) collective-permute-start(bf16[64,1024]{1,0:T(8,128)(2,1)S(1)} %copy-done.91), channel_id=1, source_target_pairs={{16,0},{24,8},{0,16},{8,24},{17,1},{25,9},{1,17},{9,25},{18,2},{26... | collective-permute-start | bytes 393224 | tf_op jit(solution)/shard_map/ppermute | solution.py:23
  54.9 11.9 %collective-permute-start.12 = (bf16[64,1024]{1,0:T(8,128)(2,1)S(1)}, bf16[64,1024]{1,0:T(8,128)(2,1)S(1)}, u32[]{:S(2)}, u32[]{:S(2)}) collective-permute-start(bf16[64,1024]{1,0:T(8,128)(2,1)S(1)} %copy-done.91), channel_id=1, source_target_pairs={{24,0},{0,8},{8,16},{16,24},{25,1},{1,9},{9,17},{17,25},{26,2},{2,... | collective-permute-start | bytes 393224 | tf_op jit(solution)/shard_map/ppermute | solution.py:23
  67.2 14.6 %collective-permute-start.13 = (bf16[6,64,1536]{2,1,0:T(8,128)(2,1)S(1)}, bf16[6,64,1536]{2,1,0:T(8,128)(2,1)S(1)}, u32[]{:S(2)}, u32[]{:S(2)}) collective-permute-start(bf16[6,64,1536]{2,1,0:T(8,128)(2,1)S(1)} %get-tuple-element.288.refs_2_), channel_id=1, source_target_pairs={{0,2},{2,0},{4,6},{6,4},{1,3},{3,1},{5,7},{7,5},{8,10},{10,8},{12,... | collective-permute-start | bytes 3538952 | tf_op jit(solution)/shard_map/ppermute | solution.py:18
  67.3 13.7 %collective-permute-start.14 = (bf16[2,2,512,128]{3,2,1,0:T(8,128)(2,1)S(1)}, bf16[2,2,512,128]{3,2,1,0:T(8,128)(2,1)S(1)}, u32[]{:S(2)}, u32[]{:S(2)}) collective-permute-start(bf16[2,2,512,128]{3,2,1,0:T(8,128)(2,1)S(1)} %get-tuple-element.289.refs_1_), channel_id=1, source_target_pairs={{0,2},{2,0},{4,6},{6,4},{1,3},{3,1},{5,7},{7,5},{8,10},{10,8},{12,... | collective-permute-start | bytes 1572872 | tf_op jit(solution)/shard_map/ppermute | solution.py:18
  67.8 11.0 %collective-permute-start.15 = (bf16[64,3072]{1,0:T(8,128)(2,1)S(1)}, bf16[64,3072]{1,0:T(8,128)(2,1)S(1)}, u32[]{:S(2)}, u32[]{:S(2)}) collective-permute-start(bf16[64,3072]{1,0:T(8,128)(2,1)S(1)} %copy-done.89), channel_id=1, source_target_pairs={{8,0},{16,8},{24,16},{0,24},{9,1},{17,9},{25,17},{1,25},{10,2},{18... | collective-permute-start | bytes 1179656 | tf_op jit(solution)/shard_map/ppermute | solution.py:23
  78.9 15.4 %collective-permute-start.17 = (bf16[64,3072]{1,0:T(8,128)(2,1)S(1)}, bf16[64,3072]{1,0:T(8,128)(2,1)S(1)}, u32[]{:S(2)}, u32[]{:S(2)}) collective-permute-start(bf16[64,3072]{1,0:T(8,128)(2,1)S(1)} %collective-permute-done.15.refs_5_), channel_id=1, source_target_pairs={{8,0},{16,8},{24,16},{0,24},{9,1},{17,9},{25,17},{1,25},{10,2},{18... | collective-permute-start | bytes 1179656 | tf_op jit(solution)/shard_map/ppermute | solution.py:23
  92.8 13.2 %collective-permute-start.16 = (bf16[1,2,144,768]{3,2,1,0:T(8,128)(2,1)S(1)}, bf16[1,2,144,768]{3,2,1,0:T(8,128)(2,1)S(1)}, u32[]{:S(2)}, u32[]{:S(2)}) collective-permute-start(bf16[1,2,144,768]{3,2,1,0:T(8,128)(2,1)S(1)} %bitcast.95), channel_id=1, source_target_pairs={{0,4},{2,6},{4,0},{6,2},{1,5},{3,7},{5,1},{7,3},{8,12},{10,14},{12... | collective-permute-start | bytes 1327112 | tf_op jit(solution)/shard_map/ppermute | solution.py:18
  94.3 12.0 %collective-permute-start.19 = (bf16[64,3072]{1,0:T(8,128)(2,1)S(1)}, bf16[64,3072]{1,0:T(8,128)(2,1)S(1)}, u32[]{:S(2)}, u32[]{:S(2)}) collective-permute-start(bf16[64,3072]{1,0:T(8,128)(2,1)S(1)} %collective-permute-done.17.refs_5_), channel_id=1, source_target_pairs={{8,0},{16,8},{24,16},{0,24},{9,1},{17,9},{25,17},{1,25},{10,2},{18... | collective-permute-start | bytes 1179656 | tf_op jit(solution)/shard_map/ppermute | solution.py:23
  94.5 18.1 %collective-permute-start.20 = (bf16[3,64,1024]{2,1,0:T(8,128)(2,1)S(1)}, bf16[3,64,1024]{2,1,0:T(8,128)(2,1)S(1)}, u32[]{:S(2)}, u32[]{:S(2)}) collective-permute-start(bf16[3,64,1024]{2,1,0:T(8,128)(2,1)S(1)} %get-tuple-element.310.refs_0_), channel_id=1, source_target_pairs={{0,4},{2,6},{4,0},{6,2},{1,5},{3,7},{5,1},{7,3},{8,12},{10,14},{12... | collective-permute-start | bytes 1179656 | tf_op jit(solution)/shard_map/ppermute | solution.py:18
  106.2 128.0 %copy-start.24 = (bf16[2,2,144,768]{3,2,1,0:T(8,128)(2,1)}, bf16[2,2,144,768]{3,2,1,0:T(8,128)(2,1)S(1)}, u32[]{:S(2)}) copy-start(bf16[2,2,144,768]{3,2,1,0:T(8,128)(2,1)S(1)} %get-tuple-element.309.refs_1_) | copy-start | bytes 2654212
  106.2 12.4 %collective-permute-start.18 = (bf16[2,2,144,768]{3,2,1,0:T(8,128)(2,1)S(1)}, bf16[2,2,144,768]{3,2,1,0:T(8,128)(2,1)}, u32[]{:S(2)}, u32[]{:S(2)}) collective-permute-start(bf16[2,2,144,768]{3,2,1,0:T(8,128)(2,1)S(1)} %get-tuple-element.309.refs_1_), channel_id=1, source_target_pairs={{0,2},{2,0},{4,6},{6,4},{1,3},{3,1},{5,7},{7,5},{8,10},{10,8},{12,... | collective-permute-start | bytes 2654216 | tf_op jit(solution)/shard_map/ppermute | solution.py:18
  113.5 7.7 %collective-permute-start.21 = (bf16[6,64,1024]{2,1,0:T(8,128)(2,1)}, bf16[6,64,1024]{2,1,0:T(8,128)(2,1)}, u32[]{:S(2)}, u32[]{:S(2)}) collective-permute-start(bf16[6,64,1024]{2,1,0:T(8,128)(2,1)} %get-tuple-element.317.refs_2_), channel_id=1, source_target_pairs={{0,2},{2,0},{4,6},{6,4},{1,3},{3,1},{5,7},{7,5},{8,10},{10,8},{12,... | collective-permute-start | bytes 2359304 | tf_op jit(solution)/shard_map/ppermute | solution.py:18
  117.1 28.4 %collective-permute-start.23 = (bf16[3,64,3072]{2,1,0:T(8,128)(2,1)S(1)}, bf16[3,64,3072]{2,1,0:T(8,128)(2,1)S(1)}, u32[]{:S(2)}, u32[]{:S(2)}) collective-permute-start(bf16[3,64,3072]{2,1,0:T(8,128)(2,1)S(1)} %get-tuple-element.331.refs_0_), channel_id=1, source_target_pairs={{0,4},{2,6},{4,0},{6,2},{1,5},{3,7},{5,1},{7,3},{8,12},{10,14},{12... | collective-permute-start | bytes 3538952 | tf_op jit(solution)/shard_map/ppermute | solution.py:18
  131.5 26.1 %collective-permute-start.27 = (bf16[512,1024]{1,0:T(8,128)(2,1)S(1)}, bf16[512,1024]{1,0:T(8,128)(2,1)S(1)}, u32[]{:S(2)}, u32[]{:S(2)}) collective-permute-start(bf16[512,1024]{1,0:T(8,128)(2,1)S(1)} %get-tuple-element.338.refs_1_), channel_id=1, source_target_pairs={{0,1},{1,0},{2,3},{3,2},{4,5},{5,4},{6,7},{7,6},{8,9},{9,8},{10,11... | collective-permute-start | bytes 3145736 | tf_op jit(solution)/shard_map/ppermute | solution.py:28
  145.7 3.8 collective-permute-start.24
  147.6 3.0 collective-permute-start.25
  147.7 4.1 collective-permute-start.26
  148.1 31.9 %collective-permute-start.22 = (bf16[512,1024]{1,0:T(8,128)(2,1)S(1)}, bf16[512,1024]{1,0:T(8,128)(2,1)S(1)}, u32[]{:S(2)}, u32[]{:S(2)}) collective-permute-start(bf16[512,1024]{1,0:T(8,128)(2,1)S(1)} %get-tuple-element.328.refs_1_), channel_id=1, source_target_pairs={{0,1},{1,0},{2,3},{3,2},{4,5},{5,4},{6,7},{7,6},{8,9},{9,8},{10,11... | collective-permute-start | bytes 3145736 | tf_op jit(solution)/shard_map/ppermute | solution.py:28
  168.4 33.4 %collective-permute-start.29 = (bf16[512,1024]{1,0:T(8,128)(2,1)S(1)}, bf16[512,1024]{1,0:T(8,128)(2,1)S(1)}, u32[]{:S(2)}, u32[]{:S(2)}) collective-permute-start(bf16[512,1024]{1,0:T(8,128)(2,1)S(1)} %get-tuple-element.348.refs_1_), channel_id=1, source_target_pairs={{0,1},{1,0},{2,3},{3,2},{4,5},{5,4},{6,7},{7,6},{8,9},{9,8},{10,11... | collective-permute-start | bytes 3145736 | tf_op jit(solution)/shard_map/ppermute | solution.py:28
  191.8 44.6 %copy-start = (f32[1024,1024]{1,0:T(8,128)}, f32[1024,1024]{1,0:T(8,128)S(1)}, u32[]{:S(2)}) copy-start(f32[1024,1024]{1,0:T(8,128)S(1)} %get-tuple-element.345.refs_0_) | copy-start | bytes 12582916
  206.5 15.9 %collective-permute-start.33 = (bf16[4,2,64,3072]{3,2,1,0:T(8,128)(2,1)S(1)}, bf16[4,2,64,3072]{3,2,1,0:T(8,128)(2,1)S(1)}, u32[]{:S(2)}, u32[]{:S(2)}) collective-permute-start(bf16[4,2,64,3072]{3,2,1,0:T(8,128)(2,1)S(1)} %get-tuple-element.367), channel_id=1, source_target_pairs={{0,2},{2,0},{4,6},{6,4},{1,3},{3,1},{5,7},{7,5},{8,10},{10,8},{12,... | collective-permute-start | bytes 9437192 | tf_op jit(solution)/shard_map/ppermute | solution.py:18
  206.6 29.9 %collective-permute-start.28 = (bf16[512,1024]{1,0:T(8,128)(2,1)}, bf16[512,1024]{1,0:T(8,128)(2,1)S(1)}, u32[]{:S(2)}, u32[]{:S(2)}) collective-permute-start(bf16[512,1024]{1,0:T(8,128)(2,1)} %get-tuple-element.347.refs_1_), channel_id=1, source_target_pairs={{0,1},{1,0},{2,3},{3,2},{4,5},{5,4},{6,7},{7,6},{8,9},{9,8},{10,11... | collective-permute-start | bytes 3145736 | tf_op jit(solution)/shard_map/ppermute | solution.py:28
  211.9 7.0 %collective-permute-start.30 = (bf16[1,1,128,768]{3,2,1,0:T(8,128)(2,1)S(1)}, bf16[1,1,128,768]{3,2,1,0:T(8,128)(2,1)S(1)}, u32[]{:S(2)}, u32[]{:S(2)}) collective-permute-start(bf16[1,1,128,768]{3,2,1,0:T(8,128)(2,1)S(1)} %bitcast.111), channel_id=1, source_target_pairs={{0,4},{2,6},{4,0},{6,2},{1,5},{3,7},{5,1},{7,3},{8,12},{10,14},{12... | collective-permute-start | bytes 589832 | tf_op jit(solution)/shard_map/ppermute | solution.py:18
  219.2 14.9 %collective-permute-start.31 = (bf16[2,1,128,768]{3,2,1,0:T(8,128)(2,1)S(1)}, bf16[2,1,128,768]{3,2,1,0:T(8,128)(2,1)S(1)}, u32[]{:S(2)}, u32[]{:S(2)}) collective-permute-start(bf16[2,1,128,768]{3,2,1,0:T(8,128)(2,1)S(1)} %get-tuple-element.363.refs_3_), channel_id=1, source_target_pairs={{0,2},{2,0},{4,6},{6,4},{1,3},{3,1},{5,7},{7,5},{8,10},{10,8},{12,... | collective-permute-start | bytes 1179656 | tf_op jit(solution)/shard_map/ppermute | solution.py:18
  222.3 11.2 %collective-permute-start.32 = (bf16[1,2,512,128]{3,2,1,0:T(8,128)(2,1)S(1)}, bf16[1,2,512,128]{3,2,1,0:T(8,128)(2,1)S(1)}, u32[]{:S(2)}, u32[]{:S(2)}) collective-permute-start(bf16[1,2,512,128]{3,2,1,0:T(8,128)(2,1)S(1)} %get-tuple-element.365), channel_id=1, source_target_pairs={{0,2},{2,0},{4,6},{6,4},{1,3},{3,1},{5,7},{7,5},{8,10},{10,8},{12,... | collective-permute-start | bytes 786440 | tf_op jit(solution)/shard_map/ppermute | solution.py:18
  224.4 48.6 %collective-permute-start.37 = (bf16[4,1,64,3072]{3,2,1,0:T(8,128)(2,1)S(1)}, bf16[4,1,64,3072]{3,2,1,0:T(8,128)(2,1)S(1)}, u32[]{:S(2)}, u32[]{:S(2)}) collective-permute-start(bf16[4,1,64,3072]{3,2,1,0:T(8,128)(2,1)S(1)} %get-tuple-element.387), channel_id=1, source_target_pairs={{0,4},{2,6},{4,0},{6,2},{1,5},{3,7},{5,1},{7,3},{8,12},{10,14},{12... | collective-permute-start | bytes 4718600 | tf_op jit(solution)/shard_map/ppermute | solution.py:18
  244.2 50.1 %collective-permute-start.34 = (bf16[1024,1024]{1,0:T(8,128)(2,1)S(1)}, bf16[1024,1024]{1,0:T(8,128)(2,1)S(1)}, u32[]{:S(2)}, u32[]{:S(2)}) collective-permute-start(bf16[1024,1024]{1,0:T(8,128)(2,1)S(1)} %get-tuple-element.375.refs_1_), channel_id=1, source_target_pairs={{0,1},{1,0},{2,3},{3,2},{4,5},{5,4},{6,7},{7,6},{8,9},{9,8},{10,11... | collective-permute-start | bytes 6291464 | tf_op jit(solution)/shard_map/ppermute | solution.py:28
  244.7 28.0 %collective-permute-start.35 = (bf16[1,1,128,768]{3,2,1,0:T(8,128)(2,1)S(1)}, bf16[1,1,128,768]{3,2,1,0:T(8,128)(2,1)S(1)}, u32[]{:S(2)}, u32[]{:S(2)}) collective-permute-start(bf16[1,1,128,768]{3,2,1,0:T(8,128)(2,1)S(1)} %bitcast.106), channel_id=1, source_target_pairs={{0,4},{2,6},{4,0},{6,2},{1,5},{3,7},{5,1},{7,3},{8,12},{10,14},{12... | collective-permute-start | bytes 589832 | tf_op jit(solution)/shard_map/ppermute | solution.py:18
  272.9 3.0 collective-permute-start.36
  302.1 11.0 %collective-permute-start.38 = (bf16[4,2,64,3072]{3,2,1,0:T(8,128)(2,1)S(1)}, bf16[4,2,64,3072]{3,2,1,0:T(8,128)(2,1)S(1)}, u32[]{:S(2)}, u32[]{:S(2)}) collective-permute-start(bf16[4,2,64,3072]{3,2,1,0:T(8,128)(2,1)S(1)} %get-tuple-element.403), channel_id=1, source_target_pairs={{0,2},{2,0},{4,6},{6,4},{1,3},{3,1},{5,7},{7,5},{8,10},{10,8},{12,... | collective-permute-start | bytes 9437192 | tf_op jit(solution)/shard_map/ppermute | solution.py:18
  302.9 5.5 %collective-permute-start.39 = (bf16[1,1,512,128]{3,2,1,0:T(8,128)(2,1)S(1)}, bf16[1,1,512,128]{3,2,1,0:T(8,128)(2,1)S(1)}, u32[]{:S(2)}, u32[]{:S(2)}) collective-permute-start(bf16[1,1,512,128]{3,2,1,0:T(8,128)(2,1)S(1)} %get-tuple-element.406), channel_id=1, source_target_pairs={{0,4},{2,6},{4,0},{6,2},{1,5},{3,7},{5,1},{7,3},{8,12},{10,14},{12... | collective-permute-start | bytes 393224 | tf_op jit(solution)/shard_map/ppermute | solution.py:18
  317.8 40.2 %collective-permute-start.46 = (bf16[4,1,64,3072]{3,2,1,0:T(8,128)(2,1)}, bf16[4,1,64,3072]{3,2,1,0:T(8,128)(2,1)}, u32[]{:S(2)}, u32[]{:S(2)}) collective-permute-start(bf16[4,1,64,3072]{3,2,1,0:T(8,128)(2,1)} %get-tuple-element.426), channel_id=1, source_target_pairs={{0,4},{2,6},{4,0},{6,2},{1,5},{3,7},{5,1},{7,3},{8,12},{10,14},{12... | collective-permute-start | bytes 4718600 | tf_op jit(solution)/shard_map/ppermute | solution.py:18
  319.5 24.3 %collective-permute-start.40 = (bf16[512,1024]{1,0:T(8,128)(2,1)}, bf16[512,1024]{1,0:T(8,128)(2,1)}, u32[]{:S(2)}, u32[]{:S(2)}) collective-permute-start(bf16[512,1024]{1,0:T(8,128)(2,1)} %get-tuple-element.411.refs_1_), channel_id=1, source_target_pairs={{0,1},{1,0},{2,3},{3,2},{4,5},{5,4},{6,7},{7,6},{8,9},{9,8},{10,11... | collective-permute-start | bytes 3145736 | tf_op jit(solution)/shard_map/ppermute | solution.py:28
  320.0 26.6 %collective-permute-start.42 = (bf16[64,3072]{1,0:T(8,128)(2,1)}, bf16[64,3072]{1,0:T(8,128)(2,1)S(1)}, u32[]{:S(2)}, u32[]{:S(2)}) collective-permute-start(bf16[64,3072]{1,0:T(8,128)(2,1)} %copy-done.55), channel_id=1, source_target_pairs={{8,0},{16,8},{24,16},{0,24},{9,1},{17,9},{25,17},{1,25},{10,2},{18... | collective-permute-start | bytes 1179656 | tf_op jit(solution)/shard_map/ppermute | solution.py:23
  320.5 33.8 %collective-permute-start.43 = (bf16[64,3072]{1,0:T(8,128)(2,1)}, bf16[64,3072]{1,0:T(8,128)(2,1)S(1)}, u32[]{:S(2)}, u32[]{:S(2)}) collective-permute-start(bf16[64,3072]{1,0:T(8,128)(2,1)} %copy-done.54), channel_id=1, source_target_pairs={{16,0},{24,8},{0,16},{8,24},{17,1},{25,9},{1,17},{9,25},{18,2},{26... | collective-permute-start | bytes 1179656 | tf_op jit(solution)/shard_map/ppermute | solution.py:23
  321.1 33.2 %collective-permute-start.44 = (bf16[64,3072]{1,0:T(8,128)(2,1)}, bf16[64,3072]{1,0:T(8,128)(2,1)S(1)}, u32[]{:S(2)}, u32[]{:S(2)}) collective-permute-start(bf16[64,3072]{1,0:T(8,128)(2,1)} %copy-done.53), channel_id=1, source_target_pairs={{24,0},{0,8},{8,16},{16,24},{25,1},{1,9},{9,17},{17,25},{26,2},{2,... | collective-permute-start | bytes 1179656 | tf_op jit(solution)/shard_map/ppermute | solution.py:23
  343.9 12.9 %collective-permute-start.41 = (bf16[1,2,512,128]{3,2,1,0:T(8,128)(2,1)S(1)}, bf16[1,2,512,128]{3,2,1,0:T(8,128)(2,1)S(1)}, u32[]{:S(2)}, u32[]{:S(2)}) collective-permute-start(bf16[1,2,512,128]{3,2,1,0:T(8,128)(2,1)S(1)} %get-tuple-element.415), channel_id=1, source_target_pairs={{0,2},{2,0},{4,6},{6,4},{1,3},{3,1},{5,7},{7,5},{8,10},{10,8},{12,... | collective-permute-start | bytes 786440 | tf_op jit(solution)/shard_map/ppermute | solution.py:18
  356.5 10.8 %collective-permute-start.48 = (bf16[1,64,3072]{2,1,0:T(8,128)(2,1)}, bf16[1,64,3072]{2,1,0:T(8,128)(2,1)}, u32[]{:S(2)}, u32[]{:S(2)}) collective-permute-start(bf16[1,64,3072]{2,1,0:T(8,128)(2,1)} %bitcast.40.refs_0_), channel_id=1, source_target_pairs={{0,4},{2,6},{4,0},{6,2},{1,5},{3,7},{5,1},{7,3},{8,12},{10,14},{12... | collective-permute-start | bytes 1179656 | tf_op jit(solution)/shard_map/ppermute | solution.py:18
  364.7 9.8 %collective-permute-start.47 = (bf16[64,3072]{1,0:T(8,128)(2,1)}, bf16[64,3072]{1,0:T(8,128)(2,1)}, u32[]{:S(2)}, u32[]{:S(2)}) collective-permute-start(bf16[64,3072]{1,0:T(8,128)(2,1)} %get-tuple-element.428), channel_id=1, source_target_pairs={{8,0},{16,8},{24,16},{0,24},{9,1},{17,9},{25,17},{1,25},{10,2},{18... | collective-permute-start | bytes 1179656 | tf_op jit(solution)/shard_map/ppermute | solution.py:23
  364.8 14.7 %collective-permute-start.45 = (bf16[1,1,512,128]{3,2,1,0:T(8,128)(2,1)}, bf16[1,1,512,128]{3,2,1,0:T(8,128)(2,1)S(1)}, u32[]{:S(2)}, u32[]{:S(2)}) collective-permute-start(bf16[1,1,512,128]{3,2,1,0:T(8,128)(2,1)} %get-tuple-element.423), channel_id=1, source_target_pairs={{0,4},{2,6},{4,0},{6,2},{1,5},{3,7},{5,1},{7,3},{8,12},{10,14},{12... | collective-permute-start | bytes 393224 | tf_op jit(solution)/shard_map/ppermute | solution.py:18
  371.9 43.9 %collective-permute-start.54 = (bf16[2,64,3072]{2,1,0:T(8,128)(2,1)}, bf16[2,64,3072]{2,1,0:T(8,128)(2,1)}, u32[]{:S(2)}, u32[]{:S(2)}) collective-permute-start(bf16[2,64,3072]{2,1,0:T(8,128)(2,1)} %get-tuple-element.455.refs_1_), channel_id=1, source_target_pairs={{0,2},{2,0},{4,6},{6,4},{1,3},{3,1},{5,7},{7,5},{8,10},{10,8},{12,... | collective-permute-start | bytes 2359304 | tf_op jit(solution)/shard_map/ppermute | solution.py:18
  389.8 9.8 %collective-permute-start.51 = (f32[1024]{0:T(1024)S(1)}, f32[1024]{0:T(1024)S(1)}, u32[]{:S(2)}, u32[]{:S(2)}) collective-permute-start(f32[1024]{0:T(1024)S(1)} %bitcast.134), channel_id=1, source_target_pairs={{0,1},{1,0},{2,3},{3,2},{4,5},{5,4},{6,7},{7,6},{8,9},{9,8},{10,11... | collective-permute-start | bytes 12296 | tf_op jit(solution)/shard_map/ppermute | solution.py:28
  391.4 10.9 %collective-permute-start.50 = (bf16[64,3072]{1,0:T(8,128)(2,1)}, bf16[64,3072]{1,0:T(8,128)(2,1)}, u32[]{:S(2)}, u32[]{:S(2)}) collective-permute-start(bf16[64,3072]{1,0:T(8,128)(2,1)} %get-tuple-element.437), channel_id=1, source_target_pairs={{8,0},{16,8},{24,16},{0,24},{9,1},{17,9},{25,17},{1,25},{10,2},{18... | collective-permute-start | bytes 1179656 | tf_op jit(solution)/shard_map/ppermute | solution.py:23
  393.9 23.8 %collective-permute-start.49 = (bf16[512,1024]{1,0:T(8,128)(2,1)}, bf16[512,1024]{1,0:T(8,128)(2,1)S(1)}, u32[]{:S(2)}, u32[]{:S(2)}) collective-permute-start(bf16[512,1024]{1,0:T(8,128)(2,1)} %get-tuple-element.434.refs_1_), channel_id=1, source_target_pairs={{0,1},{1,0},{2,3},{3,2},{4,5},{5,4},{6,7},{7,6},{8,9},{9,8},{10,11... | collective-permute-start | bytes 3145736 | tf_op jit(solution)/shard_map/ppermute | solution.py:28
  400.7 12.8 %collective-permute-start.52 = (bf16[4,2,64,512]{3,2,1,0:T(8,128)(2,1)}, bf16[4,2,64,512]{3,2,1,0:T(8,128)(2,1)S(1)}, u32[]{:S(2)}, u32[]{:S(2)}) collective-permute-start(bf16[4,2,64,512]{3,2,1,0:T(8,128)(2,1)} %get-tuple-element.570), channel_id=1, source_target_pairs={{0,2},{2,0},{4,6},{6,4},{1,3},{3,1},{5,7},{7,5},{8,10},{10,8},{12,... | collective-permute-start | bytes 1572872 | tf_op jit(solution)/shard_map/ppermute | solution.py:18
  405.9 16.0 %collective-permute-start.58 = (bf16[64,3072]{1,0:T(8,128)(2,1)S(1)}, bf16[64,3072]{1,0:T(8,128)(2,1)S(1)}, u32[]{:S(2)}, u32[]{:S(2)}) collective-permute-start(bf16[64,3072]{1,0:T(8,128)(2,1)S(1)} %get-tuple-element.462), channel_id=1, source_target_pairs={{8,0},{16,8},{24,16},{0,24},{9,1},{17,9},{25,17},{1,25},{10,2},{18... | collective-permute-start | bytes 1179656 | tf_op jit(solution)/shard_map/ppermute | solution.py:23
  414.2 7.1 %collective-permute-start.53 = (bf16[4,1,64,512]{3,2,1,0:T(8,128)(2,1)S(1)}, bf16[4,1,64,512]{3,2,1,0:T(8,128)(2,1)S(1)}, u32[]{:S(2)}, u32[]{:S(2)}) collective-permute-start(bf16[4,1,64,512]{3,2,1,0:T(8,128)(2,1)S(1)} %get-tuple-element.454), channel_id=1, source_target_pairs={{0,4},{2,6},{4,0},{6,2},{1,5},{3,7},{5,1},{7,3},{8,12},{10,14},{12... | collective-permute-start | bytes 786440 | tf_op jit(solution)/shard_map/ppermute | solution.py:18
  422.3 4.2 collective-permute-start.59
  422.9 5.0 %collective-permute-start.55 = (bf16[64,512]{1,0:T(8,128)(2,1)S(1)}, bf16[64,512]{1,0:T(8,128)(2,1)S(1)}, u32[]{:S(2)}, u32[]{:S(2)}) collective-permute-start(bf16[64,512]{1,0:T(8,128)(2,1)S(1)} %get-tuple-element.459), channel_id=1, source_target_pairs={{8,0},{16,8},{24,16},{0,24},{9,1},{17,9},{25,17},{1,25},{10,2},{18... | collective-permute-start | bytes 196616 | tf_op jit(solution)/shard_map/ppermute | solution.py:23
  425.2 5.2 %collective-permute-start.56 = (bf16[64,512]{1,0:T(8,128)(2,1)S(1)}, bf16[64,512]{1,0:T(8,128)(2,1)S(1)}, u32[]{:S(2)}, u32[]{:S(2)}) collective-permute-start(bf16[64,512]{1,0:T(8,128)(2,1)S(1)} %get-tuple-element.460), channel_id=1, source_target_pairs={{16,0},{24,8},{0,16},{8,24},{17,1},{25,9},{1,17},{9,25},{18,2},{26... | collective-permute-start | bytes 196616 | tf_op jit(solution)/shard_map/ppermute | solution.py:23
  425.2 6.1 %collective-permute-start.57 = (bf16[64,512]{1,0:T(8,128)(2,1)S(1)}, bf16[64,512]{1,0:T(8,128)(2,1)S(1)}, u32[]{:S(2)}, u32[]{:S(2)}) collective-permute-start(bf16[64,512]{1,0:T(8,128)(2,1)S(1)} %get-tuple-element.461), channel_id=1, source_target_pairs={{24,0},{0,8},{8,16},{16,24},{25,1},{1,9},{9,17},{17,25},{26,2},{2,... | collective-permute-start | bytes 196616 | tf_op jit(solution)/shard_map/ppermute | solution.py:23
  432.0 8.5 %collective-permute-start.60 = (bf16[1,64,3584]{2,1,0:T(8,128)(2,1)S(1)}, bf16[1,64,3584]{2,1,0:T(8,128)(2,1)S(1)}, u32[]{:S(2)}, u32[]{:S(2)}) collective-permute-start(bf16[1,64,3584]{2,1,0:T(8,128)(2,1)S(1)} %maximum_bitcast_fusion.refs_0_), channel_id=1, source_target_pairs={{0,4},{2,6},{4,0},{6,2},{1,5},{3,7},{5,1},{7,3},{8,12},{10,14},{12... | collective-permute-start | bytes 1376264 | tf_op jit(solution)/shard_map/ppermute | solution.py:18
  440.8 2.5 collective-permute-start.61
  (90 other events, 695.0 us)
